TPU v7x, 32 devices: a whole 2x2x4 slice. The times are simulated.
32 devices in a mesh: dp: 8 (over z, y), fsdp: 4 (over x, core).
Axes of the slice: x: 2, y: 2, z: 4, core: 2. Of those that a mesh axis runs over, the one named last changes fastest.
Arguments:
- frames: bfloat16 [16, 3072, 1024], P('dp', 'fsdp'), may hold values from -6 to 6
- lengths: int32 [16], P('dp'), may hold values from 1536 to 3072, as said below
- t_index: int32 [16], P('dp'), may hold values from 0 to 999
- w_ada: bfloat16 [1024, 6144], P(('dp', 'fsdp')), may hold values from -0.375 to 0.375
- b_ada: bfloat16 [6144], P(('dp', 'fsdp')), may hold values from -3 to 3
- w_query: bfloat16 [1024, 1024], P(('dp', 'fsdp')), may hold values from -0.1875 to 0.1875
- b_query: bfloat16 [1024], P(('dp', 'fsdp')), may hold values from -2 to 2
- w_key: bfloat16 [1024, 1024], P(('dp', 'fsdp')), may hold values from -0.1875 to 0.1875
- b_key: bfloat16 [1024], P(('dp', 'fsdp')), may hold values from -2 to 2
- w_value: bfloat16 [1024, 1024], P(('dp', 'fsdp')), may hold values from -0.1875 to 0.1875
- b_value: bfloat16 [1024], P(('dp', 'fsdp')), may hold values from -2 to 2
- w_out: bfloat16 [1024, 1024], P(('dp', 'fsdp')), may hold values from -0.75 to 0.75
- b_out: bfloat16 [1024], P(('dp', 'fsdp')), may hold values from -2 to 2
- w_up: bfloat16 [1024, 2048], P(('dp', 'fsdp')), may hold values from -0.1875 to 0.1875
- b_up: bfloat16 [2048], P(('dp', 'fsdp')), may hold values from -2 to 2
- w_down: bfloat16 [2048, 1024], P(('dp', 'fsdp')), may hold values from -0.125 to 0.125
- b_down: bfloat16 [1024], P(('dp', 'fsdp')), may hold values from -2 to 2
- grad_out: bfloat16 [16, 3072, 1024], P('dp', 'fsdp'), may hold values from -6 to 6
Outputs:
- mixed: bfloat16 [16, 3072, 1024], P('dp', 'fsdp')
- grad_frames: bfloat16 [16, 3072, 1024], P('dp', 'fsdp')
- grad_w_ada: float32 [1024, 6144], P(('dp', 'fsdp'))
- grad_b_ada: float32 [6144], P(('dp', 'fsdp'))
- grad_w_query: float32 [1024, 1024], P(('dp', 'fsdp'))
- grad_b_query: float32 [1024], P(('dp', 'fsdp'))
- grad_w_key: float32 [1024, 1024], P(('dp', 'fsdp'))
- grad_b_key: float32 [1024], P(('dp', 'fsdp'))
- grad_w_value: float32 [1024, 1024], P(('dp', 'fsdp'))
- grad_b_value: float32 [1024], P(('dp', 'fsdp'))
- grad_w_out: float32 [1024, 1024], P(('dp', 'fsdp'))
- grad_b_out: float32 [1024], P(('dp', 'fsdp'))
- grad_w_up: float32 [1024, 2048], P(('dp', 'fsdp'))
- grad_b_up: float32 [2048], P(('dp', 'fsdp'))
- grad_w_down: float32 [2048, 1024], P(('dp', 'fsdp'))
- grad_b_down: float32 [1024], P(('dp', 'fsdp'))
Inputs may be any that keep to these rules, and one draw needn't show every extreme that they name: `lengths`: in each aligned block of 2 slots (those of one index of dp) exactly one slot, drawn from the seed, has 3072 frames and the others have fewer; one slot of all has exactly half of 3072.
All inputs are finite; a program needn't handle non-finite values.
Results may differ from a plain program's by a relative error of at most 0.017.
The roundings to bfloat16 on the way count: a program that leaves them out, or rounds other values in their place, can miss the bound.
Values may be sent and summed in bfloat16 or wider, within the bound.
No kernel may reach another device: no remote copies, remote signals or barrier semaphores. Data moves between devices by JAX's collectives and lax.ppermute only.
A program may use at most 320 MiB of HBM per device.

v0:
```python
import math

import jax
import jax.numpy as jnp
from jax import lax
from jax.sharding import PartitionSpec as P

HDIM = 64


def matmul(left_side, right_side):
    return jnp.dot(left_side, right_side, preferred_element_type=jnp.float32)


def matmul_tn(left_side, right_side):
    return lax.dot_general(
        left_side, right_side, (((0,), (0,)), ((), ())), preferred_element_type=jnp.float32
    )


def matmul_nt(left_side, right_side):
    return lax.dot_general(
        left_side, right_side, (((1,), (1,)), ((), ())), preferred_element_type=jnp.float32
    )


def time_features(t_index, model_width):
    half_width = model_width // 2
    indices = jnp.arange(half_width).astype(jnp.float32)
    frequency = jnp.exp(indices * (-math.log(10000.0) / (half_width - 1)))
    angles = t_index.astype(jnp.float32)[:, None] * frequency[None, :]
    return jnp.concatenate([jnp.sin(angles), jnp.cos(angles)], axis=1)


def rotary_tables(first_frame, count_frames, head_size):
    half_size = head_size // 2
    inverse = jnp.exp(
        jnp.arange(half_size).astype(jnp.float32) * (-2.0 * math.log(10000.0) / head_size)
    )
    places = (first_frame + jnp.arange(count_frames, dtype=jnp.int32)).astype(jnp.float32)
    angles = places[:, None] * inverse[None, :]
    cosine = jnp.cos(angles)
    sine_table = jnp.sin(angles)
    return (
        jnp.concatenate([cosine, cosine], axis=1),
        jnp.concatenate([sine_table, sine_table], axis=1),
    )


def layer_norm(values):
    centered = values - jnp.mean(values, axis=-1, keepdims=True)
    return centered * lax.rsqrt(jnp.mean(centered * centered, axis=-1, keepdims=True) + 1e-06)


def gelu_tanh(values):
    return (
        0.5
        * values
        * (1.0 + jnp.tanh(0.7978845608028654 * (values + 0.044715 * values * values * values)))
    )


def modulated(values, shift_part, scale_part):
    return layer_norm(values) * (1.0 + scale_part[:, None, :]) + shift_part[:, None, :]


def rotate(values, cosine, sine_table):
    leading = values.shape[:-1]
    pieces = values.reshape(leading + (values.shape[-1] // HDIM, HDIM))
    half_size = HDIM // 2
    turned = jnp.concatenate([-pieces[..., half_size:], pieces[..., :half_size]], axis=-1)
    rotated = pieces * cosine[:, None, :] + turned * sine_table[:, None, :]
    return rotated.reshape(values.shape)


def rotate_back(values, cosine, sine_table):
    leading = values.shape[:-1]
    pieces = values.reshape(leading + (values.shape[-1] // HDIM, HDIM))
    half_size = HDIM // 2
    straight = pieces * cosine[:, None, :]
    swung = pieces * sine_table[:, None, :]
    turned = jnp.concatenate([swung[..., half_size:], -swung[..., :half_size]], axis=-1)
    return (straight + turned).reshape(values.shape)


def split_heads(values):
    return values.reshape(values.shape[0], values.shape[1] // HDIM, HDIM)


def masked_scores(queries, key_rows, key_mask):
    scores = jnp.einsum(
        "qhd,khd->hqk",
        split_heads(queries),
        split_heads(key_rows),
        preferred_element_type=jnp.float32,
    ) * HDIM ** (-0.5)
    return jnp.where(key_mask[None, None, :], scores, -1e30)


def attend_block(queries, key_rows, value_rows, key_mask):
    scores = masked_scores(queries, key_rows, key_mask)
    row_max = jnp.max(scores, axis=2, keepdims=True)
    weights = jnp.exp(scores - row_max)
    totals = jnp.sum(weights, axis=2, keepdims=True)
    probabilities = (weights / totals).astype(jnp.bfloat16)
    mixed_heads = jnp.einsum(
        "hqk,khd->qhd", probabilities, split_heads(value_rows), preferred_element_type=jnp.float32
    )
    log_total = jnp.transpose((row_max + jnp.log(totals))[:, :, 0])
    return (mixed_heads.reshape(queries.shape), log_total)


def block_grads(queries, key_rows, value_rows, d_heads, log_total, key_mask):
    scores = masked_scores(queries, key_rows, key_mask)
    probabilities = jnp.exp(scores - jnp.transpose(log_total)[:, :, None])
    d_probs = jnp.einsum(
        "qhd,khd->hqk",
        split_heads(d_heads),
        split_heads(value_rows),
        preferred_element_type=jnp.float32,
    )
    delta_sum = jnp.sum(probabilities * d_probs, axis=2, keepdims=True)
    d_scores = (probabilities * (d_probs - delta_sum)).astype(jnp.bfloat16)
    factor = HDIM ** (-0.5)
    d_query = (
        jnp.einsum(
            "hqk,khd->qhd", d_scores, split_heads(key_rows), preferred_element_type=jnp.float32
        )
        * factor
    )
    d_key = (
        jnp.einsum(
            "hqk,qhd->khd", d_scores, split_heads(queries), preferred_element_type=jnp.float32
        )
        * factor
    )
    d_value = jnp.einsum(
        "hqk,qhd->khd",
        probabilities.astype(jnp.bfloat16),
        split_heads(d_heads),
        preferred_element_type=jnp.float32,
    )
    return (
        d_query.reshape(queries.shape),
        d_key.reshape(key_rows.shape),
        d_value.reshape(value_rows.shape),
    )


def exchanged_attention(arrived, lengths):
    head_q, head_k, head_v = arrived
    row_count, key_span, col_count = head_q.shape
    block_rows = math.gcd(key_span, 512)
    key_mask = jnp.arange(key_span, dtype=jnp.int32)[None, :] < lengths[:, None]

    def one_slot(inputs):
        queries, key_rows, value_rows, slot_mask = inputs
        q_blocks = queries.reshape(key_span // block_rows, block_rows, col_count)
        mixed_f32, log_total = lax.map(
            lambda q_block: attend_block(q_block, key_rows, value_rows, slot_mask), q_blocks
        )
        return (
            mixed_f32.astype(jnp.bfloat16).reshape(key_span, col_count),
            log_total.reshape(key_span, col_count // HDIM),
        )

    heads_low, log_total = lax.map(one_slot, (head_q, head_k, head_v, key_mask))
    return (heads_low, (head_q, head_k, head_v, key_mask, log_total))


def exchanged_grads(retained, d_arrived):
    head_q, head_k, head_v, key_mask, log_total = retained
    row_count, key_span, col_count = head_q.shape
    block_rows = math.gcd(key_span, 512)
    block_count = key_span // block_rows
    cosine, sine_table = rotary_tables(0, key_span, HDIM)

    def one_slot(inputs):
        queries, key_rows, value_rows, d_rows, lse_rows, slot_mask = inputs

        def advance(running, block_in):
            q_block, d_block, lse_block = block_in
            d_query, d_key, d_value = block_grads(
                q_block, key_rows, value_rows, d_block, lse_block, slot_mask
            )
            return ((running[0] + d_key, running[1] + d_value), d_query)

        zero_rows = jnp.zeros((key_span, col_count), jnp.float32)
        (d_key, d_value), d_query = lax.scan(
            advance,
            (zero_rows, zero_rows),
            (
                queries.reshape(block_count, block_rows, col_count),
                d_rows.reshape(block_count, block_rows, col_count),
                lse_rows.reshape(block_count, block_rows, col_count // HDIM),
            ),
        )
        dq_low = rotate_back(d_query.reshape(key_span, col_count), cosine, sine_table).astype(
            jnp.bfloat16
        )
        dk_low = rotate_back(d_key, cosine, sine_table).astype(jnp.bfloat16)
        return (dq_low, dk_low, d_value.astype(jnp.bfloat16))

    return lax.map(one_slot, (head_q, head_k, head_v, d_arrived, log_total, key_mask))


def attend(q_rot, k_rot, values, lengths):
    arrived = (
        lax.all_to_all(q_rot, "fsdp", split_axis=2, concat_axis=1, tiled=True),
        lax.all_to_all(k_rot, "fsdp", split_axis=2, concat_axis=1, tiled=True),
        lax.all_to_all(values, "fsdp", split_axis=2, concat_axis=1, tiled=True),
    )
    heads_low, retained = exchanged_attention(arrived, lengths)
    return (lax.all_to_all(heads_low, "fsdp", split_axis=1, concat_axis=2, tiled=True), retained)


def forward_pass(weights, frames, lengths, t_index, first_frame):
    (
        w_ada,
        b_ada,
        w_query,
        b_query,
        w_key,
        b_key,
        w_value,
        b_value,
        w_out,
        b_out,
        w_up,
        b_up,
        w_down,
        b_down,
    ) = weights
    row_count, local_count, model_width = frames.shape
    shape_three = (row_count, local_count, model_width)
    cosine, sine_table = rotary_tables(first_frame, local_count, HDIM)
    active = jax.nn.silu(time_features(t_index, model_width)).astype(jnp.bfloat16)
    modulation = matmul(active, w_ada) + b_ada.astype(jnp.float32)
    shift_one, scale_one, gate_one, shift_two, scale_two, gate_two = jnp.split(
        modulation, 6, axis=1
    )
    inputs_f32 = frames.astype(jnp.float32)
    h_one = modulated(inputs_f32, shift_one, scale_one).astype(jnp.bfloat16)
    flat_one = h_one.reshape(row_count * local_count, model_width)
    queries = (matmul(flat_one, w_query) + b_query.astype(jnp.float32)).reshape(shape_three)
    keys_pre = (matmul(flat_one, w_key) + b_key.astype(jnp.float32)).reshape(shape_three)
    values = (
        (matmul(flat_one, w_value) + b_value.astype(jnp.float32))
        .astype(jnp.bfloat16)
        .reshape(shape_three)
    )
    q_rot = rotate(queries, cosine, sine_table).astype(jnp.bfloat16)
    k_rot = rotate(keys_pre, cosine, sine_table).astype(jnp.bfloat16)
    heads_out, retained = attend(q_rot, k_rot, values, lengths)
    query_mask = (first_frame + jnp.arange(local_count, dtype=jnp.int32))[None, :] < lengths[
        :, None
    ]
    branch = (
        matmul(heads_out.reshape(-1, model_width), w_out) + b_out.astype(jnp.float32)
    ).reshape(shape_three)
    branch = branch * query_mask[:, :, None].astype(jnp.float32)
    residual = inputs_f32 + gate_one[:, None, :] * branch
    h_two = modulated(residual, shift_two, scale_two).astype(jnp.bfloat16)
    up_proj = matmul(h_two.reshape(-1, model_width), w_up) + b_up.astype(jnp.float32)
    hidden = gelu_tanh(up_proj).astype(jnp.bfloat16)
    ff_out = (matmul(hidden, w_down) + b_down.astype(jnp.float32)).reshape(shape_three)
    mixed = residual + gate_two[:, None, :] * ff_out
    return (
        active,
        modulation,
        inputs_f32,
        h_one,
        retained,
        query_mask,
        heads_out,
        branch,
        residual,
        h_two,
        up_proj,
        hidden,
        ff_out,
        mixed,
    )


def body(
    frames,
    lengths,
    t_index,
    w_ada,
    b_ada,
    w_query,
    b_query,
    w_key,
    b_key,
    w_value,
    b_value,
    w_out,
    b_out,
    w_up,
    b_up,
    w_down,
    b_down,
    grad_out,
):
    shards = (
        w_ada,
        b_ada,
        w_query,
        b_query,
        w_key,
        b_key,
        w_value,
        b_value,
        w_out,
        b_out,
        w_up,
        b_up,
        w_down,
        b_down,
    )
    row_count, local_count, model_width = frames.shape
    shape_three = (row_count, local_count, model_width)
    first_frame = lax.axis_index("fsdp") * local_count
    weights = (
        lax.all_gather(shards[0], ("dp", "fsdp"), axis=0, tiled=True),
        lax.all_gather(shards[1], ("dp", "fsdp"), axis=0, tiled=True),
        lax.all_gather(shards[2], ("dp", "fsdp"), axis=0, tiled=True),
        lax.all_gather(shards[3], ("dp", "fsdp"), axis=0, tiled=True),
        lax.all_gather(shards[4], ("dp", "fsdp"), axis=0, tiled=True),
        lax.all_gather(shards[5], ("dp", "fsdp"), axis=0, tiled=True),
        lax.all_gather(shards[6], ("dp", "fsdp"), axis=0, tiled=True),
        lax.all_gather(shards[7], ("dp", "fsdp"), axis=0, tiled=True),
        lax.all_gather(shards[8], ("dp", "fsdp"), axis=0, tiled=True),
        lax.all_gather(shards[9], ("dp", "fsdp"), axis=0, tiled=True),
        lax.all_gather(shards[10], ("dp", "fsdp"), axis=0, tiled=True),
        lax.all_gather(shards[11], ("dp", "fsdp"), axis=0, tiled=True),
        lax.all_gather(shards[12], ("dp", "fsdp"), axis=0, tiled=True),
        lax.all_gather(shards[13], ("dp", "fsdp"), axis=0, tiled=True),
    )
    mixed = forward_pass(weights, frames, lengths, t_index, first_frame)[13].astype(jnp.bfloat16)
    weights = (
        lax.all_gather(shards[0], ("dp", "fsdp"), axis=0, tiled=True),
        lax.all_gather(shards[1], ("dp", "fsdp"), axis=0, tiled=True),
        lax.all_gather(shards[2], ("dp", "fsdp"), axis=0, tiled=True),
        lax.all_gather(shards[3], ("dp", "fsdp"), axis=0, tiled=True),
        lax.all_gather(shards[4], ("dp", "fsdp"), axis=0, tiled=True),
        lax.all_gather(shards[5], ("dp", "fsdp"), axis=0, tiled=True),
        lax.all_gather(shards[6], ("dp", "fsdp"), axis=0, tiled=True),
        lax.all_gather(shards[7], ("dp", "fsdp"), axis=0, tiled=True),
        lax.all_gather(shards[8], ("dp", "fsdp"), axis=0, tiled=True),
        lax.all_gather(shards[9], ("dp", "fsdp"), axis=0, tiled=True),
        lax.all_gather(shards[10], ("dp", "fsdp"), axis=0, tiled=True),
        lax.all_gather(shards[11], ("dp", "fsdp"), axis=0, tiled=True),
        lax.all_gather(shards[12], ("dp", "fsdp"), axis=0, tiled=True),
        lax.all_gather(shards[13], ("dp", "fsdp"), axis=0, tiled=True),
    )
    stored = forward_pass(weights, frames, lengths, t_index, first_frame)
    (
        active,
        modulation,
        inputs_f32,
        h_one,
        retained,
        query_mask,
        heads_out,
        branch,
        residual,
        h_two,
        up_proj,
        hidden,
        ff_out,
        unused_out,
    ) = stored
    (
        w_ada,
        b_ada,
        w_query,
        b_query,
        w_key,
        b_key,
        w_value,
        b_value,
        w_out,
        b_out,
        w_up,
        b_up,
        w_down,
        b_down,
    ) = weights
    shift_one, scale_one, gate_one, shift_two, scale_two, gate_two = jnp.split(
        modulation, 6, axis=1
    )
    d_mixed = grad_out.astype(jnp.float32)
    d_ff = (d_mixed * gate_two[:, None, :]).astype(jnp.bfloat16).reshape(-1, model_width)
    d_gate_two = jnp.sum(d_mixed * ff_out, axis=1)
    g_w_down = matmul_tn(hidden, d_ff)
    g_b_down = jnp.sum(d_ff.astype(jnp.float32), axis=0)
    d_hidden = matmul_nt(d_ff, w_down)
    d_up = jax.vjp(gelu_tanh, up_proj)[1](d_hidden)[0].astype(jnp.bfloat16)
    g_w_up = matmul_tn(h_two.reshape(-1, model_width), d_up)
    g_b_up = jnp.sum(d_up.astype(jnp.float32), axis=0)
    d_h_two = matmul_nt(d_up, w_up).reshape(shape_three)
    d_residual, d_shift_two, d_scale_two = jax.vjp(modulated, residual, shift_two, scale_two)[1](
        d_h_two
    )
    d_residual = d_residual + d_mixed
    d_branch = d_residual * gate_one[:, None, :] * query_mask[:, :, None].astype(jnp.float32)
    d_branch = d_branch.astype(jnp.bfloat16).reshape(-1, model_width)
    d_gate_one = jnp.sum(d_residual * branch, axis=1)
    g_w_out = matmul_tn(heads_out.reshape(-1, model_width), d_branch)
    g_b_out = jnp.sum(d_branch.astype(jnp.float32), axis=0)
    d_heads = matmul_nt(d_branch, w_out).astype(jnp.bfloat16).reshape(shape_three)
    d_arrived = lax.all_to_all(d_heads, "fsdp", split_axis=2, concat_axis=1, tiled=True)
    dq_heads, dk_heads, dv_heads = exchanged_grads(retained, d_arrived)
    dq_low, dk_low, dv_low = (
        lax.all_to_all(dq_heads, "fsdp", split_axis=1, concat_axis=2, tiled=True),
        lax.all_to_all(dk_heads, "fsdp", split_axis=1, concat_axis=2, tiled=True),
        lax.all_to_all(dv_heads, "fsdp", split_axis=1, concat_axis=2, tiled=True),
    )
    dq_low = dq_low.reshape(-1, model_width)
    dk_low = dk_low.reshape(-1, model_width)
    dv_low = dv_low.reshape(-1, model_width)
    flat_one = h_one.reshape(-1, model_width)
    g_w_query = matmul_tn(flat_one, dq_low)
    g_b_query = jnp.sum(dq_low.astype(jnp.float32), axis=0)
    g_w_key = matmul_tn(flat_one, dk_low)
    g_b_key = jnp.sum(dk_low.astype(jnp.float32), axis=0)
    g_w_value = matmul_tn(flat_one, dv_low)
    g_b_value = jnp.sum(dv_low.astype(jnp.float32), axis=0)
    d_h_one = (
        matmul_nt(dq_low, w_query) + matmul_nt(dk_low, w_key) + matmul_nt(dv_low, w_value)
    ).reshape(shape_three)
    d_inputs, d_shift_one, d_scale_one = jax.vjp(modulated, inputs_f32, shift_one, scale_one)[1](
        d_h_one
    )
    grad_frames = (d_inputs + d_residual).astype(jnp.bfloat16)
    d_modulation = jnp.concatenate(
        [d_shift_one, d_scale_one, d_gate_one, d_shift_two, d_scale_two, d_gate_two], axis=1
    )
    g_w_ada = lax.dot_general(
        active.astype(jnp.float32),
        d_modulation,
        (((0,), (0,)), ((), ())),
        precision=lax.Precision.HIGHEST,
        preferred_element_type=jnp.float32,
    )
    g_b_ada = jnp.sum(d_modulation, axis=0)
    summed = (
        lax.psum_scatter(g_w_ada, ("dp", "fsdp"), scatter_dimension=0, tiled=True),
        lax.psum_scatter(g_b_ada, ("dp", "fsdp"), scatter_dimension=0, tiled=True),
        lax.psum_scatter(g_w_query, ("dp", "fsdp"), scatter_dimension=0, tiled=True),
        lax.psum_scatter(g_b_query, ("dp", "fsdp"), scatter_dimension=0, tiled=True),
        lax.psum_scatter(g_w_key, ("dp", "fsdp"), scatter_dimension=0, tiled=True),
        lax.psum_scatter(g_b_key, ("dp", "fsdp"), scatter_dimension=0, tiled=True),
        lax.psum_scatter(g_w_value, ("dp", "fsdp"), scatter_dimension=0, tiled=True),
        lax.psum_scatter(g_b_value, ("dp", "fsdp"), scatter_dimension=0, tiled=True),
        lax.psum_scatter(g_w_out, ("dp", "fsdp"), scatter_dimension=0, tiled=True),
        lax.psum_scatter(g_b_out, ("dp", "fsdp"), scatter_dimension=0, tiled=True),
        lax.psum_scatter(g_w_up, ("dp", "fsdp"), scatter_dimension=0, tiled=True),
        lax.psum_scatter(g_b_up, ("dp", "fsdp"), scatter_dimension=0, tiled=True),
        lax.psum_scatter(g_w_down, ("dp", "fsdp"), scatter_dimension=0, tiled=True),
        lax.psum_scatter(g_b_down, ("dp", "fsdp"), scatter_dimension=0, tiled=True),
    )
    return (mixed, grad_frames) + tuple(summed)


def solution(mesh):
    return jax.shard_map(
        body,
        mesh=mesh,
        in_specs=(
            P("dp", "fsdp", None),
            P("dp"),
            P("dp"),
            P(("dp", "fsdp"), None),
            P(("dp", "fsdp")),
            P(("dp", "fsdp"), None),
            P(("dp", "fsdp")),
            P(("dp", "fsdp"), None),
            P(("dp", "fsdp")),
            P(("dp", "fsdp"), None),
            P(("dp", "fsdp")),
            P(("dp", "fsdp"), None),
            P(("dp", "fsdp")),
            P(("dp", "fsdp"), None),
            P(("dp", "fsdp")),
            P(("dp", "fsdp"), None),
            P(("dp", "fsdp")),
            P("dp", "fsdp", None),
        ),
        out_specs=(
            P("dp", "fsdp", None),
            P("dp", "fsdp", None),
            P(("dp", "fsdp"), None),
            P(("dp", "fsdp")),
            P(("dp", "fsdp"), None),
            P(("dp", "fsdp")),
            P(("dp", "fsdp"), None),
            P(("dp", "fsdp")),
            P(("dp", "fsdp"), None),
            P(("dp", "fsdp")),
            P(("dp", "fsdp"), None),
            P(("dp", "fsdp")),
            P(("dp", "fsdp"), None),
            P(("dp", "fsdp")),
            P(("dp", "fsdp"), None),
            P(("dp", "fsdp")),
        ),
        check_vma=False,
    )
```

profile of v0, /device:TPU:0, one launch (start us, length us, event | category | flops | bytes accessed | tf_op | source)
XLA Modules:
  0.0 3328.5 jit_solution(12749842496944265006)
XLA Ops:
  18.9 43.3 %all-reduce.15 = (bf16[6144]{0:T(1024)(128)(2,1)S(1)}, bf16[1024]{0:T(1024)(128)(2,1)S(1)}, bf16[1024]{0:T(1024)(128)(2,1)S(1)}, bf16[1024]{0:T(1024)(128)(2,1)S...) all-reduce(bf16[6144]{0:T(1024)(128)(2,1)S(1)} %dynamic-update-slic, ...), channel_id=1, replica_groups=mesh['dp'=8,'fsdp'=4] {'dp','fsdp'}, use_global_device_ids=true, to_apply=%add | all-reduce | flops 13312 | bytes 53248
  62.8 47.2 %all-gather.8.cloned.1.call-done = bf16[1024,6144]{1,0:T(8,128)(2,1)} async-done(((bf16[32,6144]{1,0:T(8,128)(2,1)}), bf16[1024,6144]{1,0:T(8,128)(2,1)}) %all-gather.8.cloned.1.call-update) | async-done | bytes 12582928 | tf_op jit(solution)/shard_map/all_gather | solution.py:326
  119.7 47.9 %all-gather.14.cloned.1.call-done = bf16[1024,1024]{1,0:T(8,128)(2,1)} async-done(((bf16[32,1024]{1,0:T(8,128)(2,1)}), bf16[1024,1024]{1,0:T(8,128)(2,1)}) %all-gather.14.cloned.1.call-update) | async-done | bytes 2097168 | tf_op jit(solution)/shard_map/all_gather | solution.py:332
  184.5 45.2 %all-gather.10.cloned.1.call-done = bf16[1024,1024]{1,0:T(8,128)(2,1)} async-done(((bf16[32,1024]{1,0:T(8,128)(2,1)}), bf16[1024,1024]{1,0:T(8,128)(2,1)}) %all-gather.10.cloned.1.call-update) | async-done | bytes 2097168 | tf_op jit(solution)/shard_map/all_gather | solution.py:328
  259.6 28.1 all-gather.12.cloned.1.call-done
  396.6 37.4 %all-to-all-done.1 = bf16[2,768,1024]{1,0,2:T(2,128)(2,1)} async-done(((bf16[2,768,1024]{1,0,2:T(2,128)(2,1)}), bf16[2,768,1024]{1,0,2:T(2,128)(2,1)}, u32[]{:S(2)}, u32[]{:S(2)}) %all-to-all-start.1) | async-done | bytes 3145760 | tf_op jit(solution)/shard_map/all_to_all | solution.py:210
  463.4 15.8 all-to-all-done
  487.1 395.4 %while.76 = (s32[]{:T(128)}, bf16[2,3072,256]{2,1,0:T(8,128)(2,1)}, f32[2,3072,4]{1,2,0:T(4,128)}, bf16[2,3072,256]{2,1,0:T(8,128)(2,1)}, bf16[2,3072,256]{1,2,0...) while((s32[]{:T(128)}, bf16[2,3072,256]{2,1,0:T(8,128)(2,1)}, ...), condition=%wide.region_15.16_spmd, body=%wide.region_10.15_spmd.sunk | while | flops 1686108160 | bytes 198147520 | solution.py:167
  493.6 188.6 %while.80 = (s32[]{:T(128)}, bf16[6,512,256]{1,2,0:T(8,128)(2,1)}, f32[6,512,4]{1,2,0:T(4,128)S(1)}, pred[3072]{0:T(1024)(128)(4,1)S(1)}, bf16[6,512,256]{2,1,0:...) while((s32[]{:T(128)}, bf16[6,512,256]{1,2,0:T(8,128)(2,1)}, ...), condition=%wide.region_14.14_spmd, body=%wide.region_11.13_spmd.sunk | while | flops 1686108160 | bytes 181478528 | solution.py:159
  691.3 188.2 %while.80 = (s32[]{:T(128)}, bf16[6,512,256]{1,2,0:T(8,128)(2,1)}, f32[6,512,4]{1,2,0:T(4,128)S(1)}, pred[3072]{0:T(1024)(128)(4,1)S(1)}, bf16[6,512,256]{2,1,0:...) while((s32[]{:T(128)}, bf16[6,512,256]{1,2,0:T(8,128)(2,1)}, ...), condition=%wide.region_14.14_spmd, body=%wide.region_11.13_spmd.sunk | while | flops 1686108160 | bytes 181478528 | solution.py:159
  899.1 33.4 %all-to-all-done.4 = bf16[2,3072,256]{2,0,1:T(2,128)(2,1)} async-done(((bf16[2,3072,256]{2,0,1:T(2,128)(2,1)}), bf16[2,3072,256]{2,0,1:T(2,128)(2,1)}, u32[]{:S(2)}, u32[]{:S(2)}) %all-to-all-start.4) | async-done | bytes 3145760 | tf_op jit(solution)/shard_map/all_to_all | solution.py:214
  963.8 21.4 convert_reduce_fusion
  999.7 14.2 convolution_add_fusion.1
  1045.2 36.1 %all-to-all-done.5 = bf16[2,768,1024]{1,0,2:T(2,128)(2,1)S(1)} async-done(((bf16[2,768,1024]{1,0,2:T(2,128)(2,1)}), bf16[2,768,1024]{1,0,2:T(2,128)(2,1)S(1)}, u32[]{:S(2)}, u32[]{:S(2)}) %all-to-all-start.5) | async-done | bytes 3145760 | tf_op jit(solution)/shard_map/all_to_all | solution.py:414
  1089.1 1200.3 %while.78 = (s32[]{:T(128)}, bf16[2,3072,256]{2,1,0:T(8,128)(2,1)}, bf16[2,3072,256]{1,2,0:T(8,128)(2,1)}, bf16[2,3072,256]{1,2,0:T(8,128)(2,1)}, bf16[2,3072,25...) while((s32[]{:T(128)}, bf16[2,3072,256]{2,1,0:T(8,128)(2,1)}, ...), condition=%wide.region_24.25_spmd, body=%wide.region_20.24_spmd.sunk | while | flops 4134402048 | bytes 507469792 | solution.py:204
  1103.2 548.3 %while.81 = (s32[]{:T(128)}, f32[3072,256]{0,1:T(8,128)}, f32[3072,256]{0,1:T(8,128)}, f32[6,512,256]{1,2,0:T(8,128)}, bf16[6,512,256]{2,1,0:T(8,128)(2,1)}, /*i...) while((s32[]{:T(128)}, f32[3072,256]{0,1:T(8,128)}, ...), condition=%wide.region_23.23_spmd.clone, body=%wide.region_21.22_spmd.clone.sunk | while | flops 4124964864 | bytes 289473888 | solution.py:189
  1130.8 20.8 multiply_reduce_fusion.7
  1151.6 22.0 multiply_convert_fusion.7
  1222.6 20.8 multiply_reduce_fusion.7
  1243.4 21.6 multiply_convert_fusion.7
  1313.8 20.8 multiply_reduce_fusion.7
  1334.6 21.6 multiply_convert_fusion.7
  1405.1 20.8 multiply_reduce_fusion.7
  1425.9 21.6 multiply_convert_fusion.7
  1496.4 20.8 multiply_reduce_fusion.7
  1517.2 21.6 multiply_convert_fusion.7
  1587.7 20.8 multiply_reduce_fusion.7
  1608.5 21.6 multiply_convert_fusion.7
  1703.4 547.7 %while.81 = (s32[]{:T(128)}, f32[3072,256]{0,1:T(8,128)}, f32[3072,256]{0,1:T(8,128)}, f32[6,512,256]{1,2,0:T(8,128)}, bf16[6,512,256]{2,1,0:T(8,128)(2,1)}, /*i...) while((s32[]{:T(128)}, f32[3072,256]{0,1:T(8,128)}, ...), condition=%wide.region_23.23_spmd.clone, body=%wide.region_21.22_spmd.clone.sunk | while | flops 4124964864 | bytes 289473888 | solution.py:189
  1730.8 20.8 multiply_reduce_fusion.7
  1751.6 21.6 multiply_convert_fusion.7
  1822.1 20.8 multiply_reduce_fusion.7
  1842.9 21.6 multiply_convert_fusion.7
  1913.3 20.8 multiply_reduce_fusion.7
  1934.1 21.6 multiply_convert_fusion.7
  2004.6 20.8 multiply_reduce_fusion.7
  2025.4 21.6 multiply_convert_fusion.7
  2095.9 20.8 multiply_reduce_fusion.7
  2116.7 21.6 multiply_convert_fusion.7
  2187.2 20.8 multiply_reduce_fusion.7
  2208.0 21.6 multiply_convert_fusion.7
  2296.6 39.4 %all_to_all.162 = bf16[2,3072,256]{2,0,1:T(2,128)(2,1)S(1)} all-to-all(bf16[2,3072,256]{2,0,1:T(2,128)(2,1)S(1)} %copy.167), channel_id=1, replica_groups=mesh['dp'=8,'fsdp'=4] {'fsdp'}, dimensions={1} | all-to-all | bytes 6291456 | tf_op jit(solution)/shard_map/all_to_all | solution.py:418
  2346.0 19.1 copy.165
  2365.1 55.9 %all_to_all.163 = bf16[2,3072,256]{2,0,1:T(2,128)(2,1)S(1)} all-to-all(bf16[2,3072,256]{2,0,1:T(2,128)(2,1)S(1)} %copy.165), channel_id=1, replica_groups=mesh['dp'=8,'fsdp'=4] {'fsdp'}, dimensions={1} | all-to-all | bytes 6291456 | tf_op jit(solution)/shard_map/all_to_all | solution.py:417
  2438.2 51.5 %all_to_all.164 = bf16[2,3072,256]{2,0,1:T(2,128)(2,1)S(1)} all-to-all(bf16[2,3072,256]{2,0,1:T(2,128)(2,1)S(1)} %copy.169), channel_id=1, replica_groups=mesh['dp'=8,'fsdp'=4] {'fsdp'}, dimensions={1} | all-to-all | bytes 6291456 | tf_op jit(solution)/shard_map/all_to_all | solution.py:419
  2528.7 323.3 %while.74 = (s32[]{:T(128)}, bf16[2,3072,256]{2,1,0:T(8,128)(2,1)}, bf16[2,3072,256]{2,1,0:T(8,128)(2,1)}, bf16[2,3072,256]{1,2,0:T(8,128)(2,1)}, pred[2,3072]{1...) while((s32[]{:T(128)}, bf16[2,3072,256]{2,1,0:T(8,128)(2,1)}, ...), condition=%wide.region_7.8_spmd, body=%wide.region_2.7_spmd.sunk | while | flops 1648364544 | bytes 71378248 | solution.py:167
  2534.0 153.1 %while.79 = (s32[]{:T(128)}, bf16[6,512,256]{1,2,0:T(8,128)(2,1)}, pred[3072]{0:T(1024)(128)(4,1)S(1)}, bf16[6,512,256]{2,1,0:T(8,128)(2,1)S(1)}, bf16[3072,256]...) while((s32[]{:T(128)}, bf16[6,512,256]{1,2,0:T(8,128)(2,1)}, pred[3072]{0:T(1024)(128)(4,1)S(1)}, ...), condition=%wide.region_6.6_spmd, body=%wide.region_3.5_spmd.sunk | while | flops 1648364544 | bytes 55594076 | solution.py:159
  2534.2 13.8 fusion.198
  2559.7 13.8 fusion.198
  2585.3 13.8 fusion.198
  2610.8 13.8 fusion.198
  2661.8 13.8 fusion.198
  2695.5 153.5 %while.79 = (s32[]{:T(128)}, bf16[6,512,256]{1,2,0:T(8,128)(2,1)}, pred[3072]{0:T(1024)(128)(4,1)S(1)}, bf16[6,512,256]{2,1,0:T(8,128)(2,1)S(1)}, bf16[3072,256]...) while((s32[]{:T(128)}, bf16[6,512,256]{1,2,0:T(8,128)(2,1)}, pred[3072]{0:T(1024)(128)(4,1)S(1)}, ...), condition=%wide.region_6.6_spmd, body=%wide.region_3.5_spmd.sunk | while | flops 1648364544 | bytes 55594076 | solution.py:159
  2695.7 13.8 fusion.198
  2721.2 13.8 fusion.198
  2746.7 13.8 fusion.198
  2772.2 13.9 fusion.198
  2797.9 13.8 fusion.198
  2823.6 13.8 fusion.198
  2858.6 66.3 %all_to_all.165 = bf16[2,3072,256]{2,0,1:T(2,128)(2,1)S(1)} all-to-all(bf16[2,3072,256]{2,0,1:T(2,128)(2,1)S(1)} %copy.157), channel_id=1, replica_groups=mesh['dp'=8,'fsdp'=4] {'fsdp'}, dimensions={1} | all-to-all | bytes 6291456 | tf_op jit(solution)/shard_map/all_to_all | solution.py:214
  2984.7 40.6 %all-reduce.14 = (f32[6144]{0:T(1024)S(1)}, f32[1024]{0:T(1024)S(1)}, f32[1024]{0:T(1024)S(1)}, f32[1024]{0:T(1024)S(1)}, f32[1024]{0:T(1024)S(1)}, /*index=5*/f32[2048]{0:T(1024)S(1)}, f32[1024]{0:T(1024)S(1)}) all-reduce(f32[6144]{0:T(1024)S(1)} %reduce_sum.269, ...), channel_id=3, replica_groups=mesh['dp'=8,'fsdp'=4] {'dp','fsdp'}, use_global_device_ids=true, to_apply=%region_35.36.clone | all-reduce | flops 13312 | bytes 106496
  3034.7 21.7 convolution_add_fusion.3
  3056.4 13.9 add_convert_fusion
  3073.7 248.1 %reduce-scatter.8.cloned.1.call-done = f32[32,6144]{1,0:T(8,128)} async-done(((f32[1024,6144]{1,0:T(8,128)}), f32[32,6144]{1,0:T(8,128)}) %reduce-scatter.8.cloned.1.call-update) | async-done | bytes 786448 | tf_op jit(solution)/shard_map/reduce_scatter | solution.py:450
  (977 shorter events, 1722.3 us)
Async XLA Ops:
  7.2 10.7 copy-start.109
  7.2 11.0 copy-start.110
  7.2 11.2 copy-start.111
  7.2 11.4 copy-start.112
  7.3 102.8 %all-gather.8.cloned.1.call-start = ((), (), s32[]{:S(2)}) async-start(), calls=%async_computation.16 | async-start | bytes 12976128 | tf_op jit(solution)/shard_map/all_gather | solution.py:326
  8.0 159.6 %all-gather.14.cloned.1.call-start = ((), (), s32[]{:S(2)}) async-start(), calls=%async_computation.19 | async-start | bytes 2162688 | tf_op jit(solution)/shard_map/all_gather | solution.py:332
  8.7 221.0 %all-gather.10.cloned.1.call-start = ((), (), s32[]{:S(2)}) async-start(), calls=%async_computation.17 | async-start | bytes 2162688 | tf_op jit(solution)/shard_map/all_gather | solution.py:328
  9.5 278.3 %all-gather.12.cloned.1.call-start = ((), (), s32[]{:S(2)}) async-start(), calls=%async_computation.18 | async-start | bytes 2162688 | tf_op jit(solution)/shard_map/all_gather | solution.py:330
  10.0 927.5 %all-gather.16.cloned.1.call-start = ((), (), s32[]{:S(2)}) async-start(), calls=%async_computation.20 | async-start | bytes 2162688 | tf_op jit(solution)/shard_map/all_gather | solution.py:334
  10.6 940.8 %all-gather.18.cloned.1.call-start = ((), (), s32[]{:S(2)}) async-start(), calls=%async_computation.21 | async-start | bytes 4325376 | tf_op jit(solution)/shard_map/all_gather | solution.py:336
  11.2 105.3 %copy-start.99 = (f32[32]{0:T(128)}, f32[32]{0:T(128)S(1)}, u32[]{:S(2)}) copy-start(f32[32]{0:T(128)S(1)} %multiply_exponential_fusion.1) | copy-start | bytes 388
  14.3 102.9 %copy-start.60 = (f32[2,768]{1,0:T(2,128)}, f32[2,768]{1,0:T(2,128)S(1)}, u32[]{:S(2)}) copy-start(f32[2,768]{1,0:T(2,128)S(1)} %broadcast_multiply_fusion.4) | copy-start | bytes 18436
  17.2 92.9 %copy-start.74 = (f32[2,768]{1,0:T(2,128)}, f32[2,768]{1,0:T(2,128)S(1)}, u32[]{:S(2)}) copy-start(f32[2,768]{1,0:T(2,128)S(1)} %fusion.47) | copy-start | bytes 18436
  17.2 100.0 %copy-start.66 = (f32[2,768]{1,0:T(2,128)}, f32[2,768]{1,0:T(2,128)S(1)}, u32[]{:S(2)}) copy-start(f32[2,768]{1,0:T(2,128)S(1)} %fusion.55) | copy-start | bytes 18436
  62.4 54.2 %copy-start.76 = (f32[2,512]{1,0:T(2,128)}, f32[2,512]{1,0:T(2,128)S(1)}, u32[]{:S(2)}) copy-start(f32[2,512]{1,0:T(2,128)S(1)} %get-tuple-element.637) | copy-start | bytes 12292
  62.4 54.2 %copy-start.78 = (f32[2,512]{1,0:T(2,128)}, f32[2,512]{1,0:T(2,128)S(1)}, u32[]{:S(2)}) copy-start(f32[2,512]{1,0:T(2,128)S(1)} %get-tuple-element.638) | copy-start | bytes 12292
  117.2 50.4 %copy-start.62 = (f32[2,1024]{1,0:T(2,128)}, f32[2,1024]{1,0:T(2,128)S(1)}, u32[]{:S(2)}) copy-start(f32[2,1024]{1,0:T(2,128)S(1)} %get-tuple-element.631) | copy-start | bytes 24580
  179.4 50.3 %copy-start.43 = (bf16[2,768,1024]{2,1,0:T(8,128)(2,1)S(1)}, bf16[2,768,1024]{2,1,0:T(8,128)(2,1)}, u32[]{:S(2)}) copy-start(bf16[2,768,1024]{2,1,0:T(8,128)(2,1)} %fusion.43) | copy-start | bytes 9437188
  179.4 207.6 %all-to-all-start.2 = ((bf16[2,768,1024]{1,0,2:T(2,128)(2,1)}), bf16[2,768,1024]{1,0,2:T(2,128)(2,1)}, u32[]{:S(2)}, u32[]{:S(2)}) async-start(bf16[2,768,1024]{1,0,2:T(2,128)(2,1)} %copy.155), calls=%async_computation.2 | async-start | bytes 6291456 | tf_op jit(solution)/shard_map/all_to_all | solution.py:211
  349.5 18.9 slice-start.4
  380.1 11.6 copy-start.29
  387.0 47.0 %all-to-all-start.1 = ((bf16[2,768,1024]{1,0,2:T(2,128)(2,1)}), bf16[2,768,1024]{1,0,2:T(2,128)(2,1)}, u32[]{:S(2)}, u32[]{:S(2)}) async-start(bf16[2,768,1024]{1,0,2:T(2,128)(2,1)} %copy.153), calls=%async_computation.1 | async-start | bytes 6291456 | tf_op jit(solution)/shard_map/all_to_all | solution.py:210
  391.7 46.8 %copy-start.97 = (s32[2]{0:T(128)S(1)}, s32[2]{0:T(128)}, u32[]{:S(2)}) copy-start(s32[2]{0:T(128)} %param.31) | copy-start | bytes 28
  434.0 45.2 %all-to-all-start = ((bf16[2,768,1024]{1,0,2:T(2,128)(2,1)}), bf16[2,768,1024]{1,0,2:T(2,128)(2,1)S(1)}, u32[]{:S(2)}, u32[]{:S(2)}) async-start(bf16[2,768,1024]{1,0,2:T(2,128)(2,1)} %copy.148), calls=%async_computation | async-start | bytes 6291456 | tf_op jit(solution)/shard_map/all_to_all | solution.py:209
  437.7 526.1 %all-gather.20.cloned.1.call-start = ((), (), s32[]{:S(2)}) async-start(), calls=%async_computation.22 | async-start | bytes 4325376 | tf_op jit(solution)/shard_map/all_gather | solution.py:338
  493.6 188.6 %copy-start.54 = (f32[2,3072,4]{1,2,0:T(4,128)S(1)}, f32[2,3072,4]{1,2,0:T(4,128)}, u32[]{:S(2)}) copy-start(f32[2,3072,4]{1,2,0:T(4,128)} %get-tuple-element.1131) | copy-start | bytes 294916 | tf_op jit(solution)/shard_map/while
  691.3 188.3 %copy-start.54 = (f32[2,3072,4]{1,2,0:T(4,128)S(1)}, f32[2,3072,4]{1,2,0:T(4,128)}, u32[]{:S(2)}) copy-start(f32[2,3072,4]{1,2,0:T(4,128)} %get-tuple-element.1131) | copy-start | bytes 294916 | tf_op jit(solution)/shard_map/while
  882.5 13.0 copy-start.96
  882.5 13.0 copy-start.95
  882.5 13.0 copy-start.90
  882.6 13.0 copy-start.98
  882.6 13.1 copy-start.25
  882.6 13.1 copy-start.68
  890.7 41.8 %all-to-all-start.4 = ((bf16[2,3072,256]{2,0,1:T(2,128)(2,1)}), bf16[2,3072,256]{2,0,1:T(2,128)(2,1)}, u32[]{:S(2)}, u32[]{:S(2)}) async-start(bf16[2,3072,256]{2,0,1:T(2,128)(2,1)} %copy.159), calls=%async_computation.4 | async-start | bytes 6291456 | tf_op jit(solution)/shard_map/all_to_all | solution.py:214
  895.5 42.1 %copy-start.93 = (f32[1024]{0:T(1024)}, f32[1024]{0:T(1024)S(1)}, u32[]{:S(2)}) copy-start(f32[1024]{0:T(1024)S(1)} %convert_element_type.217) | copy-start | bytes 12292
  895.5 104.1 %copy-start.91 = (f32[1024]{0:T(1024)}, f32[1024]{0:T(1024)S(1)}, u32[]{:S(2)}) copy-start(f32[1024]{0:T(1024)S(1)} %convert_element_type.222) | copy-start | bytes 12292
  895.6 104.1 %copy-start.86 = (f32[2048]{0:T(1024)}, f32[2048]{0:T(1024)S(1)}, u32[]{:S(2)}) copy-start(f32[2048]{0:T(1024)S(1)} %convert_element_type.220) | copy-start | bytes 24580
  895.7 118.2 %copy-start.58 = (f32[2,768]{1,0:T(2,128)}, f32[2,768]{1,0:T(2,128)S(1)}, u32[]{:S(2)}) copy-start(f32[2,768]{1,0:T(2,128)S(1)} %compare_convert_fusion) | copy-start | bytes 18436
  951.4 40.8 %slice-start = ((s8[6291456]{0:T(1024)(128)(4,1)}), s8[2097152]{0:T(1024)(128)(4,1)S(1)}, s32[]{:S(2)}) async-start(s8[6291456]{0:T(1024)(128)(4,1)} %bitcast.356), calls=%async_computation.30 | async-start | bytes 4194304
  963.8 21.4 copy-start.101
  963.8 28.4 slice-start.1
  995.7 18.2 slice-start.2
  999.6 14.3 copy-start.19
  999.6 14.2 copy-start.72
  999.6 14.2 copy-start.26
  999.7 14.2 slice-start.3
  1030.1 51.1 %all-to-all-start.5 = ((bf16[2,768,1024]{1,0,2:T(2,128)(2,1)}), bf16[2,768,1024]{1,0,2:T(2,128)(2,1)S(1)}, u32[]{:S(2)}, u32[]{:S(2)}) async-start(bf16[2,768,1024]{1,0,2:T(2,128)(2,1)} %copy.161), calls=%async_computation.5 | async-start | bytes 6291456 | tf_op jit(solution)/shard_map/all_to_all | solution.py:414
  1033.8 2036.5 %reduce-scatter.16.cloned.1.call-start = ((), (), s32[]{:S(2)}) async-start(), calls=%async_computation.27 | async-start | bytes 4325376 | tf_op jit(solution)/shard_map/reduce_scatter | solution.py:458
  1045.1 2025.2 %reduce-scatter.12.cloned.1.call-start = ((), (), s32[]{:S(2)}) async-start(), calls=%async_computation.25 | async-start | bytes 4325376 | tf_op jit(solution)/shard_map/reduce_scatter | solution.py:454
  1655.1 11.3 copy-start.3
  2254.6 11.3 copy-start.3
  2345.9 724.4 %reduce-scatter.10.cloned.1.call-start = ((), (), s32[]{:S(2)}) async-start(), calls=%async_computation.24 | async-start | bytes 4325376 | tf_op jit(solution)/shard_map/reduce_scatter | solution.py:452
  2431.0 639.3 %reduce-scatter.14.cloned.1.call-start = ((), (), s32[]{:S(2)}) async-start(), calls=%async_computation.26 | async-start | bytes 4325376 | tf_op jit(solution)/shard_map/reduce_scatter | solution.py:456
  2499.7 570.7 %reduce-scatter.20.cloned.1.call-start = ((), (), s32[]{:S(2)}) async-start(), calls=%async_computation.29 | async-start | bytes 8650752 | tf_op jit(solution)/shard_map/reduce_scatter | solution.py:462
  2513.6 560.1 %reduce-scatter.18.cloned.1.call-start = ((), (), s32[]{:S(2)}) async-start(), calls=%async_computation.28 | async-start | bytes 8650752 | tf_op jit(solution)/shard_map/reduce_scatter | solution.py:460
  2526.4 795.4 %reduce-scatter.8.cloned.1.call-start = ((), (), s32[]{:S(2)}) async-start(), calls=%async_computation.23 | async-start | bytes 25952256 | tf_op jit(solution)/shard_map/reduce_scatter | solution.py:450
  2931.6 23.3 copy-start.15
  2973.9 10.7 copy-start.84
  2973.9 10.7 copy-start.85
  2973.9 10.7 copy-start.89
  2974.0 55.5 %copy-start.65 = (f32[2,1024]{1,0:T(2,128)S(1)}, f32[2,1024]{1,0:T(2,128)}, u32[]{:S(2)}) copy-start(f32[2,1024]{1,0:T(2,128)} %get-tuple-element.629) | copy-start | bytes 24580
  2974.0 55.5 %copy-start.71 = (f32[2,1024]{1,0:T(2,128)S(1)}, f32[2,1024]{1,0:T(2,128)}, u32[]{:S(2)}) copy-start(f32[2,1024]{1,0:T(2,128)} %get-tuple-element.628) | copy-start | bytes 24580
  3034.7 21.7 copy-start.69
  3034.7 21.7 copy-start.73
  (181 other events, 970.9 us)
Sparse Core Ops, SparseCore 0:
  11.0 99.0 all-gather.7
  112.9 54.6 all-gather.13
  170.5 59.2 all-gather.9
  232.5 55.2 all-gather.11
  290.4 55.2 all-gather.15
  348.4 67.9 all-gather.17
  441.4 66.1 all-gather.19
  1045.2 142.4 reduce-scatter.15
  2346.0 142.6 reduce-scatter.11
  2491.5 136.7 reduce-scatter.9
  2631.1 136.7 reduce-scatter.13
  2770.7 148.3 reduce-scatter.19
  2921.9 151.7 reduce-scatter.17
  3080.5 241.2 reduce-scatter.7
where the time goes:
time: 3340 us; the launch traced here: 3330 us
  matrix products  1400 us (42%)
  waiting for transfers between devices  547 us (16%)
  local copies, waits for them, and re-layouts  543 us (16%)
  other arithmetic  500 us (15%)
  blocking collectives  297 us (9%)
    dot_general x24, matrix products, attend_block(): jnp.einsum('hqk,khd->qhd', probabilities, split_heads(value_rows), prefer...  269 us
    convert_element_type x12, other arithmetic, block_grads(): d_scores = (probabilities * (d_probs - delta_sum)).astype(jnp.bfloat16)  260 us
    dot_general x12, matrix products, block_grads(): jnp.einsum('qhd,khd->hqk', split_heads(d_heads), split_heads(value_rows),...  250 us
    reduce_scatter x1, waiting for transfers between devices, body(): lax.psum_scatter(g_w_ada, ('dp', 'fsdp'), scatter_dimension=0, tiled=True)  248 us
    dot_general x24, matrix products, masked_scores(): jnp.einsum('qhd,khd->hqk', split_heads(queries), split_heads(key_rows), p...  166 us
    sub x12, matrix products, attend_block(): weights = jnp.exp(scores - row_max)  166 us
    dot_general x12, matrix products, block_grads(): jnp.einsum('hqk,qhd->khd', probabilities.astype(jnp.bfloat16), split_head...  151 us
    while x264, local copies, waits for them, and re-layouts  138 us
  transfers between devices with their start and end apart: 19, of which 10 were waited for; matrix products, arithmetic and copies ran while one was open for 67% of the time, Pallas kernels for 0%

commit v1 on v0

v1 whole, which is shorter than its diff:
```python
import functools
import math

import jax
import jax.numpy as jnp
from jax import lax
from jax.experimental import pallas as pl
from jax.experimental.pallas import tpu as pltpu
from jax.sharding import PartitionSpec as P

HDIM = 64
HALF = HDIM // 2
SCALE = HDIM ** (-0.5)
SCALE2 = SCALE * math.log2(math.e)
AXES = ("dp", "fsdp")
F32 = jnp.float32
BF16 = jnp.bfloat16


def dot(left_side, right_side, left_dim, right_dim):
    return lax.dot_general(
        left_side,
        right_side,
        (((left_dim,), (right_dim,)), ((), ())),
        preferred_element_type=F32,
    )


def pick_block(total, wanted):
    block = min(total, wanted)
    while total % block:
        block -= 128
    return block


def attend_kernel(parts, chunk, *refs):
    q_ref, bias_ref = refs[0], refs[1]
    k_refs, v_refs = refs[2 : 2 + parts], refs[2 + parts : 2 + 2 * parts]
    o_ref, lse_ref, k_aug, v_aug, q_aug = refs[2 + 2 * parts :]
    head, block = pl.program_id(0), pl.program_id(1)
    span = k_aug.shape[0]
    part = span // parts
    q_rows = q_ref.shape[1]

    @pl.when((head == 0) & (block == 0))
    def _():
        k_aug[:, HDIM:] = bias_ref[...]
        v_aug[HDIM:, :] = jnp.ones((16, span), BF16)
        q_aug[HDIM:, :] = jnp.ones((HDIM, q_rows), BF16)

    @pl.when(block == 0)
    def _():
        for i in range(parts):
            k_aug[i * part : (i + 1) * part, :HDIM] = k_refs[i][...].T
            v_aug[:HDIM, i * part : (i + 1) * part] = v_refs[i][...]

    q_aug[:HDIM, :] = q_ref[...]
    queries = q_aug[...]
    count = span // chunk

    def scores(i):
        return dot(k_aug[i * chunk : (i + 1) * chunk, :], queries, 1, 0)

    upcoming = scores(0)
    row_max = total = None
    for i in range(count):
        current = upcoming
        if i + 1 < count:
            upcoming = scores(i + 1)
        chunk_max = jnp.max(current, axis=0, keepdims=True) * SCALE2
        new_max = chunk_max if i == 0 else jnp.maximum(row_max, chunk_max)
        weights = jnp.exp2(current * SCALE2 - new_max).astype(BF16)
        update = dot(v_aug[:, i * chunk : (i + 1) * chunk], weights, 1, 0)
        total = update if i == 0 else total * jnp.exp2(row_max - new_max) + update
        row_max = new_max
    denominator = total[HDIM : HDIM + 1, :]
    o_ref[...] = (total[:HDIM, :] / denominator).astype(BF16)
    lse_ref[...] = (row_max + jnp.log2(denominator))[None]


def attend(q_rot, k_parts, v_parts, bias_columns):
    width, rows = q_rot.shape
    parts = len(k_parts)
    span = parts * rows
    heads = width // HDIM
    q_rows = pick_block(rows, 768)
    chunk = pick_block(span, 512)
    q_spec = pl.BlockSpec((HDIM, q_rows), lambda h, j: (h, j))
    k_spec = pl.BlockSpec((HDIM, rows), lambda h, j: (h, 0))
    return pl.pallas_call(
        functools.partial(attend_kernel, parts, chunk),
        grid=(heads, rows // q_rows),
        in_specs=[q_spec, pl.BlockSpec((span, HDIM), lambda h, j: (0, 0))] + [k_spec] * (2 * parts),
        out_specs=[q_spec, pl.BlockSpec((1, 1, q_rows), lambda h, j: (h, 0, j))],
        out_shape=[
            jax.ShapeDtypeStruct((width, rows), BF16),
            jax.ShapeDtypeStruct((heads, 1, rows), F32),
        ],
        scratch_shapes=[
            pltpu.VMEM((span, 2 * HDIM), BF16),
            pltpu.VMEM((HDIM + 16, span), BF16),
            pltpu.VMEM((2 * HDIM, q_rows), BF16),
        ],
        compiler_params=pltpu.CompilerParams(vmem_limit_bytes=40 << 20),
        cost_estimate=pl.CostEstimate(
            flops=16 * heads * rows * span * HDIM,
            bytes_accessed=2 * width * (2 * rows + 2 * span),
            transcendentals=heads * rows * span,
        ),
        name="attend",
    )(q_rot, bias_columns, *k_parts, *v_parts)


def in_three(values):
    first = values.astype(BF16)
    rest = values - first.astype(F32)
    second = rest.astype(BF16)
    return first.astype(F32), second.astype(F32), rest - second.astype(F32)


def unrotate(values, cosine, sine):
    low, high = values[:HALF], values[HALF:]
    return low * cosine + high * sine, high * cosine - low * sine


def attend_back_kernel(parts, chunk, *refs):
    q_ref, do_ref, o_ref, lse_ref, bias_ref, cos_ref, sin_ref = refs[:7]
    k_refs, v_refs = refs[7 : 7 + parts], refs[7 + parts : 7 + 2 * parts]
    dq_ref = refs[7 + 2 * parts]
    dk_refs = refs[8 + 2 * parts : 8 + 3 * parts]
    dv_refs = refs[8 + 3 * parts : 8 + 4 * parts]
    k_aug, v_aug, k_rows, q_aug, do_aug, dk_acc, dv_acc = refs[8 + 4 * parts :]
    head, block = pl.program_id(0), pl.program_id(1)
    span = k_aug.shape[1]
    part = span // parts
    q_rows = q_ref.shape[1]

    @pl.when((head == 0) & (block == 0))
    def _():
        row = lax.broadcasted_iota(jnp.int32, (HDIM, span), 0)
        ones = jnp.where(row < 4, 1.0, 0.0)
        k_aug[HDIM:, :] = jnp.where(row == 0, bias_ref[...], ones).astype(BF16)
        v_aug[HDIM:, :] = jnp.where(row < 3, 1.0, 0.0).astype(BF16)
        k_rows[:, HDIM:] = jnp.zeros((span, HDIM), BF16)

    @pl.when(block == 0)
    def _():
        for i in range(parts):
            at = slice(i * part, (i + 1) * part)
            keys = k_refs[i][...]
            k_aug[:HDIM, at] = keys
            v_aug[:HDIM, at] = v_refs[i][...]
            k_rows[at, :HDIM] = keys.T
        dk_acc[...] = jnp.zeros_like(dk_acc)
        dv_acc[...] = jnp.zeros_like(dv_acc)

    queries, d_heads = q_ref[...], do_ref[...]
    delta = jnp.sum(d_heads.astype(F32) * o_ref[...].astype(F32), axis=0, keepdims=True)
    row = lax.broadcasted_iota(jnp.int32, (HDIM, q_rows), 0)
    lse_a, lse_b, lse_c = in_three(lse_ref[0] * (-1.0 / SCALE2))
    del_a, del_b, del_c = in_three(-delta)
    q_extra = jnp.where(row == 2, lse_b, jnp.where(row == 3, lse_c, 0.0))
    q_extra = jnp.where(row == 0, 1.0, jnp.where(row == 1, lse_a, q_extra))
    do_extra = jnp.where(row == 1, del_b, jnp.where(row == 2, del_c, 0.0))
    do_extra = jnp.where(row == 0, del_a, do_extra)
    q_aug[:HDIM, :] = queries
    q_aug[HDIM:, :] = q_extra.astype(BF16)
    do_aug[:HDIM, :] = d_heads
    do_aug[HDIM:, :] = do_extra.astype(BF16)
    q_side, do_side = q_aug[...].T, do_aug[...].T
    count = span // chunk

    def products(i):
        at = slice(i * chunk, (i + 1) * chunk)
        return dot(q_side, k_aug[:, at], 1, 0), dot(do_side, v_aug[:, at], 1, 0)

    upcoming = products(0)
    d_query = None
    for i in range(count):
        at = slice(i * chunk, (i + 1) * chunk)
        scores, d_probs = upcoming
        if i + 1 < count:
            upcoming = products(i + 1)
        probs = jnp.exp2(scores * SCALE2)
        d_scores = (probs * d_probs).astype(BF16)
        dv_acc[:, at] += dot(d_heads, probs.astype(BF16), 1, 0)
        dk_acc[:, at] += dot(queries, d_scores, 1, 0)
        update = dot(d_scores, k_rows[at, :], 1, 0)
        d_query = update if i == 0 else d_query + update
    first = pl.multiple_of(block * q_rows, q_rows)
    low, high = unrotate(
        d_query.T[:HDIM, :] * SCALE, cos_ref[:, pl.ds(first, q_rows)], sin_ref[:, pl.ds(first, q_rows)]
    )
    dq_ref[:HALF, :] = low.astype(BF16)
    dq_ref[HALF:, :] = high.astype(BF16)

    @pl.when(block == pl.num_programs(1) - 1)
    def _():
        for i in range(parts):
            at = slice(i * part, (i + 1) * part)
            low, high = unrotate(dk_acc[:, at] * SCALE, cos_ref[:, at], sin_ref[:, at])
            dk_refs[i][:HALF, :] = low.astype(dk_refs[i].dtype)
            dk_refs[i][HALF:, :] = high.astype(dk_refs[i].dtype)
            dv_refs[i][...] = dv_acc[:, at].astype(dv_refs[i].dtype)


def attend_back(q_rot, k_parts, v_parts, d_heads, heads_out, lse, bias_row, cosine, sine, first, count):
    width, rows = q_rot.shape
    parts = len(k_parts)
    span = parts * rows
    q_rows = pick_block(rows, 1536)
    chunk = pick_block(span, 256)
    q_spec = pl.BlockSpec((HDIM, q_rows), lambda h, j: (h + first, j))
    k_spec = pl.BlockSpec((HDIM, rows), lambda h, j: (h + first, 0))
    whole = lambda array: pl.BlockSpec(array.shape, lambda h, j: (0, 0))
    part_out = pl.BlockSpec((HDIM, rows), lambda h, j: (h, 0))
    shape = lambda kind: jax.ShapeDtypeStruct((count * HDIM, rows), kind)
    part_kinds = [F32] + [BF16] * (parts - 1)
    out = pl.pallas_call(
        functools.partial(attend_back_kernel, parts, chunk),
        grid=(count, rows // q_rows),
        in_specs=[
            q_spec,
            q_spec,
            q_spec,
            pl.BlockSpec((1, 1, q_rows), lambda h, j: (h + first, 0, j)),
            whole(bias_row),
            whole(cosine),
            whole(sine),
        ]
        + [k_spec] * (2 * parts),
        out_specs=[pl.BlockSpec((HDIM, q_rows), lambda h, j: (h, j))] + [part_out] * (2 * parts),
        out_shape=[shape(BF16)] + [shape(kind) for kind in part_kinds * 2],
        scratch_shapes=[
            pltpu.VMEM((2 * HDIM, span), BF16),
            pltpu.VMEM((2 * HDIM, span), BF16),
            pltpu.VMEM((span, 2 * HDIM), BF16),
            pltpu.VMEM((2 * HDIM, q_rows), BF16),
            pltpu.VMEM((2 * HDIM, q_rows), BF16),
            pltpu.VMEM((HDIM, span), F32),
            pltpu.VMEM((HDIM, span), F32),
        ],
        compiler_params=pltpu.CompilerParams(vmem_limit_bytes=48 << 20),
        cost_estimate=pl.CostEstimate(
            flops=40 * count * rows * span * HDIM,
            bytes_accessed=2 * count * HDIM * (8 * rows + 4 * span),
            transcendentals=count * rows * span,
        ),
        name="attend_back",
    )(q_rot, d_heads, heads_out, lse, bias_row, cosine, sine, *k_parts, *v_parts)
    return out[0], out[1 : 1 + parts], out[1 + parts :]


def time_features(t_index, model_width):
    half_width = model_width // 2
    indices = jnp.arange(half_width).astype(F32)
    frequency = jnp.exp(indices * (-math.log(10000.0) / (half_width - 1)))
    angles = t_index.astype(F32)[:, None] * frequency[None, :]
    return jnp.concatenate([jnp.sin(angles), jnp.cos(angles)], axis=1)


def rotary_tables(places):
    inverse = jnp.exp(jnp.arange(HALF).astype(F32) * (-2.0 * math.log(10000.0) / HDIM))
    angles = inverse[:, None] * places.astype(F32)[None, :]
    return jnp.cos(angles), jnp.sin(angles)


def norm_parts(values):
    centered = values - jnp.mean(values, axis=-1, keepdims=True)
    scale = lax.rsqrt(jnp.mean(centered * centered, axis=-1, keepdims=True) + 1e-06)
    return centered * scale, scale


def norm_back(normed, scale, d_normed):
    return (
        d_normed
        - jnp.mean(d_normed, axis=-1, keepdims=True)
        - normed * jnp.mean(d_normed * normed, axis=-1, keepdims=True)
    ) * scale


def gelu_tanh(values):
    return 0.5 * values * (1.0 + jnp.tanh(0.7978845608028654 * (values + 0.044715 * values * values * values)))


def rotate(values, cosine, sine):
    width, rows = values.shape
    pieces = values.reshape(width // HDIM, 2, HALF, rows)
    low, high = pieces[:, 0], pieces[:, 1]
    turned = jnp.stack([low * cosine - high * sine, high * cosine + low * sine], axis=1)
    return turned.reshape(width, rows).astype(BF16)


def make_body(mesh):
    n_dp, n_fsdp = mesh.shape["dp"], mesh.shape["fsdp"]

    def shift(values, axis, size, by):
        return lax.ppermute(values, axis, [(i, (i + by) % size) for i in range(size)])

    def body(
        frames,
        lengths,
        t_index,
        w_ada,
        b_ada,
        w_query,
        b_query,
        w_key,
        b_key,
        w_value,
        b_value,
        w_out,
        b_out,
        w_up,
        b_up,
        w_down,
        b_down,
        grad_out,
    ):
        slots, local, width = frames.shape
        group = n_fsdp // slots
        hidden_width = w_up.shape[1]
        shard = w_query.shape[0]
        ada_width = w_ada.shape[1]
        dp, fsdp = lax.axis_index("dp"), lax.axis_index("fsdp")
        me = dp * n_fsdp + fsdp
        slot, place = fsdp // group, fsdp % group
        length = lax.dynamic_index_in_dim(lengths, slot, keepdims=False)

        def swap_in(values):
            pieces = [lax.dynamic_index_in_dim(values, slot, keepdims=False)]
            for by in range(1, slots):
                to_slot = (slot + by) % slots
                away = lax.dynamic_index_in_dim(values, to_slot, keepdims=False)
                pieces.append(shift(away, "fsdp", n_fsdp, by * group))
            return jnp.concatenate(pieces, axis=0)

        def swap_out(values):
            mine = [values[:local]]
            for by in range(1, slots):
                mine.append(shift(values[by * local : (by + 1) * local], "fsdp", n_fsdp, -by * group))
            order = [lax.rem(s - slot + slots, slots) for s in range(slots)]
            stacked = jnp.stack(mine)
            return jnp.concatenate([lax.dynamic_slice_in_dim(stacked, o, 1) for o in order], axis=0)

        def places_of(member):
            at = slot * group + member
            blocks = [((at - by * group) + n_fsdp) % n_fsdp for by in range(slots)]
            return jnp.concatenate([b * local + jnp.arange(local, dtype=jnp.int32) for b in blocks])

        ring = [(i, (i // group) * group + (i % group + 1) % group) for i in range(n_fsdp)]
        back = lambda by: [(i, (i // group) * group + (i % group - by) % group) for i in range(n_fsdp)]

        extras = [b_query[:, None], b_key[:, None], b_value[:, None], b_out[:, None], b_up.reshape(shard, -1), b_down[:, None]]
        extras = jnp.concatenate(extras, axis=1)
        extras = jnp.pad(extras, ((0, 0), (0, 128 - extras.shape[1])))
        packed = lax.all_gather(
            jnp.concatenate([w_query, w_key, w_value, extras], axis=1), AXES, axis=0, tiled=True
        )
        w_qkv, biases = packed[:, : 3 * width], packed[:, 3 * width :].astype(F32)
        out_up = lax.all_gather(jnp.concatenate([w_out, w_up], axis=1), AXES, axis=0, tiled=True)
        full_out, full_up = out_up[:, :width], out_up[:, width:]
        full_down = lax.all_gather(w_down, AXES, axis=0, tiled=True)
        up_cols = b_up.shape[0] // shard
        bias_out = biases[:, 3]
        bias_up = biases[:, 4 : 4 + up_cols].reshape(-1)
        bias_down = biases[:, 4 + up_cols]

        inputs = swap_in(frames)
        rows = inputs.shape[0]
        cotangent = swap_in(grad_out)

        t_parts = [t_index] + [shift(t_index, "dp", n_dp, by) for by in range(1, n_dp)]
        t_all = jnp.concatenate(t_parts)
        active = jax.nn.silu(time_features(t_all, width)).astype(BF16)
        active_mine = lax.dynamic_slice_in_dim(active, me * shard, shard, axis=1)
        partial = dot(active_mine, w_ada, 1, 0)
        b_mine = jnp.broadcast_to(b_ada.astype(F32)[None], (partial.shape[0], b_ada.shape[0]))
        at_b = me * b_ada.shape[0]
        partial = lax.dynamic_update_slice_in_dim(
            partial, lax.dynamic_slice_in_dim(partial, at_b, b_ada.shape[0], axis=1) + b_mine, at_b, axis=1
        )
        partial = partial.reshape(n_dp, slots, ada_width)
        summed = partial[0]
        for by in range(1, n_dp):
            summed = summed + shift(partial[by], "dp", n_dp, -by)
        modulation = lax.dynamic_index_in_dim(summed, slot, keepdims=True)
        for by in range(1, n_fsdp):
            target = ((fsdp + by) % n_fsdp) // group
            modulation = modulation + shift(
                lax.dynamic_index_in_dim(summed, target, keepdims=True), "fsdp", n_fsdp, by
            )
        shift_one, scale_one, gate_one, shift_two, scale_two, gate_two = jnp.split(modulation, 6, axis=1)

        key_places = jnp.concatenate([places_of((place - by + group) % group) for by in range(group)])
        cosine, sine = rotary_tables(key_places)
        key_bias = jnp.where(key_places < length, 0.0, -1e30)
        bias_columns = jnp.pad(key_bias.astype(BF16)[:, None], ((0, 0), (0, HDIM - 1)))
        keep = (key_places[:rows] < length).astype(F32)[:, None]

        inputs_f32 = inputs.astype(F32)
        normed_one, inv_one = norm_parts(inputs_f32)
        h_one = (normed_one * (1.0 + scale_one) + shift_one).astype(BF16)
        project = lambda at: dot(w_qkv[:, at * width : (at + 1) * width], h_one, 0, 1) + biases[:, at : at + 1]
        own_cos, own_sin = cosine[:, :rows], sine[:, :rows]
        k_parts = [rotate(project(1), own_cos, own_sin)]
        v_parts = [project(2).astype(BF16)]
        q_rot = rotate(project(0), own_cos, own_sin)
        for _ in range(1, group):
            k_parts.append(lax.ppermute(k_parts[-1], "fsdp", ring))
            v_parts.append(lax.ppermute(v_parts[-1], "fsdp", ring))
        heads_out, lse = attend(q_rot, k_parts, v_parts, bias_columns)
        branch = (dot(heads_out, full_out, 0, 0) + bias_out) * keep
        residual = inputs_f32 + gate_one * branch
        normed_two, inv_two = norm_parts(residual)
        h_two = (normed_two * (1.0 + scale_two) + shift_two).astype(BF16)
        up_proj = dot(h_two, full_up, 1, 0) + bias_up
        hidden = gelu_tanh(up_proj).astype(BF16)
        ff_out = dot(hidden, full_down, 1, 0) + bias_down
        mixed = swap_out((residual + gate_two * ff_out).astype(BF16))

        d_mixed = cotangent.astype(F32)
        d_gate_two = jnp.sum(d_mixed * ff_out, axis=0)
        d_ff = (d_mixed * gate_two).astype(BF16)
        g_w_down = dot(hidden, d_ff, 0, 0)
        g_b_down = jnp.sum(d_ff.astype(F32), axis=0)
        d_hidden = dot(d_ff, full_down, 1, 1)
        d_up = jax.vjp(gelu_tanh, up_proj)[1](d_hidden)[0].astype(BF16)
        g_w_up = dot(h_two, d_up, 0, 0)
        g_b_up = jnp.sum(d_up.astype(F32), axis=0)
        d_h_two = dot(d_up, full_up, 1, 1)
        d_shift_two = jnp.sum(d_h_two, axis=0)
        d_scale_two = jnp.sum(d_h_two * normed_two, axis=0)
        d_residual = d_mixed + norm_back(normed_two, inv_two, d_h_two * (1.0 + scale_two))
        d_gate_one = jnp.sum(d_residual * branch, axis=0)
        d_branch = (d_residual * gate_one * keep).astype(BF16)
        g_w_out = dot(heads_out, d_branch, 1, 0)
        g_b_out = jnp.sum(d_branch.astype(F32), axis=0)
        d_heads = dot(full_out, d_branch, 1, 1).astype(BF16)

        def reduce_rows(values):
            return lax.psum_scatter(values.astype(BF16), AXES, scatter_dimension=0, tiled=True).astype(F32)

        sum_out_up = reduce_rows(jnp.concatenate([g_w_out, g_w_up], axis=1))
        sum_down = reduce_rows(g_w_down)

        def gather_vectors(values):
            return lax.all_gather(values[None], AXES, axis=0, tiled=True)

        early = jnp.concatenate([d_gate_one, d_shift_two, d_scale_two, d_gate_two, g_b_out, g_b_up, g_b_down])
        early_all = gather_vectors(early)

        heads = width // HDIM
        steps = 2
        each = heads // steps
        d_h_one = None
        sums, d_biases = [], []
        for step in range(steps):
            dq, dk_parts, dv_parts = attend_back(
                q_rot, k_parts, v_parts, d_heads, heads_out, lse, key_bias[None], cosine, sine, step * each, each
            )
            d_key, d_value = dk_parts[0], dv_parts[0]
            for by in range(1, group):
                d_key = d_key + lax.ppermute(dk_parts[by], "fsdp", back(by)).astype(F32)
                d_value = d_value + lax.ppermute(dv_parts[by], "fsdp", back(by)).astype(F32)
            grads = [dq, d_key.astype(BF16), d_value.astype(BF16)]
            cols = slice(step * each * HDIM, (step + 1) * each * HDIM)
            weight_grads = []
            for at, grad in enumerate(grads):
                update = dot(grad, w_qkv[:, at * width : (at + 1) * width][:, cols], 0, 1)
                d_h_one = update if d_h_one is None else d_h_one + update
                weight_grads.append(dot(h_one, grad, 0, 1))
            sums.append(reduce_rows(jnp.concatenate(weight_grads, axis=1)))
            d_biases.append([jnp.sum(grad.astype(F32), axis=1) for grad in grads])
        d_shift_one = jnp.sum(d_h_one, axis=0)
        d_scale_one = jnp.sum(d_h_one * normed_one, axis=0)
        d_inputs = norm_back(normed_one, inv_one, d_h_one * (1.0 + scale_one))
        grad_frames = swap_out((d_residual + d_inputs).astype(BF16))
        g_b_qkv = [jnp.concatenate([part[at] for part in d_biases]) for at in range(3)]
        late_all = gather_vectors(jnp.concatenate([d_shift_one, d_scale_one] + g_b_qkv))

        t_order = lax.rem(dp - jnp.arange(n_dp) + n_dp, n_dp)
        active_of = active_mine.reshape(n_dp, slots, shard)[t_order]
        active_of = jnp.repeat(active_of[:, :, None], group, axis=2).reshape(n_dp * n_fsdp, shard)

        def ada_grad(vectors):
            return lax.dot_general(
                active_of.astype(F32),
                vectors,
                (((0,), (0,)), ((), ())),
                precision=lax.Precision.HIGHEST,
                preferred_element_type=F32,
            )

        g_w_ada = jnp.concatenate([ada_grad(late_all[:, : 2 * width]), ada_grad(early_all[:, : 4 * width])], axis=1)
        all_mod = jnp.concatenate(
            [jnp.sum(late_all[:, : 2 * width], axis=0), jnp.sum(early_all[:, : 4 * width], axis=0)]
        )
        mine = lambda vector: lax.dynamic_slice_in_dim(vector, me * (vector.shape[0] // (n_dp * n_fsdp)), vector.shape[0] // (n_dp * n_fsdp))
        early_sum = jnp.sum(early_all[:, 4 * width :], axis=0)
        late_sum = jnp.sum(late_all[:, 2 * width :], axis=0)
        columns = [s.reshape(shard, 3, each * HDIM) for s in sums]
        g_qkv = [jnp.concatenate([c[:, at] for c in columns], axis=1) for at in range(3)]
        return (
            mixed,
            grad_frames,
            g_w_ada,
            mine(all_mod),
            g_qkv[0],
            mine(late_sum[:width]),
            g_qkv[1],
            mine(late_sum[width : 2 * width]),
            g_qkv[2],
            mine(late_sum[2 * width :]),
            sum_out_up[:, :width],
            mine(early_sum[:width]),
            sum_out_up[:, width:],
            mine(early_sum[width : width + hidden_width]),
            sum_down,
            mine(early_sum[width + hidden_width :]),
        )

    return body


def solution(mesh):
    rows, vector, matrix = P("dp", "fsdp", None), P(AXES), P(AXES, None)
    return jax.shard_map(
        make_body(mesh),
        mesh=mesh,
        in_specs=(rows, P("dp"), P("dp")) + (matrix, vector) * 7 + (rows,),
        out_specs=(rows, rows) + (matrix, vector) * 7,
        check_vma=False,
    )
```

time: 3340 us -> 1120 us (0.34)
  matrix products: 1400 us -> 191 us
  local copies, waits for them, and re-layouts: 543 us -> 61.6 us
  other arithmetic: 500 us -> 59.2 us
  Pallas kernels: 0 us -> 279 us
  waiting for transfers between devices: 547 us -> 361 us
  blocking collectives: 297 us -> 112 us
    dot_general x118 -> x27, matrix products: 1230 us -> 191 us  [the longest x25 189 us: dot(): lax.dot_general(left_side, right_side, (((left_dim,), (right_dim,)), ((),...]
    convert_element_type x28 -> x9, other arithmetic: 296 us -> 8.77 us  [the longest x1 4.09 us: body(): h_one = (normed_one * (1.0 + scale_one) + shift_one).astype(BF16)]
    pallas_call x0 -> x3, Pallas kernels: none -> 279 us  [the longest x2 180 us: attend_back(): pl.pallas_call(functools.partial(attend_back_kernel, parts, chunk), grid=...]
    all_to_all x4 -> x0, blocking collectives: 213 us -> none  [the longest x1 66.3 us: attend(): lax.all_to_all(heads_low, 'fsdp', split_axis=1, concat_axis=2, tiled=True)]
    while x273 -> x0, local copies, waits for them, and re-layouts: 205 us -> none
    all_gather x7 -> x4, waiting for transfers between devices: 169 us -> 0.04 us  [the longest x1 0.02 us: body(): lax.all_gather(jnp.concatenate([w_query, w_key, w_value, extras], axis=1)...]
    sub x12 -> x0, matrix products: 166 us -> none  [attend_block(): weights = jnp.exp(scores - row_max)]
    all_to_all x5 -> x0, waiting for transfers between devices: 123 us -> none  [the longest x1 37.4 us: attend(): lax.all_to_all(k_rot, 'fsdp', split_axis=2, concat_axis=1, tiled=True)]
  transfers between devices with their start and end apart: 19 -> 35, of which waited for: 10 -> 10; matrix products, arithmetic and copies ran while one was open for 67% -> 18% of each run, Pallas kernels for 0% -> 17%
where the time goes in v1:
time: 1120 us
  waiting for transfers between devices  361 us (32%)
  Pallas kernels  279 us (25%)
  matrix products  191 us (17%)
  blocking collectives  112 us (10%)
  local copies, waits for them, and re-layouts  61.6 us (6%)
  other arithmetic  59.2 us (5%)
  starting transfers between devices  34.5 us (3%)
  between operations  16.1 us (1%)
    reduce_scatter x2, waiting for transfers between devices, reduce_rows(): lax.psum_scatter(values.astype(BF16), AXES, scatter_dimension=0, tiled=True)  255 us
    dot_general x25, matrix products, dot(): lax.dot_general(left_side, right_side, (((left_dim,), (right_dim,)), ((),...  189 us
    pallas_call x2, Pallas kernels, attend_back(): pl.pallas_call(functools.partial(attend_back_kernel, parts, chunk), grid=...  180 us
    all_gather x1, blocking collectives, gather_vectors(): return lax.all_gather(values[None], AXES, axis=0, tiled=True)  112 us
    pallas_call x1, Pallas kernels, attend(): pl.pallas_call(functools.partial(attend_kernel, parts, chunk), grid=(head...  98.9 us
    unnamed x10, waiting for transfers between devices  61.4 us
    ppermute x21, waiting for transfers between devices, shift(): lax.ppermute(values, axis, [(i, (i + by) % size) for i in range(size)])  44.4 us
    ppermute x21, starting transfers between devices, shift(): lax.ppermute(values, axis, [(i, (i + by) % size) for i in range(size)])  32.1 us
  transfers between devices with their start and end apart: 35, of which 10 were waited for; matrix products, arithmetic and copies ran while one was open for 18% of the time, Pallas kernels for 17%

profile of v1, /device:TPU:0, one launch (start us, length us, event | category | flops | bytes accessed | tf_op | source)
XLA Modules:
  0.0 1115.0 jit_solution(7030789020207664449)
XLA Ops:
  10.7 5.1 collective-permute-start.6
  16.2 3.5 collective-permute-start.4
  23.2 3.3 dynamic-slice_bitcast_fusion.3
  28.1 3.2 collective-permute-start.7
  34.0 4.8 collective-permute-start.8
  40.2 4.0 collective-permute-start.11
  44.1 2.8 collective-permute-done.14
  48.6 1.9 collective-permute-done.12
  57.1 33.8 %collective-permute-done.15 = f32[1,6144]{1,0:T(1,128)S(1)} collective-permute-done((f32[1,6144]{1,0:T(1,128)S(1)}, f32[1,6144]{1,0:T(1,128)S(1)}, u32[]{:S(2)}, u32[]{:S(2)}) %collective-permute-start.15) | collective-permute-done | bytes 24608 | tf_op jit(solution)/shard_map/ppermute | solution.py:298
  92.0 2.4 collective-permute-done.16
  95.1 2.5 fusion.20
  97.6 4.1 fusion.13
  104.9 8.0 add_convert_fusion.2.refs_4_.refs_9_
  113.0 3.8 convolution_add_fusion
  116.8 3.9 convolution_add_fusion.1
  120.7 3.3 subtract_convert_fusion
  124.9 2.1 copy-done.28
  127.1 2.0 dynamic-slice_bitcast_fusion.1
  132.0 2.2 pad.9.refs_1_
  135.6 2.0 slice.268
  138.9 2.3 pad_maximum_fusion.2
  141.2 98.9 %attend.1 = (bf16[1024,1536]{1,0:T(8,128)(2,1)S(1)}, f32[16,1,1536]{2,1,0:T(1,128)S(1)}) custom-call(bf16[1024,1536]{1,0:T(8,128)(2,1)S(1)} %bitcast.85, bf16[3072,64]{1,0:T(8,128)(2,1)S(1)} %copy-done.8, bf16[1024,1536]{1,0:T(8,128)(2,1)S(1)} %bitcast.82, bf16[1024,1536]{1,0:T(8,128)(2,1)} %collective-permute-done.18.refs_3_.refs_8_, ...), custom_call_target="tpu_custom_call" | custom-call | flops 77309411328 | bytes 18874368 | tf_op jit(solution)/shard_map/attend/pallas_call | solution.py:90
  243.5 11.0 fusion.74
  255.3 13.8 %multiply_convert_fusion = (bf16[1536,2048]{1,0:T(8,128)(2,1)}, f32[1536,2048]{1,0:T(8,128)}) fusion(f32[2048]{0:T(1024)S(1)} %add.527, bf16[1024,3072]{1,0:T(8,128)(2,1)S(1)} %bitcast.124, f32[1536,1024]{1,0:T(8,128)S(1)} %get-tuple-element.69, f32[1024]{0:T(1024)S(1)} %bitcast.110, f32[1024]{0:T(1024)S(1)} %bitcast.112, f32[1536]{0:T(1024)S(1)} %add_rsqrt_fusion, ...), kind=kOutput, calls=%fused_computation.12 | convolution fusion | flops 6481772544 | bytes 29392896 | tf_op jit(solution)/shard_map/dot_general | solution.py:21
  269.2 21.2 %convert_reduce_fusion = (f32[2048]{0:T(1024)}, bf16[1536,2048]{1,0:T(8,128)(2,1)S(1)}) fusion(bf16[2048,1024]{1,0:T(8,128)(2,1)} %all-gather.11.cloned.1.call-done, f32[1024]{0:T(1024)S(1)} %bitcast.107, bf16[768,1024]{1,0:T(8,128)(2,1)} %collective-permute-done.21, bf16[768,1024]{1,0:T(8,128)(2,1)S(1)} %copy-done.35, ...), kind=kOutput, calls=%fused_computation.11 | convolution fusion | flops 6536820736 | bytes 26234880 | tf_op jit(solution)/shard_map/dot_general | solution.py:21
  290.4 15.2 %multiply_reduce_fusion = (f32[1024]{0:T(1024)}, f32[1536]{0:T(1024)S(1)}, f32[1536]{0:T(1024)S(1)}, f32[1024]{0:T(1024)}, f32[1536,1024]{1,0:T(8,128)}) fusion(f32[1536,1024]{1,0:T(8,128)S(1)} %copy-done.19, f32[1536]{0:T(1024)S(1)} %add_rsqrt_fusion, f32[1536]{0:T(1024)S(1)} %broadcast_multiply_fusion.4, f32[1024]{0:T(1024)S(1)} %bitcast.113, ...), kind=kOutput, calls=%fused_computation.39 | convolution fusion | flops 6456601600 | bytes 23105536 | tf_op jit(solution)/shard_map/dot_general | solution.py:21
  305.7 17.8 %convert_reduce_fusion.2 = (f32[1024]{0:T(1024)}, f32[1024]{0:T(1024)}, bf16[1536,1024]{1,0:T(8,128)(2,1)}, f32[1024]{0:T(1024)}, bf16[1536,1024]{1,0:T(8,128)(2,1)}, /*index=5*/f32[1536,1024]{1,0:T(8,128)}) fusion(f32[1024]{0:T(1024)S(1)} %bitcast.108, bf16[768,1024]{1,0:T(8,128)(2,1)} %collective-permute-done.21, bf16[768,1024]{1,0:T(8,128)(2,1)S(1)} %copy-done.35, ...), kind=kOutput, calls=%fused_computation.37 | convolution fusion | flops 6484915200 | bytes 38856704 | tf_op jit(solution)/shard_map/dot_general | solution.py:21
  323.4 7.9 convolution_convert_fusion.2.refs_1_
  331.3 89.9 %attend_back.3 = (bf16[512,1536]{1,0:T(8,128)(2,1)S(1)}, f32[512,1536]{1,0:T(8,128)}, bf16[512,1536]{1,0:T(8,128)(2,1)S(1)}, f32[512,1536]{1,0:T(8,128)}, bf16[512,1536]{1,0:T(8,128)(2,1)S(1)}) custom-call(bf16[1024,1536]{1,0:T(8,128)(2,1)} %bitcast.86, bf16[1024,1536]{1,0:T(8,128)(2,1)} %convolution_convert_fusion.2.refs_1_, bf16[1024,1536]{1,0:T(8,128)(2,1)} %copy-done.9, ...), custom_call_target="tpu_custom_call" | custom-call | flops 96636764160 | bytes 25165824 | tf_op jit(solution)/shard_map/attend_back/pallas_call | solution.py:219
  421.3 90.3 %attend_back.2 = (bf16[512,1536]{1,0:T(8,128)(2,1)S(1)}, f32[512,1536]{1,0:T(8,128)}, bf16[512,1536]{1,0:T(8,128)(2,1)S(1)}, f32[512,1536]{1,0:T(8,128)}, bf16[512,1536]{1,0:T(8,128)(2,1)S(1)}) custom-call(bf16[1024,1536]{1,0:T(8,128)(2,1)} %bitcast.87, bf16[1024,1536]{1,0:T(8,128)(2,1)} %convolution_convert_fusion.2.refs_1_, bf16[1024,1536]{1,0:T(8,128)(2,1)} %copy-done.9, ...), custom_call_target="tpu_custom_call" | custom-call | flops 96636764160 | bytes 25165824 | tf_op jit(solution)/shard_map/attend_back/pallas_call | solution.py:219
  512.6 5.9 fusion.54
  518.5 4.5 fusion.48
  523.0 2.0 convert_reduce_fusion.6
  525.8 2.3 copy-done.25
  528.5 4.5 fusion.52
  533.1 4.5 fusion.46
  537.6 4.4 fusion.50
  544.5 16.5 %fusion.19 = (f32[1024]{0:T(1024)S(1)}, f32[1536]{0:T(1024)S(1)}, f32[1536]{0:T(1024)S(1)}, f32[1024]{0:T(1024)S(1)}, f32[1536,1024]{1,0:T(8,128)}) fusion(f32[1536]{0:T(1024)S(1)} %copy-done.41, f32[1536]{0:T(1024)S(1)} %copy-done.39, bf16[768,1024]{1,0:T(8,128)(2,1)S(1)} %copy-done.13, bf16[768,1024]{1,0:T(8,128)(2,1)S(1)} %copy-done.11, ...), kind=kOutput, calls=%fused_computation.32 | convolution fusion | flops 1638919168 | bytes 43552768 | tf_op jit(solution)/shard_map/dot_general | solution.py:21
  561.2 10.4 multiply_reduce_fusion.1
  572.4 3.8 convolution_convert_fusion.6
  576.3 1.8 convolution_convert_fusion.5
  578.1 1.8 convolution_convert_fusion.4
  579.9 1.9 pad_maximum_fusion.8
  581.8 4.7 copy.100
  586.8 3.8 convolution_convert_fusion.9
  590.7 1.8 convolution_convert_fusion.8
  592.5 1.8 convolution_convert_fusion.7
  594.3 1.9 pad_maximum_fusion.7
  596.1 4.7 copy.98
  600.9 7.6 convolution_convert_fusion.3
  608.5 4.0 copy.97
  612.5 11.4 %convolution_convert_fusion.1 = bf16[1024,2048]{1,0:T(8,128)(2,1)S(1)} fusion(bf16[1536,2048]{1,0:T(8,128)(2,1)} %copy-done.70, f32[1536,1024]{1,0:T(8,128)} %copy-done.18, f32[1024]{0:T(1024)S(1)} %bitcast.111, f32[1024]{0:T(1024)S(1)} %bitcast.115, f32[1536]{0:T(1024)S(1)} %copy-done.54, f32[1536]{0:T(1024)S(1)} %copy-done.48), kind=kOutput, calls=%fused_computation.55 | convolution fusion | flops 6452412416 | bytes 16797696 | tf_op jit(solution)/shard_map/dot_general | solution.py:21
  624.0 3.2 pad_maximum_fusion
  627.9 11.7 %convolution_convert_fusion = bf16[2048,1024]{1,0:T(8,128)(2,1)} fusion(bf16[1536,2048]{1,0:T(8,128)(2,1)} %get-tuple-element.126, f32[1024]{0:T(1024)S(1)} %bitcast.109, bf16[768,1024]{1,0:T(8,128)(2,1)} %collective-permute-done.21, bf16[768,1024]{1,0:T(8,128)(2,1)} %get-tuple-element.84), kind=kOutput, calls=%fused_computation.54 | convolution fusion | flops 6453985280 | bytes 13635584 | tf_op jit(solution)/shard_map/dot_general | solution.py:21
  640.8 4.1 fusion.76
  649.0 112.1 %all-gather = f32[163840]{0:T(1024)} all-gather(f32[5120]{0:T(1024)S(1)} %constant_dynamic-update-slice_fusion.6), channel_id=2, replica_groups=mesh['dp'=8,'fsdp'=4] {'dp','fsdp'}, dimensions={0}, use_global_device_ids=true | all-gather | bytes 675840 | tf_op jit(solution)/shard_map/all_gather | solution.py:448
  761.1 2.0 reshape.377
  767.0 2.0 fusion.59
  769.0 3.7 fusion.39
  772.7 1.9 pad_maximum_fusion.6
  774.6 1.9 pad_maximum_fusion.4
  783.4 61.3 %reduce-scatter.13.cloned.1.call-done = bf16[32,1536]{1,0:T(8,128)(2,1)} async-done(((bf16[1024,1536]{1,0:T(8,128)(2,1)}), bf16[32,1536]{1,0:T(8,128)(2,1)}) %reduce-scatter.13.cloned.1.call-update) | async-done | bytes 98320
  847.6 116.0 %reduce-scatter.9.cloned.1.call-done = bf16[32,3072]{1,0:T(8,128)(2,1)} async-done(((bf16[1024,3072]{1,0:T(8,128)(2,1)}), bf16[32,3072]{1,0:T(8,128)(2,1)}) %reduce-scatter.9.cloned.1.call-update) | async-done | bytes 196624 | tf_op jit(solution)/shard_map/reduce_scatter | solution.py:442
  966.7 139.4 %reduce-scatter.11.cloned.1.call-done = bf16[64,1024]{1,0:T(8,128)(2,1)} async-done(((bf16[2048,1024]{1,0:T(8,128)(2,1)}), bf16[64,1024]{1,0:T(8,128)(2,1)}) %reduce-scatter.11.cloned.1.call-update) | async-done | bytes 131088 | tf_op jit(solution)/shard_map/reduce_scatter | solution.py:442
  (328 shorter events, 66.4 us)
Async XLA Ops:
  7.2 26.0 %copy-start = (bf16[32,6144]{1,0:T(8,128)(2,1)S(1)}, bf16[32,6144]{1,0:T(8,128)(2,1)}, u32[]{:S(2)}) copy-start(bf16[32,6144]{1,0:T(8,128)(2,1)} %param.21) | copy-start | bytes 1179652
  7.2 19.3 %copy-start.68 = (s32[2]{0:T(128)S(1)}, s32[2]{0:T(128)}, u32[]{:S(2)}) copy-start(s32[2]{0:T(128)} %param.20) | copy-start | bytes 28
  7.2 94.6 %all-gather.7.cloned.1.call-start = ((), (), s32[]{:S(2)}) async-start(), calls=%async_computation.4 | async-start | bytes 6758400 | tf_op jit(solution)/shard_map/all_gather | solution.py:357
  10.6 232.8 %all-gather.9.cloned.1.call-start = ((), (), s32[]{:S(2)}) async-start(), calls=%async_computation.5 | async-start | bytes 6488064 | tf_op jit(solution)/shard_map/all_gather | solution.py:361
  10.7 15.8 %collective-permute-start.6 = (s32[2]{0:T(128)}, s32[2]{0:T(128)S(1)}, u32[]{:S(2)}, u32[]{:S(2)}) collective-permute-start(s32[2]{0:T(128)} %param.20), channel_id=1, source_target_pairs={{0,24},{4,28},{8,0},{12,4},{16,8},{20,12},{24,16},{28,20},{1,25},{... | collective-permute-start | bytes 32 | tf_op jit(solution)/shard_map/ppermute | solution.py:298
  15.8 12.4 %collective-permute-start.5 = (s32[2]{0:T(128)}, s32[2]{0:T(128)S(1)}, u32[]{:S(2)}, u32[]{:S(2)}) collective-permute-start(s32[2]{0:T(128)} %param.20), channel_id=1, source_target_pairs={{0,20},{4,24},{8,28},{12,0},{16,4},{20,8},{24,12},{28,16},{1,21},{... | collective-permute-start | bytes 32 | tf_op jit(solution)/shard_map/ppermute | solution.py:298
  16.2 15.1 %collective-permute-start.4 = (s32[2]{0:T(128)}, s32[2]{0:T(128)S(1)}, u32[]{:S(2)}, u32[]{:S(2)}) collective-permute-start(s32[2]{0:T(128)} %param.20), channel_id=1, source_target_pairs={{0,16},{4,20},{8,24},{12,28},{16,0},{20,4},{24,8},{28,12},{1,17},{... | collective-permute-start | bytes 32 | tf_op jit(solution)/shard_map/ppermute | solution.py:298
  19.7 11.6 %collective-permute-start.3 = (s32[2]{0:T(128)}, s32[2]{0:T(128)S(1)}, u32[]{:S(2)}, u32[]{:S(2)}) collective-permute-start(s32[2]{0:T(128)} %param.20), channel_id=1, source_target_pairs={{0,12},{4,16},{8,20},{12,24},{16,28},{20,0},{24,4},{28,8},{1,13},{... | collective-permute-start | bytes 32 | tf_op jit(solution)/shard_map/ppermute | solution.py:298
  19.7 11.6 %collective-permute-start.2 = (s32[2]{0:T(128)}, s32[2]{0:T(128)S(1)}, u32[]{:S(2)}, u32[]{:S(2)}) collective-permute-start(s32[2]{0:T(128)} %param.20), channel_id=1, source_target_pairs={{0,8},{4,12},{8,16},{12,20},{16,24},{20,28},{24,0},{28,4},{1,9},{5... | collective-permute-start | bytes 32 | tf_op jit(solution)/shard_map/ppermute | solution.py:298
  22.3 246.9 %all-gather.11.cloned.1.call-start = ((), (), s32[]{:S(2)}) async-start(), calls=%async_computation.6 | async-start | bytes 4325376 | tf_op jit(solution)/shard_map/all_gather | solution.py:363
  26.5 71.1 %copy-start.10 = (bf16[768,1024]{1,0:T(8,128)(2,1)}, bf16[768,1024]{1,0:T(8,128)(2,1)S(1)}, u32[]{:S(2)}) copy-start(bf16[768,1024]{1,0:T(8,128)(2,1)S(1)} %get-tuple-element.90) | copy-start | bytes 4718596
  26.5 6.3 collective-permute-start.1
  28.1 4.7 collective-permute-start.7
  34.0 10.2 collective-permute-start.8
  38.7 8.2 collective-permute-start.14
  38.7 8.3 collective-permute-start.13
  38.8 11.7 %collective-permute-start.12 = (f32[2,6144]{1,0:T(2,128)S(1)}, f32[2,6144]{1,0:T(2,128)S(1)}, u32[]{:S(2)}, u32[]{:S(2)}) collective-permute-start(f32[2,6144]{1,0:T(2,128)S(1)} %get-tuple-element.103), channel_id=1, source_target_pairs={{0,12},{4,16},{8,20},{12,24},{16,28},{20,0},{24,4},{28,8},{1,13},{... | collective-permute-start | bytes 147464 | tf_op jit(solution)/shard_map/ppermute | solution.py:298
  40.2 11.2 %collective-permute-start.11 = (f32[2,6144]{1,0:T(2,128)S(1)}, f32[2,6144]{1,0:T(2,128)S(1)}, u32[]{:S(2)}, u32[]{:S(2)}) collective-permute-start(f32[2,6144]{1,0:T(2,128)S(1)} %get-tuple-element.104), channel_id=1, source_target_pairs={{0,16},{4,20},{8,24},{12,28},{16,0},{20,4},{24,8},{28,12},{1,17},{... | collective-permute-start | bytes 147464 | tf_op jit(solution)/shard_map/ppermute | solution.py:298
  44.1 7.2 collective-permute-start.10
  46.9 4.4 collective-permute-start.9
  47.1 47.5 %collective-permute-start = (bf16[768,1024]{1,0:T(8,128)(2,1)}, bf16[768,1024]{1,0:T(8,128)(2,1)S(1)}, u32[]{:S(2)}, u32[]{:S(2)}) collective-permute-start(bf16[768,1024]{1,0:T(8,128)(2,1)} %get-tuple-element.91), channel_id=1, source_target_pairs={{0,2},{1,3},{2,0},{3,1},{4,6},{5,7},{6,4},{7,5},{8,10},{9,11},{10,... | collective-permute-start | bytes 4718600 | tf_op jit(solution)/shard_map/ppermute | solution.py:298
  51.5 39.3 %collective-permute-start.15 = (f32[1,6144]{1,0:T(1,128)S(1)}, f32[1,6144]{1,0:T(1,128)S(1)}, u32[]{:S(2)}, u32[]{:S(2)}) collective-permute-start(f32[1,6144]{1,0:T(1,128)S(1)} %get-tuple-element.107), channel_id=1, source_target_pairs={{0,1},{1,2},{2,3},{3,0},{4,5},{5,6},{6,7},{7,4},{8,9},{9,10},{10,1... | collective-permute-start | bytes 73736 | tf_op jit(solution)/shard_map/ppermute | solution.py:298
  51.6 40.4 %collective-permute-start.17 = (f32[1,6144]{1,0:T(1,128)S(1)}, f32[1,6144]{1,0:T(1,128)S(1)}, u32[]{:S(2)}, u32[]{:S(2)}) collective-permute-start(f32[1,6144]{1,0:T(1,128)S(1)} %get-tuple-element.108), channel_id=1, source_target_pairs={{0,3},{1,0},{2,1},{3,2},{4,7},{5,4},{6,5},{7,6},{8,11},{9,8},{10,9... | collective-permute-start | bytes 73736 | tf_op jit(solution)/shard_map/ppermute | solution.py:298
  53.3 41.1 %collective-permute-start.16 = (f32[1,6144]{1,0:T(1,128)S(1)}, f32[1,6144]{1,0:T(1,128)S(1)}, u32[]{:S(2)}, u32[]{:S(2)}) collective-permute-start(f32[1,6144]{1,0:T(1,128)S(1)} %get-tuple-element.109), channel_id=1, source_target_pairs={{0,2},{1,3},{2,0},{3,1},{4,6},{5,7},{6,4},{7,5},{8,10},{9,11},{10,... | collective-permute-start | bytes 73736 | tf_op jit(solution)/shard_map/ppermute | solution.py:298
  94.5 160.8 %copy-start.59 = (f32[1,1024]{1,0:T(1,128)}, f32[1,1024]{1,0:T(1,128)S(1)}, u32[]{:S(2)}) copy-start(f32[1,1024]{1,0:T(1,128)S(1)} %get-tuple-element.111) | copy-start | bytes 12292
  94.5 211.1 %copy-start.57 = (f32[1,1024]{1,0:T(1,128)}, f32[1,1024]{1,0:T(1,128)S(1)}, u32[]{:S(2)}) copy-start(f32[1,1024]{1,0:T(1,128)S(1)} %get-tuple-element.110) | copy-start | bytes 12292
  94.5 211.1 %copy-start.61 = (f32[1,1024]{1,0:T(1,128)}, f32[1,1024]{1,0:T(1,128)S(1)}, u32[]{:S(2)}) copy-start(f32[1,1024]{1,0:T(1,128)S(1)} %get-tuple-element.112) | copy-start | bytes 12292
  104.9 138.6 %copy-start.51 = (f32[1024]{0:T(1024)}, f32[1024]{0:T(1024)S(1)}, u32[]{:S(2)}) copy-start(f32[1024]{0:T(1024)S(1)} %get-tuple-element.53) | copy-start | bytes 12292
  113.0 28.3 %collective-permute-start.19 = (bf16[1024,1536]{1,0:T(8,128)(2,1)}, bf16[1024,1536]{1,0:T(8,128)(2,1)}, u32[]{:S(2)}, u32[]{:S(2)}) collective-permute-start(bf16[1024,1536]{1,0:T(8,128)(2,1)} %add_convert_fusion.2.refs_4_.refs_9_), channel_id=1, source_target_pairs={{0,1},{1,0},{2,3},{3,2},{4,5},{5,4},{6,7},{7,6},{8,9},{9,8},{10,11... | collective-permute-start | bytes 9437192 | tf_op jit(solution)/shard_map/ppermute | solution.py:411
  124.3 16.9 %copy-start.2 = (bf16[16,2,32,1536]{3,2,1,0:T(8,128)(2,1)}, bf16[16,2,32,1536]{3,2,1,0:T(8,128)(2,1)S(1)}, u32[]{:S(2)}) copy-start(bf16[16,2,32,1536]{3,2,1,0:T(8,128)(2,1)S(1)} %pad_maximum_fusion.3) | copy-start | bytes 9437188
  124.4 16.9 %collective-permute-start.18 = (bf16[1024,1536]{1,0:T(8,128)(2,1)S(1)}, bf16[1024,1536]{1,0:T(8,128)(2,1)}, u32[]{:S(2)}, u32[]{:S(2)}) collective-permute-start(bf16[1024,1536]{1,0:T(8,128)(2,1)S(1)} %bitcast.81), channel_id=1, source_target_pairs={{0,1},{1,0},{2,3},{3,2},{4,5},{5,4},{6,7},{7,6},{8,9},{9,8},{10,11... | collective-permute-start | bytes 9437192 | tf_op jit(solution)/shard_map/ppermute | solution.py:410
  129.1 140.1 %collective-permute-start.21 = (bf16[768,1024]{1,0:T(8,128)(2,1)}, bf16[768,1024]{1,0:T(8,128)(2,1)}, u32[]{:S(2)}, u32[]{:S(2)}) collective-permute-start(bf16[768,1024]{1,0:T(8,128)(2,1)} %get-tuple-element.85), channel_id=1, source_target_pairs={{0,2},{1,3},{2,0},{3,1},{4,6},{5,7},{6,4},{7,5},{8,10},{9,11},{10,... | collective-permute-start | bytes 4718600 | tf_op jit(solution)/shard_map/ppermute | solution.py:298
  129.4 647.1 %all-gather.13.cloned.1.call-start = ((), (), s32[]{:S(2)}) async-start(), calls=%async_computation.9 | async-start | bytes 1081344 | tf_op jit(solution)/shard_map/all_gather | solution.py:448
  134.9 170.7 %copy-start.49 = (f32[1536]{0:T(1024)}, f32[1536]{0:T(1024)S(1)}, u32[]{:S(2)}) copy-start(f32[1536]{0:T(1024)S(1)} %fusion.70) | copy-start | bytes 18436
  243.5 11.8 %slice-start.2 = ((s8[6291456]{0:T(1024)(128)(4,1)}), s8[4194304]{0:T(1024)(128)(4,1)S(1)}, s32[]{:S(2)}) async-start(s8[6291456]{0:T(1024)(128)(4,1)} %bitcast.123), calls=%async_computation.14 | async-start | bytes 8388608
  243.5 11.8 %slice-start.3 = ((s8[6291456]{0:T(1024)(128)(4,1)}), s8[2097152]{0:T(1024)(128)(4,1)S(1)}, s32[]{:S(2)}) async-start(s8[6291456]{0:T(1024)(128)(4,1)} %bitcast.123), calls=%async_computation.15 | async-start | bytes 4194304
  254.4 14.7 %copy-start.18 = (f32[1536,1024]{1,0:T(8,128)}, f32[1536,1024]{1,0:T(8,128)S(1)}, u32[]{:S(2)}) copy-start(f32[1536,1024]{1,0:T(8,128)S(1)} %get-tuple-element.69) | copy-start | bytes 18874372
  254.4 51.2 %copy-start.47 = (f32[1536]{0:T(1024)}, f32[1536]{0:T(1024)S(1)}, u32[]{:S(2)}) copy-start(f32[1536]{0:T(1024)S(1)} %broadcast_multiply_fusion.4) | copy-start | bytes 18436
  255.2 50.4 %copy-start.53 = (f32[1536]{0:T(1024)}, f32[1536]{0:T(1024)S(1)}, u32[]{:S(2)}) copy-start(f32[1536]{0:T(1024)S(1)} %add_rsqrt_fusion) | copy-start | bytes 18436
  255.3 13.9 %copy-start.35 = (bf16[768,1024]{1,0:T(8,128)(2,1)S(1)}, bf16[768,1024]{1,0:T(8,128)(2,1)}, u32[]{:S(2)}) copy-start(bf16[768,1024]{1,0:T(8,128)(2,1)} %get-tuple-element.84) | copy-start | bytes 4718596
  269.2 21.2 %copy-start.19 = (f32[1536,1024]{1,0:T(8,128)S(1)}, f32[1536,1024]{1,0:T(8,128)}, u32[]{:S(2)}) copy-start(f32[1536,1024]{1,0:T(8,128)} %copy-done.18) | copy-start | bytes 18874372
  290.4 15.2 %copy-start.70 = (bf16[1536,2048]{1,0:T(8,128)(2,1)}, bf16[1536,2048]{1,0:T(8,128)(2,1)S(1)}, u32[]{:S(2)}) copy-start(bf16[1536,2048]{1,0:T(8,128)(2,1)S(1)} %get-tuple-element.131) | copy-start | bytes 18874372
  290.4 15.2 %copy-start.56 = (f32[1024]{0:T(1024)S(1)}, f32[1024]{0:T(1024)}, u32[]{:S(2)}) copy-start(f32[1024]{0:T(1024)} %get-tuple-element.52) | copy-start | bytes 12292
  421.2 101.8 %collective-permute-start.24 = (bf16[512,1536]{1,0:T(8,128)(2,1)S(1)}, bf16[512,1536]{1,0:T(8,128)(2,1)}, u32[]{:S(2)}, u32[]{:S(2)}) collective-permute-start(bf16[512,1536]{1,0:T(8,128)(2,1)S(1)} %get-tuple-element.37), channel_id=1, source_target_pairs={{0,1},{1,0},{2,3},{3,2},{4,5},{5,4},{6,7},{7,6},{8,9},{9,8},{10,11... | collective-permute-start | bytes 4718600 | tf_op jit(solution)/shard_map/ppermute | solution.py:464
  511.6 13.4 %collective-permute-start.22 = (bf16[512,1536]{1,0:T(8,128)(2,1)S(1)}, bf16[512,1536]{1,0:T(8,128)(2,1)S(1)}, u32[]{:S(2)}, u32[]{:S(2)}) collective-permute-start(bf16[512,1536]{1,0:T(8,128)(2,1)S(1)} %get-tuple-element.32), channel_id=1, source_target_pairs={{0,1},{1,0},{2,3},{3,2},{4,5},{5,4},{6,7},{7,6},{8,9},{9,8},{10,11... | collective-permute-start | bytes 4718600 | tf_op jit(solution)/shard_map/ppermute | solution.py:464
  512.1 30.0 %collective-permute-start.25 = (bf16[512,1536]{1,0:T(8,128)(2,1)S(1)}, bf16[512,1536]{1,0:T(8,128)(2,1)S(1)}, u32[]{:S(2)}, u32[]{:S(2)}) collective-permute-start(bf16[512,1536]{1,0:T(8,128)(2,1)S(1)} %get-tuple-element.39), channel_id=1, source_target_pairs={{0,1},{1,0},{2,3},{3,2},{4,5},{5,4},{6,7},{7,6},{8,9},{9,8},{10,11... | collective-permute-start | bytes 4718600 | tf_op jit(solution)/shard_map/ppermute | solution.py:465
  512.2 13.6 %collective-permute-start.23 = (bf16[512,1536]{1,0:T(8,128)(2,1)S(1)}, bf16[512,1536]{1,0:T(8,128)(2,1)S(1)}, u32[]{:S(2)}, u32[]{:S(2)}) collective-permute-start(bf16[512,1536]{1,0:T(8,128)(2,1)S(1)} %get-tuple-element.34), channel_id=1, source_target_pairs={{0,1},{1,0},{2,3},{3,2},{4,5},{5,4},{6,7},{7,6},{8,9},{9,8},{10,11... | collective-permute-start | bytes 4718600 | tf_op jit(solution)/shard_map/ppermute | solution.py:465
  544.5 16.6 %copy-start.50 = (f32[1536]{0:T(1024)S(1)}, f32[1536]{0:T(1024)}, u32[]{:S(2)}) copy-start(f32[1536]{0:T(1024)} %copy-done.49) | copy-start | bytes 18436
  544.5 16.6 %copy-start.52 = (f32[1024]{0:T(1024)S(1)}, f32[1024]{0:T(1024)}, u32[]{:S(2)}) copy-start(f32[1024]{0:T(1024)} %copy-done.51) | copy-start | bytes 12292
  561.1 10.5 copy-start.65
  561.1 10.5 copy-start.64
  561.1 10.5 copy-start.67
  561.1 10.5 copy-start.66
  561.1 10.5 copy-start.55
  561.1 10.5 copy-start.63
  572.3 209.5 %reduce-scatter.15.cloned.1.call-start = ((), (), s32[]{:S(2)}) async-start(), calls=%async_computation.11 | async-start | bytes 3244032
  586.5 258.2 %reduce-scatter.13.cloned.1.call-start = ((), (), s32[]{:S(2)}) async-start(), calls=%async_computation.10 | async-start | bytes 3244032
  600.8 362.7 %reduce-scatter.9.cloned.1.call-start = ((), (), s32[]{:S(2)}) async-start(), calls=%async_computation.7 | async-start | bytes 6488064 | tf_op jit(solution)/shard_map/reduce_scatter | solution.py:442
  612.5 11.5 %copy-start.16 = (bf16[1024,1024]{1,0:T(8,128)(2,1)S(1)}, bf16[1024,1024]{1,0:T(8,128)(2,1)}, u32[]{:S(2)}) copy-start(bf16[1024,1024]{1,0:T(8,128)(2,1)} %copy.97) | copy-start | bytes 6291460
  627.3 478.9 %reduce-scatter.11.cloned.1.call-start = ((), (), s32[]{:S(2)}) async-start(), calls=%async_computation.8 | async-start | bytes 4325376 | tf_op jit(solution)/shard_map/reduce_scatter | solution.py:442
  644.9 124.0 %collective-permute-start.20 = (bf16[768,1024]{1,0:T(8,128)(2,1)}, bf16[768,1024]{1,0:T(8,128)(2,1)}, u32[]{:S(2)}, u32[]{:S(2)}) collective-permute-start(bf16[768,1024]{1,0:T(8,128)(2,1)} %get-tuple-element.88), channel_id=1, source_target_pairs={{0,2},{1,3},{2,0},{3,1},{4,6},{5,7},{6,4},{7,5},{8,10},{9,11},{10,... | collective-permute-start | bytes 4718600 | tf_op jit(solution)/shard_map/ppermute | solution.py:298
  647.2 121.8 %copy-start.20 = (bf16[1,768,1024]{2,1,0:T(8,128)(2,1)S(1)}, bf16[1,768,1024]{2,1,0:T(8,128)(2,1)}, u32[]{:S(2)}) copy-start(bf16[1,768,1024]{2,1,0:T(8,128)(2,1)} %get-tuple-element.89) | copy-start | bytes 4718596
  648.6 120.3 %collective-permute-start.26 = (bf16[768,1024]{1,0:T(8,128)(2,1)}, bf16[768,1024]{1,0:T(8,128)(2,1)}, u32[]{:S(2)}, u32[]{:S(2)}) collective-permute-start(bf16[768,1024]{1,0:T(8,128)(2,1)} %get-tuple-element.82), channel_id=1, source_target_pairs={{0,2},{1,3},{2,0},{3,1},{4,6},{5,7},{6,4},{7,5},{8,10},{9,11},{10,... | collective-permute-start | bytes 4718600 | tf_op jit(solution)/shard_map/ppermute | solution.py:298
  780.9 326.8 %copy-start.1 = (bf16[32,6144]{1,0:T(8,128)(2,1)S(1)}, bf16[32,6144]{1,0:T(8,128)(2,1)}, u32[]{:S(2)}) copy-start(bf16[32,6144]{1,0:T(8,128)(2,1)} %param.21) | copy-start | bytes 1179652
  (46 other events, 193.2 us)
Sparse Core Ops, SparseCore 0:
  11.4 87.6 all-gather.6
  102.6 80.5 all-gather.8
  186.1 60.7 all-gather.10
  572.5 54.5 all-gather.12
  632.4 106.5 reduce-scatter.14
  744.2 100.4 reduce-scatter.12
  850.3 113.2 reduce-scatter.8
  966.0 140.1 reduce-scatter.10

commit v2 on v1

v2 whole, which is shorter than its diff:
```python
import functools
import math

import jax
import jax.numpy as jnp
from jax import lax
from jax.experimental import pallas as pl
from jax.experimental.pallas import tpu as pltpu
from jax.sharding import PartitionSpec as P

HDIM = 64
HALF = HDIM // 2
SCALE = HDIM ** (-0.5)
SCALE2 = SCALE * math.log2(math.e)
AXES = ("dp", "fsdp")
VMEM_LIMIT = 62 << 20
F32 = jnp.float32
BF16 = jnp.bfloat16


def dot(left_side, right_side, left_dim, right_dim):
    return lax.dot_general(
        left_side,
        right_side,
        (((left_dim,), (right_dim,)), ((), ())),
        preferred_element_type=F32,
    )


def pick_block(total, wanted):
    block = min(total, wanted)
    while total % block:
        block -= 128
    return block


def attend_kernel(parts, chunk, *refs):
    q_ref, bias_ref = refs[0], refs[1]
    k_refs, v_refs = refs[2 : 2 + parts], refs[2 + parts : 2 + 2 * parts]
    o_ref, lse_ref, k_aug, v_aug, q_aug = refs[2 + 2 * parts :]
    head, block = pl.program_id(0), pl.program_id(1)
    span = k_aug.shape[0]
    part = span // parts
    q_rows = q_ref.shape[1]

    @pl.when((head == 0) & (block == 0))
    def _():
        k_aug[:, HDIM:] = bias_ref[...]
        v_aug[HDIM:, :] = jnp.ones((16, span), BF16)
        q_aug[HDIM:, :] = jnp.ones((HDIM, q_rows), BF16)

    @pl.when(block == 0)
    def _():
        for i in range(parts):
            k_aug[i * part : (i + 1) * part, :HDIM] = k_refs[i][...].T
            v_aug[:HDIM, i * part : (i + 1) * part] = v_refs[i][...]

    q_aug[:HDIM, :] = q_ref[...]
    queries = q_aug[...]
    count = span // chunk

    def scores(i):
        return dot(k_aug[i * chunk : (i + 1) * chunk, :], queries, 1, 0)

    upcoming = scores(0)
    row_max = total = None
    for i in range(count):
        current = upcoming
        if i + 1 < count:
            upcoming = scores(i + 1)
        chunk_max = jnp.max(current, axis=0, keepdims=True) * SCALE2
        new_max = chunk_max if i == 0 else jnp.maximum(row_max, chunk_max)
        weights = jnp.exp2(current * SCALE2 - new_max).astype(BF16)
        update = dot(v_aug[:, i * chunk : (i + 1) * chunk], weights, 1, 0)
        total = update if i == 0 else total * jnp.exp2(row_max - new_max) + update
        row_max = new_max
    denominator = total[HDIM : HDIM + 1, :]
    o_ref[...] = (total[:HDIM, :] / denominator).astype(BF16)
    lse_ref[...] = (row_max + jnp.log2(denominator))[None]


def attend(q_rot, k_parts, v_parts, bias_columns, first):
    width, rows = k_parts[0].shape
    parts = len(k_parts)
    span = parts * rows
    heads = width // HDIM
    q_rows = pick_block(rows, 768)
    chunk = pick_block(span, 512)
    q_spec = pl.BlockSpec((HDIM, q_rows), lambda h, j: (h + first, j))
    k_spec = pl.BlockSpec((HDIM, rows), lambda h, j: (h, 0))
    return pl.pallas_call(
        functools.partial(attend_kernel, parts, chunk),
        grid=(heads, rows // q_rows),
        in_specs=[q_spec, pl.BlockSpec((span, HDIM), lambda h, j: (0, 0))] + [k_spec] * (2 * parts),
        out_specs=[
            pl.BlockSpec((HDIM, q_rows), lambda h, j: (h, j)),
            pl.BlockSpec((1, 1, q_rows), lambda h, j: (h, 0, j)),
        ],
        out_shape=[
            jax.ShapeDtypeStruct((width, rows), BF16),
            jax.ShapeDtypeStruct((heads, 1, rows), F32),
        ],
        scratch_shapes=[
            pltpu.VMEM((span, 2 * HDIM), BF16),
            pltpu.VMEM((HDIM + 16, span), BF16),
            pltpu.VMEM((2 * HDIM, q_rows), BF16),
        ],
        compiler_params=pltpu.CompilerParams(vmem_limit_bytes=VMEM_LIMIT),
        cost_estimate=pl.CostEstimate(
            flops=16 * heads * rows * span * HDIM,
            bytes_accessed=2 * width * (2 * rows + 2 * span),
            transcendentals=heads * rows * span,
        ),
        name="attend",
    )(q_rot, bias_columns, *k_parts, *v_parts)


def in_three(values):
    first = values.astype(BF16)
    rest = values - first.astype(F32)
    second = rest.astype(BF16)
    return first.astype(F32), second.astype(F32), rest - second.astype(F32)


def unrotate(values, cosine, sine):
    low, high = values[:HALF], values[HALF:]
    return low * cosine + high * sine, high * cosine - low * sine


def attend_back_kernel(parts, chunk, *refs):
    q_ref, do_ref, o_ref, lse_ref, bias_ref, cos_ref, sin_ref = refs[:7]
    k_refs, v_refs = refs[7 : 7 + parts], refs[7 + parts : 7 + 2 * parts]
    dq_ref = refs[7 + 2 * parts]
    dk_refs = refs[8 + 2 * parts : 8 + 3 * parts]
    dv_refs = refs[8 + 3 * parts : 8 + 4 * parts]
    k_aug, v_aug, k_rows, q_aug, do_aug, dk_acc, dv_acc = refs[8 + 4 * parts :]
    head, block = pl.program_id(0), pl.program_id(1)
    span = k_aug.shape[1]
    part = span // parts
    q_rows = q_ref.shape[1]

    @pl.when((head == 0) & (block == 0))
    def _():
        row = lax.broadcasted_iota(jnp.int32, (HDIM, span), 0)
        ones = jnp.where(row < 4, 1.0, 0.0)
        k_aug[HDIM:, :] = jnp.where(row == 0, bias_ref[...], ones).astype(BF16)
        v_aug[HDIM:, :] = jnp.where(row < 3, 1.0, 0.0).astype(BF16)
        k_rows[:, HDIM:] = jnp.zeros((span, HDIM), BF16)

    @pl.when(block == 0)
    def _():
        for i in range(parts):
            at = slice(i * part, (i + 1) * part)
            keys = k_refs[i][...]
            k_aug[:HDIM, at] = keys
            v_aug[:HDIM, at] = v_refs[i][...]
            k_rows[at, :HDIM] = keys.T
        dk_acc[...] = jnp.zeros_like(dk_acc)
        dv_acc[...] = jnp.zeros_like(dv_acc)

    queries, d_heads = q_ref[...], do_ref[...]
    delta = jnp.sum(d_heads.astype(F32) * o_ref[...].astype(F32), axis=0, keepdims=True)
    row = lax.broadcasted_iota(jnp.int32, (HDIM, q_rows), 0)
    lse_a, lse_b, lse_c = in_three(lse_ref[0] * (-1.0 / SCALE2))
    del_a, del_b, del_c = in_three(-delta)
    q_extra = jnp.where(row == 2, lse_b, jnp.where(row == 3, lse_c, 0.0))
    q_extra = jnp.where(row == 0, 1.0, jnp.where(row == 1, lse_a, q_extra))
    do_extra = jnp.where(row == 1, del_b, jnp.where(row == 2, del_c, 0.0))
    do_extra = jnp.where(row == 0, del_a, do_extra)
    q_aug[:HDIM, :] = queries
    q_aug[HDIM:, :] = q_extra.astype(BF16)
    do_aug[:HDIM, :] = d_heads
    do_aug[HDIM:, :] = do_extra.astype(BF16)
    q_side, do_side = q_aug[...].T, do_aug[...].T
    count = span // chunk

    def products(i):
        at = slice(i * chunk, (i + 1) * chunk)
        return dot(q_side, k_aug[:, at], 1, 0), dot(do_side, v_aug[:, at], 1, 0)

    upcoming = products(0)
    d_query = None
    for i in range(count):
        at = slice(i * chunk, (i + 1) * chunk)
        scores, d_probs = upcoming
        if i + 1 < count:
            upcoming = products(i + 1)
        probs = jnp.exp2(scores * SCALE2)
        d_scores = (probs * d_probs).astype(BF16)
        dv_acc[:, at] += dot(d_heads, probs.astype(BF16), 1, 0)
        dk_acc[:, at] += dot(queries, d_scores, 1, 0)
        update = dot(d_scores, k_rows[at, :], 1, 0)
        d_query = update if i == 0 else d_query + update
    first = pl.multiple_of(block * q_rows, q_rows)
    low, high = unrotate(
        d_query.T[:HDIM, :] * SCALE, cos_ref[:, pl.ds(first, q_rows)], sin_ref[:, pl.ds(first, q_rows)]
    )
    dq_ref[:HALF, :] = low.astype(BF16)
    dq_ref[HALF:, :] = high.astype(BF16)

    @pl.when(block == pl.num_programs(1) - 1)
    def _():
        for i in range(parts):
            at = slice(i * part, (i + 1) * part)
            low, high = unrotate(dk_acc[:, at] * SCALE, cos_ref[:, at], sin_ref[:, at])
            dk_refs[i][:HALF, :] = low.astype(dk_refs[i].dtype)
            dk_refs[i][HALF:, :] = high.astype(dk_refs[i].dtype)
            dv_refs[i][...] = dv_acc[:, at].astype(dv_refs[i].dtype)


def attend_back(q_rot, k_parts, v_parts, d_heads, heads_out, lse, bias_row, cosine, sine, first, within, count):
    rows = q_rot.shape[1]
    parts = len(k_parts)
    span = parts * rows
    q_rows = pick_block(rows, 1536)
    chunk = pick_block(span, 256)
    q_spec = pl.BlockSpec((HDIM, q_rows), lambda h, j: (h + first, j))
    k_spec = pl.BlockSpec((HDIM, rows), lambda h, j: (h + within, 0))
    whole = lambda array: pl.BlockSpec(array.shape, lambda h, j: (0, 0))
    part_out = pl.BlockSpec((HDIM, rows), lambda h, j: (h, 0))
    shape = lambda kind: jax.ShapeDtypeStruct((count * HDIM, rows), kind)
    part_kinds = [F32] + [BF16] * (parts - 1)
    out = pl.pallas_call(
        functools.partial(attend_back_kernel, parts, chunk),
        grid=(count, rows // q_rows),
        in_specs=[
            q_spec,
            q_spec,
            pl.BlockSpec((HDIM, q_rows), lambda h, j: (h + within, j)),
            pl.BlockSpec((1, 1, q_rows), lambda h, j: (h + within, 0, j)),
            whole(bias_row),
            whole(cosine),
            whole(sine),
        ]
        + [k_spec] * (2 * parts),
        out_specs=[pl.BlockSpec((HDIM, q_rows), lambda h, j: (h, j))] + [part_out] * (2 * parts),
        out_shape=[shape(BF16)] + [shape(kind) for kind in part_kinds * 2],
        scratch_shapes=[
            pltpu.VMEM((2 * HDIM, span), BF16),
            pltpu.VMEM((2 * HDIM, span), BF16),
            pltpu.VMEM((span, 2 * HDIM), BF16),
            pltpu.VMEM((2 * HDIM, q_rows), BF16),
            pltpu.VMEM((2 * HDIM, q_rows), BF16),
            pltpu.VMEM((HDIM, span), F32),
            pltpu.VMEM((HDIM, span), F32),
        ],
        compiler_params=pltpu.CompilerParams(vmem_limit_bytes=VMEM_LIMIT),
        cost_estimate=pl.CostEstimate(
            flops=10 * count * rows * span * HDIM,
            bytes_accessed=2 * count * HDIM * (8 * rows + 4 * span),
            transcendentals=0,
        ),
        name="attend_back",
    )(q_rot, d_heads, heads_out, lse, bias_row, cosine, sine, *k_parts, *v_parts)
    return out[0], out[1 : 1 + parts], out[1 + parts :]


def norm_parts(values):
    centered = values - jnp.mean(values, axis=-1, keepdims=True)
    scale = lax.rsqrt(jnp.mean(centered * centered, axis=-1, keepdims=True) + 1e-06)
    return centered * scale, scale


def norm_back(normed, scale, d_normed):
    return (
        d_normed
        - jnp.mean(d_normed, axis=-1, keepdims=True)
        - normed * jnp.mean(d_normed * normed, axis=-1, keepdims=True)
    ) * scale


def gelu_both(values):
    square = values * values
    bend = jnp.tanh(0.7978845608028654 * (values + 0.044715 * values * square))
    half = 0.5 * (1.0 + bend)
    slope = 0.7978845608028654 * (1.0 + 3 * 0.044715 * square)
    return values * half, half + 0.5 * values * (1.0 - bend * bend) * slope


def add_rows(values):
    return jnp.sum(values, axis=0, keepdims=True)


def store_rotated(out_ref, values, cosine, sine):
    for at in range(0, out_ref.shape[0], HDIM):
        low, high = values[at : at + HALF], values[at + HALF : at + HDIM]
        out_ref[at : at + HALF, :] = (low * cosine - high * sine).astype(BF16)
        out_ref[at + HALF : at + HDIM, :] = (high * cosine + low * sine).astype(BF16)


def either(first_ref, second_ref):
    half = pl.num_programs(0) // 2
    return jnp.where(pl.program_id(0) < half, first_ref[...], second_ref[...])


def halves_spec(inputs, rows, block, width):
    if inputs[0].shape[0] == rows:
        return [pl.BlockSpec((block, width), lambda i: (i, 0))] * 2
    half = rows // 2 // block
    return [
        pl.BlockSpec((block, width), lambda i: (jnp.minimum(i, half - 1), 0)),
        pl.BlockSpec((block, width), lambda i: (jnp.maximum(i - half, 0), 0)),
    ]


def project_kv_kernel(groups, x_ref, y_ref, vectors_ref, w_ref, cos_ref, sin_ref, h_ref, *refs):
    k_refs, v_refs = refs[:groups], refs[groups:]
    width = x_ref.shape[1]
    tall = width // groups
    normed, _ = norm_parts(either(x_ref, y_ref).astype(F32))
    h_one = (normed * (1.0 + vectors_ref[1:2, :]) + vectors_ref[0:1, :]).astype(BF16)
    h_ref[...] = h_one
    keys = (dot(h_one, w_ref[:, :width], 1, 0) + vectors_ref[7:8, :]).T
    values = (dot(h_one, w_ref[:, width:], 1, 0) + vectors_ref[8:9, :]).astype(BF16).T
    for i in range(groups):
        store_rotated(k_refs[i], keys[i * tall : (i + 1) * tall], cos_ref[...], sin_ref[...])
        v_refs[i][...] = values[i * tall : (i + 1) * tall]


def project_q_kernel(h_ref, vectors_ref, w_ref, cos_ref, sin_ref, q_ref):
    queries = dot(h_ref[...], w_ref[...], 1, 0) + vectors_ref[6:7, :]
    store_rotated(q_ref, queries.T, cos_ref[...], sin_ref[...])


def whole_spec(shape, column=0):
    return pl.BlockSpec(shape, lambda i: (0, column), pipeline_mode=pl.Buffered(1))


def project(inputs, vectors, packed, cosine, sine, groups):
    width, rows = inputs[0].shape[1], cosine.shape[1]
    block = pick_block(inputs[0].shape[0], 256)
    tall = width // groups
    row_spec = pl.BlockSpec((block, width), lambda i: (i, 0))
    turned_spec = lambda height: pl.BlockSpec((height, block), lambda i: (0, i))
    turned = lambda height: jax.ShapeDtypeStruct((height, rows), BF16)
    table_spec = turned_spec(HALF)
    params = pltpu.CompilerParams(vmem_limit_bytes=VMEM_LIMIT)
    out = pl.pallas_call(
        functools.partial(project_kv_kernel, groups),
        grid=(rows // block,),
        in_specs=halves_spec(inputs, rows, block, width)
        + [whole_spec(vectors.shape), whole_spec((width, 2 * width)), table_spec, table_spec],
        out_specs=[row_spec] + [turned_spec(tall)] * (2 * groups),
        out_shape=[jax.ShapeDtypeStruct((rows, width), BF16)] + [turned(tall)] * (2 * groups),
        compiler_params=params,
        cost_estimate=pl.CostEstimate(
            flops=8 * rows * width * width, bytes_accessed=8 * rows * width + 4 * width * width, transcendentals=0
        ),
        name="project_kv",
    )(*inputs, vectors, packed, cosine, sine)
    h_one, keys, values = out[0], out[1 : 1 + groups], out[1 + groups :]
    queries = pl.pallas_call(
        project_q_kernel,
        grid=(rows // block,),
        in_specs=[row_spec, whole_spec(vectors.shape), whole_spec((width, width), 2), table_spec, table_spec],
        out_specs=turned_spec(width),
        out_shape=turned(width),
        compiler_params=params,
        cost_estimate=pl.CostEstimate(
            flops=4 * rows * width * width, bytes_accessed=4 * rows * width + 2 * width * width, transcendentals=0
        ),
        name="project_q",
    )(h_one, vectors, packed, cosine, sine)
    return h_one, queries, keys, values


def feed_forward_kernel(parts, pieces, shard, *refs):
    o_refs = refs[:parts]
    x_ref, y_ref, cot_ref, cot_y_ref, keep_ref, w_ou_ref, w_down_ref, vectors_ref = refs[parts : parts + 8]
    mixed_ref, d_res_ref, d_heads_ref, g_rows_ref, sums_ref, g_b_up_ref = refs[parts + 8 : parts + 14]
    acc_ou, acc_down, acc_rows, acc_b_up, slope_ref, hidden_ref, staged, sems = refs[parts + 14 :]
    step = pl.program_id(0)
    width, hidden_width = x_ref.shape[1], w_down_ref.shape[0]
    piece = hidden_width // pieces

    @pl.when(step == 0)
    def _():
        for acc in (acc_ou, acc_down, acc_rows, acc_b_up):
            acc[...] = jnp.zeros_like(acc)

    gate_one, shift_two, scale_two, gate_two, b_out, b_down = [vectors_ref[i : i + 1, :] for i in (2, 3, 4, 5, 9, 10)]
    keep = keep_ref[...]
    heads_out = jnp.concatenate([ref[...] for ref in o_refs], axis=0)
    branch = (dot(heads_out, w_ou_ref[:, :width], 0, 0) + b_out) * keep
    residual = either(x_ref, y_ref).astype(F32) + gate_one * branch
    normed, inverse = norm_parts(residual)
    h_two = (normed * (1.0 + scale_two) + shift_two).astype(BF16)
    ff_out = b_down
    for i in range(pieces):
        at = slice(i * piece, (i + 1) * piece)
        value, slope = gelu_both(dot(h_two, w_ou_ref[:, width + i * piece : width + (i + 1) * piece], 1, 0) + vectors_ref[11 + i : 12 + i, :])
        slope_ref[:, at] = slope
        hidden = value.astype(BF16)
        hidden_ref[:, at] = hidden
        ff_out = ff_out + dot(hidden, w_down_ref[at, :], 1, 0)
    mixed_ref[...] = (residual + gate_two * ff_out).astype(BF16)
    d_mixed = either(cot_ref, cot_y_ref).astype(F32)
    acc_rows[3:4, :] += add_rows(d_mixed * ff_out)
    d_ff = (d_mixed * gate_two).astype(BF16)
    acc_rows[5:6, :] += add_rows(d_ff.astype(F32))
    d_h_two = None
    for i in range(pieces):
        at = slice(i * piece, (i + 1) * piece)
        up_at = slice(width + i * piece, width + (i + 1) * piece)
        acc_down[at, :] += dot(hidden_ref[:, at], d_ff, 0, 0)
        d_up = (dot(d_ff, w_down_ref[at, :], 1, 1) * slope_ref[:, at]).astype(BF16)
        acc_b_up[:, at] += add_rows(d_up.astype(F32))
        acc_ou[:, up_at] += dot(h_two, d_up, 0, 0)
        update = dot(d_up, w_ou_ref[:, up_at], 1, 1)
        d_h_two = update if i == 0 else d_h_two + update
    acc_rows[1:2, :] += add_rows(d_h_two)
    acc_rows[2:3, :] += add_rows(d_h_two * normed)
    d_residual = d_mixed + norm_back(normed, inverse, d_h_two * (1.0 + scale_two))
    d_res_ref[...] = d_residual
    acc_rows[0:1, :] += add_rows(d_residual * branch)
    d_branch = (d_residual * gate_one * keep).astype(BF16)
    acc_rows[4:5, :] += add_rows(d_branch.astype(F32))
    acc_ou[:, :width] += dot(heads_out, d_branch, 1, 0)
    d_heads_ref[...] = dot(w_ou_ref[:, :width], d_branch, 1, 1).astype(BF16)

    @pl.when(step == pl.num_programs(0) - 1)
    def _():
        sums_ref[...] = acc_rows[...]
        g_b_up_ref[...] = acc_b_up[...]
        tall = staged.shape[1]
        wide = acc_ou.shape[1]
        ups = hidden_width // width
        copies = []
        for i in range(width // tall):
            slot = i % 2
            if i >= 2:
                copies[i - 2].wait()
            staged[slot, :, :wide] = acc_ou[i * tall : (i + 1) * tall, :].astype(BF16)
            for up in range(ups):
                at = slice(wide + up * width, wide + (up + 1) * width)
                if shard % 16 == 0:
                    for j in range(0, tall, shard):
                        first = (i * tall + j) * ups + up * shard
                        staged[slot, j : j + shard, at] = acc_down[first : first + shard, :].astype(BF16)
                else:
                    first = up * width + i * tall
                    staged[slot, :, at] = acc_down[first : first + tall, :].astype(BF16)
            copies.append(pltpu.make_async_copy(staged.at[slot], g_rows_ref.at[pl.ds(i * tall, tall), :], sems.at[slot]))
            copies[i].start()
        for copy in copies[-2:]:
            copy.wait()


def feed_forward(inputs, heads_out, cotangent, keep, out_up, full_down, vectors, shard):
    rows, width = heads_out[0].shape[1], inputs[0].shape[1]
    hidden_width = full_down.shape[0]
    block = pick_block(inputs[0].shape[0], 256)
    row_spec = pl.BlockSpec((block, width), lambda i: (i, 0))
    turned_spec = lambda array: pl.BlockSpec((array, block), lambda i: (0, i))
    kinds = jax.ShapeDtypeStruct
    ou_shape, down_shape = out_up.shape, full_down.shape
    wide = ou_shape[1] + hidden_width
    return pl.pallas_call(
        functools.partial(feed_forward_kernel, len(heads_out), hidden_width // width, shard),
        grid=(rows // block,),
        in_specs=[turned_spec(part.shape[0]) for part in heads_out]
        + halves_spec(inputs, rows, block, width) * 2
        + [
            pl.BlockSpec((block, 1), lambda i: (i, 0)),
            whole_spec(ou_shape),
            whole_spec(down_shape),
            whole_spec(vectors.shape),
        ],
        out_specs=[
            row_spec,
            row_spec,
            turned_spec(width),
            pl.BlockSpec(memory_space=pl.ANY),
            whole_spec((8, width)),
            whole_spec((1, hidden_width)),
        ],
        out_shape=[
            kinds((rows, width), BF16),
            kinds((rows, width), F32),
            kinds((width, rows), BF16),
            kinds((width, wide), BF16),
            kinds((8, width), F32),
            kinds((1, hidden_width), F32),
        ],
        scratch_shapes=[
            pltpu.VMEM(ou_shape, F32),
            pltpu.VMEM(down_shape, F32),
            pltpu.VMEM((8, width), F32),
            pltpu.VMEM((1, hidden_width), F32),
            pltpu.VMEM((block, hidden_width), F32),
            pltpu.VMEM((block, hidden_width), BF16),
            pltpu.VMEM((2, pick_block(width, 256), wide), BF16),
            pltpu.SemaphoreType.DMA((2,)),
        ],
        compiler_params=pltpu.CompilerParams(vmem_limit_bytes=VMEM_LIMIT),
        cost_estimate=pl.CostEstimate(
            flops=2 * 6 * rows * width * (width + 2 * hidden_width),
            bytes_accessed=8 * rows * width + 4 * width * (width + 2 * hidden_width),
            transcendentals=rows * hidden_width,
        ),
        name="feed_forward",
    )(*heads_out, *inputs, *cotangent, keep, out_up, full_down, vectors)


def weight_grads_kernel(pieces, parts, h_ref, *refs):
    count = pieces * (1 + 2 * parts)
    per_piece = [refs[i * (1 + 2 * parts) : (i + 1) * (1 + 2 * parts)] for i in range(pieces)]
    dq_out, dk_out, dv_out, weight_ref, bias_ref = refs[count:]

    def summed(which):
        columns = []
        for piece in per_piece:
            total = piece[which][...]
            for i in range(1, parts):
                total = total + piece[which + i][...].astype(F32)
            columns.append(total.astype(BF16))
        return jnp.concatenate(columns, axis=0)

    grads = [
        jnp.concatenate([piece[0][...] for piece in per_piece], axis=0),
        summed(1),
        summed(1 + parts),
    ]
    for ref, grad in zip((dq_out, dk_out, dv_out), grads):
        ref[...] = grad
    weight_ref[...] = dot(jnp.concatenate(grads, axis=0), h_ref[...], 1, 0).T.astype(BF16)
    for i, grad in enumerate(grads):
        bias_ref[:, i : i + 1] = jnp.sum(grad.astype(F32), axis=1, keepdims=True)


def weight_grads(h_one, pieces):
    rows, width = h_one.shape
    heights = [piece[0].shape[0] for piece in pieces]
    tall = sum(heights)
    parts = len(pieces[0][1])
    kinds = jax.ShapeDtypeStruct
    whole = lambda shape: pl.BlockSpec(shape, lambda: (0, 0))
    flat = [array for piece in pieces for array in (piece[0], *piece[1], *piece[2])]
    return pl.pallas_call(
        functools.partial(weight_grads_kernel, len(pieces), parts),
        in_specs=[whole(array.shape) for array in (h_one, *flat)],
        out_specs=[whole((tall, rows))] * 3 + [whole((width, 3 * tall)), whole((tall, 128))],
        out_shape=[kinds((tall, rows), BF16)] * 3 + [kinds((width, 3 * tall), BF16), kinds((tall, 128), F32)],
        compiler_params=pltpu.CompilerParams(vmem_limit_bytes=VMEM_LIMIT),
        cost_estimate=pl.CostEstimate(
            flops=6 * rows * width * tall, bytes_accessed=16 * rows * tall + 2 * rows * width, transcendentals=0
        ),
        name="weight_grads",
    )(h_one, *flat)


def input_grads_kernel(groups, x_ref, d_res_ref, vectors_ref, w_ref, *refs):
    grad_refs, (out_ref, sums_ref) = refs[: 3 * groups], refs[3 * groups :]
    width = x_ref.shape[1]

    @pl.when(pl.program_id(0) == 0)
    def _():
        sums_ref[...] = jnp.zeros_like(sums_ref)

    turned = None
    for kind in range(3):
        first = (2, 0, 1)[kind] * width
        grad = jnp.concatenate([grad_refs[3 * g + kind][...] for g in range(groups)], axis=0)
        update = dot(w_ref[:, first : first + width], grad, 1, 0)
        turned = update if turned is None else turned + update
    d_h_one = turned.T
    normed, inverse = norm_parts(x_ref[...].astype(F32))
    sums_ref[0:1, :] += add_rows(d_h_one)
    sums_ref[1:2, :] += add_rows(d_h_one * normed)
    out_ref[...] = (d_res_ref[...] + norm_back(normed, inverse, d_h_one * (1.0 + vectors_ref[1:2, :]))).astype(BF16)


def input_grads(inputs, half, d_residual, vectors, packed, grads):
    rows, width = inputs.shape
    block = pick_block(rows, 256)
    first = half * (rows // block)
    row_spec = pl.BlockSpec((block, width), lambda i: (i, 0))
    flat = [grad for group in grads for grad in group]
    return pl.pallas_call(
        functools.partial(input_grads_kernel, len(grads)),
        grid=(rows // block,),
        in_specs=[
            row_spec,
            pl.BlockSpec((block, width), lambda i: (i + first, 0)),
            whole_spec(vectors.shape),
            whole_spec((width, 3 * width)),
        ]
        + [pl.BlockSpec((grad.shape[0], block), lambda i: (0, i + first)) for grad in flat],
        out_specs=[row_spec, whole_spec((8, width))],
        out_shape=[jax.ShapeDtypeStruct((rows, width), BF16), jax.ShapeDtypeStruct((8, width), F32)],
        compiler_params=pltpu.CompilerParams(vmem_limit_bytes=VMEM_LIMIT),
        cost_estimate=pl.CostEstimate(
            flops=6 * rows * width * width, bytes_accessed=14 * rows * width + 6 * width * width, transcendentals=0
        ),
        name="input_grads",
    )(inputs, d_residual, vectors, packed, *flat)


def time_features(t_index, model_width):
    half_width = model_width // 2
    indices = jnp.arange(half_width).astype(F32)
    frequency = jnp.exp(indices * (-math.log(10000.0) / (half_width - 1)))
    angles = t_index.astype(F32)[:, None] * frequency[None, :]
    return jnp.concatenate([jnp.sin(angles), jnp.cos(angles)], axis=1)


def rotary_tables(places):
    inverse = jnp.exp(jnp.arange(HALF).astype(F32) * (-2.0 * math.log(10000.0) / HDIM))
    angles = inverse[:, None] * places.astype(F32)[None, :]
    return jnp.cos(angles), jnp.sin(angles)


def after(values, *others):
    return lax.optimization_barrier((values,) + others)[0]


def make_body(mesh):
    n_dp, n_fsdp = mesh.shape["dp"], mesh.shape["fsdp"]
    n_pairs = n_fsdp // 2

    def shift(values, axis, size, by):
        return lax.ppermute(values, axis, [(i, (i + by) % size) for i in range(size)])

    def pick(values, index, axis=0):
        return lax.dynamic_index_in_dim(values, index, axis, keepdims=False)

    def body(
        frames,
        lengths,
        t_index,
        w_ada,
        b_ada,
        w_query,
        b_query,
        w_key,
        b_key,
        w_value,
        b_value,
        w_out,
        b_out,
        w_up,
        b_up,
        w_down,
        b_down,
        grad_out,
    ):
        slots, local, width = frames.shape
        group = n_fsdp // slots
        hidden_width = w_up.shape[1]
        shard = w_query.shape[0]
        ada_width = w_ada.shape[1]
        dp, fsdp = lax.axis_index("dp"), lax.axis_index("fsdp")
        me = dp * n_fsdp + fsdp
        slot, place = fsdp // group, fsdp % group
        other = 1 - slot
        core, pair = fsdp % 2, fsdp // 2
        side, deep, far = dp % 2, dp // 2, n_dp // 2
        length = pick(lengths, slot)

        def picked(values):
            return pick(values, slot), pick(values, other)

        split = local % 128 == 0

        def swap_in(own, away):
            parts = own, shift(away, "fsdp", n_fsdp, group)
            return parts if split else (jnp.concatenate(parts),) * 2

        def swap_out(own, away):
            whole = jnp.zeros((slots, local, width), own.dtype)
            whole = lax.dynamic_update_index_in_dim(whole, own, slot, 0)
            arrived = shift(away, "fsdp", n_fsdp, group)
            return lax.dynamic_update_index_in_dim(whole, arrived, other, 0)

        def places_of(member):
            at = slot * group + member
            blocks = [((at - by * group) + n_fsdp) % n_fsdp for by in range(slots)]
            return jnp.concatenate([b * local + jnp.arange(local, dtype=jnp.int32) for b in blocks])

        ring = lambda by: [(i, (i // group) * group + (i % group + by) % group) for i in range(n_fsdp)]

        def swap(values, axis, size):
            return lax.ppermute(values, axis, [(i, i ^ 1) for i in range(size)])

        def sum_core(values):
            values = values.reshape(n_dp, n_pairs, 2, shard, values.shape[1])
            arrived = swap(pick(values, 1 - core, 2), "fsdp", n_fsdp)
            return (pick(values, core, 2).astype(F32) + arrived.astype(F32)).astype(BF16)

        def sum_pairs(values):
            total = pick(values, pair, 1).astype(F32)
            for by in range(1, n_pairs):
                arrived = shift(pick(values, (pair + by) % n_pairs, 1), "fsdp", n_fsdp, 2 * by)
                total = total + arrived.astype(F32)
            return total.astype(BF16)

        def sum_side(values):
            values = values.reshape((far, 2) + values.shape[1:])
            arrived = swap(pick(values, 1 - side, 1), "dp", n_dp)
            return (pick(values, side, 1).astype(F32) + arrived.astype(F32)).astype(BF16)

        def sum_far(values):
            total = pick(values, deep).astype(F32)
            for by in range(1, far):
                arrived = shift(pick(values, (deep + by) % far), "dp", n_dp, 2 * by)
                total = total + arrived.astype(F32)
            return total

        def gather_dp(values):
            values = jnp.stack([values] + [shift(values, "dp", n_dp, 2 * by) for by in range(1, far)])
            return jnp.stack([values, swap(values, "dp", n_dp)])

        packed = lax.all_gather(jnp.concatenate([w_key, w_value, w_query], axis=1), AXES, axis=0, tiled=True)
        out_up = lax.all_gather(jnp.concatenate([w_out, w_up], axis=1), AXES, axis=0, tiled=True)
        full_down = lax.all_gather(w_down, AXES, axis=0, tiled=True)

        inputs = swap_in(*picked(frames))
        rows = slots * local
        own_grad, away_grad = picked(grad_out)

        t_all = gather_dp(t_index).reshape(-1)
        active = jax.nn.silu(time_features(t_all, width)).astype(BF16)
        active_mine = lax.dynamic_slice_in_dim(active, me * shard, shard, axis=1)
        partial = [dot(active_mine, w_ada, 1, 0)]
        for bias in (b_query, b_key, b_value, b_out, b_down, b_up):
            size = bias.shape[0]
            zeros = jnp.zeros((1, size * n_dp * n_fsdp), F32)
            placed = lax.dynamic_update_slice_in_dim(zeros, bias.astype(F32)[None], me * size, axis=1)
            partial.append(jnp.broadcast_to(placed, (n_dp * slots, placed.shape[1])))
        placed = lax.dynamic_update_slice_in_dim(
            jnp.zeros((1, ada_width), F32), b_ada.astype(F32)[None], me * b_ada.shape[0], axis=1
        )
        partial[0] = partial[0] + placed
        partial = jnp.concatenate(partial, axis=1).reshape(2, far, slots, -1)
        partial = partial[0] + swap(partial[1], "dp", n_dp)
        summed = partial[0]
        for by in range(1, far):
            summed = summed + shift(partial[by], "dp", n_dp, -2 * by)
        one = pick(summed, slot) + shift(pick(summed, other), "fsdp", n_fsdp, group)
        vectors = one
        for by in range(1, group):
            vectors = vectors + lax.ppermute(one, "fsdp", ring(by))
        vectors = vectors.reshape(-1, width)
        vectors = jnp.pad(vectors, ((0, -vectors.shape[0] % 8), (0, 0)))

        key_places = jnp.concatenate([places_of((place - by + group) % group) for by in range(group)])
        cosine, sine = rotary_tables(key_places)
        key_bias = jnp.where(key_places < length, 0.0, -1e30)
        bias_columns = jnp.pad(key_bias.astype(BF16)[:, None], ((0, 0), (0, HDIM - 1)))
        keep = (key_places[:rows] < length).astype(F32)[:, None]

        wide = 2
        vectors, cosine, sine, key_bias, bias_columns, keep, own_grad, away_grad = lax.optimization_barrier(
            (vectors, cosine, sine, key_bias, bias_columns, keep, own_grad, away_grad)
        )
        h_one, q_rot, keys, values = project(inputs, vectors, packed, cosine[:, :rows], sine[:, :rows], wide)
        cotangent = swap_in(own_grad, after(away_grad, keys[0]))
        heads = width // HDIM
        tall = heads // wide
        with_ring = lambda own: [own] + [lax.ppermute(own, "fsdp", ring(by)) for by in range(1, group)]
        k_parts, v_parts = [with_ring(own) for own in keys], [with_ring(own) for own in values]
        heads_out, lses = [], []
        for at in range(wide):
            out, lse = attend(q_rot, k_parts[at], v_parts[at], bias_columns, at * tall)
            heads_out.append(out)
            lses.append(lse)
        mixed, d_residual, d_heads, g_rows, sums_two, g_b_up = feed_forward(
            inputs, heads_out, cotangent, keep, out_up, full_down, vectors, shard
        )
        mixed = swap_out(mixed[:local], mixed[local:])

        if shard % 16:
            first = width + hidden_width
            g_down = jnp.concatenate([g_rows[:, first + i * width : first + (i + 1) * width] for i in range(hidden_width // width)])
            g_down = g_down.reshape(n_dp * n_fsdp, -1, shard, width)
            g_down = [g_down[:, i].reshape(-1, width) for i in range(g_down.shape[1])]
            g_rows = jnp.concatenate([g_rows[:, :first]] + g_down, axis=1)
        sum_rows = lax.psum_scatter(g_rows, AXES, scatter_dimension=0, tiled=True).astype(F32)

        grads, d_biases, moving = [], [], []
        stages = [sum_core, sum_pairs, sum_side, sum_far]

        def start_sum(pieces):
            dq, dk, dv, weight_grad, bias_grad = weight_grads(h_one, pieces)
            grads.append((dq, dk, dv))
            d_biases.append(bias_grad[:, :3])
            moving.append([0, weight_grad])
            return weight_grad

        def move_on(pick_from):
            for item in pick_from:
                if item[0] < len(stages):
                    item[1] = stages[item[0]](item[1])
                    item[0] += 1
            return [item[1] for item in pick_from]

        counts = (4, 4, 2, 2, 2, 2)
        joined = (1, 1, 2, 2)
        steps = len(counts)
        waiting, ready, first, next_sum = [], d_heads, 0, 0
        for step, each in enumerate(counts):
            part, within = first // tall, first % tall
            dq, dk_parts, dv_parts = attend_back(
                q_rot,
                k_parts[part],
                v_parts[part],
                ready,
                heads_out[part],
                lses[part],
                key_bias[None],
                cosine,
                sine,
                first,
                within,
                each,
            )
            first += each
            done = move_on(moving)
            if len(waiting) >= joined[next_sum]:
                done.append(start_sum(waiting[: joined[next_sum]]))
                waiting = waiting[joined[next_sum] :]
                next_sum += 1
            dk_parts = [dk_parts[0]] + [lax.ppermute(dk_parts[by], "fsdp", ring(-by)) for by in range(1, group)]
            dv_parts = [dv_parts[0]] + [lax.ppermute(dv_parts[by], "fsdp", ring(-by)) for by in range(1, group)]
            waiting.append((dq, dk_parts, dv_parts))
            if done and step + 1 < steps:
                ready = after(d_heads, dq, *done)
        last = start_sum(waiting)
        if split:
            rest = after(d_residual, last)
            away_frames, sums_away = input_grads(inputs[1], 1, rest, vectors, packed, grads)
            done = move_on(moving)
            rest, away_frames = lax.optimization_barrier((d_residual, away_frames, *done))[:2]
            own_frames, sums_own = input_grads(inputs[0], 0, rest, vectors, packed, grads)
            sums_one = sums_own + sums_away
        else:
            both, sums_one = input_grads(inputs[0], 0, d_residual, vectors, packed, grads)
            own_frames, away_frames = both[:local], both[local:]
        grad_frames = swap_out(own_frames, away_frames)
        for _ in stages:
            move_on(moving)
        sums = [item[1] for item in moving]

        vector = jnp.concatenate(
            [sums_one[:2], sums_two[:6], g_b_up.reshape(-1, width), jnp.concatenate(d_biases).T]
        )
        for_slot = 6
        total = vector
        for by in range(1, group):
            total = total + lax.ppermute(vector, "fsdp", ring(by))
        packs = gather_dp(total).reshape(n_dp, -1, width)
        pack = jnp.concatenate([packs[:, :for_slot].reshape(-1, width), jnp.sum(packs[:, for_slot:], axis=0)])
        across = shift(pack, "fsdp", n_fsdp, group)
        count = n_dp * for_slot
        d_mod = jnp.stack([jnp.where(slot == s, pack[:count], across[:count]).reshape(n_dp, -1) for s in range(slots)], axis=1)
        d_mod = d_mod.reshape(n_dp * slots, for_slot * width)
        d_vectors = pack[count:] + across[count:]

        g_w_ada = lax.dot_general(
            active_mine.astype(F32),
            d_mod,
            (((0,), (0,)), ((), ())),
            precision=lax.Precision.HIGHEST,
            preferred_element_type=F32,
        )

        def mine(vector):
            vector = vector.reshape(-1)
            size = vector.shape[0] // (n_dp * n_fsdp)
            return lax.dynamic_slice_in_dim(vector, me * size, size)

        ups = hidden_width // width
        columns = [values.reshape(shard, 3, -1) for values in sums]
        g_qkv = [jnp.concatenate([values[:, i] for values in columns], axis=1) for i in range(3)]
        g_down = sum_rows[:, width + hidden_width :].reshape(shard, -1, width)
        return (
            mixed,
            grad_frames,
            g_w_ada,
            mine(jnp.sum(d_mod, axis=0)),
            g_qkv[0],
            mine(d_vectors[2 + ups]),
            g_qkv[1],
            mine(d_vectors[3 + ups]),
            g_qkv[2],
            mine(d_vectors[4 + ups]),
            sum_rows[:, :width],
            mine(d_vectors[0]),
            sum_rows[:, width : width + hidden_width],
            mine(d_vectors[2 : 2 + ups]),
            jnp.swapaxes(g_down, 0, 1).reshape(w_down.shape),
            mine(d_vectors[1]),
        )

    return body


def solution(mesh):
    rows, vector, matrix = P("dp", "fsdp", None), P(AXES), P(AXES, None)
    return jax.shard_map(
        make_body(mesh),
        mesh=mesh,
        in_specs=(rows, P("dp"), P("dp")) + (matrix, vector) * 7 + (rows,),
        out_specs=(rows, rows) + (matrix, vector) * 7,
        check_vma=False,
    )
```

time: 1120 us -> 727 us (0.65)
  waiting for transfers between devices: 361 us -> 105 us
  matrix products: 191 us -> 2.92 us
  Pallas kernels: 279 us -> 440 us
  blocking collectives: 112 us -> 0 us
  starting transfers between devices: 34.5 us -> 55.3 us
  other arithmetic: 59.2 us -> 42 us
    reduce_scatter x2 -> x1, waiting for transfers between devices: 255 us -> 0.02 us  [body(): lax.psum_scatter(g_rows, AXES, scatter_dimension=0, tiled=True).astype(F32)]
    dot_general x25 -> x1, matrix products: 189 us -> 0.28 us  [dot(): lax.dot_general(left_side, right_side, (((left_dim,), (right_dim,)), ((),...]
    pallas_call x0 -> x8, Pallas kernels: none -> 143 us  [the longest x1 78.9 us: feed_forward(): pl.pallas_call(functools.partial(feed_forward_kernel, len(heads_out), hid...]
    all_gather x1 -> x0, blocking collectives: 112 us -> none  [gather_vectors(): return lax.all_gather(values[None], AXES, axis=0, tiled=True)]
    unnamed x10 -> x4, waiting for transfers between devices: 61.4 us -> 0.75 us
    unnamed x174 -> x90, local copies, waits for them, and re-layouts: 24.9 us -> 3.74 us
    reduce_sum x13 -> x4, other arithmetic: 21.3 us -> 0.79 us  [the longest x3 0.75 us: body(): jnp.sum(d_mod, axis=0)]
    ppermute x6 -> x29, waiting for transfers between devices: 0.02 us -> 18.3 us  [the longest x11 17.3 us: swap(): return lax.ppermute(values, axis, [(i, i ^ 1) for i in range(size)])]
  transfers between devices with their start and end apart: 35 -> 64, of which waited for: 10 -> 20; matrix products, arithmetic and copies ran while one was open for 18% -> 13% of each run, Pallas kernels for 17% -> 50%
where the time goes in v2:
time: 727 us; the launch traced here: 722 us
  Pallas kernels  440 us (61%)
  waiting for transfers between devices  105 us (14%)
  local copies, waits for them, and re-layouts  61 us (8%)
  starting transfers between devices  55.3 us (8%)
  other arithmetic  42 us (6%)
  between operations  15.3 us (2%)
    pallas_call x6, Pallas kernels, attend_back(): pl.pallas_call(functools.partial(attend_back_kernel, parts, chunk), grid=...  194 us
    pallas_call x2, Pallas kernels, attend(): pl.pallas_call(functools.partial(attend_kernel, parts, chunk), grid=(head...  103 us
    pallas_call x1, Pallas kernels, feed_forward(): pl.pallas_call(functools.partial(feed_forward_kernel, len(heads_out), hid...  78.9 us
    ppermute x31, waiting for transfers between devices, shift(): lax.ppermute(values, axis, [(i, (i + by) % size) for i in range(size)])  54 us
    ppermute x31, starting transfers between devices, shift(): lax.ppermute(values, axis, [(i, (i + by) % size) for i in range(size)])  41.7 us
    pallas_call x4, Pallas kernels, weight_grads(): pl.pallas_call(functools.partial(weight_grads_kernel, len(pieces), parts)...  30.1 us
    all_gather x1, waiting for transfers between devices, body(): lax.all_gather(jnp.concatenate([w_key, w_value, w_query], axis=1), AXES,...  17.4 us
    ppermute x11, waiting for transfers between devices, swap(): return lax.ppermute(values, axis, [(i, i ^ 1) for i in range(size)])  17.3 us
  transfers between devices with their start and end apart: 64, of which 20 were waited for; matrix products, arithmetic and copies ran while one was open for 13% of the time, Pallas kernels for 50%

profile of v2, /device:TPU:0, one launch (start us, length us, event | category | flops | bytes accessed | tf_op | source)
XLA Modules:
  0.0 721.7 jit_solution(2832408992280193561)
XLA Ops:
  7.2 1.6 pad_maximum_fusion.4
  9.7 3.1 collective-permute-start.1
  12.8 2.6 collective-permute-start.2
  16.8 4.0 dynamic-slice_bitcast_fusion.2
  24.1 1.6 collective-permute-start.4
  25.8 2.0 collective-permute-done.4
  30.7 1.5 collective-permute-start.5
  32.3 2.2 multiply_sine_fusion
  36.4 2.2 squeeze.177
  38.6 2.2 collective-permute-done.5
  42.6 1.7 collective-permute-start.7
  44.8 1.9 add_compare_fusion
  46.8 3.0 collective-permute-done.6
  49.8 6.4 collective-permute-done.7
  56.6 2.0 dynamic-slice_bitcast_fusion
  58.7 5.8 collective-permute-done.9
  72.1 17.4 %all-gather.4.cloned.1.call-done.w_ref = bf16[1024,3072]{1,0:T(8,128)(2,1)} async-done(((bf16[32,3072]{1,0:T(8,128)(2,1)}), bf16[1024,3072]{1,0:T(8,128)(2,1)}) %all-gather.4.cloned.1.call-update) | async-done | bytes 6291472 | tf_op jit(solution)/shard_map/all_gather | solution.py:713
  89.5 13.6 %project_kv.1 = (bf16[1536,1024]{1,0:T(8,128)(2,1)}, bf16[512,1536]{1,0:T(8,128)(2,1)}, bf16[512,1536]{1,0:T(8,128)(2,1)}, bf16[512,1536]{1,0:T(8,128)(2,1)}, bf16[512,1536]{1,0:T(8,128)(2,1)}) custom-call(bf16[768,1024]{1,0:T(8,128)(2,1)} %get-tuple-element.193.x_ref.refs_2_, bf16[768,1024]{1,0:T(8,128)(2,1)} %collective-permute-done.y_ref.refs_3_.x_ref, ...), custom_call_target="tpu_custom_call" | custom-call | flops 12884901888 | bytes 16777216 | tf_op jit(solution)/shard_map/project_kv/pallas_call | solution.py:338
  105.4 8.7 %project_q.1.refs_0_ = bf16[1024,1536]{1,0:T(8,128)(2,1)} custom-call(bf16[1536,1024]{1,0:T(8,128)(2,1)} %get-tuple-element.104.h_ref, f32[16,1024]{1,0:T(8,128)} %pad.8.vectors_ref.refs_9_, bf16[1024,3072]{1,0:T(8,128)(2,1)} %all-gather.4.cloned.1.call-done.w_ref, f32[32,1536]{1,0:T(8,128)} %slice.132.cos_ref, f32[32,1536]{1,0:T(8,128)} %slice.133.sin_ref), custom_call_target="tpu_custom_call" | custom-call | flops 6442450944 | bytes 8388608 | tf_op jit(solution)/shard_map/project_q/pallas_call | solution.py:352
  114.1 51.6 %attend.3 = (bf16[512,1536]{1,0:T(8,128)(2,1)}, f32[8,1,1536]{2,1,0:T(1,128)}) custom-call(bf16[1024,1536]{1,0:T(8,128)(2,1)} %project_q.1.refs_0_, bf16[3072,64]{1,0:T(8,128)(2,1)} %pad.9.refs_1_, bf16[512,1536]{1,0:T(8,128)(2,1)} %get-tuple-element.109.refs_2_.refs_7_, bf16[512,1536]{1,0:T(8,128)(2,1)} %collective-permute-done.13.refs_3_.refs_8_, ...), custom_call_target="tpu_custom_call" | custom-call | flops 38654705664 | bytes 9437184 | tf_op jit(solution)/shard_map/attend/pallas_call | solution.py:91
  165.8 51.5 %attend.2 = (bf16[512,1536]{1,0:T(8,128)(2,1)}, f32[8,1,1536]{2,1,0:T(1,128)}) custom-call(bf16[1024,1536]{1,0:T(8,128)(2,1)} %project_q.1.refs_0_, bf16[3072,64]{1,0:T(8,128)(2,1)} %pad.9.refs_1_, bf16[512,1536]{1,0:T(8,128)(2,1)} %get-tuple-element.106.refs_2_.refs_7_, bf16[512,1536]{1,0:T(8,128)(2,1)} %collective-permute-done.11.refs_3_.refs_8_, ...), custom_call_target="tpu_custom_call" | custom-call | flops 38654705664 | bytes 9437184 | tf_op jit(solution)/shard_map/attend/pallas_call | solution.py:91
  217.2 14.5 %all-gather.6.cloned.1.call-done.refs_7_ = bf16[1024,3072]{1,0:T(8,128)(2,1)} async-done(((bf16[32,3072]{1,0:T(8,128)(2,1)}), bf16[1024,3072]{1,0:T(8,128)(2,1)}) %all-gather.6.cloned.1.call-update) | async-done | bytes 6291472 | tf_op jit(solution)/shard_map/all_gather | solution.py:714
  231.7 78.9 %feed_forward.1 = (bf16[1536,1024]{1,0:T(8,128)(2,1)}, f32[1536,1024]{1,0:T(8,128)}, bf16[1024,1536]{1,0:T(8,128)(2,1)}, bf16[1024,5120]{1,0:T(8,128)(2,1)}, f32[8,1024]{1,0:T(8,128)}, /*index=5*/f32[1,2048]{1,0:T(1,128)}) custom-call(bf16[512,1536]{1,0:T(8,128)(2,1)} %get-tuple-element.108.refs_0_.refs_2_, ...), custom_call_target="tpu_custom_call" | custom-call | flops 96636764160 | bytes 33554432 | tf_op jit(solution)/shard_map/feed_forward/pallas_call | solution.py:458
  310.8 46.7 %attend_back.7 = (bf16[256,1536]{1,0:T(8,128)(2,1)}, f32[256,1536]{1,0:T(8,128)}, bf16[256,1536]{1,0:T(8,128)(2,1)}, f32[256,1536]{1,0:T(8,128)}, bf16[256,1536]{1,0:T(8,128)(2,1)}) custom-call(bf16[1024,1536]{1,0:T(8,128)(2,1)} %project_q.1.refs_0_, bf16[1024,1536]{1,0:T(8,128)(2,1)} %get-tuple-element.153.refs_1_, ...), custom_call_target="tpu_custom_call" | custom-call | flops 12079595520 | bytes 12582912 | tf_op jit(solution)/shard_map/attend_back/pallas_call | solution.py:223
  358.1 46.9 %attend_back.6 = (bf16[256,1536]{1,0:T(8,128)(2,1)}, f32[256,1536]{1,0:T(8,128)}, bf16[256,1536]{1,0:T(8,128)(2,1)}, f32[256,1536]{1,0:T(8,128)}, bf16[256,1536]{1,0:T(8,128)(2,1)}) custom-call(bf16[1024,1536]{1,0:T(8,128)(2,1)} %project_q.1.refs_0_, bf16[1024,1536]{1,0:T(8,128)(2,1)} %get-tuple-element.153.refs_1_, ...), custom_call_target="tpu_custom_call" | custom-call | flops 12079595520 | bytes 12582912 | tf_op jit(solution)/shard_map/attend_back/pallas_call | solution.py:223
  406.8 2.7 slice.135
  410.9 2.1 broadcast.108.clone
  415.4 7.6 %weight_grads.4 = (bf16[256,1536]{1,0:T(8,128)(2,1)}, bf16[256,1536]{1,0:T(8,128)(2,1)}, bf16[256,1536]{1,0:T(8,128)(2,1)}, bf16[1024,768]{1,0:T(8,128)(2,1)}, f32[256,128]{1,0:T(8,128)}) custom-call(bf16[1536,1024]{1,0:T(8,128)(2,1)} %get-tuple-element.104.h_ref, bf16[256,1536]{1,0:T(8,128)(2,1)} %get-tuple-element.122.refs_0_, ...), custom_call_target="tpu_custom_call" | custom-call | flops 2415919104 | bytes 9437184 | tf_op jit(solution)/shard_map/weight_grads/pallas_call | solution.py:539
  423.0 1.5 constant_dynamic-slice_fusion.12
  424.7 25.4 %attend_back.8 = (bf16[128,1536]{1,0:T(8,128)(2,1)}, f32[128,1536]{1,0:T(8,128)}, bf16[128,1536]{1,0:T(8,128)(2,1)}, f32[128,1536]{1,0:T(8,128)}, bf16[128,1536]{1,0:T(8,128)(2,1)}) custom-call(bf16[1024,1536]{1,0:T(8,128)(2,1)} %project_q.1.refs_0_, bf16[1024,1536]{1,0:T(8,128)(2,1)} %get-tuple-element.153.refs_1_, ...), custom_call_target="tpu_custom_call" | custom-call | flops 6039797760 | bytes 6291456 | tf_op jit(solution)/shard_map/attend_back/pallas_call | solution.py:223
  450.8 7.5 %weight_grads.5 = (bf16[256,1536]{1,0:T(8,128)(2,1)}, bf16[256,1536]{1,0:T(8,128)(2,1)}, bf16[256,1536]{1,0:T(8,128)(2,1)}, bf16[1024,768]{1,0:T(8,128)(2,1)}, f32[256,128]{1,0:T(8,128)}) custom-call(bf16[1536,1024]{1,0:T(8,128)(2,1)} %get-tuple-element.104.h_ref, bf16[256,1536]{1,0:T(8,128)(2,1)} %get-tuple-element.121.refs_0_, ...), custom_call_target="tpu_custom_call" | custom-call | flops 2415919104 | bytes 9437184 | tf_op jit(solution)/shard_map/weight_grads/pallas_call | solution.py:539
  458.3 2.4 constant_dynamic-slice_fusion.10
  463.6 24.8 %attend_back.9 = (bf16[128,1536]{1,0:T(8,128)(2,1)}, f32[128,1536]{1,0:T(8,128)}, bf16[128,1536]{1,0:T(8,128)(2,1)}, f32[128,1536]{1,0:T(8,128)}, bf16[128,1536]{1,0:T(8,128)(2,1)}) custom-call(bf16[1024,1536]{1,0:T(8,128)(2,1)} %project_q.1.refs_0_, bf16[1024,1536]{1,0:T(8,128)(2,1)} %get-tuple-element.153.refs_1_, ...), custom_call_target="tpu_custom_call" | custom-call | flops 6039797760 | bytes 6291456 | tf_op jit(solution)/shard_map/attend_back/pallas_call | solution.py:223
  489.2 1.6 fusion.3
  491.7 2.7 bitcast_dynamic-update-slice_fusion.2
  494.4 5.7 collective-permute-done.22
  500.8 25.2 %attend_back.10 = (bf16[128,1536]{1,0:T(8,128)(2,1)}, f32[128,1536]{1,0:T(8,128)}, bf16[128,1536]{1,0:T(8,128)(2,1)}, f32[128,1536]{1,0:T(8,128)}, bf16[128,1536]{1,0:T(8,128)(2,1)}) custom-call(bf16[1024,1536]{1,0:T(8,128)(2,1)} %project_q.1.refs_0_, bf16[1024,1536]{1,0:T(8,128)(2,1)} %get-tuple-element.153.refs_1_, ...), custom_call_target="tpu_custom_call" | custom-call | flops 6039797760 | bytes 6291456 | tf_op jit(solution)/shard_map/attend_back/pallas_call | solution.py:223
  528.1 7.5 %weight_grads.6 = (bf16[256,1536]{1,0:T(8,128)(2,1)}, bf16[256,1536]{1,0:T(8,128)(2,1)}, bf16[256,1536]{1,0:T(8,128)(2,1)}, bf16[1024,768]{1,0:T(8,128)(2,1)}, f32[256,128]{1,0:T(8,128)}) custom-call(bf16[1536,1024]{1,0:T(8,128)(2,1)} %get-tuple-element.104.h_ref, bf16[128,1536]{1,0:T(8,128)(2,1)} %get-tuple-element.130.refs_0_, ...), custom_call_target="tpu_custom_call" | custom-call | flops 2415919104 | bytes 9437184 | tf_op jit(solution)/shard_map/weight_grads/pallas_call | solution.py:539
  536.7 1.5 constant_dynamic-slice_fusion.8
  542.4 3.8 collective-permute-done.37
  546.1 1.8 collective-permute-start.36
  548.0 25.0 %attend_back.11 = (bf16[128,1536]{1,0:T(8,128)(2,1)}, f32[128,1536]{1,0:T(8,128)}, bf16[128,1536]{1,0:T(8,128)(2,1)}, f32[128,1536]{1,0:T(8,128)}, bf16[128,1536]{1,0:T(8,128)(2,1)}) custom-call(bf16[1024,1536]{1,0:T(8,128)(2,1)} %project_q.1.refs_0_, bf16[1024,1536]{1,0:T(8,128)(2,1)} %get-tuple-element.153.refs_1_, ...), custom_call_target="tpu_custom_call" | custom-call | flops 6039797760 | bytes 6291456 | tf_op jit(solution)/shard_map/attend_back/pallas_call | solution.py:223
  573.3 1.8 collective-permute-start.39
  575.1 2.2 collective-permute-start.40
  577.4 1.7 collective-permute-done.38
  582.9 7.5 %weight_grads.7 = (bf16[256,1536]{1,0:T(8,128)(2,1)}, bf16[256,1536]{1,0:T(8,128)(2,1)}, bf16[256,1536]{1,0:T(8,128)(2,1)}, bf16[1024,768]{1,0:T(8,128)(2,1)}, f32[256,128]{1,0:T(8,128)}) custom-call(bf16[1536,1024]{1,0:T(8,128)(2,1)} %get-tuple-element.104.h_ref, bf16[128,1536]{1,0:T(8,128)(2,1)} %get-tuple-element.139.refs_0_, ...), custom_call_target="tpu_custom_call" | custom-call | flops 2415919104 | bytes 9437184 | tf_op jit(solution)/shard_map/weight_grads/pallas_call | solution.py:539
  590.4 1.5 constant_dynamic-slice_fusion.6
  596.0 11.6 %input_grads.2 = (bf16[768,1024]{1,0:T(8,128)(2,1)}, f32[8,1024]{1,0:T(8,128)}) custom-call(bf16[768,1024]{1,0:T(8,128)(2,1)} %collective-permute-done.y_ref.refs_3_.x_ref, f32[1536,1024]{1,0:T(8,128)} %get-tuple-element.174.d_res_ref, f32[16,1024]{1,0:T(8,128)} %pad.8.vectors_ref.refs_9_, bf16[1024,3072]{1,0:T(8,128)(2,1)} %all-gather.4.cloned.1.call-done.w_ref, ...), custom_call_target="tpu_custom_call" | custom-call | flops 4831838208 | bytes 17301504 | tf_op jit(solution)/shard_map/input_grads/pallas_call | solution.py:579
  610.2 2.2 fusion.1
  612.4 3.2 collective-permute-done.51
  617.5 1.9 collective-permute-start.53
  620.3 2.1 broadcast.108.clone.1
  622.4 11.4 %input_grads.3 = (bf16[2,768,1024]{2,1,0:T(8,128)(2,1)}, f32[8,1024]{1,0:T(8,128)S(1)}) fusion(bf16[2,768,1024]{2,1,0:T(8,128)(2,1)} %broadcast.108.clone.1, s32[]{:T(128)S(6)} %select_n.215, bf16[768,1024]{1,0:T(8,128)(2,1)S(1)} %copy-done.2, f32[1536,1024]{1,0:T(8,128)} %get-tuple-element.174.d_res_ref, f32[16,1024]{1,0:T(8,128)S(1)} %copy-done.15, ...), kind=kCustom, calls=%fused_computation.11 | custom fusion | flops 4831838208 | bytes 25264132 | tf_op jit(solution)/shard_map/input_grads/pallas_call | solution.py:579
  635.7 1.5 collective-permute-start.55
  641.6 2.7 collective-permute-start.48
  646.3 1.8 collective-permute-done.47
  650.2 6.1 collective-permute-done.49
  659.4 26.5 %collective-permute-done.50 = f32[55,1024]{1,0:T(8,128)S(1)} collective-permute-done((f32[55,1024]{1,0:T(8,128)S(1)}, f32[55,1024]{1,0:T(8,128)S(1)}, u32[]{:S(2)}, u32[]{:S(2)}) %collective-permute-start.50) | collective-permute-done | bytes 225312 | tf_op jit(solution)/shard_map/ppermute | solution.py:622
  689.9 2.6 fusion.32
  695.9 2.7 collective-permute-start.59
  705.9 1.7 bitcast_dynamic-update-slice_fusion
  707.6 2.1 fusion.39
  709.8 1.9 reshape.286
  711.6 1.7 copy.152
  (331 shorter events, 85.3 us)
Async XLA Ops:
  7.2 82.3 %all-gather.4.cloned.1.call-start = ((), (), s32[]{:S(2)}) async-start(), calls=%async_computation.1 | async-start | bytes 6488064 | tf_op jit(solution)/shard_map/all_gather | solution.py:713
  8.9 208.3 %all-gather.8.cloned.1.call-start = ((), (), s32[]{:S(2)}) async-start(), calls=%async_computation.3 | async-start | bytes 4325376 | tf_op jit(solution)/shard_map/all_gather | solution.py:715
  9.7 222.1 %all-gather.6.cloned.1.call-start = ((), (), s32[]{:S(2)}) async-start(), calls=%async_computation.2 | async-start | bytes 6488064 | tf_op jit(solution)/shard_map/all_gather | solution.py:714
  9.7 14.4 %collective-permute-start.1 = (s32[2]{0:T(128)}, s32[2]{0:T(128)S(1)}, u32[]{:S(2)}, u32[]{:S(2)}) collective-permute-start(s32[2]{0:T(128)} %param.20), channel_id=1, source_target_pairs={{0,8},{4,12},{8,16},{12,20},{16,24},{20,28},{24,0},{28,4},{1,9},{5... | collective-permute-start | bytes 32 | tf_op jit(solution)/shard_map/ppermute | solution.py:622
  12.8 11.3 %collective-permute-start.2 = (s32[2]{0:T(128)}, s32[2]{0:T(128)S(1)}, u32[]{:S(2)}, u32[]{:S(2)}) collective-permute-start(s32[2]{0:T(128)} %param.20), channel_id=1, source_target_pairs={{0,16},{4,20},{8,24},{12,28},{16,0},{20,4},{24,8},{28,12},{1,17},{... | collective-permute-start | bytes 32 | tf_op jit(solution)/shard_map/ppermute | solution.py:622
  15.4 8.7 %collective-permute-start.3 = (s32[2]{0:T(128)}, s32[2]{0:T(128)S(1)}, u32[]{:S(2)}, u32[]{:S(2)}) collective-permute-start(s32[2]{0:T(128)} %param.20), channel_id=1, source_target_pairs={{0,24},{4,28},{8,0},{12,4},{16,8},{20,12},{24,16},{28,20},{1,25},{... | collective-permute-start | bytes 32 | tf_op jit(solution)/shard_map/ppermute | solution.py:622
  20.8 51.4 %collective-permute-start = (bf16[768,1024]{1,0:T(8,128)(2,1)}, bf16[768,1024]{1,0:T(8,128)(2,1)}, u32[]{:S(2)}, u32[]{:S(2)}) collective-permute-start(bf16[768,1024]{1,0:T(8,128)(2,1)} %get-tuple-element.192), channel_id=1, source_target_pairs={{0,2},{1,3},{2,0},{3,1},{4,6},{5,7},{6,4},{7,5},{8,10},{9,11},{10,... | collective-permute-start | bytes 4718600 | tf_op jit(solution)/shard_map/ppermute | solution.py:622
  23.0 684.6 %reduce-scatter.2.cloned.1.call-start = ((), (), s32[]{:S(2)}) async-start(), calls=%async_computation.4 | async-start | bytes 10813440 | tf_op jit(solution)/shard_map/reduce_scatter | solution.py:778
  24.1 3.7 collective-permute-start.4
  30.7 10.0 %collective-permute-start.5 = (f32[4,2,13312]{2,1,0:T(2,128)}, f32[4,2,13312]{2,1,0:T(2,128)}, u32[]{:S(2)}, u32[]{:S(2)}) collective-permute-start(f32[4,2,13312]{2,1,0:T(2,128)} %squeeze.178), channel_id=1, source_target_pairs={{0,4},{4,0},{8,12},{12,8},{16,20},{20,16},{24,28},{28,24},{1,5},{5... | collective-permute-start | bytes 1277960 | tf_op jit(solution)/shard_map/ppermute | solution.py:683
  42.2 7.6 %collective-permute-start.6 = (f32[2,13312]{1,0:T(2,128)S(1)}, f32[2,13312]{1,0:T(2,128)S(1)}, u32[]{:S(2)}, u32[]{:S(2)}) collective-permute-start(f32[2,13312]{1,0:T(2,128)S(1)} %get-tuple-element.206), channel_id=1, source_target_pairs={{0,24},{4,28},{8,0},{12,4},{16,8},{20,12},{24,16},{28,20},{1,25},{... | collective-permute-start | bytes 319496 | tf_op jit(solution)/shard_map/ppermute | solution.py:622
  42.6 13.6 %collective-permute-start.7 = (f32[2,13312]{1,0:T(2,128)S(1)}, f32[2,13312]{1,0:T(2,128)S(1)}, u32[]{:S(2)}, u32[]{:S(2)}) collective-permute-start(f32[2,13312]{1,0:T(2,128)S(1)} %get-tuple-element.208), channel_id=1, source_target_pairs={{0,16},{4,20},{8,24},{12,28},{16,0},{20,4},{24,8},{28,12},{1,17},{... | collective-permute-start | bytes 319496 | tf_op jit(solution)/shard_map/ppermute | solution.py:622
  44.3 11.9 %collective-permute-start.8 = (f32[2,13312]{1,0:T(2,128)S(1)}, f32[2,13312]{1,0:T(2,128)S(1)}, u32[]{:S(2)}, u32[]{:S(2)}) collective-permute-start(f32[2,13312]{1,0:T(2,128)S(1)} %get-tuple-element.207), channel_id=1, source_target_pairs={{0,8},{4,12},{8,16},{12,20},{16,24},{20,28},{24,0},{28,4},{1,9},{5... | collective-permute-start | bytes 319496 | tf_op jit(solution)/shard_map/ppermute | solution.py:622
  56.4 8.0 %collective-permute-start.9 = (f32[13312]{0:T(1024)S(1)}, f32[13312]{0:T(1024)S(1)}, u32[]{:S(2)}, u32[]{:S(2)}) collective-permute-start(f32[13312]{0:T(1024)S(1)} %bitcast.243), channel_id=1, source_target_pairs={{0,2},{1,3},{2,0},{3,1},{4,6},{5,7},{6,4},{7,5},{8,10},{9,11},{10,... | collective-permute-start | bytes 159752 | tf_op jit(solution)/shard_map/ppermute | solution.py:622
  64.5 5.6 collective-permute-start.10
  103.2 11.0 %collective-permute-start.13 = (bf16[512,1536]{1,0:T(8,128)(2,1)}, bf16[512,1536]{1,0:T(8,128)(2,1)}, u32[]{:S(2)}, u32[]{:S(2)}) collective-permute-start(bf16[512,1536]{1,0:T(8,128)(2,1)} %get-tuple-element.109.refs_2_.refs_7_), channel_id=1, source_target_pairs={{0,1},{1,0},{2,3},{3,2},{4,5},{5,4},{6,7},{7,6},{8,9},{9,8},{10,11... | collective-permute-start | bytes 4718600 | tf_op jit(solution)/shard_map/ppermute | solution.py:760
  103.5 10.7 %collective-permute-start.14 = (bf16[512,1536]{1,0:T(8,128)(2,1)}, bf16[512,1536]{1,0:T(8,128)(2,1)}, u32[]{:S(2)}, u32[]{:S(2)}) collective-permute-start(bf16[512,1536]{1,0:T(8,128)(2,1)} %get-tuple-element.110.refs_4_.refs_9_), channel_id=1, source_target_pairs={{0,1},{1,0},{2,3},{3,2},{4,5},{5,4},{6,7},{7,6},{8,9},{9,8},{10,11... | collective-permute-start | bytes 4718600 | tf_op jit(solution)/shard_map/ppermute | solution.py:760
  103.7 62.0 %collective-permute-start.11 = (bf16[512,1536]{1,0:T(8,128)(2,1)}, bf16[512,1536]{1,0:T(8,128)(2,1)}, u32[]{:S(2)}, u32[]{:S(2)}) collective-permute-start(bf16[512,1536]{1,0:T(8,128)(2,1)} %get-tuple-element.106.refs_2_.refs_7_), channel_id=1, source_target_pairs={{0,1},{1,0},{2,3},{3,2},{4,5},{5,4},{6,7},{7,6},{8,9},{9,8},{10,11... | collective-permute-start | bytes 4718600 | tf_op jit(solution)/shard_map/ppermute | solution.py:760
  104.0 127.8 %collective-permute-start.15 = (bf16[768,1024]{1,0:T(8,128)(2,1)S(1)}, bf16[768,1024]{1,0:T(8,128)(2,1)}, u32[]{:S(2)}, u32[]{:S(2)}) collective-permute-start(bf16[768,1024]{1,0:T(8,128)(2,1)S(1)} %copy-done.11), channel_id=1, source_target_pairs={{0,2},{1,3},{2,0},{3,1},{4,6},{5,7},{6,4},{7,5},{8,10},{9,11},{10,... | collective-permute-start | bytes 4718600 | tf_op jit(solution)/shard_map/ppermute | solution.py:622
  105.4 60.4 %collective-permute-start.12 = (bf16[512,1536]{1,0:T(8,128)(2,1)}, bf16[512,1536]{1,0:T(8,128)(2,1)}, u32[]{:S(2)}, u32[]{:S(2)}) collective-permute-start(bf16[512,1536]{1,0:T(8,128)(2,1)} %get-tuple-element.107.refs_4_.refs_9_), channel_id=1, source_target_pairs={{0,1},{1,0},{2,3},{3,2},{4,5},{5,4},{6,7},{7,6},{8,9},{9,8},{10,11... | collective-permute-start | bytes 4718600 | tf_op jit(solution)/shard_map/ppermute | solution.py:760
  357.5 56.8 %collective-permute-start.17 = (bf16[256,1536]{1,0:T(8,128)(2,1)}, bf16[256,1536]{1,0:T(8,128)(2,1)S(1)}, u32[]{:S(2)}, u32[]{:S(2)}) collective-permute-start(bf16[256,1536]{1,0:T(8,128)(2,1)} %get-tuple-element.124), channel_id=1, source_target_pairs={{0,1},{1,0},{2,3},{3,2},{4,5},{5,4},{6,7},{7,6},{8,9},{9,8},{10,11... | collective-permute-start | bytes 2359304 | tf_op jit(solution)/shard_map/ppermute | solution.py:823
  357.9 56.4 %collective-permute-start.18 = (bf16[256,1536]{1,0:T(8,128)(2,1)}, bf16[256,1536]{1,0:T(8,128)(2,1)S(1)}, u32[]{:S(2)}, u32[]{:S(2)}) collective-permute-start(bf16[256,1536]{1,0:T(8,128)(2,1)} %get-tuple-element.126), channel_id=1, source_target_pairs={{0,1},{1,0},{2,3},{3,2},{4,5},{5,4},{6,7},{7,6},{8,9},{9,8},{10,11... | collective-permute-start | bytes 2359304 | tf_op jit(solution)/shard_map/ppermute | solution.py:824
  405.0 45.7 %collective-permute-start.20 = (bf16[256,1536]{1,0:T(8,128)(2,1)}, bf16[256,1536]{1,0:T(8,128)(2,1)}, u32[]{:S(2)}, u32[]{:S(2)}) collective-permute-start(bf16[256,1536]{1,0:T(8,128)(2,1)} %get-tuple-element.132), channel_id=1, source_target_pairs={{0,1},{1,0},{2,3},{3,2},{4,5},{5,4},{6,7},{7,6},{8,9},{9,8},{10,11... | collective-permute-start | bytes 2359304 | tf_op jit(solution)/shard_map/ppermute | solution.py:823
  405.3 45.4 %collective-permute-start.21 = (bf16[256,1536]{1,0:T(8,128)(2,1)}, bf16[256,1536]{1,0:T(8,128)(2,1)}, u32[]{:S(2)}, u32[]{:S(2)}) collective-permute-start(bf16[256,1536]{1,0:T(8,128)(2,1)} %get-tuple-element.134), channel_id=1, source_target_pairs={{0,1},{1,0},{2,3},{3,2},{4,5},{5,4},{6,7},{7,6},{8,9},{9,8},{10,11... | collective-permute-start | bytes 2359304 | tf_op jit(solution)/shard_map/ppermute | solution.py:824
  409.5 82.0 %collective-permute-start.16 = (bf16[768,1024]{1,0:T(8,128)(2,1)}, bf16[768,1024]{1,0:T(8,128)(2,1)}, u32[]{:S(2)}, u32[]{:S(2)}) collective-permute-start(bf16[768,1024]{1,0:T(8,128)(2,1)} %slice.135), channel_id=1, source_target_pairs={{0,2},{1,3},{2,0},{3,1},{4,6},{5,7},{6,4},{7,5},{8,10},{9,11},{10,... | collective-permute-start | bytes 4718600 | tf_op jit(solution)/shard_map/ppermute | solution.py:622
  424.6 37.6 %collective-permute-start.19 = (bf16[8,2,32,768]{3,2,0,1:T(8,128)(2,1)S(1)}, bf16[8,2,32,768]{3,2,0,1:T(8,128)(2,1)}, u32[]{:S(2)}, u32[]{:S(2)}) collective-permute-start(bf16[8,2,32,768]{3,2,0,1:T(8,128)(2,1)S(1)} %bitcast.229), channel_id=1, source_target_pairs={{0,1},{1,0},{2,3},{3,2},{4,5},{5,4},{6,7},{7,6},{8,9},{9,8},{10,11... | collective-permute-start | bytes 2359304 | tf_op jit(solution)/shard_map/ppermute | solution.py:683
  450.1 75.9 %collective-permute-start.28 = (bf16[128,1536]{1,0:T(8,128)(2,1)}, bf16[128,1536]{1,0:T(8,128)(2,1)}, u32[]{:S(2)}, u32[]{:S(2)}) collective-permute-start(bf16[128,1536]{1,0:T(8,128)(2,1)} %get-tuple-element.145), channel_id=1, source_target_pairs={{0,1},{1,0},{2,3},{3,2},{4,5},{5,4},{6,7},{7,6},{8,9},{9,8},{10,11... | collective-permute-start | bytes 1179656 | tf_op jit(solution)/shard_map/ppermute | solution.py:823
  450.7 76.9 %collective-permute-start.29 = (bf16[128,1536]{1,0:T(8,128)(2,1)}, bf16[128,1536]{1,0:T(8,128)(2,1)}, u32[]{:S(2)}, u32[]{:S(2)}) collective-permute-start(bf16[128,1536]{1,0:T(8,128)(2,1)} %get-tuple-element.147), channel_id=1, source_target_pairs={{0,1},{1,0},{2,3},{3,2},{4,5},{5,4},{6,7},{7,6},{8,9},{9,8},{10,11... | collective-permute-start | bytes 1179656 | tf_op jit(solution)/shard_map/ppermute | solution.py:824
  461.7 27.0 %collective-permute-start.23 = (bf16[8,2,32,768]{3,2,0,1:T(8,128)(2,1)}, bf16[8,2,32,768]{3,2,0,1:T(8,128)(2,1)}, u32[]{:S(2)}, u32[]{:S(2)}) collective-permute-start(bf16[8,2,32,768]{3,2,0,1:T(8,128)(2,1)} %bitcast.206), channel_id=1, source_target_pairs={{0,1},{1,0},{2,3},{3,2},{4,5},{5,4},{6,7},{7,6},{8,9},{9,8},{10,11... | collective-permute-start | bytes 2359304 | tf_op jit(solution)/shard_map/ppermute | solution.py:683
  488.4 39.2 %collective-permute-start.30 = (bf16[128,1536]{1,0:T(8,128)(2,1)}, bf16[128,1536]{1,0:T(8,128)(2,1)}, u32[]{:S(2)}, u32[]{:S(2)}) collective-permute-start(bf16[128,1536]{1,0:T(8,128)(2,1)} %get-tuple-element.149), channel_id=1, source_target_pairs={{0,1},{1,0},{2,3},{3,2},{4,5},{5,4},{6,7},{7,6},{8,9},{9,8},{10,11... | collective-permute-start | bytes 1179656 | tf_op jit(solution)/shard_map/ppermute | solution.py:823
  488.7 11.5 %collective-permute-start.22 = (bf16[8,32,768]{2,1,0:T(8,128)(2,1)S(1)}, bf16[8,32,768]{2,1,0:T(8,128)(2,1)S(1)}, u32[]{:S(2)}, u32[]{:S(2)}) collective-permute-start(bf16[8,32,768]{2,1,0:T(8,128)(2,1)S(1)} %dynamic-slice_bitcast_fusion.7), channel_id=1, source_target_pairs={{0,2},{1,3},{2,0},{3,1},{4,6},{5,7},{6,4},{7,5},{8,10},{9,11},{10,... | collective-permute-start | bytes 1179656 | tf_op jit(solution)/shard_map/ppermute | solution.py:622
  491.6 36.5 %collective-permute-start.31 = (bf16[128,1536]{1,0:T(8,128)(2,1)}, bf16[128,1536]{1,0:T(8,128)(2,1)}, u32[]{:S(2)}, u32[]{:S(2)}) collective-permute-start(bf16[128,1536]{1,0:T(8,128)(2,1)} %get-tuple-element.151), channel_id=1, source_target_pairs={{0,1},{1,0},{2,3},{3,2},{4,5},{5,4},{6,7},{7,6},{8,9},{9,8},{10,11... | collective-permute-start | bytes 1179656 | tf_op jit(solution)/shard_map/ppermute | solution.py:824
  500.1 35.5 %collective-permute-start.27 = (bf16[8,32,768]{2,1,0:T(8,128)(2,1)}, bf16[8,32,768]{2,1,0:T(8,128)(2,1)}, u32[]{:S(2)}, u32[]{:S(2)}) collective-permute-start(bf16[8,32,768]{2,1,0:T(8,128)(2,1)} %dynamic-slice_bitcast_fusion.6), channel_id=1, source_target_pairs={{0,2},{1,3},{2,0},{3,1},{4,6},{5,7},{6,4},{7,5},{8,10},{9,11},{10,... | collective-permute-start | bytes 1179656 | tf_op jit(solution)/shard_map/ppermute | solution.py:622
  526.1 13.8 %collective-permute-start.26 = (bf16[4,32,768]{2,1,0:T(8,128)(2,1)S(1)}, bf16[4,32,768]{2,1,0:T(8,128)(2,1)S(1)}, u32[]{:S(2)}, u32[]{:S(2)}) collective-permute-start(bf16[4,32,768]{2,1,0:T(8,128)(2,1)S(1)} %dynamic-slice_bitcast_fusion.11), channel_id=1, source_target_pairs={{0,4},{4,0},{8,12},{12,8},{16,20},{20,16},{24,28},{28,24},{1,5},{5... | collective-permute-start | bytes 589832 | tf_op jit(solution)/shard_map/ppermute | solution.py:683
  527.6 54.3 %collective-permute-start.24 = (bf16[128,1536]{1,0:T(8,128)(2,1)}, bf16[128,1536]{1,0:T(8,128)(2,1)}, u32[]{:S(2)}, u32[]{:S(2)}) collective-permute-start(bf16[128,1536]{1,0:T(8,128)(2,1)} %get-tuple-element.141), channel_id=1, source_target_pairs={{0,1},{1,0},{2,3},{3,2},{4,5},{5,4},{6,7},{7,6},{8,9},{9,8},{10,11... | collective-permute-start | bytes 1179656 | tf_op jit(solution)/shard_map/ppermute | solution.py:823
  527.6 54.3 %collective-permute-start.25 = (bf16[128,1536]{1,0:T(8,128)(2,1)}, bf16[128,1536]{1,0:T(8,128)(2,1)}, u32[]{:S(2)}, u32[]{:S(2)}) collective-permute-start(bf16[128,1536]{1,0:T(8,128)(2,1)} %get-tuple-element.143), channel_id=1, source_target_pairs={{0,1},{1,0},{2,3},{3,2},{4,5},{5,4},{6,7},{7,6},{8,9},{9,8},{10,11... | collective-permute-start | bytes 1179656 | tf_op jit(solution)/shard_map/ppermute | solution.py:824
  539.2 6.9 collective-permute-start.37
  540.0 33.1 %collective-permute-start.34 = (bf16[32,768]{1,0:T(8,128)(2,1)S(1)}, bf16[32,768]{1,0:T(8,128)(2,1)S(1)}, u32[]{:S(2)}, u32[]{:S(2)}) collective-permute-start(bf16[32,768]{1,0:T(8,128)(2,1)S(1)} %get-tuple-element.222), channel_id=1, source_target_pairs={{0,8},{4,12},{8,16},{12,20},{16,24},{20,28},{24,0},{28,4},{1,9},{5... | collective-permute-start | bytes 147464 | tf_op jit(solution)/shard_map/ppermute | solution.py:622
  541.5 31.8 %collective-permute-start.35 = (bf16[32,768]{1,0:T(8,128)(2,1)S(1)}, bf16[32,768]{1,0:T(8,128)(2,1)S(1)}, u32[]{:S(2)}, u32[]{:S(2)}) collective-permute-start(bf16[32,768]{1,0:T(8,128)(2,1)S(1)} %get-tuple-element.224), channel_id=1, source_target_pairs={{0,16},{4,20},{8,24},{12,28},{16,0},{20,4},{24,8},{28,12},{1,17},{... | collective-permute-start | bytes 147464 | tf_op jit(solution)/shard_map/ppermute | solution.py:622
  546.1 29.0 %collective-permute-start.36 = (bf16[32,768]{1,0:T(8,128)(2,1)S(1)}, bf16[32,768]{1,0:T(8,128)(2,1)S(1)}, u32[]{:S(2)}, u32[]{:S(2)}) collective-permute-start(bf16[32,768]{1,0:T(8,128)(2,1)S(1)} %get-tuple-element.223), channel_id=1, source_target_pairs={{0,24},{4,28},{8,0},{12,4},{16,8},{20,12},{24,16},{28,20},{1,25},{... | collective-permute-start | bytes 147464 | tf_op jit(solution)/shard_map/ppermute | solution.py:622
  573.1 6.0 collective-permute-start.38
  573.3 5.8 collective-permute-start.39
  575.1 4.7 collective-permute-start.40
  579.1 13.9 %collective-permute-start.41 = (bf16[8,2,32,768]{3,2,0,1:T(8,128)(2,1)}, bf16[8,2,32,768]{3,2,0,1:T(8,128)(2,1)}, u32[]{:S(2)}, u32[]{:S(2)}) collective-permute-start(bf16[8,2,32,768]{3,2,0,1:T(8,128)(2,1)} %bitcast.205), channel_id=1, source_target_pairs={{0,1},{1,0},{2,3},{3,2},{4,5},{5,4},{6,7},{7,6},{8,9},{9,8},{10,11... | collective-permute-start | bytes 2359304 | tf_op jit(solution)/shard_map/ppermute | solution.py:683
  579.1 3.2 collective-permute-start.32
  579.8 3.1 collective-permute-start.33
  592.8 17.4 %collective-permute-start.43 = (bf16[8,2,32,768]{3,2,0,1:T(8,128)(2,1)}, bf16[8,2,32,768]{3,2,0,1:T(8,128)(2,1)}, u32[]{:S(2)}, u32[]{:S(2)}) collective-permute-start(bf16[8,2,32,768]{3,2,0,1:T(8,128)(2,1)} %bitcast.204), channel_id=1, source_target_pairs={{0,1},{1,0},{2,3},{3,2},{4,5},{5,4},{6,7},{7,6},{8,9},{9,8},{10,11... | collective-permute-start | bytes 2359304 | tf_op jit(solution)/shard_map/ppermute | solution.py:683
  595.3 12.2 %collective-permute-start.42 = (bf16[8,32,768]{2,1,0:T(8,128)(2,1)S(1)}, bf16[8,32,768]{2,1,0:T(8,128)(2,1)}, u32[]{:S(2)}, u32[]{:S(2)}) collective-permute-start(bf16[8,32,768]{2,1,0:T(8,128)(2,1)S(1)} %dynamic-slice_bitcast_fusion.5), channel_id=1, source_target_pairs={{0,2},{1,3},{2,0},{3,1},{4,6},{5,7},{6,4},{7,5},{8,10},{9,11},{10,... | collective-permute-start | bytes 1179656 | tf_op jit(solution)/shard_map/ppermute | solution.py:622
  608.7 7.0 collective-permute-start.51
  616.4 20.8 %collective-permute-start.52 = (bf16[32,768]{1,0:T(8,128)(2,1)}, bf16[32,768]{1,0:T(8,128)(2,1)S(1)}, u32[]{:S(2)}, u32[]{:S(2)}) collective-permute-start(bf16[32,768]{1,0:T(8,128)(2,1)} %get-tuple-element.213), channel_id=1, source_target_pairs={{0,8},{4,12},{8,16},{12,20},{16,24},{20,28},{24,0},{28,4},{1,9},{5... | collective-permute-start | bytes 147464 | tf_op jit(solution)/shard_map/ppermute | solution.py:622
  617.5 20.3 %collective-permute-start.53 = (bf16[32,768]{1,0:T(8,128)(2,1)}, bf16[32,768]{1,0:T(8,128)(2,1)S(1)}, u32[]{:S(2)}, u32[]{:S(2)}) collective-permute-start(bf16[32,768]{1,0:T(8,128)(2,1)} %get-tuple-element.215), channel_id=1, source_target_pairs={{0,16},{4,20},{8,24},{12,28},{16,0},{20,4},{24,8},{28,12},{1,17},{... | collective-permute-start | bytes 147464 | tf_op jit(solution)/shard_map/ppermute | solution.py:622
  619.5 19.0 %collective-permute-start.54 = (bf16[32,768]{1,0:T(8,128)(2,1)S(1)}, bf16[32,768]{1,0:T(8,128)(2,1)}, u32[]{:S(2)}, u32[]{:S(2)}) collective-permute-start(bf16[32,768]{1,0:T(8,128)(2,1)S(1)} %get-tuple-element.214), channel_id=1, source_target_pairs={{0,24},{4,28},{8,0},{12,4},{16,8},{20,12},{24,16},{28,20},{1,25},{... | collective-permute-start | bytes 147464 | tf_op jit(solution)/shard_map/ppermute | solution.py:622
  635.6 3.7 collective-permute-start.45
  635.7 22.3 %collective-permute-start.55 = (bf16[8,32,768]{2,1,0:T(8,128)(2,1)S(1)}, bf16[8,32,768]{2,1,0:T(8,128)(2,1)S(1)}, u32[]{:S(2)}, u32[]{:S(2)}) collective-permute-start(bf16[8,32,768]{2,1,0:T(8,128)(2,1)S(1)} %dynamic-slice_bitcast_fusion.4), channel_id=1, source_target_pairs={{0,2},{1,3},{2,0},{3,1},{4,6},{5,7},{6,4},{7,5},{8,10},{9,11},{10,... | collective-permute-start | bytes 1179656 | tf_op jit(solution)/shard_map/ppermute | solution.py:622
  637.2 68.7 %collective-permute-start.44 = (bf16[768,1024]{1,0:T(8,128)(2,1)}, bf16[768,1024]{1,0:T(8,128)(2,1)}, u32[]{:S(2)}, u32[]{:S(2)}) collective-permute-start(bf16[768,1024]{1,0:T(8,128)(2,1)} %get-tuple-element.176), channel_id=1, source_target_pairs={{0,2},{1,3},{2,0},{3,1},{4,6},{5,7},{6,4},{7,5},{8,10},{9,11},{10,... | collective-permute-start | bytes 4718600 | tf_op jit(solution)/shard_map/ppermute | solution.py:622
  639.4 6.9 collective-permute-start.46
  640.6 7.4 %collective-permute-start.47 = (f32[13,1024]{1,0:T(8,128)S(1)}, f32[13,1024]{1,0:T(8,128)S(1)}, u32[]{:S(2)}, u32[]{:S(2)}) collective-permute-start(f32[13,1024]{1,0:T(8,128)S(1)} %fusion.33), channel_id=1, source_target_pairs={{0,16},{4,20},{8,24},{12,28},{16,0},{20,4},{24,8},{28,12},{1,17},{... | collective-permute-start | bytes 159752 | tf_op jit(solution)/shard_map/ppermute | solution.py:622
  641.6 6.4 collective-permute-start.48
  648.1 8.2 %collective-permute-start.49 = (f32[4,13,1024]{2,1,0:T(8,128)S(1)}, f32[4,13,1024]{2,1,0:T(8,128)S(1)}, u32[]{:S(2)}, u32[]{:S(2)}) collective-permute-start(f32[4,13,1024]{2,1,0:T(8,128)S(1)} %get-tuple-element.212), channel_id=1, source_target_pairs={{0,4},{4,0},{8,12},{12,8},{16,20},{20,16},{24,28},{28,24},{1,5},{5... | collective-permute-start | bytes 638984 | tf_op jit(solution)/shard_map/ppermute | solution.py:683
  656.5 29.4 %collective-permute-start.50 = (f32[55,1024]{1,0:T(8,128)S(1)}, f32[55,1024]{1,0:T(8,128)S(1)}, u32[]{:S(2)}, u32[]{:S(2)}) collective-permute-start(f32[55,1024]{1,0:T(8,128)S(1)} %pad_maximum_fusion.3), channel_id=1, source_target_pairs={{0,2},{1,3},{2,0},{3,1},{4,6},{5,7},{6,4},{7,5},{8,10},{9,11},{10,... | collective-permute-start | bytes 675848 | tf_op jit(solution)/shard_map/ppermute | solution.py:622
  658.8 33.7 %collective-permute-start.56 = (bf16[4,32,768]{2,1,0:T(8,128)(2,1)}, bf16[4,32,768]{2,1,0:T(8,128)(2,1)}, u32[]{:S(2)}, u32[]{:S(2)}) collective-permute-start(bf16[4,32,768]{2,1,0:T(8,128)(2,1)} %dynamic-slice_bitcast_fusion.8), channel_id=1, source_target_pairs={{0,4},{4,0},{8,12},{12,8},{16,20},{20,16},{24,28},{28,24},{1,5},{5... | collective-permute-start | bytes 589832 | tf_op jit(solution)/shard_map/ppermute | solution.py:683
  693.7 6.4 collective-permute-start.57
  694.9 6.5 collective-permute-start.58
  695.9 5.5 collective-permute-start.59
  (41 other events, 352.5 us)
Sparse Core Ops, SparseCore 0:
  11.5 78.0 all-gather.3
  92.4 68.2 all-gather.7
  163.5 68.1 all-gather.5
  310.8 163.7 reduce-scatter.1

commit v3 on v2

--- a/solution.py
+++ b/solution.py
@@ -295,11 +295,11 @@
 
 def halves_spec(inputs, rows, block, width):
     if inputs[0].shape[0] == rows:
-        return [pl.BlockSpec((block, width), lambda i: (i, 0))] * 2
+        return [pl.BlockSpec((block, width), lambda i, *_: (i, 0))] * 2
     half = rows // 2 // block
     return [
-        pl.BlockSpec((block, width), lambda i: (jnp.minimum(i, half - 1), 0)),
-        pl.BlockSpec((block, width), lambda i: (jnp.maximum(i - half, 0), 0)),
+        pl.BlockSpec((block, width), lambda i, *_: (jnp.minimum(i, half - 1), 0)),
+        pl.BlockSpec((block, width), lambda i, *_: (jnp.maximum(i - half, 0), 0)),
     ]
 
 
@@ -323,7 +323,7 @@
 
 
 def whole_spec(shape, column=0):
-    return pl.BlockSpec(shape, lambda i: (0, column), pipeline_mode=pl.Buffered(1))
+    return pl.BlockSpec(shape, lambda i, *_: (0, column), pipeline_mode=pl.Buffered(1))
 
 
 def project(inputs, vectors, packed, cosine, sine, groups):
@@ -364,49 +364,59 @@
     return h_one, queries, keys, values
 
 
-def feed_forward_kernel(parts, pieces, shard, *refs):
+def feed_forward_kernel(parts, pieces, split, slot_ref, *refs):
     o_refs = refs[:parts]
-    x_ref, y_ref, cot_ref, cot_y_ref, keep_ref, w_ou_ref, w_down_ref, vectors_ref = refs[parts : parts + 8]
-    mixed_ref, d_res_ref, d_heads_ref, g_rows_ref, sums_ref, g_b_up_ref = refs[parts + 8 : parts + 14]
-    acc_ou, acc_down, acc_rows, acc_b_up, slope_ref, hidden_ref, staged, sems = refs[parts + 14 :]
-    step = pl.program_id(0)
-    width, hidden_width = x_ref.shape[1], w_down_ref.shape[0]
-    piece = hidden_width // pieces
+    x_ref, y_ref, cot_ref, cot_y_ref, keep_ref, w_ref, vectors_ref = refs[parts : parts + 7]
+    own_ref, away_ref, d_res_ref, d_heads_ref, g_rows_ref, sums_ref = refs[parts + 7 : parts + 13]
+    acc, acc_rows, slope_ref, hidden_ref, staged, sems = refs[parts + 13 :]
+    step, count = pl.program_id(0), pl.num_programs(0)
+    width = x_ref.shape[1]
 
     @pl.when(step == 0)
     def _():
-        for acc in (acc_ou, acc_down, acc_rows, acc_b_up):
-            acc[...] = jnp.zeros_like(acc)
+        acc[...] = jnp.zeros_like(acc)
+        acc_rows[...] = jnp.zeros_like(acc_rows)
 
     gate_one, shift_two, scale_two, gate_two, b_out, b_down = [vectors_ref[i : i + 1, :] for i in (2, 3, 4, 5, 9, 10)]
+    out_at = slice(0, width)
+    up_at = [slice((1 + i) * width, (2 + i) * width) for i in range(pieces)]
+    down_at = [slice((1 + pieces + i) * width, (2 + pieces + i) * width) for i in range(pieces)]
     keep = keep_ref[...]
     heads_out = jnp.concatenate([ref[...] for ref in o_refs], axis=0)
-    branch = (dot(heads_out, w_ou_ref[:, :width], 0, 0) + b_out) * keep
+    branch = (dot(heads_out, w_ref[:, out_at], 0, 0) + b_out) * keep
     residual = either(x_ref, y_ref).astype(F32) + gate_one * branch
     normed, inverse = norm_parts(residual)
     h_two = (normed * (1.0 + scale_two) + shift_two).astype(BF16)
     ff_out = b_down
     for i in range(pieces):
-        at = slice(i * piece, (i + 1) * piece)
-        value, slope = gelu_both(dot(h_two, w_ou_ref[:, width + i * piece : width + (i + 1) * piece], 1, 0) + vectors_ref[11 + i : 12 + i, :])
-        slope_ref[:, at] = slope
+        value, slope = gelu_both(dot(h_two, w_ref[:, up_at[i]], 1, 0) + vectors_ref[11 + i : 12 + i, :])
+        slope_ref[i] = slope
         hidden = value.astype(BF16)
-        hidden_ref[:, at] = hidden
-        ff_out = ff_out + dot(hidden, w_down_ref[at, :], 1, 0)
-    mixed_ref[...] = (residual + gate_two * ff_out).astype(BF16)
+        hidden_ref[i] = hidden
+        ff_out = ff_out + dot(hidden, w_ref[:, down_at[i]], 1, 0)
+    mixed = (residual + gate_two * ff_out).astype(BF16)
+    if split:
+
+        @pl.when(step < count // 2)
+        def _():
+            own_ref[0] = mixed
+
+        @pl.when(step >= count // 2)
+        def _():
+            away_ref[...] = mixed
+    else:
+        own_ref[...] = mixed
     d_mixed = either(cot_ref, cot_y_ref).astype(F32)
     acc_rows[3:4, :] += add_rows(d_mixed * ff_out)
     d_ff = (d_mixed * gate_two).astype(BF16)
     acc_rows[5:6, :] += add_rows(d_ff.astype(F32))
     d_h_two = None
     for i in range(pieces):
-        at = slice(i * piece, (i + 1) * piece)
-        up_at = slice(width + i * piece, width + (i + 1) * piece)
-        acc_down[at, :] += dot(hidden_ref[:, at], d_ff, 0, 0)
-        d_up = (dot(d_ff, w_down_ref[at, :], 1, 1) * slope_ref[:, at]).astype(BF16)
-        acc_b_up[:, at] += add_rows(d_up.astype(F32))
-        acc_ou[:, up_at] += dot(h_two, d_up, 0, 0)
-        update = dot(d_up, w_ou_ref[:, up_at], 1, 1)
+        acc[:, down_at[i]] += dot(hidden_ref[i], d_ff, 0, 0)
+        d_up = (dot(d_ff, w_ref[:, down_at[i]], 1, 1) * slope_ref[i]).astype(BF16)
+        acc_rows[6 + i : 7 + i, :] += add_rows(d_up.astype(F32))
+        acc[:, up_at[i]] += dot(h_two, d_up, 0, 0)
+        update = dot(d_up, w_ref[:, up_at[i]], 1, 1)
         d_h_two = update if i == 0 else d_h_two + update
     acc_rows[1:2, :] += add_rows(d_h_two)
     acc_rows[2:3, :] += add_rows(d_h_two * normed)
@@ -415,132 +425,130 @@
     acc_rows[0:1, :] += add_rows(d_residual * branch)
     d_branch = (d_residual * gate_one * keep).astype(BF16)
     acc_rows[4:5, :] += add_rows(d_branch.astype(F32))
-    acc_ou[:, :width] += dot(heads_out, d_branch, 1, 0)
-    d_heads_ref[...] = dot(w_ou_ref[:, :width], d_branch, 1, 1).astype(BF16)
-
-    @pl.when(step == pl.num_programs(0) - 1)
+    acc[:, out_at] += dot(heads_out, d_branch, 1, 0)
+    d_heads_ref[...] = dot(w_ref[:, out_at], d_branch, 1, 1).astype(BF16)
+
+    @pl.when(step == count - 1)
     def _():
         sums_ref[...] = acc_rows[...]
-        g_b_up_ref[...] = acc_b_up[...]
         tall = staged.shape[1]
-        wide = acc_ou.shape[1]
-        ups = hidden_width // width
         copies = []
         for i in range(width // tall):
             slot = i % 2
             if i >= 2:
                 copies[i - 2].wait()
-            staged[slot, :, :wide] = acc_ou[i * tall : (i + 1) * tall, :].astype(BF16)
-            for up in range(ups):
-                at = slice(wide + up * width, wide + (up + 1) * width)
-                if shard % 16 == 0:
-                    for j in range(0, tall, shard):
-                        first = (i * tall + j) * ups + up * shard
-                        staged[slot, j : j + shard, at] = acc_down[first : first + shard, :].astype(BF16)
-                else:
-                    first = up * width + i * tall
-                    staged[slot, :, at] = acc_down[first : first + tall, :].astype(BF16)
+            staged[slot] = acc[i * tall : (i + 1) * tall, :].astype(BF16)
             copies.append(pltpu.make_async_copy(staged.at[slot], g_rows_ref.at[pl.ds(i * tall, tall), :], sems.at[slot]))
             copies[i].start()
         for copy in copies[-2:]:
             copy.wait()
 
 
-def feed_forward(inputs, heads_out, cotangent, keep, out_up, full_down, vectors, shard):
+def feed_forward(slot, inputs, heads_out, cotangent, keep, packed, vectors, slots):
     rows, width = heads_out[0].shape[1], inputs[0].shape[1]
-    hidden_width = full_down.shape[0]
+    pieces = (packed.shape[1] // width - 1) // 2
     block = pick_block(inputs[0].shape[0], 256)
-    row_spec = pl.BlockSpec((block, width), lambda i: (i, 0))
-    turned_spec = lambda array: pl.BlockSpec((array, block), lambda i: (0, i))
+    local = rows // slots
+    split = inputs[0].shape[0] == local
+    half = local // block
+    row_spec = pl.BlockSpec((block, width), lambda i, *_: (i, 0))
+    turned_spec = lambda height: pl.BlockSpec((height, block), lambda i, *_: (0, i))
     kinds = jax.ShapeDtypeStruct
-    ou_shape, down_shape = out_up.shape, full_down.shape
-    wide = ou_shape[1] + hidden_width
+    if split:
+        mixed_specs = [
+            pl.BlockSpec((1, block, width), lambda i, at: (at[0], jnp.minimum(i, half - 1), 0)),
+            pl.BlockSpec((block, width), lambda i, *_: (jnp.maximum(i - half, 0), 0)),
+        ]
+        mixed_shapes = [kinds((slots, local, width), BF16), kinds((local, width), BF16)]
+    else:
+        mixed_specs = [row_spec, whole_spec((8, 128))]
+        mixed_shapes = [kinds((rows, width), BF16), kinds((8, 128), BF16)]
     return pl.pallas_call(
-        functools.partial(feed_forward_kernel, len(heads_out), hidden_width // width, shard),
-        grid=(rows // block,),
-        in_specs=[turned_spec(part.shape[0]) for part in heads_out]
-        + halves_spec(inputs, rows, block, width) * 2
+        functools.partial(feed_forward_kernel, len(heads_out), pieces, split),
+        grid_spec=pltpu.PrefetchScalarGridSpec(
+            num_scalar_prefetch=1,
+            grid=(rows // block,),
+            in_specs=[turned_spec(part.shape[0]) for part in heads_out]
+            + halves_spec(inputs, rows, block, width) * 2
+            + [
+                pl.BlockSpec((block, 1), lambda i, *_: (i, 0)),
+                whole_spec(packed.shape),
+                whole_spec(vectors.shape),
+            ],
+            out_specs=mixed_specs
+            + [
+                row_spec,
+                turned_spec(width),
+                pl.BlockSpec(memory_space=pl.ANY),
+                whole_spec((8, width)),
+            ],
+            scratch_shapes=[
+                pltpu.VMEM(packed.shape, F32),
+                pltpu.VMEM((8, width), F32),
+                pltpu.VMEM((pieces, block, width), F32),
+                pltpu.VMEM((pieces, block, width), BF16),
+                pltpu.VMEM((2, pick_block(width, 256), packed.shape[1]), BF16),
+                pltpu.SemaphoreType.DMA((2,)),
+            ],
+        ),
+        out_shape=mixed_shapes
         + [
-            pl.BlockSpec((block, 1), lambda i: (i, 0)),
-            whole_spec(ou_shape),
-            whole_spec(down_shape),
-            whole_spec(vectors.shape),
-        ],
-        out_specs=[
-            row_spec,
-            row_spec,
-            turned_spec(width),
-            pl.BlockSpec(memory_space=pl.ANY),
-            whole_spec((8, width)),
-            whole_spec((1, hidden_width)),
-        ],
-        out_shape=[
-            kinds((rows, width), BF16),
             kinds((rows, width), F32),
             kinds((width, rows), BF16),
-            kinds((width, wide), BF16),
+            kinds(packed.shape, BF16),
             kinds((8, width), F32),
-            kinds((1, hidden_width), F32),
-        ],
-        scratch_shapes=[
-            pltpu.VMEM(ou_shape, F32),
-            pltpu.VMEM(down_shape, F32),
-            pltpu.VMEM((8, width), F32),
-            pltpu.VMEM((1, hidden_width), F32),
-            pltpu.VMEM((block, hidden_width), F32),
-            pltpu.VMEM((block, hidden_width), BF16),
-            pltpu.VMEM((2, pick_block(width, 256), wide), BF16),
-            pltpu.SemaphoreType.DMA((2,)),
         ],
         compiler_params=pltpu.CompilerParams(vmem_limit_bytes=VMEM_LIMIT),
         cost_estimate=pl.CostEstimate(
-            flops=2 * 6 * rows * width * (width + 2 * hidden_width),
-            bytes_accessed=8 * rows * width + 4 * width * (width + 2 * hidden_width),
-            transcendentals=rows * hidden_width,
+            flops=6 * rows * width * packed.shape[1],
+            bytes_accessed=8 * rows * width + 4 * width * packed.shape[1],
+            transcendentals=0,
         ),
         name="feed_forward",
-    )(*heads_out, *inputs, *cotangent, keep, out_up, full_down, vectors)
+    )(slot, *heads_out, *inputs, *cotangent, keep, packed, vectors)
 
 
 def weight_grads_kernel(pieces, parts, h_ref, *refs):
     count = pieces * (1 + 2 * parts)
     per_piece = [refs[i * (1 + 2 * parts) : (i + 1) * (1 + 2 * parts)] for i in range(pieces)]
-    dq_out, dk_out, dv_out, weight_ref, bias_ref = refs[count:]
-
-    def summed(which):
-        columns = []
+    dk_out, dv_out, weight_ref, bias_ref, grads_ref = refs[count:]
+    tall = dk_out.shape[0]
+
+    @pl.when(pl.program_id(0) == 0)
+    def _():
+        first = 0
         for piece in per_piece:
-            total = piece[which][...]
-            for i in range(1, parts):
-                total = total + piece[which + i][...].astype(F32)
-            columns.append(total.astype(BF16))
-        return jnp.concatenate(columns, axis=0)
-
-    grads = [
-        jnp.concatenate([piece[0][...] for piece in per_piece], axis=0),
-        summed(1),
-        summed(1 + parts),
-    ]
-    for ref, grad in zip((dq_out, dk_out, dv_out), grads):
-        ref[...] = grad
-    weight_ref[...] = dot(jnp.concatenate(grads, axis=0), h_ref[...], 1, 0).T.astype(BF16)
-    for i, grad in enumerate(grads):
-        bias_ref[:, i : i + 1] = jnp.sum(grad.astype(F32), axis=1, keepdims=True)
+            height = piece[0].shape[0]
+            for kind in range(3):
+                start = (0, 1, 1 + parts)[kind]
+                total = piece[start][...]
+                for i in range(1, parts if kind else 1):
+                    total = total + piece[start + i][...].astype(F32)
+                total = total.astype(BF16)
+                grads_ref[kind * tall + first : kind * tall + first + height, :] = total
+                bias_ref[first : first + height, kind : kind + 1] = jnp.sum(total.astype(F32), axis=1, keepdims=True)
+            first += height
+        dk_out[...] = grads_ref[tall : 2 * tall, :]
+        dv_out[...] = grads_ref[2 * tall :, :]
+
+    weight_ref[...] = dot(grads_ref[...], h_ref[...], 1, 0).T.astype(BF16)
 
 
 def weight_grads(h_one, pieces):
     rows, width = h_one.shape
-    heights = [piece[0].shape[0] for piece in pieces]
-    tall = sum(heights)
+    tall = sum(piece[0].shape[0] for piece in pieces)
     parts = len(pieces[0][1])
+    block = pick_block(width, 256)
     kinds = jax.ShapeDtypeStruct
-    whole = lambda shape: pl.BlockSpec(shape, lambda: (0, 0))
     flat = [array for piece in pieces for array in (piece[0], *piece[1], *piece[2])]
     return pl.pallas_call(
         functools.partial(weight_grads_kernel, len(pieces), parts),
-        in_specs=[whole(array.shape) for array in (h_one, *flat)],
-        out_specs=[whole((tall, rows))] * 3 + [whole((width, 3 * tall)), whole((tall, 128))],
-        out_shape=[kinds((tall, rows), BF16)] * 3 + [kinds((width, 3 * tall), BF16), kinds((tall, 128), F32)],
+        grid=(width // block,),
+        in_specs=[pl.BlockSpec((rows, block), lambda i: (0, i))] + [whole_spec(array.shape) for array in flat],
+        out_specs=[whole_spec((tall, rows))] * 2
+        + [pl.BlockSpec((block, 3 * tall), lambda i: (i, 0)), whole_spec((tall, 128))],
+        out_shape=[kinds((tall, rows), BF16)] * 2 + [kinds((width, 3 * tall), BF16), kinds((tall, 128), F32)],
+        scratch_shapes=[pltpu.VMEM((3 * tall, rows), BF16)],
         compiler_params=pltpu.CompilerParams(vmem_limit_bytes=VMEM_LIMIT),
         cost_estimate=pl.CostEstimate(
             flops=6 * rows * width * tall, bytes_accessed=16 * rows * tall + 2 * rows * width, transcendentals=0
@@ -549,8 +557,8 @@
     )(h_one, *flat)
 
 
-def input_grads_kernel(groups, x_ref, d_res_ref, vectors_ref, w_ref, *refs):
-    grad_refs, (out_ref, sums_ref) = refs[: 3 * groups], refs[3 * groups :]
+def input_grads_kernel(counts, slot_ref, x_ref, d_res_ref, vectors_ref, w_ref, *refs):
+    grad_refs, (out_ref, sums_ref) = refs[:-2], refs[-2:]
     width = x_ref.shape[1]
 
     @pl.when(pl.program_id(0) == 0)
@@ -558,42 +566,52 @@
         sums_ref[...] = jnp.zeros_like(sums_ref)
 
     turned = None
+    used = 0
     for kind in range(3):
         first = (2, 0, 1)[kind] * width
-        grad = jnp.concatenate([grad_refs[3 * g + kind][...] for g in range(groups)], axis=0)
+        grad = jnp.concatenate([ref[...] for ref in grad_refs[used : used + counts[kind]]], axis=0)
+        used += counts[kind]
         update = dot(w_ref[:, first : first + width], grad, 1, 0)
         turned = update if turned is None else turned + update
     d_h_one = turned.T
     normed, inverse = norm_parts(x_ref[...].astype(F32))
     sums_ref[0:1, :] += add_rows(d_h_one)
     sums_ref[1:2, :] += add_rows(d_h_one * normed)
-    out_ref[...] = (d_res_ref[...] + norm_back(normed, inverse, d_h_one * (1.0 + vectors_ref[1:2, :]))).astype(BF16)
-
-
-def input_grads(inputs, half, d_residual, vectors, packed, grads):
+    grad = (d_res_ref[...] + norm_back(normed, inverse, d_h_one * (1.0 + vectors_ref[1:2, :]))).astype(BF16)
+    out_ref[...] = grad.reshape(out_ref.shape)
+
+
+def input_grads(slot, slots, inputs, half, d_residual, vectors, packed, grads):
     rows, width = inputs.shape
     block = pick_block(rows, 256)
     first = half * (rows // block)
-    row_spec = pl.BlockSpec((block, width), lambda i: (i, 0))
-    flat = [grad for group in grads for grad in group]
+    row_spec = pl.BlockSpec((block, width), lambda i, *_: (i, 0))
+    flat = [grad for kind in grads for grad in kind]
+    out_spec, out_shape = row_spec, (rows, width)
+    if slots:
+        out_spec = pl.BlockSpec((1, block, width), lambda i, at: (at[0], i, 0))
+        out_shape = (slots, rows, width)
     return pl.pallas_call(
-        functools.partial(input_grads_kernel, len(grads)),
-        grid=(rows // block,),
-        in_specs=[
-            row_spec,
-            pl.BlockSpec((block, width), lambda i: (i + first, 0)),
-            whole_spec(vectors.shape),
-            whole_spec((width, 3 * width)),
-        ]
-        + [pl.BlockSpec((grad.shape[0], block), lambda i: (0, i + first)) for grad in flat],
-        out_specs=[row_spec, whole_spec((8, width))],
-        out_shape=[jax.ShapeDtypeStruct((rows, width), BF16), jax.ShapeDtypeStruct((8, width), F32)],
+        functools.partial(input_grads_kernel, [len(kind) for kind in grads]),
+        grid_spec=pltpu.PrefetchScalarGridSpec(
+            num_scalar_prefetch=1,
+            grid=(rows // block,),
+            in_specs=[
+                row_spec,
+                pl.BlockSpec((block, width), lambda i, *_: (i + first, 0)),
+                whole_spec(vectors.shape),
+                whole_spec((width, 3 * width)),
+            ]
+            + [pl.BlockSpec((grad.shape[0], block), lambda i, *_: (0, i + first)) for grad in flat],
+            out_specs=[out_spec, whole_spec((8, width))],
+        ),
+        out_shape=[jax.ShapeDtypeStruct(out_shape, BF16), jax.ShapeDtypeStruct((8, width), F32)],
         compiler_params=pltpu.CompilerParams(vmem_limit_bytes=VMEM_LIMIT),
         cost_estimate=pl.CostEstimate(
             flops=6 * rows * width * width, bytes_accessed=14 * rows * width + 6 * width * width, transcendentals=0
         ),
         name="input_grads",
-    )(inputs, d_residual, vectors, packed, *flat)
+    )(slot, inputs, d_residual, vectors, packed, *flat)
 
 
 def time_features(t_index, model_width):
@@ -666,11 +684,12 @@
             parts = own, shift(away, "fsdp", n_fsdp, group)
             return parts if split else (jnp.concatenate(parts),) * 2
 
-        def swap_out(own, away):
-            whole = jnp.zeros((slots, local, width), own.dtype)
-            whole = lax.dynamic_update_index_in_dim(whole, own, slot, 0)
+        def swap_out(whole, away):
             arrived = shift(away, "fsdp", n_fsdp, group)
-            return lax.dynamic_update_index_in_dim(whole, arrived, other, 0)
+            return lax.dynamic_update_index_in_dim(whole, arrived, other, 0), arrived
+
+        def placed_own(own):
+            return lax.dynamic_update_index_in_dim(jnp.zeros((slots, local, width), own.dtype), own, slot, 0)
 
         def places_of(member):
             at = slot * group + member
@@ -685,19 +704,20 @@
         def sum_core(values):
             values = values.reshape(n_dp, n_pairs, 2, shard, values.shape[1])
             arrived = swap(pick(values, 1 - core, 2), "fsdp", n_fsdp)
-            return (pick(values, core, 2).astype(F32) + arrived.astype(F32)).astype(BF16)
+            return pick(values, core, 2).astype(F32) + arrived.astype(F32)
 
         def sum_pairs(values):
-            total = pick(values, pair, 1).astype(F32)
+            axis = values.ndim - 3
+            total = pick(values, pair, axis).astype(F32)
             for by in range(1, n_pairs):
-                arrived = shift(pick(values, (pair + by) % n_pairs, 1), "fsdp", n_fsdp, 2 * by)
+                arrived = shift(pick(values, (pair + by) % n_pairs, axis), "fsdp", n_fsdp, 2 * by)
                 total = total + arrived.astype(F32)
-            return total.astype(BF16)
+            return total
 
         def sum_side(values):
             values = values.reshape((far, 2) + values.shape[1:])
             arrived = swap(pick(values, 1 - side, 1), "dp", n_dp)
-            return (pick(values, side, 1).astype(F32) + arrived.astype(F32)).astype(BF16)
+            return pick(values, side, 1).astype(F32) + arrived.astype(F32)
 
         def sum_far(values):
             total = pick(values, deep).astype(F32)
@@ -711,8 +731,10 @@
             return jnp.stack([values, swap(values, "dp", n_dp)])
 
         packed = lax.all_gather(jnp.concatenate([w_key, w_value, w_query], axis=1), AXES, axis=0, tiled=True)
-        out_up = lax.all_gather(jnp.concatenate([w_out, w_up], axis=1), AXES, axis=0, tiled=True)
-        full_down = lax.all_gather(w_down, AXES, axis=0, tiled=True)
+        ups = hidden_width // width
+        w_up_turned = w_up.reshape(shard, n_dp * n_fsdp, ups, shard).swapaxes(1, 2).reshape(w_up.shape)
+        downs = [w_down[i * shard : (i + 1) * shard] for i in range(ups)]
+        packed_two = lax.all_gather(jnp.concatenate([w_out, w_up_turned, *downs], axis=1), AXES, axis=0, tiled=True)
 
         inputs = swap_in(*picked(frames))
         rows = slots * local
@@ -722,7 +744,7 @@
         active = jax.nn.silu(time_features(t_all, width)).astype(BF16)
         active_mine = lax.dynamic_slice_in_dim(active, me * shard, shard, axis=1)
         partial = [dot(active_mine, w_ada, 1, 0)]
-        for bias in (b_query, b_key, b_value, b_out, b_down, b_up):
+        for bias in (b_query, b_key, b_value, b_out, b_down, *jnp.split(b_up, ups)):
             size = bias.shape[0]
             zeros = jnp.zeros((1, size * n_dp * n_fsdp), F32)
             placed = lax.dynamic_update_slice_in_dim(zeros, bias.astype(F32)[None], me * size, axis=1)
@@ -764,36 +786,41 @@
             out, lse = attend(q_rot, k_parts[at], v_parts[at], bias_columns, at * tall)
             heads_out.append(out)
             lses.append(lse)
-        mixed, d_residual, d_heads, g_rows, sums_two, g_b_up = feed_forward(
-            inputs, heads_out, cotangent, keep, out_up, full_down, vectors, shard
+        at_slot = slot.reshape(1).astype(jnp.int32)
+        mixed, away_mixed, d_residual, d_heads, g_rows, sums_two = feed_forward(
+            at_slot, inputs, heads_out, cotangent, keep, packed_two, vectors, slots
         )
-        mixed = swap_out(mixed[:local], mixed[local:])
-
-        if shard % 16:
-            first = width + hidden_width
-            g_down = jnp.concatenate([g_rows[:, first + i * width : first + (i + 1) * width] for i in range(hidden_width // width)])
-            g_down = g_down.reshape(n_dp * n_fsdp, -1, shard, width)
-            g_down = [g_down[:, i].reshape(-1, width) for i in range(g_down.shape[1])]
-            g_rows = jnp.concatenate([g_rows[:, :first]] + g_down, axis=1)
+        if not split:
+            mixed, away_mixed = placed_own(mixed[:local]), mixed[local:]
+        mixed, _ = swap_out(mixed, away_mixed)
+
         sum_rows = lax.psum_scatter(g_rows, AXES, scatter_dimension=0, tiled=True).astype(F32)
-
-        grads, d_biases, moving = [], [], []
-        stages = [sum_core, sum_pairs, sum_side, sum_far]
-
-        def start_sum(pieces):
-            dq, dk, dv, weight_grad, bias_grad = weight_grads(h_one, pieces)
-            grads.append((dq, dk, dv))
+        g_out = sum_rows[:, :width]
+        g_up = sum_rows[:, width : width + hidden_width].reshape(shard, ups, n_dp * n_fsdp, shard)
+        g_up = g_up.swapaxes(1, 2).reshape(w_up.shape)
+        g_down = jnp.concatenate([sum_rows[:, (1 + ups + i) * width : (2 + ups + i) * width] for i in range(ups)])
+
+        grads, d_biases, moving = ([], [], []), [], []
+
+        def start_sum(pieces, stages):
+            dk, dv, weight_grad, bias_grad = weight_grads(h_one, pieces)
+            grads[0].extend(piece[0] for piece in pieces)
+            grads[1].append(dk)
+            grads[2].append(dv)
             d_biases.append(bias_grad[:, :3])
-            moving.append([0, weight_grad])
+            moving.append([list(stages), weight_grad])
             return weight_grad
 
-        def move_on(pick_from):
-            for item in pick_from:
-                if item[0] < len(stages):
-                    item[1] = stages[item[0]](item[1])
-                    item[0] += 1
-            return [item[1] for item in pick_from]
-
+        def move_on():
+            for item in moving:
+                if item[0]:
+                    item[1] = item[0].pop(0)(item[1])
+                    if item[0]:
+                        item[1] = item[1].astype(BF16)
+            return [item[1] for item in moving]
+
+        first_pairs = (sum_core, sum_pairs, sum_side, sum_far)
+        last_pairs = (sum_core, sum_side, sum_far, sum_pairs)
         counts = (4, 4, 2, 2, 2, 2)
         joined = (1, 1, 2, 2)
         steps = len(counts)
@@ -815,34 +842,35 @@
                 each,
             )
             first += each
-            done = move_on(moving)
+            done = move_on()
             if len(waiting) >= joined[next_sum]:
-                done.append(start_sum(waiting[: joined[next_sum]]))
+                done.append(start_sum(waiting[: joined[next_sum]], first_pairs))
                 waiting = waiting[joined[next_sum] :]
                 next_sum += 1
             dk_parts = [dk_parts[0]] + [lax.ppermute(dk_parts[by], "fsdp", ring(-by)) for by in range(1, group)]
             dv_parts = [dv_parts[0]] + [lax.ppermute(dv_parts[by], "fsdp", ring(-by)) for by in range(1, group)]
             waiting.append((dq, dk_parts, dv_parts))
+            if step == steps - 2:
+                done += [g_out, g_up, g_down]
             if done and step + 1 < steps:
                 ready = after(d_heads, dq, *done)
-        last = start_sum(waiting)
+        last = start_sum(waiting, last_pairs)
         if split:
             rest = after(d_residual, last)
-            away_frames, sums_away = input_grads(inputs[1], 1, rest, vectors, packed, grads)
-            done = move_on(moving)
-            rest, away_frames = lax.optimization_barrier((d_residual, away_frames, *done))[:2]
-            own_frames, sums_own = input_grads(inputs[0], 0, rest, vectors, packed, grads)
+            away_frames, sums_away = input_grads(at_slot, 0, inputs[1], 1, rest, vectors, packed, grads)
+            rest, away_frames = lax.optimization_barrier((d_residual, away_frames, *move_on()))[:2]
+            own_frames, sums_own = input_grads(at_slot, slots, inputs[0], 0, rest, vectors, packed, grads)
             sums_one = sums_own + sums_away
         else:
-            both, sums_one = input_grads(inputs[0], 0, d_residual, vectors, packed, grads)
-            own_frames, away_frames = both[:local], both[local:]
-        grad_frames = swap_out(own_frames, away_frames)
-        for _ in stages:
-            move_on(moving)
+            both, sums_one = input_grads(at_slot, 0, inputs[0], 0, d_residual, vectors, packed, grads)
+            own_frames, away_frames = placed_own(both[:local]), both[local:]
+        grad_frames, arrived = swap_out(own_frames, away_frames)
+        for _ in first_pairs:
+            move_on()
         sums = [item[1] for item in moving]
 
         vector = jnp.concatenate(
-            [sums_one[:2], sums_two[:6], g_b_up.reshape(-1, width), jnp.concatenate(d_biases).T]
+            [sums_one[:2], sums_two[: 6 + ups], jnp.concatenate(d_biases).T]
         )
         for_slot = 6
         total = vector
@@ -850,7 +878,7 @@
             total = total + lax.ppermute(vector, "fsdp", ring(by))
         packs = gather_dp(total).reshape(n_dp, -1, width)
         pack = jnp.concatenate([packs[:, :for_slot].reshape(-1, width), jnp.sum(packs[:, for_slot:], axis=0)])
-        across = shift(pack, "fsdp", n_fsdp, group)
+        across = shift(after(pack, arrived), "fsdp", n_fsdp, group)
         count = n_dp * for_slot
         d_mod = jnp.stack([jnp.where(slot == s, pack[:count], across[:count]).reshape(n_dp, -1) for s in range(slots)], axis=1)
         d_mod = d_mod.reshape(n_dp * slots, for_slot * width)
@@ -869,10 +897,8 @@
             size = vector.shape[0] // (n_dp * n_fsdp)
             return lax.dynamic_slice_in_dim(vector, me * size, size)
 
-        ups = hidden_width // width
         columns = [values.reshape(shard, 3, -1) for values in sums]
         g_qkv = [jnp.concatenate([values[:, i] for values in columns], axis=1) for i in range(3)]
-        g_down = sum_rows[:, width + hidden_width :].reshape(shard, -1, width)
         return (
             mixed,
             grad_frames,
@@ -884,11 +910,11 @@
             mine(d_vectors[3 + ups]),
             g_qkv[2],
             mine(d_vectors[4 + ups]),
-            sum_rows[:, :width],
+            g_out,
             mine(d_vectors[0]),
-            sum_rows[:, width : width + hidden_width],
-            mine(d_vectors[2 : 2 + ups]),
-            jnp.swapaxes(g_down, 0, 1).reshape(w_down.shape),
+            g_up,
+            jnp.concatenate([mine(d_vectors[2 + i]) for i in range(ups)]),
+            g_down,
             mine(d_vectors[1]),
         )
 

time: 727 us -> 706 us (0.971)
  Pallas kernels: 440 us -> 458 us
  other arithmetic: 42 us -> 26.4 us
  local copies, waits for them, and re-layouts: 61 us -> 45.6 us
  waiting for transfers between devices: 105 us -> 94.6 us
    pallas_call x2 -> x3, Pallas kernels: 90.5 us -> 105 us  [the longest x1 82.4 us: feed_forward(): pl.pallas_call(functools.partial(feed_forward_kernel, len(heads_out), pie...]
    all_gather x2 -> x1, waiting for transfers between devices: 14.5 us -> 0.02 us  [body(): lax.all_gather(jnp.concatenate([w_out, w_up_turned, *downs], axis=1), AXE...]
    pallas_call x2 -> x0, other arithmetic: 12.1 us -> none  [the longest x1 11.4 us: input_grads(): pl.pallas_call(functools.partial(input_grads_kernel, len(grads)), grid=(r...]
  transfers between devices with their start and end apart: 64 -> 63, of which waited for: 20 -> 24; matrix products, arithmetic and copies ran while one was open for 13% -> 9% of each run, Pallas kernels for 50% -> 51%
where the time goes in v3:
time: 706 us; the launch traced here: 700 us
  Pallas kernels  458 us (65%)
  waiting for transfers between devices  94.6 us (13%)
  starting transfers between devices  57.8 us (8%)
  local copies, waits for them, and re-layouts  45.6 us (6%)
  other arithmetic  26.4 us (4%)
  between operations  15.5 us (2%)
    pallas_call x6, Pallas kernels, attend_back(): pl.pallas_call(functools.partial(attend_back_kernel, parts, chunk), grid=...  194 us
    pallas_call x2, Pallas kernels, attend(): pl.pallas_call(functools.partial(attend_kernel, parts, chunk), grid=(head...  103 us
    pallas_call x1, Pallas kernels, feed_forward(): pl.pallas_call(functools.partial(feed_forward_kernel, len(heads_out), pie...  82.4 us
    ppermute x31, waiting for transfers between devices, shift(): lax.ppermute(values, axis, [(i, (i + by) % size) for i in range(size)])  56 us
    ppermute x31, starting transfers between devices, shift(): lax.ppermute(values, axis, [(i, (i + by) % size) for i in range(size)])  42.1 us
    pallas_call x4, Pallas kernels, weight_grads(): pl.pallas_call(functools.partial(weight_grads_kernel, len(pieces), parts)...  33.7 us
    pallas_call x2, Pallas kernels, input_grads(): pl.pallas_call(functools.partial(input_grads_kernel, [len(kind) for kind...  23.1 us
    ppermute x11, waiting for transfers between devices, swap(): return lax.ppermute(values, axis, [(i, i ^ 1) for i in range(size)])  18.8 us
  transfers between devices with their start and end apart: 63, of which 24 were waited for; matrix products, arithmetic and copies ran while one was open for 9% of the time, Pallas kernels for 51%

profile of v3, /device:TPU:0, one launch (start us, length us, event | category | flops | bytes accessed | tf_op | source)
XLA Modules:
  0.0 700.0 jit_solution(10608998438460153149)
XLA Ops:
  7.2 1.6 pad_maximum_fusion.6
  9.0 3.1 collective-permute-start.1
  12.0 2.6 collective-permute-start.2
  16.0 3.9 dynamic-slice_bitcast_fusion.2
  19.9 1.5 collective-permute-start
  24.6 1.6 collective-permute-start.4
  26.3 2.0 collective-permute-done.4
  31.2 1.5 collective-permute-start.5
  32.7 2.2 multiply_sine_fusion
  36.9 2.2 squeeze.182
  39.0 2.2 collective-permute-done.5
  43.1 1.7 collective-permute-start.7
  45.3 1.9 add_compare_fusion
  47.2 2.9 collective-permute-done.6
  50.2 6.8 collective-permute-done.7
  57.8 2.0 dynamic-slice_bitcast_fusion
  59.8 3.7 collective-permute-done.9
  71.3 18.2 %all-gather.3.cloned.1.call-done.w_ref = bf16[1024,3072]{1,0:T(8,128)(2,1)} async-done(((bf16[32,3072]{1,0:T(8,128)(2,1)}), bf16[1024,3072]{1,0:T(8,128)(2,1)}) %all-gather.3.cloned.1.call-update) | async-done | bytes 6291472 | tf_op jit(solution)/shard_map/all_gather | solution.py:733
  89.4 13.7 %project_kv.1 = (bf16[1536,1024]{1,0:T(8,128)(2,1)}, bf16[512,1536]{1,0:T(8,128)(2,1)}, bf16[512,1536]{1,0:T(8,128)(2,1)}, bf16[512,1536]{1,0:T(8,128)(2,1)}, bf16[512,1536]{1,0:T(8,128)(2,1)}) custom-call(bf16[768,1024]{1,0:T(8,128)(2,1)} %get-tuple-element.183.x_ref.refs_2_, bf16[768,1024]{1,0:T(8,128)(2,1)} %collective-permute-done.y_ref.refs_3_.x_ref, ...), custom_call_target="tpu_custom_call" | custom-call | flops 12884901888 | bytes 16777216 | tf_op jit(solution)/shard_map/project_kv/pallas_call | solution.py:338
  105.3 8.7 %project_q.1.refs_0_ = bf16[1024,1536]{1,0:T(8,128)(2,1)} custom-call(bf16[1536,1024]{1,0:T(8,128)(2,1)} %get-tuple-element.101.h_ref, f32[16,1024]{1,0:T(8,128)} %pad.8.vectors_ref.refs_8_, bf16[1024,3072]{1,0:T(8,128)(2,1)} %all-gather.3.cloned.1.call-done.w_ref, f32[32,1536]{1,0:T(8,128)} %slice.135.cos_ref, f32[32,1536]{1,0:T(8,128)} %slice.136.sin_ref), custom_call_target="tpu_custom_call" | custom-call | flops 6442450944 | bytes 8388608 | tf_op jit(solution)/shard_map/project_q/pallas_call | solution.py:352
  114.1 51.6 %attend.3 = (bf16[512,1536]{1,0:T(8,128)(2,1)}, f32[8,1,1536]{2,1,0:T(1,128)}) custom-call(bf16[1024,1536]{1,0:T(8,128)(2,1)} %project_q.1.refs_0_, bf16[3072,64]{1,0:T(8,128)(2,1)} %pad.9.refs_1_, bf16[512,1536]{1,0:T(8,128)(2,1)} %get-tuple-element.106.refs_2_.refs_7_, bf16[512,1536]{1,0:T(8,128)(2,1)} %collective-permute-done.13.refs_3_.refs_8_, ...), custom_call_target="tpu_custom_call" | custom-call | flops 38654705664 | bytes 9437184 | tf_op jit(solution)/shard_map/attend/pallas_call | solution.py:91
  165.7 51.4 %attend.2 = (bf16[512,1536]{1,0:T(8,128)(2,1)}, f32[8,1,1536]{2,1,0:T(1,128)}) custom-call(bf16[1024,1536]{1,0:T(8,128)(2,1)} %project_q.1.refs_0_, bf16[3072,64]{1,0:T(8,128)(2,1)} %pad.9.refs_1_, bf16[512,1536]{1,0:T(8,128)(2,1)} %get-tuple-element.103.refs_2_.refs_7_, bf16[512,1536]{1,0:T(8,128)(2,1)} %collective-permute-done.11.refs_3_.refs_8_, ...), custom_call_target="tpu_custom_call" | custom-call | flops 38654705664 | bytes 9437184 | tf_op jit(solution)/shard_map/attend/pallas_call | solution.py:91
  217.2 82.4 %feed_forward.1 = (bf16[2,768,1024]{2,1,0:T(8,128)(2,1)}, bf16[768,1024]{1,0:T(8,128)(2,1)}, f32[1536,1024]{1,0:T(8,128)}, bf16[1024,1536]{1,0:T(8,128)(2,1)}, b...) custom-call(s32[1]{0:T(128)} %bitcast.slot_ref, bf16[512,1536]{1,0:T(8,128)(2,1)} %get-tuple-element.105.refs_0_.refs_2_, ...), custom_call_target="tpu_custom_call" | custom-call | flops 48318382080 | bytes 33554432 | tf_op jit(solution)/shard_map/feed_forward/pallas_call | solution.py:466
  299.7 46.7 %attend_back.7 = (bf16[256,1536]{1,0:T(8,128)(2,1)}, f32[256,1536]{1,0:T(8,128)}, bf16[256,1536]{1,0:T(8,128)(2,1)}, f32[256,1536]{1,0:T(8,128)}, bf16[256,1536]{1,0:T(8,128)(2,1)}) custom-call(bf16[1024,1536]{1,0:T(8,128)(2,1)} %project_q.1.refs_0_, bf16[1024,1536]{1,0:T(8,128)(2,1)} %get-tuple-element.152.refs_1_, ...), custom_call_target="tpu_custom_call" | custom-call | flops 12079595520 | bytes 12582912 | tf_op jit(solution)/shard_map/attend_back/pallas_call | solution.py:223
  347.1 46.9 %attend_back.6 = (bf16[256,1536]{1,0:T(8,128)(2,1)}, f32[256,1536]{1,0:T(8,128)}, bf16[256,1536]{1,0:T(8,128)(2,1)}, f32[256,1536]{1,0:T(8,128)}, bf16[256,1536]{1,0:T(8,128)(2,1)}) custom-call(bf16[1024,1536]{1,0:T(8,128)(2,1)} %project_q.1.refs_0_, bf16[1024,1536]{1,0:T(8,128)(2,1)} %get-tuple-element.152.refs_1_, ...), custom_call_target="tpu_custom_call" | custom-call | flops 12079595520 | bytes 12582912 | tf_op jit(solution)/shard_map/attend_back/pallas_call | solution.py:223
  396.4 8.7 %weight_grads.4 = (bf16[256,1536]{1,0:T(8,128)(2,1)}, bf16[256,1536]{1,0:T(8,128)(2,1)}, bf16[1024,768]{1,0:T(8,128)(2,1)}, f32[256,128]{1,0:T(8,128)}) custom-call(bf16[1536,1024]{1,0:T(8,128)(2,1)} %get-tuple-element.101.h_ref, bf16[256,1536]{1,0:T(8,128)(2,1)} %get-tuple-element.120.refs_0_, f32[256,1536]{1,0:T(8,128)} %get-tuple-element.121.refs_1_, ...), custom_call_target="tpu_custom_call" | custom-call | flops 2415919104 | bytes 9437184 | tf_op jit(solution)/shard_map/weight_grads/pallas_call | solution.py:544
  405.1 1.5 constant_dynamic-slice_fusion.12
  406.8 24.8 %attend_back.8 = (bf16[128,1536]{1,0:T(8,128)(2,1)}, f32[128,1536]{1,0:T(8,128)}, bf16[128,1536]{1,0:T(8,128)(2,1)}, f32[128,1536]{1,0:T(8,128)}, bf16[128,1536]{1,0:T(8,128)(2,1)}) custom-call(bf16[1024,1536]{1,0:T(8,128)(2,1)} %project_q.1.refs_0_, bf16[1024,1536]{1,0:T(8,128)(2,1)} %get-tuple-element.152.refs_1_, ...), custom_call_target="tpu_custom_call" | custom-call | flops 6039797760 | bytes 6291456 | tf_op jit(solution)/shard_map/attend_back/pallas_call | solution.py:223
  432.3 8.3 %weight_grads.5 = (bf16[256,1536]{1,0:T(8,128)(2,1)}, bf16[256,1536]{1,0:T(8,128)(2,1)}, bf16[1024,768]{1,0:T(8,128)(2,1)}, f32[256,128]{1,0:T(8,128)}) custom-call(bf16[1536,1024]{1,0:T(8,128)(2,1)} %get-tuple-element.101.h_ref, bf16[256,1536]{1,0:T(8,128)(2,1)} %get-tuple-element.119.refs_0_.refs_1_, f32[256,1536]{1,0:T(8,128)} %get-tuple-element.129.refs_1_, ...), custom_call_target="tpu_custom_call" | custom-call | flops 2415919104 | bytes 9437184 | tf_op jit(solution)/shard_map/weight_grads/pallas_call | solution.py:544
  440.6 2.4 constant_dynamic-slice_fusion.10
  447.0 25.0 %attend_back.9 = (bf16[128,1536]{1,0:T(8,128)(2,1)}, f32[128,1536]{1,0:T(8,128)}, bf16[128,1536]{1,0:T(8,128)(2,1)}, f32[128,1536]{1,0:T(8,128)}, bf16[128,1536]{1,0:T(8,128)(2,1)}) custom-call(bf16[1024,1536]{1,0:T(8,128)(2,1)} %project_q.1.refs_0_, bf16[1024,1536]{1,0:T(8,128)(2,1)} %get-tuple-element.152.refs_1_, ...), custom_call_target="tpu_custom_call" | custom-call | flops 6039797760 | bytes 6291456 | tf_op jit(solution)/shard_map/attend_back/pallas_call | solution.py:223
  473.7 1.7 fusion.3
  476.3 1.6 bitcast_dynamic-update-slice_fusion.1
  477.9 5.9 collective-permute-done.22
  485.2 25.3 %attend_back.10 = (bf16[128,1536]{1,0:T(8,128)(2,1)}, f32[128,1536]{1,0:T(8,128)}, bf16[128,1536]{1,0:T(8,128)(2,1)}, f32[128,1536]{1,0:T(8,128)}, bf16[128,1536]{1,0:T(8,128)(2,1)}) custom-call(bf16[1024,1536]{1,0:T(8,128)(2,1)} %project_q.1.refs_0_, bf16[1024,1536]{1,0:T(8,128)(2,1)} %get-tuple-element.152.refs_1_, ...), custom_call_target="tpu_custom_call" | custom-call | flops 6039797760 | bytes 6291456 | tf_op jit(solution)/shard_map/attend_back/pallas_call | solution.py:223
  511.8 8.3 %weight_grads.6 = (bf16[256,1536]{1,0:T(8,128)(2,1)}, bf16[256,1536]{1,0:T(8,128)(2,1)}, bf16[1024,768]{1,0:T(8,128)(2,1)}, f32[256,128]{1,0:T(8,128)}) custom-call(bf16[1536,1024]{1,0:T(8,128)(2,1)} %get-tuple-element.101.h_ref, bf16[128,1536]{1,0:T(8,128)(2,1)} %get-tuple-element.128.refs_0_.refs_2_, f32[128,1536]{1,0:T(8,128)} %get-tuple-element.142.refs_1_, ...), custom_call_target="tpu_custom_call" | custom-call | flops 2415919104 | bytes 9437184 | tf_op jit(solution)/shard_map/weight_grads/pallas_call | solution.py:544
  520.2 1.5 constant_dynamic-slice_fusion.8
  526.6 1.6 collective-permute-start.34
  530.4 1.8 collective-permute-start.36
  532.6 1.6 collective-permute-done.35
  534.6 3.6 collective-permute-start.40
  541.4 2.0 collective-permute-start.42
  543.6 8.2 %collective-permute-done.42 = bf16[8,32,768]{2,1,0:T(8,128)(2,1)S(1)} collective-permute-done((bf16[8,32,768]{2,1,0:T(8,128)(2,1)S(1)}, bf16[8,32,768]{2,1,0:T(8,128)(2,1)S(1)}, u32[]{:S(2)}, u32[]{:S(2)}) %collective-permute-start.42) | collective-permute-done | bytes 393248 | tf_op jit(solution)/shard_map/ppermute | solution.py:640
  551.9 1.7 collective-permute-start.51
  554.3 3.4 collective-permute-done.51
  560.1 1.5 collective-permute-start.54
  563.7 2.1 reshape.284
  567.2 24.8 %attend_back.11 = (bf16[128,1536]{1,0:T(8,128)(2,1)}, f32[128,1536]{1,0:T(8,128)}, bf16[128,1536]{1,0:T(8,128)(2,1)}, f32[128,1536]{1,0:T(8,128)}, bf16[128,1536]{1,0:T(8,128)(2,1)}) custom-call(bf16[1024,1536]{1,0:T(8,128)(2,1)} %project_q.1.refs_0_, bf16[1024,1536]{1,0:T(8,128)(2,1)} %get-tuple-element.152.refs_1_, ...), custom_call_target="tpu_custom_call" | custom-call | flops 6039797760 | bytes 6291456 | tf_op jit(solution)/shard_map/attend_back/pallas_call | solution.py:223
  595.3 8.4 %weight_grads.7 = (bf16[256,1536]{1,0:T(8,128)(2,1)}, bf16[256,1536]{1,0:T(8,128)(2,1)}, bf16[1024,768]{1,0:T(8,128)(2,1)}, f32[256,128]{1,0:T(8,128)}) custom-call(bf16[1536,1024]{1,0:T(8,128)(2,1)} %get-tuple-element.101.h_ref, bf16[128,1536]{1,0:T(8,128)(2,1)} %get-tuple-element.137.refs_0_.refs_4_, f32[128,1536]{1,0:T(8,128)} %get-tuple-element.138.refs_1_, ...), custom_call_target="tpu_custom_call" | custom-call | flops 2415919104 | bytes 9437184 | tf_op jit(solution)/shard_map/weight_grads/pallas_call | solution.py:544
  605.4 11.6 %input_grads.2 = (bf16[768,1024]{1,0:T(8,128)(2,1)}, f32[8,1024]{1,0:T(8,128)}) custom-call(s32[1]{0:T(128)} %bitcast.slot_ref, bf16[768,1024]{1,0:T(8,128)(2,1)} %collective-permute-done.y_ref.refs_3_.x_ref, f32[1536,1024]{1,0:T(8,128)} %get-tuple-element.169.d_res_ref, f32[16,1024]{1,0:T(8,128)} %pad.8.vectors_ref.refs_8_, ...), custom_call_target="tpu_custom_call" | custom-call | flops 4831838208 | bytes 17301504 | tf_op jit(solution)/shard_map/input_grads/pallas_call | solution.py:594
  618.4 11.5 %input_grads.3 = (bf16[2,768,1024]{2,1,0:T(8,128)(2,1)}, f32[8,1024]{1,0:T(8,128)}) custom-call(s32[1]{0:T(128)} %bitcast.slot_ref, bf16[768,1024]{1,0:T(8,128)(2,1)} %get-tuple-element.183.x_ref.refs_2_, f32[1536,1024]{1,0:T(8,128)} %get-tuple-element.169.d_res_ref, f32[16,1024]{1,0:T(8,128)} %pad.8.vectors_ref.refs_8_, ...), custom_call_target="tpu_custom_call" | custom-call | flops 4831838208 | bytes 17301504 | tf_op jit(solution)/shard_map/input_grads/pallas_call | solution.py:594
  632.7 1.6 collective-permute-start.47
  634.3 2.8 collective-permute-start.48
  637.1 1.7 collective-permute-start.55
  638.9 2.2 collective-permute-done.47
  641.2 1.7 collective-permute-start.49
  643.3 10.0 %collective-permute-done.49 = f32[4,13,1024]{2,1,0:T(8,128)S(1)} collective-permute-done((f32[4,13,1024]{2,1,0:T(8,128)S(1)}, f32[4,13,1024]{2,1,0:T(8,128)S(1)}, u32[]{:S(2)}, u32[]{:S(2)}) %collective-permute-start.49) | collective-permute-done | bytes 213024 | tf_op jit(solution)/shard_map/ppermute | solution.py:702
  654.7 2.9 collective-permute-start.58
  657.6 3.5 collective-permute-done.56
  661.1 2.2 collective-permute-done.57
  663.3 1.8 collective-permute-start.59
  665.2 13.8 %collective-permute-done.59 = bf16[32,768]{1,0:T(8,128)(2,1)S(1)} collective-permute-done((bf16[32,768]{1,0:T(8,128)(2,1)S(1)}, bf16[32,768]{1,0:T(8,128)(2,1)S(1)}, u32[]{:S(2)}, u32[]{:S(2)}) %collective-permute-start.59) | collective-permute-done | bytes 49184 | tf_op jit(solution)/shard_map/ppermute | solution.py:640
  681.7 2.7 bitcast_dynamic-update-slice_fusion
  684.4 2.8 collective-permute-done.50
  (335 shorter events, 72.8 us)
Async XLA Ops:
  7.2 82.2 %all-gather.3.cloned.1.call-start = ((), (), s32[]{:S(2)}) async-start(), calls=%async_computation.1 | async-start | bytes 6488064 | tf_op jit(solution)/shard_map/all_gather | solution.py:733
  8.9 208.3 %all-gather.5.cloned.1.call-start = ((), (), s32[]{:S(2)}) async-start(), calls=%async_computation.2 | async-start | bytes 10813440 | tf_op jit(solution)/shard_map/all_gather | solution.py:737
  9.0 15.6 %collective-permute-start.1 = (s32[2]{0:T(128)}, s32[2]{0:T(128)S(1)}, u32[]{:S(2)}, u32[]{:S(2)}) collective-permute-start(s32[2]{0:T(128)} %param.20), channel_id=1, source_target_pairs={{0,8},{4,12},{8,16},{12,20},{16,24},{20,28},{24,0},{28,4},{1,9},{5... | collective-permute-start | bytes 32 | tf_op jit(solution)/shard_map/ppermute | solution.py:640
  12.0 12.5 %collective-permute-start.2 = (s32[2]{0:T(128)}, s32[2]{0:T(128)S(1)}, u32[]{:S(2)}, u32[]{:S(2)}) collective-permute-start(s32[2]{0:T(128)} %param.20), channel_id=1, source_target_pairs={{0,16},{4,20},{8,24},{12,28},{16,0},{20,4},{24,8},{28,12},{1,17},{... | collective-permute-start | bytes 32 | tf_op jit(solution)/shard_map/ppermute | solution.py:640
  14.6 9.9 %collective-permute-start.3 = (s32[2]{0:T(128)}, s32[2]{0:T(128)S(1)}, u32[]{:S(2)}, u32[]{:S(2)}) collective-permute-start(s32[2]{0:T(128)} %param.20), channel_id=1, source_target_pairs={{0,24},{4,28},{8,0},{12,4},{16,8},{20,12},{24,16},{28,20},{1,25},{... | collective-permute-start | bytes 32 | tf_op jit(solution)/shard_map/ppermute | solution.py:640
  19.9 51.4 %collective-permute-start = (bf16[768,1024]{1,0:T(8,128)(2,1)}, bf16[768,1024]{1,0:T(8,128)(2,1)}, u32[]{:S(2)}, u32[]{:S(2)}) collective-permute-start(bf16[768,1024]{1,0:T(8,128)(2,1)} %get-tuple-element.182), channel_id=1, source_target_pairs={{0,2},{1,3},{2,0},{3,1},{4,6},{5,7},{6,4},{7,5},{8,10},{9,11},{10,... | collective-permute-start | bytes 4718600 | tf_op jit(solution)/shard_map/ppermute | solution.py:640
  23.3 538.3 %reduce-scatter.2.cloned.1.call-start = ((), (), s32[]{:S(2)}) async-start(), calls=%async_computation.3 | async-start | bytes 10813440 | tf_op jit(solution)/shard_map/reduce_scatter | solution.py:797
  24.6 3.7 collective-permute-start.4
  31.2 10.0 %collective-permute-start.5 = (f32[4,2,13312]{2,1,0:T(2,128)}, f32[4,2,13312]{2,1,0:T(2,128)}, u32[]{:S(2)}, u32[]{:S(2)}) collective-permute-start(f32[4,2,13312]{2,1,0:T(2,128)} %squeeze.183), channel_id=1, source_target_pairs={{0,4},{4,0},{8,12},{12,8},{16,20},{20,16},{24,28},{28,24},{1,5},{5... | collective-permute-start | bytes 1277960 | tf_op jit(solution)/shard_map/ppermute | solution.py:702
  34.9 35.6 %copy-start.5 = (f32[32,3072]{1,0:T(8,128)}, f32[32,3072]{1,0:T(8,128)S(1)}, u32[]{:S(2)}) copy-start(f32[32,3072]{1,0:T(8,128)S(1)} %get-tuple-element.100.refs_6_) | copy-start | bytes 1179652
  42.6 7.6 %collective-permute-start.6 = (f32[2,13312]{1,0:T(2,128)S(1)}, f32[2,13312]{1,0:T(2,128)S(1)}, u32[]{:S(2)}, u32[]{:S(2)}) collective-permute-start(f32[2,13312]{1,0:T(2,128)S(1)} %get-tuple-element.194), channel_id=1, source_target_pairs={{0,24},{4,28},{8,0},{12,4},{16,8},{20,12},{24,16},{28,20},{1,25},{... | collective-permute-start | bytes 319496 | tf_op jit(solution)/shard_map/ppermute | solution.py:640
  43.1 13.9 %collective-permute-start.7 = (f32[2,13312]{1,0:T(2,128)S(1)}, f32[2,13312]{1,0:T(2,128)S(1)}, u32[]{:S(2)}, u32[]{:S(2)}) collective-permute-start(f32[2,13312]{1,0:T(2,128)S(1)} %get-tuple-element.196), channel_id=1, source_target_pairs={{0,16},{4,20},{8,24},{12,28},{16,0},{20,4},{24,8},{28,12},{1,17},{... | collective-permute-start | bytes 319496 | tf_op jit(solution)/shard_map/ppermute | solution.py:640
  44.8 12.2 %collective-permute-start.8 = (f32[2,13312]{1,0:T(2,128)S(1)}, f32[2,13312]{1,0:T(2,128)S(1)}, u32[]{:S(2)}, u32[]{:S(2)}) collective-permute-start(f32[2,13312]{1,0:T(2,128)S(1)} %get-tuple-element.195), channel_id=1, source_target_pairs={{0,8},{4,12},{8,16},{12,20},{16,24},{20,28},{24,0},{28,4},{1,9},{5... | collective-permute-start | bytes 319496 | tf_op jit(solution)/shard_map/ppermute | solution.py:640
  57.2 6.4 collective-permute-start.9
  63.6 5.6 collective-permute-start.10
  103.1 11.0 %collective-permute-start.13 = (bf16[512,1536]{1,0:T(8,128)(2,1)}, bf16[512,1536]{1,0:T(8,128)(2,1)}, u32[]{:S(2)}, u32[]{:S(2)}) collective-permute-start(bf16[512,1536]{1,0:T(8,128)(2,1)} %get-tuple-element.106.refs_2_.refs_7_), channel_id=1, source_target_pairs={{0,1},{1,0},{2,3},{3,2},{4,5},{5,4},{6,7},{7,6},{8,9},{9,8},{10,11... | collective-permute-start | bytes 4718600 | tf_op jit(solution)/shard_map/ppermute | solution.py:782
  103.4 10.7 %collective-permute-start.14 = (bf16[512,1536]{1,0:T(8,128)(2,1)}, bf16[512,1536]{1,0:T(8,128)(2,1)}, u32[]{:S(2)}, u32[]{:S(2)}) collective-permute-start(bf16[512,1536]{1,0:T(8,128)(2,1)} %get-tuple-element.107.refs_4_.refs_9_), channel_id=1, source_target_pairs={{0,1},{1,0},{2,3},{3,2},{4,5},{5,4},{6,7},{7,6},{8,9},{9,8},{10,11... | collective-permute-start | bytes 4718600 | tf_op jit(solution)/shard_map/ppermute | solution.py:782
  103.6 62.1 %collective-permute-start.11 = (bf16[512,1536]{1,0:T(8,128)(2,1)}, bf16[512,1536]{1,0:T(8,128)(2,1)}, u32[]{:S(2)}, u32[]{:S(2)}) collective-permute-start(bf16[512,1536]{1,0:T(8,128)(2,1)} %get-tuple-element.103.refs_2_.refs_7_), channel_id=1, source_target_pairs={{0,1},{1,0},{2,3},{3,2},{4,5},{5,4},{6,7},{7,6},{8,9},{9,8},{10,11... | collective-permute-start | bytes 4718600 | tf_op jit(solution)/shard_map/ppermute | solution.py:782
  103.9 113.2 %collective-permute-start.15 = (bf16[768,1024]{1,0:T(8,128)(2,1)S(1)}, bf16[768,1024]{1,0:T(8,128)(2,1)}, u32[]{:S(2)}, u32[]{:S(2)}) collective-permute-start(bf16[768,1024]{1,0:T(8,128)(2,1)S(1)} %copy-done.3), channel_id=1, source_target_pairs={{0,2},{1,3},{2,0},{3,1},{4,6},{5,7},{6,4},{7,5},{8,10},{9,11},{10,... | collective-permute-start | bytes 4718600 | tf_op jit(solution)/shard_map/ppermute | solution.py:640
  105.3 60.4 %collective-permute-start.12 = (bf16[512,1536]{1,0:T(8,128)(2,1)}, bf16[512,1536]{1,0:T(8,128)(2,1)}, u32[]{:S(2)}, u32[]{:S(2)}) collective-permute-start(bf16[512,1536]{1,0:T(8,128)(2,1)} %get-tuple-element.104.refs_4_.refs_9_), channel_id=1, source_target_pairs={{0,1},{1,0},{2,3},{3,2},{4,5},{5,4},{6,7},{7,6},{8,9},{9,8},{10,11... | collective-permute-start | bytes 4718600 | tf_op jit(solution)/shard_map/ppermute | solution.py:782
  346.4 48.8 %collective-permute-start.17 = (bf16[256,1536]{1,0:T(8,128)(2,1)}, bf16[256,1536]{1,0:T(8,128)(2,1)S(1)}, u32[]{:S(2)}, u32[]{:S(2)}) collective-permute-start(bf16[256,1536]{1,0:T(8,128)(2,1)} %get-tuple-element.122), channel_id=1, source_target_pairs={{0,1},{1,0},{2,3},{3,2},{4,5},{5,4},{6,7},{7,6},{8,9},{9,8},{10,11... | collective-permute-start | bytes 2359304 | tf_op jit(solution)/shard_map/ppermute | solution.py:850
  347.0 48.2 %collective-permute-start.18 = (bf16[256,1536]{1,0:T(8,128)(2,1)}, bf16[256,1536]{1,0:T(8,128)(2,1)S(1)}, u32[]{:S(2)}, u32[]{:S(2)}) collective-permute-start(bf16[256,1536]{1,0:T(8,128)(2,1)} %get-tuple-element.124), channel_id=1, source_target_pairs={{0,1},{1,0},{2,3},{3,2},{4,5},{5,4},{6,7},{7,6},{8,9},{9,8},{10,11... | collective-permute-start | bytes 2359304 | tf_op jit(solution)/shard_map/ppermute | solution.py:851
  394.0 38.1 %collective-permute-start.20 = (bf16[256,1536]{1,0:T(8,128)(2,1)}, bf16[256,1536]{1,0:T(8,128)(2,1)}, u32[]{:S(2)}, u32[]{:S(2)}) collective-permute-start(bf16[256,1536]{1,0:T(8,128)(2,1)} %get-tuple-element.130), channel_id=1, source_target_pairs={{0,1},{1,0},{2,3},{3,2},{4,5},{5,4},{6,7},{7,6},{8,9},{9,8},{10,11... | collective-permute-start | bytes 2359304 | tf_op jit(solution)/shard_map/ppermute | solution.py:850
  394.5 37.8 %collective-permute-start.21 = (bf16[256,1536]{1,0:T(8,128)(2,1)}, bf16[256,1536]{1,0:T(8,128)(2,1)}, u32[]{:S(2)}, u32[]{:S(2)}) collective-permute-start(bf16[256,1536]{1,0:T(8,128)(2,1)} %get-tuple-element.132), channel_id=1, source_target_pairs={{0,1},{1,0},{2,3},{3,2},{4,5},{5,4},{6,7},{7,6},{8,9},{9,8},{10,11... | collective-permute-start | bytes 2359304 | tf_op jit(solution)/shard_map/ppermute | solution.py:851
  394.6 81.6 %collective-permute-start.16 = (bf16[768,1024]{1,0:T(8,128)(2,1)}, bf16[768,1024]{1,0:T(8,128)(2,1)}, u32[]{:S(2)}, u32[]{:S(2)}) collective-permute-start(bf16[768,1024]{1,0:T(8,128)(2,1)} %get-tuple-element.114), channel_id=1, source_target_pairs={{0,2},{1,3},{2,0},{3,1},{4,6},{5,7},{6,4},{7,5},{8,10},{9,11},{10,... | collective-permute-start | bytes 4718600 | tf_op jit(solution)/shard_map/ppermute | solution.py:640
  406.7 39.0 %collective-permute-start.19 = (bf16[8,2,32,768]{3,2,0,1:T(8,128)(2,1)S(1)}, bf16[8,2,32,768]{3,2,0,1:T(8,128)(2,1)}, u32[]{:S(2)}, u32[]{:S(2)}) collective-permute-start(bf16[8,2,32,768]{3,2,0,1:T(8,128)(2,1)S(1)} %bitcast.232), channel_id=1, source_target_pairs={{0,1},{1,0},{2,3},{3,2},{4,5},{5,4},{6,7},{7,6},{8,9},{9,8},{10,11... | collective-permute-start | bytes 2359304 | tf_op jit(solution)/shard_map/ppermute | solution.py:702
  431.7 79.5 %collective-permute-start.28 = (bf16[128,1536]{1,0:T(8,128)(2,1)}, bf16[128,1536]{1,0:T(8,128)(2,1)}, u32[]{:S(2)}, u32[]{:S(2)}) collective-permute-start(bf16[128,1536]{1,0:T(8,128)(2,1)} %get-tuple-element.143), channel_id=1, source_target_pairs={{0,1},{1,0},{2,3},{3,2},{4,5},{5,4},{6,7},{7,6},{8,9},{9,8},{10,11... | collective-permute-start | bytes 1179656 | tf_op jit(solution)/shard_map/ppermute | solution.py:850
  432.1 79.7 %collective-permute-start.29 = (bf16[128,1536]{1,0:T(8,128)(2,1)}, bf16[128,1536]{1,0:T(8,128)(2,1)}, u32[]{:S(2)}, u32[]{:S(2)}) collective-permute-start(bf16[128,1536]{1,0:T(8,128)(2,1)} %get-tuple-element.145), channel_id=1, source_target_pairs={{0,1},{1,0},{2,3},{3,2},{4,5},{5,4},{6,7},{7,6},{8,9},{9,8},{10,11... | collective-permute-start | bytes 1179656 | tf_op jit(solution)/shard_map/ppermute | solution.py:851
  443.9 28.3 %collective-permute-start.23 = (bf16[8,2,32,768]{3,2,0,1:T(8,128)(2,1)}, bf16[8,2,32,768]{3,2,0,1:T(8,128)(2,1)}, u32[]{:S(2)}, u32[]{:S(2)}) collective-permute-start(bf16[8,2,32,768]{3,2,0,1:T(8,128)(2,1)} %bitcast.205), channel_id=1, source_target_pairs={{0,1},{1,0},{2,3},{3,2},{4,5},{5,4},{6,7},{7,6},{8,9},{9,8},{10,11... | collective-permute-start | bytes 2359304 | tf_op jit(solution)/shard_map/ppermute | solution.py:702
  472.0 39.8 %collective-permute-start.30 = (bf16[128,1536]{1,0:T(8,128)(2,1)}, bf16[128,1536]{1,0:T(8,128)(2,1)}, u32[]{:S(2)}, u32[]{:S(2)}) collective-permute-start(bf16[128,1536]{1,0:T(8,128)(2,1)} %get-tuple-element.147), channel_id=1, source_target_pairs={{0,1},{1,0},{2,3},{3,2},{4,5},{5,4},{6,7},{7,6},{8,9},{9,8},{10,11... | collective-permute-start | bytes 1179656 | tf_op jit(solution)/shard_map/ppermute | solution.py:850
  472.3 11.5 %collective-permute-start.22 = (bf16[8,32,768]{2,1,0:T(8,128)(2,1)S(1)}, bf16[8,32,768]{2,1,0:T(8,128)(2,1)S(1)}, u32[]{:S(2)}, u32[]{:S(2)}) collective-permute-start(bf16[8,32,768]{2,1,0:T(8,128)(2,1)S(1)} %dynamic-slice_bitcast_fusion.8), channel_id=1, source_target_pairs={{0,2},{1,3},{2,0},{3,1},{4,6},{5,7},{6,4},{7,5},{8,10},{9,11},{10,... | collective-permute-start | bytes 1179656 | tf_op jit(solution)/shard_map/ppermute | solution.py:640
  476.2 35.6 %collective-permute-start.31 = (bf16[128,1536]{1,0:T(8,128)(2,1)}, bf16[128,1536]{1,0:T(8,128)(2,1)}, u32[]{:S(2)}, u32[]{:S(2)}) collective-permute-start(bf16[128,1536]{1,0:T(8,128)(2,1)} %get-tuple-element.149), channel_id=1, source_target_pairs={{0,1},{1,0},{2,3},{3,2},{4,5},{5,4},{6,7},{7,6},{8,9},{9,8},{10,11... | collective-permute-start | bytes 1179656 | tf_op jit(solution)/shard_map/ppermute | solution.py:851
  483.7 38.6 %collective-permute-start.27 = (bf16[8,32,768]{2,1,0:T(8,128)(2,1)}, bf16[8,32,768]{2,1,0:T(8,128)(2,1)}, u32[]{:S(2)}, u32[]{:S(2)}) collective-permute-start(bf16[8,32,768]{2,1,0:T(8,128)(2,1)} %dynamic-slice_bitcast_fusion.7), channel_id=1, source_target_pairs={{0,2},{1,3},{2,0},{3,1},{4,6},{5,7},{6,4},{7,5},{8,10},{9,11},{10,... | collective-permute-start | bytes 1179656 | tf_op jit(solution)/shard_map/ppermute | solution.py:640
  511.2 14.4 %collective-permute-start.26 = (bf16[4,32,768]{2,1,0:T(8,128)(2,1)}, bf16[4,32,768]{2,1,0:T(8,128)(2,1)}, u32[]{:S(2)}, u32[]{:S(2)}) collective-permute-start(bf16[4,32,768]{2,1,0:T(8,128)(2,1)} %dynamic-slice_bitcast_fusion.11), channel_id=1, source_target_pairs={{0,4},{4,0},{8,12},{12,8},{16,20},{20,16},{24,28},{28,24},{1,5},{5... | collective-permute-start | bytes 589832 | tf_op jit(solution)/shard_map/ppermute | solution.py:702
  511.8 82.1 %collective-permute-start.24 = (bf16[128,1536]{1,0:T(8,128)(2,1)}, bf16[128,1536]{1,0:T(8,128)(2,1)}, u32[]{:S(2)}, u32[]{:S(2)}) collective-permute-start(bf16[128,1536]{1,0:T(8,128)(2,1)} %get-tuple-element.139), channel_id=1, source_target_pairs={{0,1},{1,0},{2,3},{3,2},{4,5},{5,4},{6,7},{7,6},{8,9},{9,8},{10,11... | collective-permute-start | bytes 1179656 | tf_op jit(solution)/shard_map/ppermute | solution.py:850
  521.8 18.2 %collective-permute-start.41 = (bf16[8,2,32,768]{3,2,0,1:T(8,128)(2,1)S(1)}, bf16[8,2,32,768]{3,2,0,1:T(8,128)(2,1)}, u32[]{:S(2)}, u32[]{:S(2)}) collective-permute-start(bf16[8,2,32,768]{3,2,0,1:T(8,128)(2,1)S(1)} %bitcast.231), channel_id=1, source_target_pairs={{0,1},{1,0},{2,3},{3,2},{4,5},{5,4},{6,7},{7,6},{8,9},{9,8},{10,11... | collective-permute-start | bytes 2359304 | tf_op jit(solution)/shard_map/ppermute | solution.py:702
  523.5 6.9 collective-permute-start.37
  526.6 6.0 collective-permute-start.34
  528.2 6.0 collective-permute-start.35
  530.4 4.2 collective-permute-start.36
  532.6 6.0 collective-permute-start.38
  534.2 5.7 collective-permute-start.39
  534.6 5.3 collective-permute-start.40
  538.6 55.4 %collective-permute-start.25 = (bf16[128,1536]{1,0:T(8,128)(2,1)}, bf16[128,1536]{1,0:T(8,128)(2,1)}, u32[]{:S(2)}, u32[]{:S(2)}) collective-permute-start(bf16[128,1536]{1,0:T(8,128)(2,1)} %get-tuple-element.141), channel_id=1, source_target_pairs={{0,1},{1,0},{2,3},{3,2},{4,5},{5,4},{6,7},{7,6},{8,9},{9,8},{10,11... | collective-permute-start | bytes 1179656 | tf_op jit(solution)/shard_map/ppermute | solution.py:851
  541.4 10.3 %collective-permute-start.42 = (bf16[8,32,768]{2,1,0:T(8,128)(2,1)S(1)}, bf16[8,32,768]{2,1,0:T(8,128)(2,1)S(1)}, u32[]{:S(2)}, u32[]{:S(2)}) collective-permute-start(bf16[8,32,768]{2,1,0:T(8,128)(2,1)S(1)} %dynamic-slice_bitcast_fusion.6), channel_id=1, source_target_pairs={{0,2},{1,3},{2,0},{3,1},{4,6},{5,7},{6,4},{7,5},{8,10},{9,11},{10,... | collective-permute-start | bytes 1179656 | tf_op jit(solution)/shard_map/ppermute | solution.py:640
  551.9 5.7 collective-permute-start.51
  557.7 34.3 %collective-permute-start.52 = (bf16[32,768]{1,0:T(8,128)(2,1)S(1)}, bf16[32,768]{1,0:T(8,128)(2,1)S(1)}, u32[]{:S(2)}, u32[]{:S(2)}) collective-permute-start(bf16[32,768]{1,0:T(8,128)(2,1)S(1)} %get-tuple-element.205), channel_id=1, source_target_pairs={{0,8},{4,12},{8,16},{12,20},{16,24},{20,28},{24,0},{28,4},{1,9},{5... | collective-permute-start | bytes 147464 | tf_op jit(solution)/shard_map/ppermute | solution.py:640
  558.8 33.3 %collective-permute-start.53 = (bf16[32,768]{1,0:T(8,128)(2,1)S(1)}, bf16[32,768]{1,0:T(8,128)(2,1)S(1)}, u32[]{:S(2)}, u32[]{:S(2)}) collective-permute-start(bf16[32,768]{1,0:T(8,128)(2,1)S(1)} %get-tuple-element.207), channel_id=1, source_target_pairs={{0,16},{4,20},{8,24},{12,28},{16,0},{20,4},{24,8},{28,12},{1,17},{... | collective-permute-start | bytes 147464 | tf_op jit(solution)/shard_map/ppermute | solution.py:640
  560.1 33.8 %collective-permute-start.54 = (bf16[32,768]{1,0:T(8,128)(2,1)S(1)}, bf16[32,768]{1,0:T(8,128)(2,1)S(1)}, u32[]{:S(2)}, u32[]{:S(2)}) collective-permute-start(bf16[32,768]{1,0:T(8,128)(2,1)S(1)} %get-tuple-element.206), channel_id=1, source_target_pairs={{0,24},{4,28},{8,0},{12,4},{16,8},{20,12},{24,16},{28,20},{1,25},{... | collective-permute-start | bytes 147464 | tf_op jit(solution)/shard_map/ppermute | solution.py:640
  592.0 2.0 collective-permute-start.32
  592.1 2.5 collective-permute-start.33
  605.0 12.0 %collective-permute-start.43 = (bf16[8,2,32,768]{3,2,1,0:T(8,128)(2,1)S(1)}, bf16[8,2,32,768]{3,2,1,0:T(8,128)(2,1)S(1)}, u32[]{:S(2)}, u32[]{:S(2)}) collective-permute-start(bf16[8,2,32,768]{3,2,1,0:T(8,128)(2,1)S(1)} %dynamic-slice_bitcast_fusion.4), channel_id=1, source_target_pairs={{0,1},{1,0},{2,3},{3,2},{4,5},{5,4},{6,7},{7,6},{8,9},{9,8},{10,11... | collective-permute-start | bytes 2359304 | tf_op jit(solution)/shard_map/ppermute | solution.py:702
  630.7 1.3 collective-permute-start.45
  632.1 6.8 collective-permute-start.46
  632.7 8.5 %collective-permute-start.47 = (f32[13,1024]{1,0:T(8,128)S(1)}, f32[13,1024]{1,0:T(8,128)S(1)}, u32[]{:S(2)}, u32[]{:S(2)}) collective-permute-start(f32[13,1024]{1,0:T(8,128)S(1)} %fusion.34), channel_id=1, source_target_pairs={{0,16},{4,20},{8,24},{12,28},{16,0},{20,4},{24,8},{28,12},{1,17},{... | collective-permute-start | bytes 159752 | tf_op jit(solution)/shard_map/ppermute | solution.py:640
  634.3 6.9 collective-permute-start.48
  637.1 16.3 %collective-permute-start.55 = (bf16[4,2,32,768]{3,2,1,0:T(8,128)(2,1)S(1)}, bf16[4,2,32,768]{3,2,1,0:T(8,128)(2,1)S(1)}, u32[]{:S(2)}, u32[]{:S(2)}) collective-permute-start(bf16[4,2,32,768]{3,2,1,0:T(8,128)(2,1)S(1)} %dynamic-slice_bitcast_fusion.5), channel_id=1, source_target_pairs={{0,4},{4,0},{8,12},{12,8},{16,20},{20,16},{24,28},{28,24},{1,5},{5... | collective-permute-start | bytes 1179656 | tf_op jit(solution)/shard_map/ppermute | solution.py:702
  641.2 12.1 %collective-permute-start.49 = (f32[4,13,1024]{2,1,0:T(8,128)S(1)}, f32[4,13,1024]{2,1,0:T(8,128)S(1)}, u32[]{:S(2)}, u32[]{:S(2)}) collective-permute-start(f32[4,13,1024]{2,1,0:T(8,128)S(1)} %get-tuple-element.204), channel_id=1, source_target_pairs={{0,4},{4,0},{8,12},{12,8},{16,20},{20,16},{24,28},{28,24},{1,5},{5... | collective-permute-start | bytes 638984 | tf_op jit(solution)/shard_map/ppermute | solution.py:702
  642.9 38.2 %collective-permute-start.44 = (bf16[768,1024]{1,0:T(8,128)(2,1)}, bf16[768,1024]{1,0:T(8,128)(2,1)}, u32[]{:S(2)}, u32[]{:S(2)}) collective-permute-start(bf16[768,1024]{1,0:T(8,128)(2,1)} %get-tuple-element.171), channel_id=1, source_target_pairs={{0,2},{1,3},{2,0},{3,1},{4,6},{5,7},{6,4},{7,5},{8,10},{9,11},{10,... | collective-permute-start | bytes 4718600 | tf_op jit(solution)/shard_map/ppermute | solution.py:640
  653.6 7.4 %collective-permute-start.56 = (bf16[2,32,768]{2,1,0:T(8,128)(2,1)S(1)}, bf16[2,32,768]{2,1,0:T(8,128)(2,1)S(1)}, u32[]{:S(2)}, u32[]{:S(2)}) collective-permute-start(bf16[2,32,768]{2,1,0:T(8,128)(2,1)S(1)} %get-tuple-element.197), channel_id=1, source_target_pairs={{0,8},{4,12},{8,16},{12,20},{16,24},{20,28},{24,0},{28,4},{1,9},{5... | collective-permute-start | bytes 294920 | tf_op jit(solution)/shard_map/ppermute | solution.py:640
  653.7 9.6 %collective-permute-start.57 = (bf16[2,32,768]{2,1,0:T(8,128)(2,1)S(1)}, bf16[2,32,768]{2,1,0:T(8,128)(2,1)S(1)}, u32[]{:S(2)}, u32[]{:S(2)}) collective-permute-start(bf16[2,32,768]{2,1,0:T(8,128)(2,1)S(1)} %get-tuple-element.199), channel_id=1, source_target_pairs={{0,16},{4,20},{8,24},{12,28},{16,0},{20,4},{24,8},{28,12},{1,17},{... | collective-permute-start | bytes 294920 | tf_op jit(solution)/shard_map/ppermute | solution.py:640
  654.7 8.6 %collective-permute-start.58 = (bf16[2,32,768]{2,1,0:T(8,128)(2,1)S(1)}, bf16[2,32,768]{2,1,0:T(8,128)(2,1)S(1)}, u32[]{:S(2)}, u32[]{:S(2)}) collective-permute-start(bf16[2,32,768]{2,1,0:T(8,128)(2,1)S(1)} %get-tuple-element.198), channel_id=1, source_target_pairs={{0,24},{4,28},{8,0},{12,4},{16,8},{20,12},{24,16},{28,20},{1,25},{... | collective-permute-start | bytes 294920 | tf_op jit(solution)/shard_map/ppermute | solution.py:640
  663.3 15.6 %collective-permute-start.59 = (bf16[32,768]{1,0:T(8,128)(2,1)S(1)}, bf16[32,768]{1,0:T(8,128)(2,1)S(1)}, u32[]{:S(2)}, u32[]{:S(2)}) collective-permute-start(bf16[32,768]{1,0:T(8,128)(2,1)S(1)} %dynamic-slice_bitcast_fusion.15), channel_id=1, source_target_pairs={{0,2},{1,3},{2,0},{3,1},{4,6},{5,7},{6,4},{7,5},{8,10},{9,11},{10,... | collective-permute-start | bytes 147464 | tf_op jit(solution)/shard_map/ppermute | solution.py:640
  681.1 6.0 collective-permute-start.50
  (43 other events, 279.5 us)
Sparse Core Ops, SparseCore 0:
  11.5 77.9 all-gather.2
  92.3 94.9 all-gather.4
  299.7 165.8 reduce-scatter.1

commit v4 on v3

--- a/solution.py
+++ b/solution.py
@@ -246,7 +246,7 @@
         ],
         compiler_params=pltpu.CompilerParams(vmem_limit_bytes=VMEM_LIMIT),
         cost_estimate=pl.CostEstimate(
-            flops=10 * count * rows * span * HDIM,
+            flops=40 * count * rows * span * HDIM,
             bytes_accessed=2 * count * HDIM * (8 * rows + 4 * span),
             transcendentals=0,
         ),
@@ -508,53 +508,51 @@
     )(slot, *heads_out, *inputs, *cotangent, keep, packed, vectors)
 
 
-def weight_grads_kernel(pieces, parts, h_ref, *refs):
-    count = pieces * (1 + 2 * parts)
-    per_piece = [refs[i * (1 + 2 * parts) : (i + 1) * (1 + 2 * parts)] for i in range(pieces)]
-    dk_out, dv_out, weight_ref, bias_ref, grads_ref = refs[count:]
-    tall = dk_out.shape[0]
-
-    @pl.when(pl.program_id(0) == 0)
-    def _():
-        first = 0
-        for piece in per_piece:
-            height = piece[0].shape[0]
-            for kind in range(3):
-                start = (0, 1, 1 + parts)[kind]
-                total = piece[start][...]
-                for i in range(1, parts if kind else 1):
-                    total = total + piece[start + i][...].astype(F32)
-                total = total.astype(BF16)
-                grads_ref[kind * tall + first : kind * tall + first + height, :] = total
-                bias_ref[first : first + height, kind : kind + 1] = jnp.sum(total.astype(F32), axis=1, keepdims=True)
-            first += height
-        dk_out[...] = grads_ref[tall : 2 * tall, :]
-        dv_out[...] = grads_ref[2 * tall :, :]
-
-    weight_ref[...] = dot(grads_ref[...], h_ref[...], 1, 0).T.astype(BF16)
-
-
-def weight_grads(h_one, pieces):
+def weight_grads_kernel(parts, h_ref, dq_ref, *refs):
+    dk_refs, dv_refs = refs[:parts], refs[parts : 2 * parts]
+    dk_out, dv_out, weight_ref, bias_ref = refs[2 * parts :]
+
+    def summed(pieces):
+        total = pieces[0][...]
+        for ref in pieces[1:]:
+            total = total + ref[...].astype(F32)
+        return total.astype(BF16)
+
+    grads = [dq_ref[...], summed(dk_refs), summed(dv_refs)]
+    dk_out[...] = grads[1]
+    dv_out[...] = grads[2]
+    weight_ref[...] = dot(jnp.concatenate(grads, axis=0), h_ref[...], 1, 0).T.astype(BF16)
+    for i, grad in enumerate(grads):
+        bias_ref[:, i : i + 1] = jnp.sum(grad.astype(F32), axis=1, keepdims=True)
+
+
+def weight_grads(h_one, d_query, dk_parts, dv_parts):
     rows, width = h_one.shape
-    tall = sum(piece[0].shape[0] for piece in pieces)
-    parts = len(pieces[0][1])
-    block = pick_block(width, 256)
+    tall = d_query.shape[0]
+    block = pick_block(tall, 128)
+    spec = pl.BlockSpec((block, rows), lambda i: (i, 0))
     kinds = jax.ShapeDtypeStruct
-    flat = [array for piece in pieces for array in (piece[0], *piece[1], *piece[2])]
+    parts = len(dk_parts)
     return pl.pallas_call(
-        functools.partial(weight_grads_kernel, len(pieces), parts),
-        grid=(width // block,),
-        in_specs=[pl.BlockSpec((rows, block), lambda i: (0, i))] + [whole_spec(array.shape) for array in flat],
-        out_specs=[whole_spec((tall, rows))] * 2
-        + [pl.BlockSpec((block, 3 * tall), lambda i: (i, 0)), whole_spec((tall, 128))],
-        out_shape=[kinds((tall, rows), BF16)] * 2 + [kinds((width, 3 * tall), BF16), kinds((tall, 128), F32)],
-        scratch_shapes=[pltpu.VMEM((3 * tall, rows), BF16)],
+        functools.partial(weight_grads_kernel, parts),
+        grid=(tall // block,),
+        in_specs=[whole_spec((rows, width))] + [spec] * (1 + 2 * parts),
+        out_specs=[
+            spec,
+            spec,
+            pl.BlockSpec((width, 3 * block), lambda i: (0, i)),
+            pl.BlockSpec((block, 128), lambda i: (i, 0)),
+        ],
+        out_shape=[
+            kinds((tall, rows), BF16),
+            kinds((tall, rows), BF16),
+            kinds((width, 3 * tall), BF16),
+            kinds((tall, 128), F32),
+        ],
         compiler_params=pltpu.CompilerParams(vmem_limit_bytes=VMEM_LIMIT),
-        cost_estimate=pl.CostEstimate(
-            flops=6 * rows * width * tall, bytes_accessed=16 * rows * tall + 2 * rows * width, transcendentals=0
-        ),
+        cost_estimate=pl.CostEstimate(flops=0, bytes_accessed=0, transcendentals=0),
         name="weight_grads",
-    )(h_one, *flat)
+    )(h_one, d_query, *dk_parts, *dv_parts)
 
 
 def input_grads_kernel(counts, slot_ref, x_ref, d_res_ref, vectors_ref, w_ref, *refs):
@@ -607,9 +605,7 @@
         ),
         out_shape=[jax.ShapeDtypeStruct(out_shape, BF16), jax.ShapeDtypeStruct((8, width), F32)],
         compiler_params=pltpu.CompilerParams(vmem_limit_bytes=VMEM_LIMIT),
-        cost_estimate=pl.CostEstimate(
-            flops=6 * rows * width * width, bytes_accessed=14 * rows * width + 6 * width * width, transcendentals=0
-        ),
+        cost_estimate=pl.CostEstimate(flops=0, bytes_accessed=0, transcendentals=0),
         name="input_grads",
     )(slot, inputs, d_residual, vectors, packed, *flat)
 
@@ -800,31 +796,17 @@
         g_up = g_up.swapaxes(1, 2).reshape(w_up.shape)
         g_down = jnp.concatenate([sum_rows[:, (1 + ups + i) * width : (2 + ups + i) * width] for i in range(ups)])
 
-        grads, d_biases, moving = ([], [], []), [], []
-
-        def start_sum(pieces, stages):
-            dk, dv, weight_grad, bias_grad = weight_grads(h_one, pieces)
-            grads[0].extend(piece[0] for piece in pieces)
-            grads[1].append(dk)
-            grads[2].append(dv)
+        grads, d_biases, weight_sums = ([], [], []), [], []
+
+        def sum_parts(dq, dk_parts, dv_parts):
+            dk, dv, weight_grad, bias_grad = weight_grads(h_one, dq, dk_parts, dv_parts)
+            for kind, grad in zip(grads, (dq, dk, dv)):
+                kind.append(grad)
             d_biases.append(bias_grad[:, :3])
-            moving.append([list(stages), weight_grad])
             return weight_grad
 
-        def move_on():
-            for item in moving:
-                if item[0]:
-                    item[1] = item[0].pop(0)(item[1])
-                    if item[0]:
-                        item[1] = item[1].astype(BF16)
-            return [item[1] for item in moving]
-
-        first_pairs = (sum_core, sum_pairs, sum_side, sum_far)
-        last_pairs = (sum_core, sum_side, sum_far, sum_pairs)
-        counts = (4, 4, 2, 2, 2, 2)
-        joined = (1, 1, 2, 2)
-        steps = len(counts)
-        waiting, ready, first, next_sum = [], d_heads, 0, 0
+        counts = (tall, tall // 2, tall // 2)
+        first, ready, arrived = 0, d_heads, []
         for step, each in enumerate(counts):
             part, within = first // tall, first % tall
             dq, dk_parts, dv_parts = attend_back(
@@ -842,32 +824,34 @@
                 each,
             )
             first += each
-            done = move_on()
-            if len(waiting) >= joined[next_sum]:
-                done.append(start_sum(waiting[: joined[next_sum]], first_pairs))
-                waiting = waiting[joined[next_sum] :]
-                next_sum += 1
             dk_parts = [dk_parts[0]] + [lax.ppermute(dk_parts[by], "fsdp", ring(-by)) for by in range(1, group)]
             dv_parts = [dv_parts[0]] + [lax.ppermute(dv_parts[by], "fsdp", ring(-by)) for by in range(1, group)]
-            waiting.append((dq, dk_parts, dv_parts))
-            if step == steps - 2:
-                done += [g_out, g_up, g_down]
-            if done and step + 1 < steps:
-                ready = after(d_heads, dq, *done)
-        last = start_sum(waiting, last_pairs)
+            arrived.append((dq, dk_parts, dv_parts))
+            if step == 1:
+                arrived[0][1][0] = after(arrived[0][1][0], dq)
+                weight_sums.append(sum_parts(*arrived[0]))
+                ready = after(d_heads, dq, weight_sums[0])
+        early_sum = lax.psum_scatter(weight_sums[0], AXES, scatter_dimension=0, tiled=True).astype(F32)
+        weight_sums.append(sum_parts(*arrived[1]))
+        halves = [sum_core(weight_sums[1])]
+        arrived[2][1][0] = after(arrived[2][1][0], weight_sums[1])
+        weight_sums.append(sum_parts(*arrived[2]))
+        halves.append(sum_core(weight_sums[2]))
         if split:
-            rest = after(d_residual, last)
+            rest = after(d_residual, weight_sums[2])
             away_frames, sums_away = input_grads(at_slot, 0, inputs[1], 1, rest, vectors, packed, grads)
-            rest, away_frames = lax.optimization_barrier((d_residual, away_frames, *move_on()))[:2]
+            core_sums = jnp.concatenate(halves, axis=-1).astype(BF16)
+            rest, away_frames, core_sums = lax.optimization_barrier((d_residual, away_frames, core_sums))
             own_frames, sums_own = input_grads(at_slot, slots, inputs[0], 0, rest, vectors, packed, grads)
             sums_one = sums_own + sums_away
         else:
+            core_sums = jnp.concatenate(halves, axis=-1).astype(BF16)
             both, sums_one = input_grads(at_slot, 0, inputs[0], 0, d_residual, vectors, packed, grads)
             own_frames, away_frames = placed_own(both[:local]), both[local:]
-        grad_frames, arrived = swap_out(own_frames, away_frames)
-        for _ in first_pairs:
-            move_on()
-        sums = [item[1] for item in moving]
+        grad_frames, frames_arrived = swap_out(own_frames, away_frames)
+        side_sums = sum_side(core_sums).astype(BF16)
+        late_sum = sum_pairs(sum_far(side_sums).astype(BF16))
+        sums = [early_sum, late_sum]
 
         vector = jnp.concatenate(
             [sums_one[:2], sums_two[: 6 + ups], jnp.concatenate(d_biases).T]
@@ -878,7 +862,8 @@
             total = total + lax.ppermute(vector, "fsdp", ring(by))
         packs = gather_dp(total).reshape(n_dp, -1, width)
         pack = jnp.concatenate([packs[:, :for_slot].reshape(-1, width), jnp.sum(packs[:, for_slot:], axis=0)])
-        across = shift(after(pack, arrived), "fsdp", n_fsdp, group)
+        pack, g_out, g_up, g_down, _ = lax.optimization_barrier((pack, g_out, g_up, g_down, frames_arrived))
+        across = shift(pack, "fsdp", n_fsdp, group)
         count = n_dp * for_slot
         d_mod = jnp.stack([jnp.where(slot == s, pack[:count], across[:count]).reshape(n_dp, -1) for s in range(slots)], axis=1)
         d_mod = d_mod.reshape(n_dp * slots, for_slot * width)
@@ -897,8 +882,8 @@
             size = vector.shape[0] // (n_dp * n_fsdp)
             return lax.dynamic_slice_in_dim(vector, me * size, size)
 
-        columns = [values.reshape(shard, 3, -1) for values in sums]
-        g_qkv = [jnp.concatenate([values[:, i] for values in columns], axis=1) for i in range(3)]
+        columns = jnp.concatenate(sums, axis=1).reshape(shard, -1, 3, pick_block(tall // 2 * HDIM, 128))
+        g_qkv = [columns[:, :, i].reshape(shard, width) for i in range(3)]
         return (
             mixed,
             grad_frames,

time: 706 us -> 757 us (1.072)
  waiting for transfers between devices: 94.6 us -> 195 us
  starting transfers between devices: 57.8 us -> 33.2 us
  Pallas kernels: 458 us -> 443 us
    reduce_scatter x1, waiting for transfers between devices: 0.01 us -> 84.7 us  [body(): lax.psum_scatter(g_rows, AXES, scatter_dimension=0, tiled=True).astype(F32)]
    ppermute x31 -> x19, waiting for transfers between devices: 56 us -> 83.5 us  [shift(): lax.ppermute(values, axis, [(i, (i + by) % size) for i in range(size)])]
    ppermute x31 -> x19, starting transfers between devices: 42.1 us -> 24.3 us  [shift(): lax.ppermute(values, axis, [(i, (i + by) % size) for i in range(size)])]
    ppermute x11 -> x6, waiting for transfers between devices: 18.8 us -> 7.22 us  [swap(): return lax.ppermute(values, axis, [(i, i ^ 1) for i in range(size)])]
    pallas_call x6 -> x3, Pallas kernels: 194 us -> 185 us  [attend_back(): pl.pallas_call(functools.partial(attend_back_kernel, parts, chunk), grid=...]
    pallas_call x4 -> x3, Pallas kernels: 33.7 us -> 25.9 us  [weight_grads(): pl.pallas_call(functools.partial(weight_grads_kernel, parts), grid=(tall...]
  transfers between devices with their start and end apart: 63 -> 41, of which waited for: 24 -> 16; matrix products, arithmetic and copies ran while one was open for 9% -> 6% of each run, Pallas kernels for 51% -> 34%
where the time goes in v4:
time: 757 us; the launch traced here: 751 us
  Pallas kernels  443 us (59%)
  waiting for transfers between devices  195 us (26%)
  local copies, waits for them, and re-layouts  42.1 us (6%)
  starting transfers between devices  33.2 us (4%)
  other arithmetic  21.2 us (3%)
  between operations  15.1 us (2%)
    pallas_call x3, Pallas kernels, attend_back(): pl.pallas_call(functools.partial(attend_back_kernel, parts, chunk), grid=...  185 us
    pallas_call x2, Pallas kernels, attend(): pl.pallas_call(functools.partial(attend_kernel, parts, chunk), grid=(head...  103 us
    reduce_scatter x1, waiting for transfers between devices, body(): lax.psum_scatter(g_rows, AXES, scatter_dimension=0, tiled=True).astype(F32)  84.7 us
    ppermute x19, waiting for transfers between devices, shift(): lax.ppermute(values, axis, [(i, (i + by) % size) for i in range(size)])  83.5 us
    pallas_call x1, Pallas kernels, feed_forward(): pl.pallas_call(functools.partial(feed_forward_kernel, len(heads_out), pie...  82.3 us
    pallas_call x3, Pallas kernels, weight_grads(): pl.pallas_call(functools.partial(weight_grads_kernel, parts), grid=(tall...  25.9 us
    ppermute x19, starting transfers between devices, shift(): lax.ppermute(values, axis, [(i, (i + by) % size) for i in range(size)])  24.3 us
    pallas_call x2, Pallas kernels, input_grads(): pl.pallas_call(functools.partial(input_grads_kernel, [len(kind) for kind...  24.2 us
  transfers between devices with their start and end apart: 41, of which 16 were waited for; matrix products, arithmetic and copies ran while one was open for 6% of the time, Pallas kernels for 34%

profile of v4, /device:TPU:0, one launch (start us, length us, event | category | flops | bytes accessed | tf_op | source)
XLA Modules:
  0.0 751.2 jit_solution(17334079121935802684)
XLA Ops:
  7.2 1.6 pad_maximum_fusion.8
  9.0 3.1 collective-permute-start.1
  12.0 2.6 collective-permute-start.2
  14.6 1.3 collective-permute-start.3
  16.0 3.9 dynamic-slice_bitcast_fusion.2
  19.9 1.5 collective-permute-start
  24.7 1.6 collective-permute-start.4
  26.3 2.0 collective-permute-done.4
  30.3 1.0 squeeze.82
  31.3 1.5 collective-permute-start.5
  32.8 2.3 multiply_sine_fusion
  35.7 1.3 fusion.10
  37.0 2.2 squeeze.81
  39.1 2.1 collective-permute-done.5
  41.3 1.4 add.302
  43.2 1.7 collective-permute-start.7
  45.4 1.9 add_compare_fusion
  47.3 3.2 collective-permute-done.6
  50.5 6.7 collective-permute-done.7
  58.1 2.0 dynamic-slice_bitcast_fusion
  60.1 3.5 collective-permute-done.9
  63.7 1.2 compare_select_fusion.1
  64.9 1.1 copy.81
  67.0 1.2 copy.80
  68.2 1.0 pad.9.refs_1_
  71.3 18.2 %all-gather.3.cloned.1.call-done.w_ref = bf16[1024,3072]{1,0:T(8,128)(2,1)} async-done(((bf16[32,3072]{1,0:T(8,128)(2,1)}), bf16[1024,3072]{1,0:T(8,128)(2,1)}) %all-gather.3.cloned.1.call-update) | async-done | bytes 6291472 | tf_op jit(solution)/shard_map/all_gather | solution.py:729
  89.5 13.7 %project_kv.1 = (bf16[1536,1024]{1,0:T(8,128)(2,1)}, bf16[512,1536]{1,0:T(8,128)(2,1)}, bf16[512,1536]{1,0:T(8,128)(2,1)}, bf16[512,1536]{1,0:T(8,128)(2,1)}, bf16[512,1536]{1,0:T(8,128)(2,1)}) custom-call(bf16[768,1024]{1,0:T(8,128)(2,1)} %get-tuple-element.154.x_ref.refs_2_, bf16[768,1024]{1,0:T(8,128)(2,1)} %collective-permute-done.y_ref.refs_3_.x_ref, ...), custom_call_target="tpu_custom_call" | custom-call | flops 12884901888 | bytes 16777216 | tf_op jit(solution)/shard_map/project_kv/pallas_call | solution.py:338
  103.9 1.4 collective-permute-start.15
  105.3 8.8 %project_q.1.refs_0_ = bf16[1024,1536]{1,0:T(8,128)(2,1)} custom-call(bf16[1536,1024]{1,0:T(8,128)(2,1)} %get-tuple-element.85.h_ref, f32[16,1024]{1,0:T(8,128)} %pad.8.vectors_ref.refs_8_, bf16[1024,3072]{1,0:T(8,128)(2,1)} %all-gather.3.cloned.1.call-done.w_ref, f32[32,1536]{1,0:T(8,128)} %slice.112.cos_ref, f32[32,1536]{1,0:T(8,128)} %slice.113.sin_ref), custom_call_target="tpu_custom_call" | custom-call | flops 6442450944 | bytes 8388608 | tf_op jit(solution)/shard_map/project_q/pallas_call | solution.py:352
  114.2 51.6 %attend.3 = (bf16[512,1536]{1,0:T(8,128)(2,1)}, f32[8,1,1536]{2,1,0:T(1,128)}) custom-call(bf16[1024,1536]{1,0:T(8,128)(2,1)} %project_q.1.refs_0_, bf16[3072,64]{1,0:T(8,128)(2,1)} %pad.9.refs_1_, bf16[512,1536]{1,0:T(8,128)(2,1)} %get-tuple-element.90.refs_2_.refs_7_, bf16[512,1536]{1,0:T(8,128)(2,1)} %collective-permute-done.13.refs_3_.refs_8_, ...), custom_call_target="tpu_custom_call" | custom-call | flops 38654705664 | bytes 9437184 | tf_op jit(solution)/shard_map/attend/pallas_call | solution.py:91
  165.8 51.4 %attend.2 = (bf16[512,1536]{1,0:T(8,128)(2,1)}, f32[8,1,1536]{2,1,0:T(1,128)}) custom-call(bf16[1024,1536]{1,0:T(8,128)(2,1)} %project_q.1.refs_0_, bf16[3072,64]{1,0:T(8,128)(2,1)} %pad.9.refs_1_, bf16[512,1536]{1,0:T(8,128)(2,1)} %get-tuple-element.87.refs_2_.refs_7_, bf16[512,1536]{1,0:T(8,128)(2,1)} %collective-permute-done.11.refs_3_.refs_8_, ...), custom_call_target="tpu_custom_call" | custom-call | flops 38654705664 | bytes 9437184 | tf_op jit(solution)/shard_map/attend/pallas_call | solution.py:91
  217.3 82.3 %feed_forward.1 = (bf16[2,768,1024]{2,1,0:T(8,128)(2,1)}, bf16[768,1024]{1,0:T(8,128)(2,1)}, f32[1536,1024]{1,0:T(8,128)}, bf16[1024,1536]{1,0:T(8,128)(2,1)}, b...) custom-call(s32[1]{0:T(128)} %bitcast.slot_ref, bf16[512,1536]{1,0:T(8,128)(2,1)} %get-tuple-element.89.refs_0_.refs_2_, ...), custom_call_target="tpu_custom_call" | custom-call | flops 48318382080 | bytes 33554432 | tf_op jit(solution)/shard_map/feed_forward/pallas_call | solution.py:466
  299.6 90.6 %attend_back.4 = (bf16[512,1536]{1,0:T(8,128)(2,1)}, f32[512,1536]{1,0:T(8,128)}, bf16[512,1536]{1,0:T(8,128)(2,1)}, f32[512,1536]{1,0:T(8,128)}, bf16[512,1536]{1,0:T(8,128)(2,1)}) custom-call(bf16[1024,1536]{1,0:T(8,128)(2,1)} %project_q.1.refs_0_, bf16[1024,1536]{1,0:T(8,128)(2,1)} %get-tuple-element.112.refs_1_, ...), custom_call_target="tpu_custom_call" | custom-call | flops 96636764160 | bytes 25165824 | tf_op jit(solution)/shard_map/attend_back/pallas_call | solution.py:223
  390.8 46.9 %attend_back.3 = (bf16[256,1536]{1,0:T(8,128)(2,1)}, f32[256,1536]{1,0:T(8,128)}, bf16[256,1536]{1,0:T(8,128)(2,1)}, f32[256,1536]{1,0:T(8,128)}, bf16[256,1536]{1,0:T(8,128)(2,1)}) custom-call(bf16[1024,1536]{1,0:T(8,128)(2,1)} %project_q.1.refs_0_, bf16[1024,1536]{1,0:T(8,128)(2,1)} %get-tuple-element.112.refs_1_, ...), custom_call_target="tpu_custom_call" | custom-call | flops 48318382080 | bytes 12582912 | tf_op jit(solution)/shard_map/attend_back/pallas_call | solution.py:223
  437.8 1.2 copy-done.4
  439.0 11.0 %weight_grads.3 = (bf16[512,1536]{1,0:T(8,128)(2,1)}, bf16[512,1536]{1,0:T(8,128)(2,1)}, bf16[1024,1536]{1,0:T(8,128)(2,1)}, f32[512,128]{1,0:T(8,128)}) custom-call(bf16[1536,1024]{1,0:T(8,128)(2,1)} %get-tuple-element.85.h_ref, bf16[512,1536]{1,0:T(8,128)(2,1)} %get-tuple-element.105.dq_ref.refs_0_, f32[512,1536]{1,0:T(8,128)} %get-tuple-element.107.refs_0_, ...), custom_call_target="tpu_custom_call" | custom-call | tf_op jit(solution)/shard_map/weight_grads/pallas_call | solution.py:536
  451.2 47.0 %attend_back.5 = (bf16[256,1536]{1,0:T(8,128)(2,1)}, f32[256,1536]{1,0:T(8,128)}, bf16[256,1536]{1,0:T(8,128)(2,1)}, f32[256,1536]{1,0:T(8,128)}, bf16[256,1536]{1,0:T(8,128)(2,1)}) custom-call(bf16[1024,1536]{1,0:T(8,128)(2,1)} %project_q.1.refs_0_, bf16[1024,1536]{1,0:T(8,128)(2,1)} %get-tuple-element.112.refs_1_, ...), custom_call_target="tpu_custom_call" | custom-call | flops 48318382080 | bytes 12582912 | tf_op jit(solution)/shard_map/attend_back/pallas_call | solution.py:223
  499.7 7.6 %weight_grads.4 = (bf16[256,1536]{1,0:T(8,128)(2,1)}, bf16[256,1536]{1,0:T(8,128)(2,1)}, bf16[1024,768]{1,0:T(8,128)(2,1)}, f32[256,128]{1,0:T(8,128)}) custom-call(bf16[1536,1024]{1,0:T(8,128)(2,1)} %get-tuple-element.85.h_ref, bf16[256,1536]{1,0:T(8,128)(2,1)} %get-tuple-element.103.dq_ref.refs_1_, f32[256,1536]{1,0:T(8,128)} %get-tuple-element.115.refs_0_, ...), custom_call_target="tpu_custom_call" | custom-call | tf_op jit(solution)/shard_map/weight_grads/pallas_call | solution.py:536
  507.3 2.1 dynamic-slice_bitcast_fusion.6
  510.7 7.3 weight_grads.5
  518.0 2.3 dynamic-slice_bitcast_fusion.5
  521.0 1.1 fusion.3
  522.4 12.2 %input_grads.2 = (bf16[768,1024]{1,0:T(8,128)(2,1)}, f32[8,1024]{1,0:T(8,128)}) custom-call(s32[1]{0:T(128)} %bitcast.slot_ref, bf16[768,1024]{1,0:T(8,128)(2,1)} %collective-permute-done.y_ref.refs_3_.x_ref, f32[1536,1024]{1,0:T(8,128)} %get-tuple-element.133.d_res_ref, f32[16,1024]{1,0:T(8,128)} %pad.8.vectors_ref.refs_8_, ...), custom_call_target="tpu_custom_call" | custom-call | tf_op jit(solution)/shard_map/input_grads/pallas_call | solution.py:592
  534.6 1.4 fusion.2
  537.1 1.5 collective-permute-start.32
  538.6 12.0 %input_grads.3 = (bf16[2,768,1024]{2,1,0:T(8,128)(2,1)}, f32[8,1024]{1,0:T(8,128)}) custom-call(s32[1]{0:T(128)} %bitcast.slot_ref, bf16[768,1024]{1,0:T(8,128)(2,1)} %get-tuple-element.154.x_ref.refs_2_, f32[1536,1024]{1,0:T(8,128)} %get-tuple-element.133.d_res_ref, f32[16,1024]{1,0:T(8,128)} %pad.8.vectors_ref.refs_8_, ...), custom_call_target="tpu_custom_call" | custom-call | tf_op jit(solution)/shard_map/input_grads/pallas_call | solution.py:592
  551.6 1.1 collective-permute-done.26
  552.7 1.6 collective-permute-start.27
  555.3 2.3 collective-permute-start.29
  558.2 2.7 bitcast_dynamic-update-slice_fusion.1
  563.0 1.3 fusion.1
  564.4 1.8 collective-permute-start.33
  566.2 1.7 collective-permute-start.34
  567.9 1.5 collective-permute-start.35
  569.4 3.1 collective-permute-done.30
  572.7 3.6 collective-permute-done.33
  576.3 7.6 %collective-permute-done.34 = bf16[2,32,1536]{2,1,0:T(8,128)(2,1)S(1)} collective-permute-done((bf16[2,32,1536]{2,1,0:T(8,128)(2,1)S(1)}, bf16[2,32,1536]{2,1,0:T(8,128)(2,1)S(1)}, u32[]{:S(2)}, u32[]{:S(2)}) %collective-permute-start.34) | collective-permute-done | bytes 196640 | tf_op jit(solution)/shard_map/ppermute | solution.py:636
  584.6 52.0 %collective-permute-done.36 = bf16[32,1536]{1,0:T(8,128)(2,1)S(1)} collective-permute-done((bf16[32,1536]{1,0:T(8,128)(2,1)S(1)}, bf16[32,1536]{1,0:T(8,128)(2,1)S(1)}, u32[]{:S(2)}, u32[]{:S(2)}) %collective-permute-start.36) | collective-permute-done | bytes 98336 | tf_op jit(solution)/shard_map/ppermute | solution.py:636
  636.6 2.7 bitcast_dynamic-update-slice_fusion
  640.5 1.0 slice_reduce_fusion.1
  642.2 84.7 %reduce-scatter.3.cloned.1.call-done = bf16[32,5120]{1,0:T(8,128)(2,1)} async-done(((bf16[1024,5120]{1,0:T(8,128)(2,1)}), bf16[32,5120]{1,0:T(8,128)(2,1)}) %reduce-scatter.3.cloned.1.call-update) | async-done | bytes 327696 | tf_op jit(solution)/shard_map/reduce_scatter | solution.py:793
  729.0 2.1 reshape.239
  733.2 5.3 collective-permute-done.31
  740.5 1.5 fusion.21
  (233 shorter events, 34.1 us)
Async XLA Ops:
  7.2 21.6 %copy-start = (bf16[32,6144]{1,0:T(8,128)(2,1)S(1)}, bf16[32,6144]{1,0:T(8,128)(2,1)}, u32[]{:S(2)}) copy-start(bf16[32,6144]{1,0:T(8,128)(2,1)} %param.21) | copy-start | bytes 1179652
  7.2 82.3 %all-gather.3.cloned.1.call-start = ((), (), s32[]{:S(2)}) async-start(), calls=%async_computation.2 | async-start | bytes 6488064 | tf_op jit(solution)/shard_map/all_gather | solution.py:729
  8.9 208.4 %all-gather.5.cloned.1.call-start = ((), (), s32[]{:S(2)}) async-start(), calls=%async_computation.3 | async-start | bytes 10813440 | tf_op jit(solution)/shard_map/all_gather | solution.py:733
  9.0 15.6 %collective-permute-start.1 = (s32[2]{0:T(128)}, s32[2]{0:T(128)S(1)}, u32[]{:S(2)}, u32[]{:S(2)}) collective-permute-start(s32[2]{0:T(128)} %param.20), channel_id=1, source_target_pairs={{0,8},{4,12},{8,16},{12,20},{16,24},{20,28},{24,0},{28,4},{1,9},{5... | collective-permute-start | bytes 32 | tf_op jit(solution)/shard_map/ppermute | solution.py:636
  12.0 12.6 %collective-permute-start.2 = (s32[2]{0:T(128)}, s32[2]{0:T(128)S(1)}, u32[]{:S(2)}, u32[]{:S(2)}) collective-permute-start(s32[2]{0:T(128)} %param.20), channel_id=1, source_target_pairs={{0,16},{4,20},{8,24},{12,28},{16,0},{20,4},{24,8},{28,12},{1,17},{... | collective-permute-start | bytes 32 | tf_op jit(solution)/shard_map/ppermute | solution.py:636
  14.6 10.0 %collective-permute-start.3 = (s32[2]{0:T(128)}, s32[2]{0:T(128)S(1)}, u32[]{:S(2)}, u32[]{:S(2)}) collective-permute-start(s32[2]{0:T(128)} %param.20), channel_id=1, source_target_pairs={{0,24},{4,28},{8,0},{12,4},{16,8},{20,12},{24,16},{28,20},{1,25},{... | collective-permute-start | bytes 32 | tf_op jit(solution)/shard_map/ppermute | solution.py:636
  16.0 5.4 copy-start.18
  19.9 2.6 copy-start.19
  19.9 2.7 copy-start.23
  19.9 51.4 %collective-permute-start = (bf16[768,1024]{1,0:T(8,128)(2,1)}, bf16[768,1024]{1,0:T(8,128)(2,1)}, u32[]{:S(2)}, u32[]{:S(2)}) collective-permute-start(bf16[768,1024]{1,0:T(8,128)(2,1)} %get-tuple-element.153), channel_id=1, source_target_pairs={{0,2},{1,3},{2,0},{3,1},{4,6},{5,7},{6,4},{7,5},{8,10},{9,11},{10,... | collective-permute-start | bytes 4718600 | tf_op jit(solution)/shard_map/ppermute | solution.py:636
  21.8 2.1 copy-start.29
  21.8 2.2 copy-start.30
  21.8 2.3 copy-start.31
  21.8 2.4 copy-start.32
  21.8 2.5 copy-start.33
  21.8 2.6 copy-start.26
  21.9 2.8 copy-start.27
  23.4 615.9 %reduce-scatter.5.cloned.1.call-start = ((), (), s32[]{:S(2)}) async-start(), calls=%async_computation.5 | async-start | bytes 3244032 | tf_op jit(solution)/shard_map/reduce_scatter | solution.py:834
  24.7 3.7 collective-permute-start.4
  29.4 5.7 copy-start.34
  31.3 10.0 %collective-permute-start.5 = (f32[4,2,13312]{2,1,0:T(2,128)}, f32[4,2,13312]{2,1,0:T(2,128)}, u32[]{:S(2)}, u32[]{:S(2)}) collective-permute-start(f32[4,2,13312]{2,1,0:T(2,128)} %squeeze.82), channel_id=1, source_target_pairs={{0,4},{4,0},{8,12},{12,8},{16,20},{20,16},{24,28},{28,24},{1,5},{5... | collective-permute-start | bytes 1277960 | tf_op jit(solution)/shard_map/ppermute | solution.py:698
  35.0 35.6 %copy-start.9 = (f32[32,3072]{1,0:T(8,128)}, f32[32,3072]{1,0:T(8,128)S(1)}, u32[]{:S(2)}) copy-start(f32[32,3072]{1,0:T(8,128)S(1)} %get-tuple-element.84.refs_6_) | copy-start | bytes 1179652
  37.0 21.1 %copy-start.3 = (bf16[2,768,1024]{2,1,0:T(8,128)(2,1)S(1)}, bf16[2,768,1024]{2,1,0:T(8,128)(2,1)}, u32[]{:S(2)}) copy-start(bf16[2,768,1024]{2,1,0:T(8,128)(2,1)} %param.35) | copy-start | bytes 9437188
  42.7 7.9 %collective-permute-start.6 = (f32[2,13312]{1,0:T(2,128)S(1)}, f32[2,13312]{1,0:T(2,128)S(1)}, u32[]{:S(2)}, u32[]{:S(2)}) collective-permute-start(f32[2,13312]{1,0:T(2,128)S(1)} %get-tuple-element.162), channel_id=1, source_target_pairs={{0,24},{4,28},{8,0},{12,4},{16,8},{20,12},{24,16},{28,20},{1,25},{... | collective-permute-start | bytes 319496 | tf_op jit(solution)/shard_map/ppermute | solution.py:636
  43.2 14.0 %collective-permute-start.7 = (f32[2,13312]{1,0:T(2,128)S(1)}, f32[2,13312]{1,0:T(2,128)S(1)}, u32[]{:S(2)}, u32[]{:S(2)}) collective-permute-start(f32[2,13312]{1,0:T(2,128)S(1)} %get-tuple-element.164), channel_id=1, source_target_pairs={{0,16},{4,20},{8,24},{12,28},{16,0},{20,4},{24,8},{28,12},{1,17},{... | collective-permute-start | bytes 319496 | tf_op jit(solution)/shard_map/ppermute | solution.py:636
  44.9 12.4 %collective-permute-start.8 = (f32[2,13312]{1,0:T(2,128)S(1)}, f32[2,13312]{1,0:T(2,128)S(1)}, u32[]{:S(2)}, u32[]{:S(2)}) collective-permute-start(f32[2,13312]{1,0:T(2,128)S(1)} %get-tuple-element.163), channel_id=1, source_target_pairs={{0,8},{4,12},{8,16},{12,20},{16,24},{20,28},{24,0},{28,4},{1,9},{5... | collective-permute-start | bytes 319496 | tf_op jit(solution)/shard_map/ppermute | solution.py:636
  57.4 6.1 collective-permute-start.9
  63.6 5.7 collective-permute-start.10
  67.0 2.9 copy-start.10
  89.5 14.5 %copy-start.7 = (bf16[768,1024]{1,0:T(8,128)(2,1)S(1)}, bf16[768,1024]{1,0:T(8,128)(2,1)}, u32[]{:S(2)}) copy-start(bf16[768,1024]{1,0:T(8,128)(2,1)} %get-tuple-element.95) | copy-start | bytes 4718596
  103.1 11.1 %collective-permute-start.13 = (bf16[512,1536]{1,0:T(8,128)(2,1)}, bf16[512,1536]{1,0:T(8,128)(2,1)}, u32[]{:S(2)}, u32[]{:S(2)}) collective-permute-start(bf16[512,1536]{1,0:T(8,128)(2,1)} %get-tuple-element.90.refs_2_.refs_7_), channel_id=1, source_target_pairs={{0,1},{1,0},{2,3},{3,2},{4,5},{5,4},{6,7},{7,6},{8,9},{9,8},{10,11... | collective-permute-start | bytes 4718600 | tf_op jit(solution)/shard_map/ppermute | solution.py:778
  103.4 10.8 %collective-permute-start.14 = (bf16[512,1536]{1,0:T(8,128)(2,1)}, bf16[512,1536]{1,0:T(8,128)(2,1)}, u32[]{:S(2)}, u32[]{:S(2)}) collective-permute-start(bf16[512,1536]{1,0:T(8,128)(2,1)} %get-tuple-element.91.refs_4_.refs_9_), channel_id=1, source_target_pairs={{0,1},{1,0},{2,3},{3,2},{4,5},{5,4},{6,7},{7,6},{8,9},{9,8},{10,11... | collective-permute-start | bytes 4718600 | tf_op jit(solution)/shard_map/ppermute | solution.py:778
  103.6 62.1 %collective-permute-start.11 = (bf16[512,1536]{1,0:T(8,128)(2,1)}, bf16[512,1536]{1,0:T(8,128)(2,1)}, u32[]{:S(2)}, u32[]{:S(2)}) collective-permute-start(bf16[512,1536]{1,0:T(8,128)(2,1)} %get-tuple-element.87.refs_2_.refs_7_), channel_id=1, source_target_pairs={{0,1},{1,0},{2,3},{3,2},{4,5},{5,4},{6,7},{7,6},{8,9},{9,8},{10,11... | collective-permute-start | bytes 4718600 | tf_op jit(solution)/shard_map/ppermute | solution.py:778
  103.9 113.3 %collective-permute-start.15 = (bf16[768,1024]{1,0:T(8,128)(2,1)S(1)}, bf16[768,1024]{1,0:T(8,128)(2,1)}, u32[]{:S(2)}, u32[]{:S(2)}) collective-permute-start(bf16[768,1024]{1,0:T(8,128)(2,1)S(1)} %copy-done.7), channel_id=1, source_target_pairs={{0,2},{1,3},{2,0},{3,1},{4,6},{5,7},{6,4},{7,5},{8,10},{9,11},{10,... | collective-permute-start | bytes 4718600 | tf_op jit(solution)/shard_map/ppermute | solution.py:636
  105.3 60.5 %collective-permute-start.12 = (bf16[512,1536]{1,0:T(8,128)(2,1)}, bf16[512,1536]{1,0:T(8,128)(2,1)}, u32[]{:S(2)}, u32[]{:S(2)}) collective-permute-start(bf16[512,1536]{1,0:T(8,128)(2,1)} %get-tuple-element.88.refs_4_.refs_9_), channel_id=1, source_target_pairs={{0,1},{1,0},{2,3},{3,2},{4,5},{5,4},{6,7},{7,6},{8,9},{9,8},{10,11... | collective-permute-start | bytes 4718600 | tf_op jit(solution)/shard_map/ppermute | solution.py:778
  390.2 47.6 %collective-permute-start.17 = (bf16[512,1536]{1,0:T(8,128)(2,1)}, bf16[512,1536]{1,0:T(8,128)(2,1)S(1)}, u32[]{:S(2)}, u32[]{:S(2)}) collective-permute-start(bf16[512,1536]{1,0:T(8,128)(2,1)} %get-tuple-element.108), channel_id=1, source_target_pairs={{0,1},{1,0},{2,3},{3,2},{4,5},{5,4},{6,7},{7,6},{8,9},{9,8},{10,11... | collective-permute-start | bytes 4718600 | tf_op jit(solution)/shard_map/ppermute | solution.py:827
  390.8 47.0 %collective-permute-start.18 = (bf16[512,1536]{1,0:T(8,128)(2,1)}, bf16[512,1536]{1,0:T(8,128)(2,1)}, u32[]{:S(2)}, u32[]{:S(2)}) collective-permute-start(bf16[512,1536]{1,0:T(8,128)(2,1)} %get-tuple-element.110), channel_id=1, source_target_pairs={{0,1},{1,0},{2,3},{3,2},{4,5},{5,4},{6,7},{7,6},{8,9},{9,8},{10,11... | collective-permute-start | bytes 4718600 | tf_op jit(solution)/shard_map/ppermute | solution.py:828
  450.0 276.8 %reduce-scatter.3.cloned.1.call-start = ((), (), s32[]{:S(2)}) async-start(), calls=%async_computation.4 | async-start | bytes 10813440 | tf_op jit(solution)/shard_map/reduce_scatter | solution.py:793
  450.6 48.2 %collective-permute-start.19 = (bf16[256,1536]{1,0:T(8,128)(2,1)}, bf16[256,1536]{1,0:T(8,128)(2,1)S(1)}, u32[]{:S(2)}, u32[]{:S(2)}) collective-permute-start(bf16[256,1536]{1,0:T(8,128)(2,1)} %get-tuple-element.116), channel_id=1, source_target_pairs={{0,1},{1,0},{2,3},{3,2},{4,5},{5,4},{6,7},{7,6},{8,9},{9,8},{10,11... | collective-permute-start | bytes 2359304 | tf_op jit(solution)/shard_map/ppermute | solution.py:827
  451.1 47.7 %collective-permute-start.20 = (bf16[256,1536]{1,0:T(8,128)(2,1)}, bf16[256,1536]{1,0:T(8,128)(2,1)}, u32[]{:S(2)}, u32[]{:S(2)}) collective-permute-start(bf16[256,1536]{1,0:T(8,128)(2,1)} %get-tuple-element.118), channel_id=1, source_target_pairs={{0,1},{1,0},{2,3},{3,2},{4,5},{5,4},{6,7},{7,6},{8,9},{9,8},{10,11... | collective-permute-start | bytes 2359304 | tf_op jit(solution)/shard_map/ppermute | solution.py:828
  498.2 11.6 %collective-permute-start.21 = (bf16[256,1536]{1,0:T(8,128)(2,1)}, bf16[256,1536]{1,0:T(8,128)(2,1)S(1)}, u32[]{:S(2)}, u32[]{:S(2)}) collective-permute-start(bf16[256,1536]{1,0:T(8,128)(2,1)} %get-tuple-element.121), channel_id=1, source_target_pairs={{0,1},{1,0},{2,3},{3,2},{4,5},{5,4},{6,7},{7,6},{8,9},{9,8},{10,11... | collective-permute-start | bytes 2359304 | tf_op jit(solution)/shard_map/ppermute | solution.py:827
  498.7 11.1 %collective-permute-start.22 = (bf16[256,1536]{1,0:T(8,128)(2,1)}, bf16[256,1536]{1,0:T(8,128)(2,1)}, u32[]{:S(2)}, u32[]{:S(2)}) collective-permute-start(bf16[256,1536]{1,0:T(8,128)(2,1)} %get-tuple-element.123), channel_id=1, source_target_pairs={{0,1},{1,0},{2,3},{3,2},{4,5},{5,4},{6,7},{7,6},{8,9},{9,8},{10,11... | collective-permute-start | bytes 2359304 | tf_op jit(solution)/shard_map/ppermute | solution.py:828
  509.4 11.6 %collective-permute-start.23 = (bf16[8,2,32,768]{3,2,1,0:T(8,128)(2,1)}, bf16[8,2,32,768]{3,2,1,0:T(8,128)(2,1)S(1)}, u32[]{:S(2)}, u32[]{:S(2)}) collective-permute-start(bf16[8,2,32,768]{3,2,1,0:T(8,128)(2,1)} %dynamic-slice_bitcast_fusion.6), channel_id=1, source_target_pairs={{0,1},{1,0},{2,3},{3,2},{4,5},{5,4},{6,7},{7,6},{8,9},{9,8},{10,11... | collective-permute-start | bytes 2359304 | tf_op jit(solution)/shard_map/ppermute | solution.py:698
  510.7 10.2 %copy-start.20 = (f32[256,128]{1,0:T(8,128)S(1)}, f32[256,128]{1,0:T(8,128)}, u32[]{:S(2)}) copy-start(f32[256,128]{1,0:T(8,128)} %get-tuple-element.140) | copy-start | bytes 393220
  518.0 3.0 copy-start.5
  520.3 1.9 copy-start.21
  520.3 14.2 %collective-permute-start.24 = (bf16[8,2,32,768]{3,2,1,0:T(8,128)(2,1)}, bf16[8,2,32,768]{3,2,1,0:T(8,128)(2,1)}, u32[]{:S(2)}, u32[]{:S(2)}) collective-permute-start(bf16[8,2,32,768]{3,2,1,0:T(8,128)(2,1)} %dynamic-slice_bitcast_fusion.5), channel_id=1, source_target_pairs={{0,1},{1,0},{2,3},{3,2},{4,5},{5,4},{6,7},{7,6},{8,9},{9,8},{10,11... | collective-permute-start | bytes 2359304 | tf_op jit(solution)/shard_map/ppermute | solution.py:698
  520.4 37.8 %collective-permute-start.16 = (bf16[768,1024]{1,0:T(8,128)(2,1)}, bf16[768,1024]{1,0:T(8,128)(2,1)}, u32[]{:S(2)}, u32[]{:S(2)}) collective-permute-start(bf16[768,1024]{1,0:T(8,128)(2,1)} %get-tuple-element.98), channel_id=1, source_target_pairs={{0,2},{1,3},{2,0},{3,1},{4,6},{5,7},{6,4},{7,5},{8,10},{9,11},{10,... | collective-permute-start | bytes 4718600 | tf_op jit(solution)/shard_map/ppermute | solution.py:636
  522.3 12.2 %copy-start.6 = (bf16[1024,768]{1,0:T(8,128)(2,1)S(1)}, bf16[1024,768]{1,0:T(8,128)(2,1)}, u32[]{:S(2)}) copy-start(bf16[1024,768]{1,0:T(8,128)(2,1)} %get-tuple-element.124) | copy-start | bytes 4718596
  537.1 14.3 %copy-start.22 = (f32[8,1024]{1,0:T(8,128)S(1)}, f32[8,1024]{1,0:T(8,128)}, u32[]{:S(2)}) copy-start(f32[8,1024]{1,0:T(8,128)} %get-tuple-element.138) | copy-start | bytes 98308
  537.1 25.9 %collective-permute-start.32 = (bf16[4,2,32,1536]{3,2,1,0:T(8,128)(2,1)}, bf16[4,2,32,1536]{3,2,1,0:T(8,128)(2,1)}, u32[]{:S(2)}, u32[]{:S(2)}) collective-permute-start(bf16[4,2,32,1536]{3,2,1,0:T(8,128)(2,1)} %dynamic-slice_bitcast_fusion.4), channel_id=1, source_target_pairs={{0,4},{4,0},{8,12},{12,8},{16,20},{20,16},{24,28},{28,24},{1,5},{5... | collective-permute-start | bytes 2359304 | tf_op jit(solution)/shard_map/ppermute | solution.py:698
  551.4 1.3 collective-permute-start.26
  552.7 8.7 %collective-permute-start.27 = (f32[13,1024]{1,0:T(8,128)S(1)}, f32[13,1024]{1,0:T(8,128)S(1)}, u32[]{:S(2)}, u32[]{:S(2)}) collective-permute-start(f32[13,1024]{1,0:T(8,128)S(1)} %fusion.20), channel_id=1, source_target_pairs={{0,8},{4,12},{8,16},{12,20},{16,24},{20,28},{24,0},{28,4},{1,9},{5... | collective-permute-start | bytes 159752 | tf_op jit(solution)/shard_map/ppermute | solution.py:636
  554.3 7.7 %collective-permute-start.28 = (f32[13,1024]{1,0:T(8,128)S(1)}, f32[13,1024]{1,0:T(8,128)S(1)}, u32[]{:S(2)}, u32[]{:S(2)}) collective-permute-start(f32[13,1024]{1,0:T(8,128)S(1)} %fusion.20), channel_id=1, source_target_pairs={{0,16},{4,20},{8,24},{12,28},{16,0},{20,4},{24,8},{28,12},{1,17},{... | collective-permute-start | bytes 159752 | tf_op jit(solution)/shard_map/ppermute | solution.py:636
  555.3 6.8 collective-permute-start.29
  560.8 75.7 %collective-permute-start.25 = (bf16[768,1024]{1,0:T(8,128)(2,1)}, bf16[768,1024]{1,0:T(8,128)(2,1)}, u32[]{:S(2)}, u32[]{:S(2)}) collective-permute-start(bf16[768,1024]{1,0:T(8,128)(2,1)} %get-tuple-element.135), channel_id=1, source_target_pairs={{0,2},{1,3},{2,0},{3,1},{4,6},{5,7},{6,4},{7,5},{8,10},{9,11},{10,... | collective-permute-start | bytes 4718600 | tf_op jit(solution)/shard_map/ppermute | solution.py:636
  562.1 10.4 %collective-permute-start.30 = (f32[4,13,1024]{2,1,0:T(8,128)S(1)}, f32[4,13,1024]{2,1,0:T(8,128)S(1)}, u32[]{:S(2)}, u32[]{:S(2)}) collective-permute-start(f32[4,13,1024]{2,1,0:T(8,128)S(1)} %get-tuple-element.169), channel_id=1, source_target_pairs={{0,4},{4,0},{8,12},{12,8},{16,20},{20,16},{24,28},{28,24},{1,5},{5... | collective-permute-start | bytes 638984 | tf_op jit(solution)/shard_map/ppermute | solution.py:698
  564.4 11.9 %collective-permute-start.33 = (bf16[2,32,1536]{2,1,0:T(8,128)(2,1)S(1)}, bf16[2,32,1536]{2,1,0:T(8,128)(2,1)S(1)}, u32[]{:S(2)}, u32[]{:S(2)}) collective-permute-start(bf16[2,32,1536]{2,1,0:T(8,128)(2,1)S(1)} %get-tuple-element.157), channel_id=1, source_target_pairs={{0,8},{4,12},{8,16},{12,20},{16,24},{20,28},{24,0},{28,4},{1,9},{5... | collective-permute-start | bytes 589832 | tf_op jit(solution)/shard_map/ppermute | solution.py:636
  566.2 17.7 %collective-permute-start.34 = (bf16[2,32,1536]{2,1,0:T(8,128)(2,1)S(1)}, bf16[2,32,1536]{2,1,0:T(8,128)(2,1)S(1)}, u32[]{:S(2)}, u32[]{:S(2)}) collective-permute-start(bf16[2,32,1536]{2,1,0:T(8,128)(2,1)S(1)} %get-tuple-element.159), channel_id=1, source_target_pairs={{0,16},{4,20},{8,24},{12,28},{16,0},{20,4},{24,8},{28,12},{1,17},{... | collective-permute-start | bytes 589832 | tf_op jit(solution)/shard_map/ppermute | solution.py:636
  567.9 16.4 %collective-permute-start.35 = (bf16[2,32,1536]{2,1,0:T(8,128)(2,1)S(1)}, bf16[2,32,1536]{2,1,0:T(8,128)(2,1)S(1)}, u32[]{:S(2)}, u32[]{:S(2)}) collective-permute-start(bf16[2,32,1536]{2,1,0:T(8,128)(2,1)S(1)} %get-tuple-element.158), channel_id=1, source_target_pairs={{0,24},{4,28},{8,0},{12,4},{16,8},{20,12},{24,16},{28,20},{1,25},{... | collective-permute-start | bytes 589832 | tf_op jit(solution)/shard_map/ppermute | solution.py:636
  584.5 52.1 %collective-permute-start.36 = (bf16[32,1536]{1,0:T(8,128)(2,1)S(1)}, bf16[32,1536]{1,0:T(8,128)(2,1)S(1)}, u32[]{:S(2)}, u32[]{:S(2)}) collective-permute-start(bf16[32,1536]{1,0:T(8,128)(2,1)S(1)} %dynamic-slice_bitcast_fusion.10), channel_id=1, source_target_pairs={{0,2},{1,3},{2,0},{3,1},{4,6},{5,7},{6,4},{7,5},{8,10},{9,11},{10,... | collective-permute-start | bytes 294920 | tf_op jit(solution)/shard_map/ppermute | solution.py:636
  728.1 2.9 copy-start.8
  732.4 6.0 collective-permute-start.31
  739.6 4.9 copy-start.1
  (12 other events, 15.8 us)
Sparse Core Ops, SparseCore 0:
  11.5 77.9 all-gather.2
  92.3 94.9 all-gather.4
  450.2 100.1 reduce-scatter.4
  552.5 174.3 reduce-scatter.2

commit v5 on v4

--- a/solution.py
+++ b/solution.py
@@ -246,8 +246,8 @@
         ],
         compiler_params=pltpu.CompilerParams(vmem_limit_bytes=VMEM_LIMIT),
         cost_estimate=pl.CostEstimate(
-            flops=40 * count * rows * span * HDIM,
-            bytes_accessed=2 * count * HDIM * (8 * rows + 4 * span),
+            flops=5 * count * rows * span * HDIM,
+            bytes_accessed=0,
             transcendentals=0,
         ),
         name="attend_back",
@@ -605,7 +605,9 @@
         ),
         out_shape=[jax.ShapeDtypeStruct(out_shape, BF16), jax.ShapeDtypeStruct((8, width), F32)],
         compiler_params=pltpu.CompilerParams(vmem_limit_bytes=VMEM_LIMIT),
-        cost_estimate=pl.CostEstimate(flops=0, bytes_accessed=0, transcendentals=0),
+        cost_estimate=pl.CostEstimate(
+            flops=16 * rows * width * width, bytes_accessed=14 * rows * width + 6 * width * width, transcendentals=0
+        ),
         name="input_grads",
     )(slot, inputs, d_residual, vectors, packed, *flat)
 
@@ -680,9 +682,13 @@
             parts = own, shift(away, "fsdp", n_fsdp, group)
             return parts if split else (jnp.concatenate(parts),) * 2
 
-        def swap_out(whole, away):
-            arrived = shift(away, "fsdp", n_fsdp, group)
-            return lax.dynamic_update_index_in_dim(whole, arrived, other, 0), arrived
+        def swap_out(whole, away, pieces=1):
+            arrived = []
+            for first in range(0, local, local // pieces):
+                piece = shift(away[first : first + local // pieces], "fsdp", n_fsdp, group)
+                arrived.append(piece)
+                whole = lax.dynamic_update_slice(whole, piece[None], (other, first, 0))
+            return whole, arrived
 
         def placed_own(own):
             return lax.dynamic_update_index_in_dim(jnp.zeros((slots, local, width), own.dtype), own, slot, 0)
@@ -798,15 +804,16 @@
 
         grads, d_biases, weight_sums = ([], [], []), [], []
 
-        def sum_parts(dq, dk_parts, dv_parts):
-            dk, dv, weight_grad, bias_grad = weight_grads(h_one, dq, dk_parts, dv_parts)
-            for kind, grad in zip(grads, (dq, dk, dv)):
-                kind.append(grad)
-            d_biases.append(bias_grad[:, :3])
-            return weight_grad
-
-        counts = (tall, tall // 2, tall // 2)
-        first, ready, arrived = 0, d_heads, []
+        def sum_parts(pieces):
+            sums = [weight_grads(h_one, *piece) for piece in pieces]
+            for piece, (dk, dv, _, bias_grad) in zip(pieces, sums):
+                for kind, grad in zip(grads, (piece[0], dk, dv)):
+                    kind.append(grad)
+                d_biases.append(bias_grad[:, :3])
+            return jnp.concatenate([values[2] for values in sums], axis=1)
+
+        counts = (tall, tall // 4, tall // 4, tall // 2)
+        first, ready, arrived, moving = 0, d_heads, [], None
         for step, each in enumerate(counts):
             part, within = first // tall, first % tall
             dq, dk_parts, dv_parts = attend_back(
@@ -829,14 +836,20 @@
             arrived.append((dq, dk_parts, dv_parts))
             if step == 1:
                 arrived[0][1][0] = after(arrived[0][1][0], dq)
-                weight_sums.append(sum_parts(*arrived[0]))
+                weight_sums.append(sum_parts([arrived[0]]))
+                moving = sum_core(weight_sums[0]).astype(BF16)
                 ready = after(d_heads, dq, weight_sums[0])
-        early_sum = lax.psum_scatter(weight_sums[0], AXES, scatter_dimension=0, tiled=True).astype(F32)
-        weight_sums.append(sum_parts(*arrived[1]))
+            if step == 2:
+                moving = after(moving, dq)
+                ready = after(d_heads, dq, moving)
+        early_pairs = sum_pairs(moving).astype(BF16)
+        arrived[2][1][0] = after(arrived[2][1][0], dq)
+        weight_sums.append(sum_parts(arrived[1:3]))
         halves = [sum_core(weight_sums[1])]
-        arrived[2][1][0] = after(arrived[2][1][0], weight_sums[1])
-        weight_sums.append(sum_parts(*arrived[2]))
+        arrived[3][1][0] = after(arrived[3][1][0], weight_sums[1], sum_rows)
+        weight_sums.append(sum_parts(arrived[3:]))
         halves.append(sum_core(weight_sums[2]))
+        early_sum = sum_far(sum_side(early_pairs).astype(BF16))
         if split:
             rest = after(d_residual, weight_sums[2])
             away_frames, sums_away = input_grads(at_slot, 0, inputs[1], 1, rest, vectors, packed, grads)
@@ -848,7 +861,7 @@
             core_sums = jnp.concatenate(halves, axis=-1).astype(BF16)
             both, sums_one = input_grads(at_slot, 0, inputs[0], 0, d_residual, vectors, packed, grads)
             own_frames, away_frames = placed_own(both[:local]), both[local:]
-        grad_frames, frames_arrived = swap_out(own_frames, away_frames)
+        grad_frames, frames_arrived = swap_out(own_frames, away_frames, 3)
         side_sums = sum_side(core_sums).astype(BF16)
         late_sum = sum_pairs(sum_far(side_sums).astype(BF16))
         sums = [early_sum, late_sum]
@@ -857,12 +870,13 @@
             [sums_one[:2], sums_two[: 6 + ups], jnp.concatenate(d_biases).T]
         )
         for_slot = 6
+        vector = after(vector, *frames_arrived[:2])
         total = vector
         for by in range(1, group):
             total = total + lax.ppermute(vector, "fsdp", ring(by))
         packs = gather_dp(total).reshape(n_dp, -1, width)
         pack = jnp.concatenate([packs[:, :for_slot].reshape(-1, width), jnp.sum(packs[:, for_slot:], axis=0)])
-        pack, g_out, g_up, g_down, _ = lax.optimization_barrier((pack, g_out, g_up, g_down, frames_arrived))
+        pack, g_out, g_up, g_down, _ = lax.optimization_barrier((pack, g_out, g_up, g_down, frames_arrived[2]))
         across = shift(pack, "fsdp", n_fsdp, group)
         count = n_dp * for_slot
         d_mod = jnp.stack([jnp.where(slot == s, pack[:count], across[:count]).reshape(n_dp, -1) for s in range(slots)], axis=1)

time: 757 us -> 668 us (0.88)
  waiting for transfers between devices: 195 us -> 73 us
  starting transfers between devices: 33.2 us -> 45.5 us
  local copies, waits for them, and re-layouts: 42.1 us -> 53.7 us
    reduce_scatter x1, waiting for transfers between devices: 84.7 us -> 0.01 us  [body(): lax.psum_scatter(g_rows, AXES, scatter_dimension=0, tiled=True).astype(F32)]
    ppermute x19 -> x25, waiting for transfers between devices: 83.5 us -> 37.4 us  [shift(): lax.ppermute(values, axis, [(i, (i + by) % size) for i in range(size)])]
    ppermute x19 -> x25, starting transfers between devices: 24.3 us -> 34.8 us  [shift(): lax.ppermute(values, axis, [(i, (i + by) % size) for i in range(size)])]
    pallas_call x3 -> x4, Pallas kernels: 185 us -> 188 us  [attend_back(): pl.pallas_call(functools.partial(attend_back_kernel, parts, chunk), grid=...]
    pallas_call x3 -> x4, Pallas kernels: 25.9 us -> 28.6 us  [weight_grads(): pl.pallas_call(functools.partial(weight_grads_kernel, parts), grid=(tall...]
  transfers between devices with their start and end apart: 41 -> 50, of which waited for: 16 -> 18; matrix products, arithmetic and copies ran while one was open for 6% -> 9% of each run, Pallas kernels for 34% -> 54%
where the time goes in v5:
time: 668 us; the launch traced here: 660 us
  Pallas kernels  447 us (67%)
  waiting for transfers between devices  73 us (11%)
  local copies, waits for them, and re-layouts  53.7 us (8%)
  starting transfers between devices  45.5 us (7%)
  other arithmetic  24.2 us (4%)
  between operations  15.2 us (2%)
    pallas_call x4, Pallas kernels, attend_back(): pl.pallas_call(functools.partial(attend_back_kernel, parts, chunk), grid=...  188 us
    pallas_call x2, Pallas kernels, attend(): pl.pallas_call(functools.partial(attend_kernel, parts, chunk), grid=(head...  103 us
    pallas_call x1, Pallas kernels, feed_forward(): pl.pallas_call(functools.partial(feed_forward_kernel, len(heads_out), pie...  82 us
    ppermute x25, waiting for transfers between devices, shift(): lax.ppermute(values, axis, [(i, (i + by) % size) for i in range(size)])  37.4 us
    ppermute x25, starting transfers between devices, shift(): lax.ppermute(values, axis, [(i, (i + by) % size) for i in range(size)])  34.8 us
    pallas_call x4, Pallas kernels, weight_grads(): pl.pallas_call(functools.partial(weight_grads_kernel, parts), grid=(tall...  28.6 us
    pallas_call x2, Pallas kernels, input_grads(): pl.pallas_call(functools.partial(input_grads_kernel, [len(kind) for kind...  23.1 us
    all_gather x1, waiting for transfers between devices, body(): lax.all_gather(jnp.concatenate([w_key, w_value, w_query], axis=1), AXES,...  20.4 us
  transfers between devices with their start and end apart: 50, of which 18 were waited for; matrix products, arithmetic and copies ran while one was open for 9% of the time, Pallas kernels for 54%

profile of v5, /device:TPU:0, one launch (start us, length us, event | category | flops | bytes accessed | tf_op | source)
XLA Modules:
  0.0 660.4 jit_solution(11453129643403381320)
XLA Ops:
  7.2 1.6 pad_maximum_fusion.8
  9.0 3.1 collective-permute-start.1
  12.0 2.6 collective-permute-start.2
  14.6 1.3 collective-permute-start.3
  16.0 3.4 dynamic-slice_bitcast_fusion.2
  19.4 1.5 collective-permute-start
  24.1 1.6 collective-permute-start.4
  25.8 2.0 collective-permute-done.4
  29.9 1.5 collective-permute-start.5
  31.5 1.4 multiply_sine_fusion
  34.6 5.4 collective-permute-done.5
  41.7 1.7 collective-permute-start.7
  44.9 4.0 collective-permute-done.6
  49.0 6.1 collective-permute-done.7
  56.3 3.9 dynamic-slice_bitcast_fusion
  60.2 2.6 collective-permute-done.9
  69.0 20.4 %all-gather.3.cloned.1.call-done.w_ref = bf16[1024,3072]{1,0:T(8,128)(2,1)} async-done(((bf16[32,3072]{1,0:T(8,128)(2,1)}), bf16[1024,3072]{1,0:T(8,128)(2,1)}) %all-gather.3.cloned.1.call-update) | async-done | bytes 6291472 | tf_op jit(solution)/shard_map/all_gather | solution.py:735
  89.5 13.6 %project_kv.1 = (bf16[1536,1024]{1,0:T(8,128)(2,1)}, bf16[512,1536]{1,0:T(8,128)(2,1)}, bf16[512,1536]{1,0:T(8,128)(2,1)}, bf16[512,1536]{1,0:T(8,128)(2,1)}, bf16[512,1536]{1,0:T(8,128)(2,1)}) custom-call(bf16[768,1024]{1,0:T(8,128)(2,1)} %get-tuple-element.182.x_ref.refs_2_, bf16[768,1024]{1,0:T(8,128)(2,1)} %collective-permute-done.y_ref.refs_3_.x_ref, ...), custom_call_target="tpu_custom_call" | custom-call | flops 12884901888 | bytes 16777216 | tf_op jit(solution)/shard_map/project_kv/pallas_call | solution.py:338
  103.8 1.4 collective-permute-start.15
  105.2 8.7 %project_q.1.refs_0_ = bf16[1024,1536]{1,0:T(8,128)(2,1)} custom-call(bf16[1536,1024]{1,0:T(8,128)(2,1)} %get-tuple-element.98.h_ref, f32[16,1024]{1,0:T(8,128)} %pad.8.vectors_ref.refs_8_, bf16[1024,3072]{1,0:T(8,128)(2,1)} %all-gather.3.cloned.1.call-done.w_ref, f32[32,1536]{1,0:T(8,128)} %slice.124.cos_ref, f32[32,1536]{1,0:T(8,128)} %slice.125.sin_ref), custom_call_target="tpu_custom_call" | custom-call | flops 6442450944 | bytes 8388608 | tf_op jit(solution)/shard_map/project_q/pallas_call | solution.py:352
  115.1 51.6 %attend.3 = (bf16[512,1536]{1,0:T(8,128)(2,1)}, f32[8,1,1536]{2,1,0:T(1,128)}) custom-call(bf16[1024,1536]{1,0:T(8,128)(2,1)} %project_q.1.refs_0_, bf16[3072,64]{1,0:T(8,128)(2,1)} %pad.9.refs_1_, bf16[512,1536]{1,0:T(8,128)(2,1)} %get-tuple-element.103.refs_2_.refs_7_, bf16[512,1536]{1,0:T(8,128)(2,1)} %copy-done.2, ...), custom_call_target="tpu_custom_call" | custom-call | flops 38654705664 | bytes 9437184 | tf_op jit(solution)/shard_map/attend/pallas_call | solution.py:91
  166.7 51.4 %attend.2 = (bf16[512,1536]{1,0:T(8,128)(2,1)}, f32[8,1,1536]{2,1,0:T(1,128)}) custom-call(bf16[1024,1536]{1,0:T(8,128)(2,1)} %project_q.1.refs_0_, bf16[3072,64]{1,0:T(8,128)(2,1)} %pad.9.refs_1_, bf16[512,1536]{1,0:T(8,128)(2,1)} %get-tuple-element.100.refs_2_.refs_7_, bf16[512,1536]{1,0:T(8,128)(2,1)} %collective-permute-done.11.refs_3_.refs_8_, ...), custom_call_target="tpu_custom_call" | custom-call | flops 38654705664 | bytes 9437184 | tf_op jit(solution)/shard_map/attend/pallas_call | solution.py:91
  218.2 82.0 %feed_forward.1 = (bf16[2,768,1024]{2,1,0:T(8,128)(2,1)}, bf16[768,1024]{1,0:T(8,128)(2,1)}, f32[1536,1024]{1,0:T(8,128)}, bf16[1024,1536]{1,0:T(8,128)(2,1)}, b...) custom-call(s32[1]{0:T(128)} %bitcast.slot_ref, bf16[512,1536]{1,0:T(8,128)(2,1)} %get-tuple-element.102.refs_0_.refs_2_, ...), custom_call_target="tpu_custom_call" | custom-call | flops 48318382080 | bytes 33554432 | tf_op jit(solution)/shard_map/feed_forward/pallas_call | solution.py:466
  300.3 90.6 %attend_back.5 = (bf16[512,1536]{1,0:T(8,128)(2,1)}, f32[512,1536]{1,0:T(8,128)}, bf16[512,1536]{1,0:T(8,128)(2,1)}, f32[512,1536]{1,0:T(8,128)}, bf16[512,1536]{1,0:T(8,128)(2,1)}) custom-call(bf16[1024,1536]{1,0:T(8,128)(2,1)} %project_q.1.refs_0_, bf16[1024,1536]{1,0:T(8,128)(2,1)} %get-tuple-element.128.refs_1_, ...), custom_call_target="tpu_custom_call" | custom-call | flops 12079595520 | tf_op jit(solution)/shard_map/attend_back/pallas_call | solution.py:223
  391.5 25.2 %attend_back.4 = (bf16[128,1536]{1,0:T(8,128)(2,1)}, f32[128,1536]{1,0:T(8,128)}, bf16[128,1536]{1,0:T(8,128)(2,1)}, f32[128,1536]{1,0:T(8,128)}, bf16[128,1536]{1,0:T(8,128)(2,1)}) custom-call(bf16[1024,1536]{1,0:T(8,128)(2,1)} %project_q.1.refs_0_, bf16[1024,1536]{1,0:T(8,128)(2,1)} %get-tuple-element.128.refs_1_, ...), custom_call_target="tpu_custom_call" | custom-call | flops 3019898880 | tf_op jit(solution)/shard_map/attend_back/pallas_call | solution.py:223
  417.8 11.2 %weight_grads.4 = (bf16[512,1536]{1,0:T(8,128)(2,1)}, bf16[512,1536]{1,0:T(8,128)(2,1)}, bf16[1024,1536]{1,0:T(8,128)(2,1)}, f32[512,128]{1,0:T(8,128)}) custom-call(bf16[1536,1024]{1,0:T(8,128)(2,1)} %get-tuple-element.98.h_ref, bf16[512,1536]{1,0:T(8,128)(2,1)} %get-tuple-element.118.dq_ref.refs_0_, f32[512,1536]{1,0:T(8,128)} %get-tuple-element.120.refs_0_, ...), custom_call_target="tpu_custom_call" | custom-call | tf_op jit(solution)/shard_map/weight_grads/pallas_call | solution.py:536
  429.1 3.3 constant_dynamic-slice_fusion.8
  434.6 2.7 collective-permute-done.20.refs_1_
  438.1 5.1 weight_grads.5
  443.1 24.8 %attend_back.6 = (bf16[128,1536]{1,0:T(8,128)(2,1)}, f32[128,1536]{1,0:T(8,128)}, bf16[128,1536]{1,0:T(8,128)(2,1)}, f32[128,1536]{1,0:T(8,128)}, bf16[128,1536]{1,0:T(8,128)(2,1)}) custom-call(bf16[1024,1536]{1,0:T(8,128)(2,1)} %project_q.1.refs_0_, bf16[1024,1536]{1,0:T(8,128)(2,1)} %get-tuple-element.128.refs_1_, ...), custom_call_target="tpu_custom_call" | custom-call | flops 3019898880 | tf_op jit(solution)/shard_map/attend_back/pallas_call | solution.py:223
  468.0 2.3 fusion.1
  473.5 47.4 %attend_back.7 = (bf16[256,1536]{1,0:T(8,128)(2,1)}, f32[256,1536]{1,0:T(8,128)}, bf16[256,1536]{1,0:T(8,128)(2,1)}, f32[256,1536]{1,0:T(8,128)}, bf16[256,1536]{1,0:T(8,128)(2,1)}) custom-call(bf16[1024,1536]{1,0:T(8,128)(2,1)} %project_q.1.refs_0_, bf16[1024,1536]{1,0:T(8,128)(2,1)} %get-tuple-element.128.refs_1_, ...), custom_call_target="tpu_custom_call" | custom-call | flops 6039797760 | tf_op jit(solution)/shard_map/attend_back/pallas_call | solution.py:223
  521.7 5.0 weight_grads.6
  526.7 2.2 constant_dynamic-update-slice_fusion
  528.9 1.5 fusion.3
  530.5 1.5 collective-permute-start.38
  533.0 1.7 bitcast_dynamic-update-slice_fusion
  534.7 1.6 copy-done.33
  537.9 3.9 collective-permute-done.38
  543.0 1.5 collective-permute-start.39
  545.4 2.2 collective-permute-start.41
  547.6 2.2 fusion.5
  550.7 2.6 collective-permute-done.40
  555.0 7.2 %weight_grads.7 = (bf16[256,1536]{1,0:T(8,128)(2,1)}, bf16[256,1536]{1,0:T(8,128)(2,1)}, bf16[1024,768]{1,0:T(8,128)(2,1)}, f32[256,128]{1,0:T(8,128)}) custom-call(bf16[1536,1024]{1,0:T(8,128)(2,1)} %get-tuple-element.98.h_ref, bf16[256,1536]{1,0:T(8,128)(2,1)} %get-tuple-element.129.dq_ref.refs_3_, f32[256,1536]{1,0:T(8,128)} %get-tuple-element.143.refs_0_, ...), custom_call_target="tpu_custom_call" | custom-call | tf_op jit(solution)/shard_map/weight_grads/pallas_call | solution.py:536
  562.2 2.1 dynamic-slice_bitcast_fusion.6
  565.6 2.1 reshape.254
  569.1 11.6 %input_grads.2 = (bf16[768,1024]{1,0:T(8,128)(2,1)}, f32[8,1024]{1,0:T(8,128)}) custom-call(s32[1]{0:T(128)} %bitcast.slot_ref, bf16[768,1024]{1,0:T(8,128)(2,1)} %collective-permute-done.y_ref.refs_3_.x_ref, f32[1536,1024]{1,0:T(8,128)} %get-tuple-element.158.d_res_ref, f32[16,1024]{1,0:T(8,128)} %pad.8.vectors_ref.refs_8_, ...), custom_call_target="tpu_custom_call" | custom-call | flops 12884901888 | bytes 17301504 | tf_op jit(solution)/shard_map/input_grads/pallas_call | solution.py:592
  580.8 1.4 fusion.4
  582.3 1.3 copy-done.12
  589.8 11.5 %input_grads.3 = (bf16[2,768,1024]{2,1,0:T(8,128)(2,1)}, f32[8,1024]{1,0:T(8,128)}) custom-call(s32[1]{0:T(128)} %bitcast.slot_ref, bf16[768,1024]{1,0:T(8,128)(2,1)} %get-tuple-element.182.x_ref.refs_2_, f32[1536,1024]{1,0:T(8,128)} %get-tuple-element.158.d_res_ref, f32[16,1024]{1,0:T(8,128)} %pad.8.vectors_ref.refs_8_, ...), custom_call_target="tpu_custom_call" | custom-call | flops 12884901888 | bytes 17301504 | tf_op jit(solution)/shard_map/input_grads/pallas_call | solution.py:592
  602.1 8.9 %collective-permute-done.29 = bf16[256,1024]{1,0:T(8,128)(2,1)} collective-permute-done((bf16[256,1024]{1,0:T(8,128)(2,1)}, bf16[256,1024]{1,0:T(8,128)(2,1)}, u32[]{:S(2)}, u32[]{:S(2)}) %collective-permute-start.29) | collective-permute-done | bytes 524320 | tf_op jit(solution)/shard_map/ppermute | solution.py:638
  611.1 1.9 bitcast_dynamic-update-slice_fusion.3
  612.9 1.9 bitcast_dynamic-update-slice_fusion.2
  614.8 2.7 collective-permute-start.32
  618.6 1.4 collective-permute-start.34
  620.1 1.8 collective-permute-done.30
  621.9 1.9 bitcast_dynamic-update-slice_fusion.1
  624.4 1.4 collective-permute-start.35
  625.8 1.3 fusion.2
  627.2 1.8 collective-permute-start.43
  629.0 1.4 collective-permute-start.44
  633.8 3.2 collective-permute-done.43
  637.0 6.6 collective-permute-done.44
  646.9 1.5 fusion.25
  (282 shorter events, 58.6 us)
Async XLA Ops:
  7.2 21.1 %copy-start = (bf16[32,6144]{1,0:T(8,128)(2,1)S(1)}, bf16[32,6144]{1,0:T(8,128)(2,1)}, u32[]{:S(2)}) copy-start(bf16[32,6144]{1,0:T(8,128)(2,1)} %param.21) | copy-start | bytes 1179652
  7.2 82.3 %all-gather.3.cloned.1.call-start = ((), (), s32[]{:S(2)}) async-start(), calls=%async_computation.1 | async-start | bytes 6488064 | tf_op jit(solution)/shard_map/all_gather | solution.py:735
  8.9 209.3 %all-gather.5.cloned.1.call-start = ((), (), s32[]{:S(2)}) async-start(), calls=%async_computation.2 | async-start | bytes 10813440 | tf_op jit(solution)/shard_map/all_gather | solution.py:739
  9.0 15.1 %collective-permute-start.1 = (s32[2]{0:T(128)}, s32[2]{0:T(128)S(1)}, u32[]{:S(2)}, u32[]{:S(2)}) collective-permute-start(s32[2]{0:T(128)} %param.20), channel_id=1, source_target_pairs={{0,8},{4,12},{8,16},{12,20},{16,24},{20,28},{24,0},{28,4},{1,9},{5... | collective-permute-start | bytes 32 | tf_op jit(solution)/shard_map/ppermute | solution.py:638
  12.0 12.0 %collective-permute-start.2 = (s32[2]{0:T(128)}, s32[2]{0:T(128)S(1)}, u32[]{:S(2)}, u32[]{:S(2)}) collective-permute-start(s32[2]{0:T(128)} %param.20), channel_id=1, source_target_pairs={{0,16},{4,20},{8,24},{12,28},{16,0},{20,4},{24,8},{28,12},{1,17},{... | collective-permute-start | bytes 32 | tf_op jit(solution)/shard_map/ppermute | solution.py:638
  14.6 9.4 %collective-permute-start.3 = (s32[2]{0:T(128)}, s32[2]{0:T(128)S(1)}, u32[]{:S(2)}, u32[]{:S(2)}) collective-permute-start(s32[2]{0:T(128)} %param.20), channel_id=1, source_target_pairs={{0,24},{4,28},{8,0},{12,4},{16,8},{20,12},{24,16},{28,20},{1,25},{... | collective-permute-start | bytes 32 | tf_op jit(solution)/shard_map/ppermute | solution.py:638
  16.0 4.9 copy-start.24
  19.4 49.7 %collective-permute-start = (bf16[768,1024]{1,0:T(8,128)(2,1)S(1)}, bf16[768,1024]{1,0:T(8,128)(2,1)}, u32[]{:S(2)}, u32[]{:S(2)}) collective-permute-start(bf16[768,1024]{1,0:T(8,128)(2,1)S(1)} %get-tuple-element.181), channel_id=1, source_target_pairs={{0,2},{1,3},{2,0},{3,1},{4,6},{5,7},{6,4},{7,5},{8,10},{9,11},{10,... | collective-permute-start | bytes 4718600 | tf_op jit(solution)/shard_map/ppermute | solution.py:638
  22.8 531.3 %reduce-scatter.2.cloned.1.call-start = ((), (), s32[]{:S(2)}) async-start(), calls=%async_computation.3 | async-start | bytes 10813440 | tf_op jit(solution)/shard_map/reduce_scatter | solution.py:799
  24.1 3.7 collective-permute-start.4
  28.9 4.1 copy-start.42
  29.9 10.0 %collective-permute-start.5 = (f32[4,2,13312]{2,1,0:T(2,128)}, f32[4,2,13312]{2,1,0:T(2,128)}, u32[]{:S(2)}, u32[]{:S(2)}) collective-permute-start(f32[4,2,13312]{2,1,0:T(2,128)} %squeeze.108), channel_id=1, source_target_pairs={{0,4},{4,0},{8,12},{12,8},{16,20},{20,16},{24,28},{28,24},{1,5},{5... | collective-permute-start | bytes 1277960 | tf_op jit(solution)/shard_map/ppermute | solution.py:704
  32.9 34.8 %copy-start.4 = (f32[32,3072]{1,0:T(8,128)}, f32[32,3072]{1,0:T(8,128)S(1)}, u32[]{:S(2)}) copy-start(f32[32,3072]{1,0:T(8,128)S(1)} %get-tuple-element.96.refs_5_) | copy-start | bytes 1179652
  32.9 35.4 %copy-start.3 = (f32[32,3072]{1,0:T(8,128)}, f32[32,3072]{1,0:T(8,128)S(1)}, u32[]{:S(2)}) copy-start(f32[32,3072]{1,0:T(8,128)S(1)} %get-tuple-element.97.refs_6_) | copy-start | bytes 1179652
  41.2 7.8 %collective-permute-start.6 = (f32[2,13312]{1,0:T(2,128)S(1)}, f32[2,13312]{1,0:T(2,128)S(1)}, u32[]{:S(2)}, u32[]{:S(2)}) collective-permute-start(f32[2,13312]{1,0:T(2,128)S(1)} %get-tuple-element.193), channel_id=1, source_target_pairs={{0,24},{4,28},{8,0},{12,4},{16,8},{20,12},{24,16},{28,20},{1,25},{... | collective-permute-start | bytes 319496 | tf_op jit(solution)/shard_map/ppermute | solution.py:638
  41.7 13.4 %collective-permute-start.7 = (f32[2,13312]{1,0:T(2,128)S(1)}, f32[2,13312]{1,0:T(2,128)S(1)}, u32[]{:S(2)}, u32[]{:S(2)}) collective-permute-start(f32[2,13312]{1,0:T(2,128)S(1)} %get-tuple-element.195), channel_id=1, source_target_pairs={{0,16},{4,20},{8,24},{12,28},{16,0},{20,4},{24,8},{28,12},{1,17},{... | collective-permute-start | bytes 319496 | tf_op jit(solution)/shard_map/ppermute | solution.py:638
  43.4 11.7 %collective-permute-start.8 = (f32[2,13312]{1,0:T(2,128)S(1)}, f32[2,13312]{1,0:T(2,128)S(1)}, u32[]{:S(2)}, u32[]{:S(2)}) collective-permute-start(f32[2,13312]{1,0:T(2,128)S(1)} %get-tuple-element.194), channel_id=1, source_target_pairs={{0,8},{4,12},{8,16},{12,20},{16,24},{20,28},{24,0},{28,4},{1,9},{5... | collective-permute-start | bytes 319496 | tf_op jit(solution)/shard_map/ppermute | solution.py:638
  55.3 7.5 %collective-permute-start.9 = (f32[13312]{0:T(1024)S(1)}, f32[13312]{0:T(1024)S(1)}, u32[]{:S(2)}, u32[]{:S(2)}) collective-permute-start(f32[13312]{0:T(1024)S(1)} %bitcast.186), channel_id=1, source_target_pairs={{0,2},{1,3},{2,0},{3,1},{4,6},{5,7},{6,4},{7,5},{8,10},{9,11},{10,... | collective-permute-start | bytes 159752 | tf_op jit(solution)/shard_map/ppermute | solution.py:638
  62.8 4.2 collective-permute-start.10
  103.0 10.9 %collective-permute-start.13 = (bf16[512,1536]{1,0:T(8,128)(2,1)}, bf16[512,1536]{1,0:T(8,128)(2,1)S(1)}, u32[]{:S(2)}, u32[]{:S(2)}) collective-permute-start(bf16[512,1536]{1,0:T(8,128)(2,1)} %get-tuple-element.103.refs_2_.refs_7_), channel_id=1, source_target_pairs={{0,1},{1,0},{2,3},{3,2},{4,5},{5,4},{6,7},{7,6},{8,9},{9,8},{10,11... | collective-permute-start | bytes 4718600 | tf_op jit(solution)/shard_map/ppermute | solution.py:784
  103.3 10.7 %collective-permute-start.14 = (bf16[512,1536]{1,0:T(8,128)(2,1)}, bf16[512,1536]{1,0:T(8,128)(2,1)}, u32[]{:S(2)}, u32[]{:S(2)}) collective-permute-start(bf16[512,1536]{1,0:T(8,128)(2,1)} %get-tuple-element.104.refs_4_.refs_9_), channel_id=1, source_target_pairs={{0,1},{1,0},{2,3},{3,2},{4,5},{5,4},{6,7},{7,6},{8,9},{9,8},{10,11... | collective-permute-start | bytes 4718600 | tf_op jit(solution)/shard_map/ppermute | solution.py:784
  103.5 63.2 %collective-permute-start.11 = (bf16[512,1536]{1,0:T(8,128)(2,1)}, bf16[512,1536]{1,0:T(8,128)(2,1)}, u32[]{:S(2)}, u32[]{:S(2)}) collective-permute-start(bf16[512,1536]{1,0:T(8,128)(2,1)} %get-tuple-element.100.refs_2_.refs_7_), channel_id=1, source_target_pairs={{0,1},{1,0},{2,3},{3,2},{4,5},{5,4},{6,7},{7,6},{8,9},{9,8},{10,11... | collective-permute-start | bytes 4718600 | tf_op jit(solution)/shard_map/ppermute | solution.py:784
  103.8 114.4 %collective-permute-start.15 = (bf16[768,1024]{1,0:T(8,128)(2,1)}, bf16[768,1024]{1,0:T(8,128)(2,1)}, u32[]{:S(2)}, u32[]{:S(2)}) collective-permute-start(bf16[768,1024]{1,0:T(8,128)(2,1)} %get-tuple-element.108), channel_id=1, source_target_pairs={{0,2},{1,3},{2,0},{3,1},{4,6},{5,7},{6,4},{7,5},{8,10},{9,11},{10,... | collective-permute-start | bytes 4718600 | tf_op jit(solution)/shard_map/ppermute | solution.py:638
  105.2 61.5 %collective-permute-start.12 = (bf16[512,1536]{1,0:T(8,128)(2,1)}, bf16[512,1536]{1,0:T(8,128)(2,1)}, u32[]{:S(2)}, u32[]{:S(2)}) collective-permute-start(bf16[512,1536]{1,0:T(8,128)(2,1)} %get-tuple-element.101.refs_4_.refs_9_), channel_id=1, source_target_pairs={{0,1},{1,0},{2,3},{3,2},{4,5},{5,4},{6,7},{7,6},{8,9},{9,8},{10,11... | collective-permute-start | bytes 4718600 | tf_op jit(solution)/shard_map/ppermute | solution.py:784
  390.9 25.8 %collective-permute-start.17 = (bf16[512,1536]{1,0:T(8,128)(2,1)}, bf16[512,1536]{1,0:T(8,128)(2,1)S(1)}, u32[]{:S(2)}, u32[]{:S(2)}) collective-permute-start(bf16[512,1536]{1,0:T(8,128)(2,1)} %get-tuple-element.121), channel_id=1, source_target_pairs={{0,1},{1,0},{2,3},{3,2},{4,5},{5,4},{6,7},{7,6},{8,9},{9,8},{10,11... | collective-permute-start | bytes 4718600 | tf_op jit(solution)/shard_map/ppermute | solution.py:834
  391.4 25.3 %collective-permute-start.18 = (bf16[512,1536]{1,0:T(8,128)(2,1)}, bf16[512,1536]{1,0:T(8,128)(2,1)}, u32[]{:S(2)}, u32[]{:S(2)}) collective-permute-start(bf16[512,1536]{1,0:T(8,128)(2,1)} %get-tuple-element.123), channel_id=1, source_target_pairs={{0,1},{1,0},{2,3},{3,2},{4,5},{5,4},{6,7},{7,6},{8,9},{9,8},{10,11... | collective-permute-start | bytes 4718600 | tf_op jit(solution)/shard_map/ppermute | solution.py:835
  432.5 35.5 %collective-permute-start.19 = (bf16[8,2,32,1536]{3,2,0,1:T(8,128)(2,1)S(1)}, bf16[8,2,32,1536]{3,2,0,1:T(8,128)(2,1)}, u32[]{:S(2)}, u32[]{:S(2)}) collective-permute-start(bf16[8,2,32,1536]{3,2,0,1:T(8,128)(2,1)S(1)} %bitcast.165), channel_id=1, source_target_pairs={{0,1},{1,0},{2,3},{3,2},{4,5},{5,4},{6,7},{7,6},{8,9},{9,8},{10,11... | collective-permute-start | bytes 4718600 | tf_op jit(solution)/shard_map/ppermute | solution.py:704
  433.4 3.9 collective-permute-start.20
  433.8 3.6 collective-permute-start.21
  433.9 99.0 %collective-permute-start.16 = (bf16[768,1024]{1,0:T(8,128)(2,1)}, bf16[768,1024]{1,0:T(8,128)(2,1)}, u32[]{:S(2)}, u32[]{:S(2)}) collective-permute-start(bf16[768,1024]{1,0:T(8,128)(2,1)} %get-tuple-element.111), channel_id=1, source_target_pairs={{0,2},{1,3},{2,0},{3,1},{4,6},{5,7},{6,4},{7,5},{8,10},{9,11},{10,... | collective-permute-start | bytes 4718600 | tf_op jit(solution)/shard_map/ppermute | solution.py:638
  471.3 57.6 %collective-permute-start.37 = (bf16[8,32,1536]{2,1,0:T(8,128)(2,1)}, bf16[8,32,1536]{2,1,0:T(8,128)(2,1)}, u32[]{:S(2)}, u32[]{:S(2)}) collective-permute-start(bf16[8,32,1536]{2,1,0:T(8,128)(2,1)} %dynamic-slice_bitcast_fusion.5), channel_id=1, source_target_pairs={{0,2},{1,3},{2,0},{3,1},{4,6},{5,7},{6,4},{7,5},{8,10},{9,11},{10,... | collective-permute-start | bytes 2359304 | tf_op jit(solution)/shard_map/ppermute | solution.py:638
  472.9 48.0 %collective-permute-start.22 = (bf16[128,1536]{1,0:T(8,128)(2,1)}, bf16[128,1536]{1,0:T(8,128)(2,1)S(1)}, u32[]{:S(2)}, u32[]{:S(2)}) collective-permute-start(bf16[128,1536]{1,0:T(8,128)(2,1)} %get-tuple-element.138), channel_id=1, source_target_pairs={{0,1},{1,0},{2,3},{3,2},{4,5},{5,4},{6,7},{7,6},{8,9},{9,8},{10,11... | collective-permute-start | bytes 1179656 | tf_op jit(solution)/shard_map/ppermute | solution.py:834
  473.2 47.7 %collective-permute-start.23 = (bf16[128,1536]{1,0:T(8,128)(2,1)}, bf16[128,1536]{1,0:T(8,128)(2,1)}, u32[]{:S(2)}, u32[]{:S(2)}) collective-permute-start(bf16[128,1536]{1,0:T(8,128)(2,1)} %get-tuple-element.140), channel_id=1, source_target_pairs={{0,1},{1,0},{2,3},{3,2},{4,5},{5,4},{6,7},{7,6},{8,9},{9,8},{10,11... | collective-permute-start | bytes 1179656 | tf_op jit(solution)/shard_map/ppermute | solution.py:835
  528.9 3.1 copy-start.5
  528.9 4.0 copy-start.32
  530.5 11.4 %collective-permute-start.38 = (bf16[4,32,1536]{2,1,0:T(8,128)(2,1)S(1)}, bf16[4,32,1536]{2,1,0:T(8,128)(2,1)}, u32[]{:S(2)}, u32[]{:S(2)}) collective-permute-start(bf16[4,32,1536]{2,1,0:T(8,128)(2,1)S(1)} %dynamic-slice_bitcast_fusion.8), channel_id=1, source_target_pairs={{0,4},{4,0},{8,12},{12,8},{16,20},{20,16},{24,28},{28,24},{1,5},{5... | collective-permute-start | bytes 1179656 | tf_op jit(solution)/shard_map/ppermute | solution.py:704
  532.9 12.5 %collective-permute-start.26 = (bf16[8,2,32,768]{3,2,1,0:T(8,128)(2,1)}, bf16[8,2,32,768]{3,2,1,0:T(8,128)(2,1)}, u32[]{:S(2)}, u32[]{:S(2)}) collective-permute-start(bf16[8,2,32,768]{3,2,1,0:T(8,128)(2,1)} %dynamic-slice_bitcast_fusion.7), channel_id=1, source_target_pairs={{0,1},{1,0},{2,3},{3,2},{4,5},{5,4},{6,7},{7,6},{8,9},{9,8},{10,11... | collective-permute-start | bytes 2359304 | tf_op jit(solution)/shard_map/ppermute | solution.py:704
  532.9 3.4 copy-start.23
  533.0 8.9 %copy-start.9 = (bf16[8,32,1536]{2,1,0:T(8,128)(2,1)S(1)}, bf16[8,32,1536]{2,1,0:T(8,128)(2,1)}, u32[]{:S(2)}) copy-start(bf16[8,32,1536]{2,1,0:T(8,128)(2,1)} %copy-done.8) | copy-start | bytes 2359300
  534.7 12.9 %copy-start.6 = (bf16[1024,768]{1,0:T(8,128)(2,1)S(1)}, bf16[1024,768]{1,0:T(8,128)(2,1)}, u32[]{:S(2)}) copy-start(bf16[1024,768]{1,0:T(8,128)(2,1)} %constant_dynamic-update-slice_fusion) | copy-start | bytes 4718596
  536.4 17.6 %collective-permute-start.24 = (bf16[256,1536]{1,0:T(8,128)(2,1)}, bf16[256,1536]{1,0:T(8,128)(2,1)S(1)}, u32[]{:S(2)}, u32[]{:S(2)}) collective-permute-start(bf16[256,1536]{1,0:T(8,128)(2,1)} %get-tuple-element.144), channel_id=1, source_target_pairs={{0,1},{1,0},{2,3},{3,2},{4,5},{5,4},{6,7},{7,6},{8,9},{9,8},{10,11... | collective-permute-start | bytes 2359304 | tf_op jit(solution)/shard_map/ppermute | solution.py:834
  537.0 17.1 %collective-permute-start.25 = (bf16[256,1536]{1,0:T(8,128)(2,1)}, bf16[256,1536]{1,0:T(8,128)(2,1)}, u32[]{:S(2)}, u32[]{:S(2)}) collective-permute-start(bf16[256,1536]{1,0:T(8,128)(2,1)} %get-tuple-element.146), channel_id=1, source_target_pairs={{0,1},{1,0},{2,3},{3,2},{4,5},{5,4},{6,7},{7,6},{8,9},{9,8},{10,11... | collective-permute-start | bytes 2359304 | tf_op jit(solution)/shard_map/ppermute | solution.py:835
  543.0 7.7 %collective-permute-start.39 = (bf16[32,1536]{1,0:T(8,128)(2,1)S(1)}, bf16[32,1536]{1,0:T(8,128)(2,1)S(1)}, u32[]{:S(2)}, u32[]{:S(2)}) collective-permute-start(bf16[32,1536]{1,0:T(8,128)(2,1)S(1)} %get-tuple-element.196), channel_id=1, source_target_pairs={{0,8},{4,12},{8,16},{12,20},{16,24},{20,28},{24,0},{28,4},{1,9},{5... | collective-permute-start | bytes 294920 | tf_op jit(solution)/shard_map/ppermute | solution.py:638
  544.5 8.9 %collective-permute-start.40 = (bf16[32,1536]{1,0:T(8,128)(2,1)S(1)}, bf16[32,1536]{1,0:T(8,128)(2,1)S(1)}, u32[]{:S(2)}, u32[]{:S(2)}) collective-permute-start(bf16[32,1536]{1,0:T(8,128)(2,1)S(1)} %get-tuple-element.198), channel_id=1, source_target_pairs={{0,16},{4,20},{8,24},{12,28},{16,0},{20,4},{24,8},{28,12},{1,17},{... | collective-permute-start | bytes 294920 | tf_op jit(solution)/shard_map/ppermute | solution.py:638
  545.4 7.9 %collective-permute-start.41 = (bf16[32,1536]{1,0:T(8,128)(2,1)S(1)}, bf16[32,1536]{1,0:T(8,128)(2,1)S(1)}, u32[]{:S(2)}, u32[]{:S(2)}) collective-permute-start(bf16[32,1536]{1,0:T(8,128)(2,1)S(1)} %get-tuple-element.197), channel_id=1, source_target_pairs={{0,24},{4,28},{8,0},{12,4},{16,8},{20,12},{24,16},{28,20},{1,25},{... | collective-permute-start | bytes 294920 | tf_op jit(solution)/shard_map/ppermute | solution.py:638
  564.3 16.4 %collective-permute-start.27 = (bf16[8,2,32,768]{3,2,1,0:T(8,128)(2,1)}, bf16[8,2,32,768]{3,2,1,0:T(8,128)(2,1)}, u32[]{:S(2)}, u32[]{:S(2)}) collective-permute-start(bf16[8,2,32,768]{3,2,1,0:T(8,128)(2,1)} %dynamic-slice_bitcast_fusion.6), channel_id=1, source_target_pairs={{0,1},{1,0},{2,3},{3,2},{4,5},{5,4},{6,7},{7,6},{8,9},{9,8},{10,11... | collective-permute-start | bytes 2359304 | tf_op jit(solution)/shard_map/ppermute | solution.py:704
  569.1 11.7 %copy-start.11 = (bf16[1024,768]{1,0:T(8,128)(2,1)S(1)}, bf16[1024,768]{1,0:T(8,128)(2,1)}, u32[]{:S(2)}) copy-start(bf16[1024,768]{1,0:T(8,128)(2,1)} %get-tuple-element.147) | copy-start | bytes 4718596
  584.8 17.3 %collective-permute-start.28 = (bf16[256,1024]{1,0:T(8,128)(2,1)}, bf16[256,1024]{1,0:T(8,128)(2,1)}, u32[]{:S(2)}, u32[]{:S(2)}) collective-permute-start(bf16[256,1024]{1,0:T(8,128)(2,1)} %get-tuple-element.185), channel_id=1, source_target_pairs={{0,2},{1,3},{2,0},{3,1},{4,6},{5,7},{6,4},{7,5},{8,10},{9,11},{10,... | collective-permute-start | bytes 1572872 | tf_op jit(solution)/shard_map/ppermute | solution.py:638
  586.0 25.1 %collective-permute-start.29 = (bf16[256,1024]{1,0:T(8,128)(2,1)}, bf16[256,1024]{1,0:T(8,128)(2,1)}, u32[]{:S(2)}, u32[]{:S(2)}) collective-permute-start(bf16[256,1024]{1,0:T(8,128)(2,1)} %get-tuple-element.184), channel_id=1, source_target_pairs={{0,2},{1,3},{2,0},{3,1},{4,6},{5,7},{6,4},{7,5},{8,10},{9,11},{10,... | collective-permute-start | bytes 1572872 | tf_op jit(solution)/shard_map/ppermute | solution.py:638
  586.8 35.1 %collective-permute-start.30 = (bf16[256,1024]{1,0:T(8,128)(2,1)}, bf16[256,1024]{1,0:T(8,128)(2,1)}, u32[]{:S(2)}, u32[]{:S(2)}) collective-permute-start(bf16[256,1024]{1,0:T(8,128)(2,1)} %get-tuple-element.183), channel_id=1, source_target_pairs={{0,2},{1,3},{2,0},{3,1},{4,6},{5,7},{6,4},{7,5},{8,10},{9,11},{10,... | collective-permute-start | bytes 1572872 | tf_op jit(solution)/shard_map/ppermute | solution.py:638
  588.9 13.2 %copy-start.29 = (f32[8,1024]{1,0:T(8,128)S(1)}, f32[8,1024]{1,0:T(8,128)}, u32[]{:S(2)}) copy-start(f32[8,1024]{1,0:T(8,128)} %get-tuple-element.163) | copy-start | bytes 98308
  588.9 36.9 %collective-permute-start.42 = (bf16[4,2,32,1536]{3,2,1,0:T(8,128)(2,1)}, bf16[4,2,32,1536]{3,2,1,0:T(8,128)(2,1)}, u32[]{:S(2)}, u32[]{:S(2)}) collective-permute-start(bf16[4,2,32,1536]{3,2,1,0:T(8,128)(2,1)} %dynamic-slice_bitcast_fusion.4), channel_id=1, source_target_pairs={{0,4},{4,0},{8,12},{12,8},{16,20},{20,16},{24,28},{28,24},{1,5},{5... | collective-permute-start | bytes 2359304 | tf_op jit(solution)/shard_map/ppermute | solution.py:704
  611.1 3.7 collective-permute-start.31
  614.8 9.0 %collective-permute-start.32 = (f32[13,1024]{1,0:T(8,128)S(1)}, f32[13,1024]{1,0:T(8,128)S(1)}, u32[]{:S(2)}, u32[]{:S(2)}) collective-permute-start(f32[13,1024]{1,0:T(8,128)S(1)} %add.375), channel_id=1, source_target_pairs={{0,8},{4,12},{8,16},{12,20},{16,24},{20,28},{24,0},{28,4},{1,9},{5... | collective-permute-start | bytes 159752 | tf_op jit(solution)/shard_map/ppermute | solution.py:638
  617.5 6.6 %collective-permute-start.33 = (f32[13,1024]{1,0:T(8,128)S(1)}, f32[13,1024]{1,0:T(8,128)S(1)}, u32[]{:S(2)}, u32[]{:S(2)}) collective-permute-start(f32[13,1024]{1,0:T(8,128)S(1)} %add.375), channel_id=1, source_target_pairs={{0,16},{4,20},{8,24},{12,28},{16,0},{20,4},{24,8},{28,12},{1,17},{... | collective-permute-start | bytes 159752 | tf_op jit(solution)/shard_map/ppermute | solution.py:638
  618.6 5.7 collective-permute-start.34
  624.4 8.0 %collective-permute-start.35 = (f32[4,13,1024]{2,1,0:T(8,128)S(1)}, f32[4,13,1024]{2,1,0:T(8,128)S(1)}, u32[]{:S(2)}, u32[]{:S(2)}) collective-permute-start(f32[4,13,1024]{2,1,0:T(8,128)S(1)} %get-tuple-element.203), channel_id=1, source_target_pairs={{0,4},{4,0},{8,12},{12,8},{16,20},{20,16},{24,28},{28,24},{1,5},{5... | collective-permute-start | bytes 638984 | tf_op jit(solution)/shard_map/ppermute | solution.py:704
  627.2 9.8 %collective-permute-start.43 = (bf16[2,32,1536]{2,1,0:T(8,128)(2,1)S(1)}, bf16[2,32,1536]{2,1,0:T(8,128)(2,1)S(1)}, u32[]{:S(2)}, u32[]{:S(2)}) collective-permute-start(bf16[2,32,1536]{2,1,0:T(8,128)(2,1)S(1)} %get-tuple-element.188), channel_id=1, source_target_pairs={{0,8},{4,12},{8,16},{12,20},{16,24},{20,28},{24,0},{28,4},{1,9},{5... | collective-permute-start | bytes 589832 | tf_op jit(solution)/shard_map/ppermute | solution.py:638
  629.0 14.6 %collective-permute-start.44 = (bf16[2,32,1536]{2,1,0:T(8,128)(2,1)S(1)}, bf16[2,32,1536]{2,1,0:T(8,128)(2,1)S(1)}, u32[]{:S(2)}, u32[]{:S(2)}) collective-permute-start(bf16[2,32,1536]{2,1,0:T(8,128)(2,1)S(1)} %get-tuple-element.190), channel_id=1, source_target_pairs={{0,16},{4,20},{8,24},{12,28},{16,0},{20,4},{24,8},{28,12},{1,17},{... | collective-permute-start | bytes 589832 | tf_op jit(solution)/shard_map/ppermute | solution.py:638
  630.4 13.1 %collective-permute-start.45 = (bf16[2,32,1536]{2,1,0:T(8,128)(2,1)S(1)}, bf16[2,32,1536]{2,1,0:T(8,128)(2,1)S(1)}, u32[]{:S(2)}, u32[]{:S(2)}) collective-permute-start(bf16[2,32,1536]{2,1,0:T(8,128)(2,1)S(1)} %get-tuple-element.189), channel_id=1, source_target_pairs={{0,24},{4,28},{8,0},{12,4},{16,8},{20,12},{24,16},{28,20},{1,25},{... | collective-permute-start | bytes 589832 | tf_op jit(solution)/shard_map/ppermute | solution.py:638
  632.6 12.2 %collective-permute-start.36 = (f32[55,1024]{1,0:T(8,128)S(1)}, f32[55,1024]{1,0:T(8,128)S(1)}, u32[]{:S(2)}, u32[]{:S(2)}) collective-permute-start(f32[55,1024]{1,0:T(8,128)S(1)} %pad_maximum_fusion.7), channel_id=1, source_target_pairs={{0,2},{1,3},{2,0},{3,1},{4,6},{5,7},{6,4},{7,5},{8,10},{9,11},{10,... | collective-permute-start | bytes 675848 | tf_op jit(solution)/shard_map/ppermute | solution.py:638
  643.7 7.1 %collective-permute-start.46 = (bf16[32,1536]{1,0:T(8,128)(2,1)S(1)}, bf16[32,1536]{1,0:T(8,128)(2,1)S(1)}, u32[]{:S(2)}, u32[]{:S(2)}) collective-permute-start(bf16[32,1536]{1,0:T(8,128)(2,1)S(1)} %dynamic-slice_bitcast_fusion.12), channel_id=1, source_target_pairs={{0,2},{1,3},{2,0},{3,1},{4,6},{5,7},{6,4},{7,5},{8,10},{9,11},{10,... | collective-permute-start | bytes 294920 | tf_op jit(solution)/shard_map/ppermute | solution.py:638
  646.2 4.7 copy-start.16
  650.8 2.8 copy-start.1
  (29 other events, 50.4 us)
Sparse Core Ops, SparseCore 0:
  11.5 77.9 all-gather.2
  92.3 94.6 all-gather.4
  300.4 151.6 reduce-scatter.1

commit v6 on v5

--- a/solution.py
+++ b/solution.py
@@ -627,7 +627,7 @@
 
 
 def after(values, *others):
-    return lax.optimization_barrier((values,) + others)[0]
+    return lax.optimization_barrier((values,) + others)[0] if others else values
 
 
 def make_body(mesh):
@@ -682,13 +682,18 @@
             parts = own, shift(away, "fsdp", n_fsdp, group)
             return parts if split else (jnp.concatenate(parts),) * 2
 
-        def swap_out(whole, away, pieces=1):
+        def swap_out(away, pieces=1):
             arrived = []
             for first in range(0, local, local // pieces):
-                piece = shift(away[first : first + local // pieces], "fsdp", n_fsdp, group)
-                arrived.append(piece)
+                arrived.append(shift(away[first : first + local // pieces], "fsdp", n_fsdp, group))
+            return arrived
+
+        def placed_away(whole, arrived):
+            first = 0
+            for piece in arrived:
                 whole = lax.dynamic_update_slice(whole, piece[None], (other, first, 0))
-            return whole, arrived
+                first += piece.shape[0]
+            return whole
 
         def placed_own(own):
             return lax.dynamic_update_index_in_dim(jnp.zeros((slots, local, width), own.dtype), own, slot, 0)
@@ -703,28 +708,28 @@
         def swap(values, axis, size):
             return lax.ppermute(values, axis, [(i, i ^ 1) for i in range(size)])
 
-        def sum_core(values):
+        def sum_core(values, *others):
             values = values.reshape(n_dp, n_pairs, 2, shard, values.shape[1])
-            arrived = swap(pick(values, 1 - core, 2), "fsdp", n_fsdp)
+            arrived = after(swap(pick(values, 1 - core, 2), "fsdp", n_fsdp), *others)
             return pick(values, core, 2).astype(F32) + arrived.astype(F32)
 
-        def sum_pairs(values):
+        def sum_pairs(values, *others):
             axis = values.ndim - 3
             total = pick(values, pair, axis).astype(F32)
             for by in range(1, n_pairs):
-                arrived = shift(pick(values, (pair + by) % n_pairs, axis), "fsdp", n_fsdp, 2 * by)
+                arrived = after(shift(pick(values, (pair + by) % n_pairs, axis), "fsdp", n_fsdp, 2 * by), *others)
                 total = total + arrived.astype(F32)
             return total
 
-        def sum_side(values):
+        def sum_side(values, *others):
             values = values.reshape((far, 2) + values.shape[1:])
-            arrived = swap(pick(values, 1 - side, 1), "dp", n_dp)
+            arrived = after(swap(pick(values, 1 - side, 1), "dp", n_dp), *others)
             return pick(values, side, 1).astype(F32) + arrived.astype(F32)
 
-        def sum_far(values):
+        def sum_far(values, *others):
             total = pick(values, deep).astype(F32)
             for by in range(1, far):
-                arrived = shift(pick(values, (deep + by) % far), "dp", n_dp, 2 * by)
+                arrived = after(shift(pick(values, (deep + by) % far), "dp", n_dp, 2 * by), *others)
                 total = total + arrived.astype(F32)
             return total
 
@@ -794,13 +799,9 @@
         )
         if not split:
             mixed, away_mixed = placed_own(mixed[:local]), mixed[local:]
-        mixed, _ = swap_out(mixed, away_mixed)
+        mixed_arrived = swap_out(away_mixed)
 
         sum_rows = lax.psum_scatter(g_rows, AXES, scatter_dimension=0, tiled=True).astype(F32)
-        g_out = sum_rows[:, :width]
-        g_up = sum_rows[:, width : width + hidden_width].reshape(shard, ups, n_dp * n_fsdp, shard)
-        g_up = g_up.swapaxes(1, 2).reshape(w_up.shape)
-        g_down = jnp.concatenate([sum_rows[:, (1 + ups + i) * width : (2 + ups + i) * width] for i in range(ups)])
 
         grads, d_biases, weight_sums = ([], [], []), [], []
 
@@ -810,7 +811,7 @@
                 for kind, grad in zip(grads, (piece[0], dk, dv)):
                     kind.append(grad)
                 d_biases.append(bias_grad[:, :3])
-            return jnp.concatenate([values[2] for values in sums], axis=1)
+            return [values[2] for values in sums]
 
         counts = (tall, tall // 4, tall // 4, tall // 2)
         first, ready, arrived, moving = 0, d_heads, [], None
@@ -836,35 +837,33 @@
             arrived.append((dq, dk_parts, dv_parts))
             if step == 1:
                 arrived[0][1][0] = after(arrived[0][1][0], dq)
-                weight_sums.append(sum_parts([arrived[0]]))
+                weight_sums += sum_parts([arrived[0]])
                 moving = sum_core(weight_sums[0]).astype(BF16)
-                ready = after(d_heads, dq, weight_sums[0])
+                ready = after(d_heads, dq, weight_sums[0], *mixed_arrived)
             if step == 2:
+                arrived[1][1][0] = after(arrived[1][1][0], dq)
                 moving = after(moving, dq)
                 ready = after(d_heads, dq, moving)
-        early_pairs = sum_pairs(moving).astype(BF16)
+        early_sum = sum_pairs(moving, dq).astype(BF16)
         arrived[2][1][0] = after(arrived[2][1][0], dq)
-        weight_sums.append(sum_parts(arrived[1:3]))
-        halves = [sum_core(weight_sums[1])]
-        arrived[3][1][0] = after(arrived[3][1][0], weight_sums[1], sum_rows)
-        weight_sums.append(sum_parts(arrived[3:]))
-        halves.append(sum_core(weight_sums[2]))
-        early_sum = sum_far(sum_side(early_pairs).astype(BF16))
+        weight_sums += sum_parts(arrived[1:3])
+        arrived[3][1][0] = after(arrived[3][1][0], weight_sums[2], sum_rows)
+        weight_sums += sum_parts(arrived[3:])
+        early_sum = sum_side(early_sum, weight_sums[3]).astype(BF16)
         if split:
-            rest = after(d_residual, weight_sums[2])
+            rest = after(d_residual, weight_sums[3], early_sum)
             away_frames, sums_away = input_grads(at_slot, 0, inputs[1], 1, rest, vectors, packed, grads)
-            core_sums = jnp.concatenate(halves, axis=-1).astype(BF16)
+            core_sums = [sum_core(values, away_frames) for values in weight_sums[1:]]
+            core_sums = jnp.concatenate(core_sums, axis=-1).astype(BF16)
             rest, away_frames, core_sums = lax.optimization_barrier((d_residual, away_frames, core_sums))
             own_frames, sums_own = input_grads(at_slot, slots, inputs[0], 0, rest, vectors, packed, grads)
             sums_one = sums_own + sums_away
         else:
-            core_sums = jnp.concatenate(halves, axis=-1).astype(BF16)
+            core_sums = jnp.concatenate([sum_core(values) for values in weight_sums[1:]], axis=-1).astype(BF16)
             both, sums_one = input_grads(at_slot, 0, inputs[0], 0, d_residual, vectors, packed, grads)
             own_frames, away_frames = placed_own(both[:local]), both[local:]
-        grad_frames, frames_arrived = swap_out(own_frames, away_frames, 3)
+        frames_arrived = swap_out(away_frames, 3)
         side_sums = sum_side(core_sums).astype(BF16)
-        late_sum = sum_pairs(sum_far(side_sums).astype(BF16))
-        sums = [early_sum, late_sum]
 
         vector = jnp.concatenate(
             [sums_one[:2], sums_two[: 6 + ups], jnp.concatenate(d_biases).T]
@@ -874,9 +873,21 @@
         total = vector
         for by in range(1, group):
             total = total + lax.ppermute(vector, "fsdp", ring(by))
+        total, side_sums = lax.optimization_barrier((total, side_sums))
+        all_sums = sum_far(jnp.concatenate([early_sum[:, None], side_sums], axis=1))
+        sums = [all_sums[0], sum_pairs(all_sums[1:].astype(BF16))]
+        sum_rows, mixed = after(sum_rows, total), after(mixed, total)
+        g_out = sum_rows[:, :width]
+        g_up = sum_rows[:, width : width + hidden_width].reshape(shard, ups, n_dp * n_fsdp, shard)
+        g_up = g_up.swapaxes(1, 2).reshape(w_up.shape)
+        g_down = jnp.concatenate([sum_rows[:, (1 + ups + i) * width : (2 + ups + i) * width] for i in range(ups)])
+        mixed = placed_away(mixed, mixed_arrived)
         packs = gather_dp(total).reshape(n_dp, -1, width)
         pack = jnp.concatenate([packs[:, :for_slot].reshape(-1, width), jnp.sum(packs[:, for_slot:], axis=0)])
-        pack, g_out, g_up, g_down, _ = lax.optimization_barrier((pack, g_out, g_up, g_down, frames_arrived[2]))
+        pack, g_out, g_up, g_down, mixed, _ = lax.optimization_barrier(
+            (pack, g_out, g_up, g_down, mixed, frames_arrived[2])
+        )
+        grad_frames = placed_away(own_frames, frames_arrived)
         across = shift(pack, "fsdp", n_fsdp, group)
         count = n_dp * for_slot
         d_mod = jnp.stack([jnp.where(slot == s, pack[:count], across[:count]).reshape(n_dp, -1) for s in range(slots)], axis=1)

time: 668 us -> 703 us (1.052)
  waiting for transfers between devices: 73 us -> 108 us
    ppermute x25 -> x22, waiting for transfers between devices: 37.4 us -> 77.3 us  [shift(): lax.ppermute(values, axis, [(i, (i + by) % size) for i in range(size)])]
    ppermute x25 -> x22, starting transfers between devices: 34.8 us -> 30.7 us  [shift(): lax.ppermute(values, axis, [(i, (i + by) % size) for i in range(size)])]
  transfers between devices with their start and end apart: 50 -> 48, of which waited for: 18 -> 12; matrix products, arithmetic and copies ran while one was open for 9% -> 10% of each run, Pallas kernels for 54% -> 53%
where the time goes in v6:
time: 703 us; the launch traced here: 692 us
  Pallas kernels  447 us (64%)
  waiting for transfers between devices  108 us (15%)
  local copies, waits for them, and re-layouts  53.2 us (8%)
  starting transfers between devices  41.2 us (6%)
  other arithmetic  25.9 us (4%)
  between operations  15.1 us (2%)
    pallas_call x4, Pallas kernels, attend_back(): pl.pallas_call(functools.partial(attend_back_kernel, parts, chunk), grid=...  188 us
    pallas_call x2, Pallas kernels, attend(): pl.pallas_call(functools.partial(attend_kernel, parts, chunk), grid=(head...  103 us
    pallas_call x1, Pallas kernels, feed_forward(): pl.pallas_call(functools.partial(feed_forward_kernel, len(heads_out), pie...  82.1 us
    ppermute x22, waiting for transfers between devices, shift(): lax.ppermute(values, axis, [(i, (i + by) % size) for i in range(size)])  77.3 us
    ppermute x22, starting transfers between devices, shift(): lax.ppermute(values, axis, [(i, (i + by) % size) for i in range(size)])  30.7 us
    pallas_call x4, Pallas kernels, weight_grads(): pl.pallas_call(functools.partial(weight_grads_kernel, parts), grid=(tall...  28.6 us
    pallas_call x2, Pallas kernels, input_grads(): pl.pallas_call(functools.partial(input_grads_kernel, [len(kind) for kind...  23 us
    all_gather x1, waiting for transfers between devices, body(): lax.all_gather(jnp.concatenate([w_key, w_value, w_query], axis=1), AXES,...  20.5 us
  transfers between devices with their start and end apart: 48, of which 12 were waited for; matrix products, arithmetic and copies ran while one was open for 10% of the time, Pallas kernels for 53%

profile of v6, /device:TPU:0, one launch (start us, length us, event | category | flops | bytes accessed | tf_op | source)
XLA Modules:
  0.0 692.3 jit_solution(11388938999269535061)
XLA Ops:
  7.2 1.6 pad_maximum_fusion.7
  9.0 3.1 collective-permute-start.1
  12.0 2.6 collective-permute-start.2
  14.6 1.3 collective-permute-start.3
  16.0 3.4 dynamic-slice_bitcast_fusion.2
  19.4 1.5 collective-permute-start
  24.1 1.6 collective-permute-start.4
  25.8 2.0 collective-permute-done.4
  30.0 1.5 collective-permute-start.5
  31.5 1.4 multiply_sine_fusion
  34.6 5.4 collective-permute-done.5
  40.0 1.2 add.327
  41.8 1.7 collective-permute-start.7
  45.0 4.0 collective-permute-done.6
  49.0 6.1 collective-permute-done.7
  56.4 3.9 dynamic-slice_bitcast_fusion
  60.3 2.5 collective-permute-done.9
  62.9 1.3 compare_select_fusion.1
  69.0 20.5 %all-gather.3.cloned.1.call-done.w_ref = bf16[1024,3072]{1,0:T(8,128)(2,1)} async-done(((bf16[32,3072]{1,0:T(8,128)(2,1)}), bf16[1024,3072]{1,0:T(8,128)(2,1)}) %all-gather.3.cloned.1.call-update) | async-done | bytes 6291472 | tf_op jit(solution)/shard_map/all_gather | solution.py:740
  89.5 13.6 %project_kv.1 = (bf16[1536,1024]{1,0:T(8,128)(2,1)}, bf16[512,1536]{1,0:T(8,128)(2,1)}, bf16[512,1536]{1,0:T(8,128)(2,1)}, bf16[512,1536]{1,0:T(8,128)(2,1)}, bf16[512,1536]{1,0:T(8,128)(2,1)}) custom-call(bf16[768,1024]{1,0:T(8,128)(2,1)} %get-tuple-element.204.x_ref.refs_2_, bf16[768,1024]{1,0:T(8,128)(2,1)} %collective-permute-done.y_ref.refs_3_.x_ref, ...), custom_call_target="tpu_custom_call" | custom-call | flops 12884901888 | bytes 16777216 | tf_op jit(solution)/shard_map/project_kv/pallas_call | solution.py:338
  103.9 1.4 collective-permute-start.15
  105.3 8.8 %project_q.1.refs_0_ = bf16[1024,1536]{1,0:T(8,128)(2,1)} custom-call(bf16[1536,1024]{1,0:T(8,128)(2,1)} %get-tuple-element.109.h_ref, f32[16,1024]{1,0:T(8,128)} %pad.8.vectors_ref.refs_8_, bf16[1024,3072]{1,0:T(8,128)(2,1)} %all-gather.3.cloned.1.call-done.w_ref, f32[32,1536]{1,0:T(8,128)} %slice.131.cos_ref, f32[32,1536]{1,0:T(8,128)} %slice.132.sin_ref), custom_call_target="tpu_custom_call" | custom-call | flops 6442450944 | bytes 8388608 | tf_op jit(solution)/shard_map/project_q/pallas_call | solution.py:352
  115.2 51.6 %attend.3 = (bf16[512,1536]{1,0:T(8,128)(2,1)}, f32[8,1,1536]{2,1,0:T(1,128)}) custom-call(bf16[1024,1536]{1,0:T(8,128)(2,1)} %project_q.1.refs_0_, bf16[3072,64]{1,0:T(8,128)(2,1)} %pad.9.refs_1_, bf16[512,1536]{1,0:T(8,128)(2,1)} %get-tuple-element.114.refs_2_.refs_7_, bf16[512,1536]{1,0:T(8,128)(2,1)} %copy-done.2, ...), custom_call_target="tpu_custom_call" | custom-call | flops 38654705664 | bytes 9437184 | tf_op jit(solution)/shard_map/attend/pallas_call | solution.py:91
  166.8 51.4 %attend.2 = (bf16[512,1536]{1,0:T(8,128)(2,1)}, f32[8,1,1536]{2,1,0:T(1,128)}) custom-call(bf16[1024,1536]{1,0:T(8,128)(2,1)} %project_q.1.refs_0_, bf16[3072,64]{1,0:T(8,128)(2,1)} %pad.9.refs_1_, bf16[512,1536]{1,0:T(8,128)(2,1)} %get-tuple-element.111.refs_2_.refs_7_, bf16[512,1536]{1,0:T(8,128)(2,1)} %collective-permute-done.11.refs_3_.refs_8_, ...), custom_call_target="tpu_custom_call" | custom-call | flops 38654705664 | bytes 9437184 | tf_op jit(solution)/shard_map/attend/pallas_call | solution.py:91
  218.3 82.1 %feed_forward.1 = (bf16[2,768,1024]{2,1,0:T(8,128)(2,1)}, bf16[768,1024]{1,0:T(8,128)(2,1)}, f32[1536,1024]{1,0:T(8,128)}, bf16[1024,1536]{1,0:T(8,128)(2,1)}, b...) custom-call(s32[1]{0:T(128)} %bitcast.slot_ref, bf16[512,1536]{1,0:T(8,128)(2,1)} %get-tuple-element.113.refs_0_.refs_2_, ...), custom_call_target="tpu_custom_call" | custom-call | flops 48318382080 | bytes 33554432 | tf_op jit(solution)/shard_map/feed_forward/pallas_call | solution.py:466
  300.4 90.6 %attend_back.5 = (bf16[512,1536]{1,0:T(8,128)(2,1)}, f32[512,1536]{1,0:T(8,128)}, bf16[512,1536]{1,0:T(8,128)(2,1)}, f32[512,1536]{1,0:T(8,128)}, bf16[512,1536]{1,0:T(8,128)(2,1)}) custom-call(bf16[1024,1536]{1,0:T(8,128)(2,1)} %project_q.1.refs_0_, bf16[1024,1536]{1,0:T(8,128)(2,1)} %get-tuple-element.138.refs_1_, ...), custom_call_target="tpu_custom_call" | custom-call | flops 12079595520 | tf_op jit(solution)/shard_map/attend_back/pallas_call | solution.py:223
  391.6 25.2 %attend_back.4 = (bf16[128,1536]{1,0:T(8,128)(2,1)}, f32[128,1536]{1,0:T(8,128)}, bf16[128,1536]{1,0:T(8,128)(2,1)}, f32[128,1536]{1,0:T(8,128)}, bf16[128,1536]{1,0:T(8,128)(2,1)}) custom-call(bf16[1024,1536]{1,0:T(8,128)(2,1)} %project_q.1.refs_0_, bf16[1024,1536]{1,0:T(8,128)(2,1)} %get-tuple-element.138.refs_1_, ...), custom_call_target="tpu_custom_call" | custom-call | flops 3019898880 | tf_op jit(solution)/shard_map/attend_back/pallas_call | solution.py:223
  418.7 11.2 %weight_grads.4 = (bf16[512,1536]{1,0:T(8,128)(2,1)}, bf16[512,1536]{1,0:T(8,128)(2,1)}, bf16[1024,1536]{1,0:T(8,128)(2,1)}, f32[512,128]{1,0:T(8,128)}) custom-call(bf16[1536,1024]{1,0:T(8,128)(2,1)} %get-tuple-element.109.h_ref, bf16[512,1536]{1,0:T(8,128)(2,1)} %get-tuple-element.127.dq_ref.refs_0_, f32[512,1536]{1,0:T(8,128)} %get-tuple-element.129.refs_0_, ...), custom_call_target="tpu_custom_call" | custom-call | tf_op jit(solution)/shard_map/weight_grads/pallas_call | solution.py:536
  429.9 3.4 constant_dynamic-slice_fusion.8
  433.6 38.7 %collective-permute-done.18 = bf16[768,1024]{1,0:T(8,128)(2,1)} collective-permute-done((bf16[768,1024]{1,0:T(8,128)(2,1)}, bf16[768,1024]{1,0:T(8,128)(2,1)}, u32[]{:S(2)}, u32[]{:S(2)}) %collective-permute-start.18) | collective-permute-done | bytes 1572896 | tf_op jit(solution)/shard_map/ppermute | solution.py:638
  472.3 24.8 %attend_back.6 = (bf16[128,1536]{1,0:T(8,128)(2,1)}, f32[128,1536]{1,0:T(8,128)}, bf16[128,1536]{1,0:T(8,128)(2,1)}, f32[128,1536]{1,0:T(8,128)}, bf16[128,1536]{1,0:T(8,128)(2,1)}) custom-call(bf16[1024,1536]{1,0:T(8,128)(2,1)} %project_q.1.refs_0_, bf16[1024,1536]{1,0:T(8,128)(2,1)} %get-tuple-element.138.refs_1_, ...), custom_call_target="tpu_custom_call" | custom-call | flops 3019898880 | tf_op jit(solution)/shard_map/attend_back/pallas_call | solution.py:223
  497.2 2.3 fusion.1
  501.0 47.5 %attend_back.7 = (bf16[256,1536]{1,0:T(8,128)(2,1)}, f32[256,1536]{1,0:T(8,128)}, bf16[256,1536]{1,0:T(8,128)(2,1)}, f32[256,1536]{1,0:T(8,128)}, bf16[256,1536]{1,0:T(8,128)(2,1)}) custom-call(bf16[1024,1536]{1,0:T(8,128)(2,1)} %project_q.1.refs_0_, bf16[1024,1536]{1,0:T(8,128)(2,1)} %get-tuple-element.138.refs_1_, ...), custom_call_target="tpu_custom_call" | custom-call | flops 6039797760 | tf_op jit(solution)/shard_map/attend_back/pallas_call | solution.py:223
  549.1 1.3 fusion.4
  552.5 5.1 weight_grads.7
  557.6 1.5 copy.112
  559.8 1.8 dynamic-slice_bitcast_fusion.8
  562.5 5.0 weight_grads.5
  567.6 1.8 dynamic-slice_bitcast_fusion.7
  569.7 1.5 copy.113
  571.2 1.9 convert_element_type.207
  573.1 7.3 %weight_grads.6 = (bf16[256,1536]{1,0:T(8,128)(2,1)}, bf16[256,1536]{1,0:T(8,128)(2,1)}, bf16[1024,768]{1,0:T(8,128)(2,1)}, f32[256,128]{1,0:T(8,128)}) custom-call(bf16[1536,1024]{1,0:T(8,128)(2,1)} %get-tuple-element.109.h_ref, bf16[256,1536]{1,0:T(8,128)(2,1)} %get-tuple-element.139.dq_ref.refs_3_, f32[256,1536]{1,0:T(8,128)} %get-tuple-element.148.refs_0_, ...), custom_call_target="tpu_custom_call" | custom-call | tf_op jit(solution)/shard_map/weight_grads/pallas_call | solution.py:536
  581.9 11.5 %input_grads.2 = (bf16[768,1024]{1,0:T(8,128)(2,1)}, f32[8,1024]{1,0:T(8,128)}) custom-call(s32[1]{0:T(128)} %bitcast.slot_ref, bf16[768,1024]{1,0:T(8,128)(2,1)} %collective-permute-done.y_ref.refs_3_.x_ref, f32[1536,1024]{1,0:T(8,128)} %get-tuple-element.174.d_res_ref, f32[16,1024]{1,0:T(8,128)} %pad.8.vectors_ref.refs_8_, ...), custom_call_target="tpu_custom_call" | custom-call | flops 12884901888 | bytes 17301504 | tf_op jit(solution)/shard_map/input_grads/pallas_call | solution.py:592
  593.5 1.7 copy.114
  597.1 1.2 fusion.5
  601.9 2.0 collective-permute-start.31
  604.0 2.0 collective-permute-start.39
  606.0 11.5 %input_grads.3 = (bf16[2,768,1024]{2,1,0:T(8,128)(2,1)}, f32[8,1024]{1,0:T(8,128)}) custom-call(s32[1]{0:T(128)} %bitcast.slot_ref, bf16[768,1024]{1,0:T(8,128)(2,1)} %get-tuple-element.204.x_ref.refs_2_, f32[1536,1024]{1,0:T(8,128)} %get-tuple-element.174.d_res_ref, f32[16,1024]{1,0:T(8,128)} %pad.8.vectors_ref.refs_8_, ...), custom_call_target="tpu_custom_call" | custom-call | flops 12884901888 | bytes 17301504 | tf_op jit(solution)/shard_map/input_grads/pallas_call | solution.py:592
  618.3 9.9 %collective-permute-done.32 = bf16[256,1024]{1,0:T(8,128)(2,1)} collective-permute-done((bf16[256,1024]{1,0:T(8,128)(2,1)}, bf16[256,1024]{1,0:T(8,128)(2,1)}, u32[]{:S(2)}, u32[]{:S(2)}) %collective-permute-start.32) | collective-permute-done | bytes 524320 | tf_op jit(solution)/shard_map/ppermute | solution.py:638
  628.2 1.9 bitcast_dynamic-update-slice_fusion.3
  630.1 1.9 bitcast_dynamic-update-slice_fusion.2
  632.0 6.9 collective-permute-done.39
  638.9 1.9 bitcast_dynamic-update-slice_fusion.1
  640.8 1.3 fusion.2
  642.2 4.2 collective-permute-start.36
  648.1 2.2 collective-permute-start.41
  652.1 2.1 reshape.261
  654.2 2.5 collective-permute-start.43
  657.8 2.7 bitcast_dynamic-update-slice_fusion
  660.5 2.7 collective-permute-done.38
  663.4 1.8 collective-permute-start.40
  665.2 5.7 collective-permute-done.42
  673.5 3.3 collective-permute-done.44
  681.6 1.5 fusion.31
  (258 shorter events, 48.4 us)
Async XLA Ops:
  7.2 21.1 %copy-start = (bf16[32,6144]{1,0:T(8,128)(2,1)S(1)}, bf16[32,6144]{1,0:T(8,128)(2,1)}, u32[]{:S(2)}) copy-start(bf16[32,6144]{1,0:T(8,128)(2,1)} %param.21) | copy-start | bytes 1179652
  7.2 82.3 %all-gather.3.cloned.1.call-start = ((), (), s32[]{:S(2)}) async-start(), calls=%async_computation.1 | async-start | bytes 6488064 | tf_op jit(solution)/shard_map/all_gather | solution.py:740
  8.9 209.4 %all-gather.5.cloned.1.call-start = ((), (), s32[]{:S(2)}) async-start(), calls=%async_computation.2 | async-start | bytes 10813440 | tf_op jit(solution)/shard_map/all_gather | solution.py:744
  9.0 15.1 %collective-permute-start.1 = (s32[2]{0:T(128)}, s32[2]{0:T(128)S(1)}, u32[]{:S(2)}, u32[]{:S(2)}) collective-permute-start(s32[2]{0:T(128)} %param.20), channel_id=1, source_target_pairs={{0,8},{4,12},{8,16},{12,20},{16,24},{20,28},{24,0},{28,4},{1,9},{5... | collective-permute-start | bytes 32 | tf_op jit(solution)/shard_map/ppermute | solution.py:638
  12.0 12.0 %collective-permute-start.2 = (s32[2]{0:T(128)}, s32[2]{0:T(128)S(1)}, u32[]{:S(2)}, u32[]{:S(2)}) collective-permute-start(s32[2]{0:T(128)} %param.20), channel_id=1, source_target_pairs={{0,16},{4,20},{8,24},{12,28},{16,0},{20,4},{24,8},{28,12},{1,17},{... | collective-permute-start | bytes 32 | tf_op jit(solution)/shard_map/ppermute | solution.py:638
  14.6 9.5 %collective-permute-start.3 = (s32[2]{0:T(128)}, s32[2]{0:T(128)S(1)}, u32[]{:S(2)}, u32[]{:S(2)}) collective-permute-start(s32[2]{0:T(128)} %param.20), channel_id=1, source_target_pairs={{0,24},{4,28},{8,0},{12,4},{16,8},{20,12},{24,16},{28,20},{1,25},{... | collective-permute-start | bytes 32 | tf_op jit(solution)/shard_map/ppermute | solution.py:638
  16.0 4.9 copy-start.18
  19.4 2.6 copy-start.19
  19.4 2.7 copy-start.20
  19.4 49.7 %collective-permute-start = (bf16[768,1024]{1,0:T(8,128)(2,1)S(1)}, bf16[768,1024]{1,0:T(8,128)(2,1)}, u32[]{:S(2)}, u32[]{:S(2)}) collective-permute-start(bf16[768,1024]{1,0:T(8,128)(2,1)S(1)} %get-tuple-element.203), channel_id=1, source_target_pairs={{0,2},{1,3},{2,0},{3,1},{4,6},{5,7},{6,4},{7,5},{8,10},{9,11},{10,... | collective-permute-start | bytes 4718600 | tf_op jit(solution)/shard_map/ppermute | solution.py:638
  21.3 2.6 copy-start.22
  21.3 2.8 copy-start.23
  22.8 548.4 %reduce-scatter.2.cloned.1.call-start = ((), (), s32[]{:S(2)}) async-start(), calls=%async_computation.3 | async-start | bytes 10813440 | tf_op jit(solution)/shard_map/reduce_scatter | solution.py:804
  24.1 3.7 collective-permute-start.4
  28.9 4.1 copy-start.30
  30.0 10.0 %collective-permute-start.5 = (f32[4,2,13312]{2,1,0:T(2,128)}, f32[4,2,13312]{2,1,0:T(2,128)}, u32[]{:S(2)}, u32[]{:S(2)}) collective-permute-start(f32[4,2,13312]{2,1,0:T(2,128)} %squeeze.103), channel_id=1, source_target_pairs={{0,4},{4,0},{8,12},{12,8},{16,20},{20,16},{24,28},{28,24},{1,5},{5... | collective-permute-start | bytes 1277960 | tf_op jit(solution)/shard_map/ppermute | solution.py:709
  32.9 34.7 %copy-start.4 = (f32[32,3072]{1,0:T(8,128)}, f32[32,3072]{1,0:T(8,128)S(1)}, u32[]{:S(2)}) copy-start(f32[32,3072]{1,0:T(8,128)S(1)} %get-tuple-element.107.refs_5_) | copy-start | bytes 1179652
  32.9 35.4 %copy-start.3 = (f32[32,3072]{1,0:T(8,128)}, f32[32,3072]{1,0:T(8,128)S(1)}, u32[]{:S(2)}) copy-start(f32[32,3072]{1,0:T(8,128)S(1)} %get-tuple-element.108.refs_6_) | copy-start | bytes 1179652
  41.2 7.7 %collective-permute-start.6 = (f32[2,13312]{1,0:T(2,128)S(1)}, f32[2,13312]{1,0:T(2,128)S(1)}, u32[]{:S(2)}, u32[]{:S(2)}) collective-permute-start(f32[2,13312]{1,0:T(2,128)S(1)} %get-tuple-element.218), channel_id=1, source_target_pairs={{0,24},{4,28},{8,0},{12,4},{16,8},{20,12},{24,16},{28,20},{1,25},{... | collective-permute-start | bytes 319496 | tf_op jit(solution)/shard_map/ppermute | solution.py:638
  41.8 13.4 %collective-permute-start.7 = (f32[2,13312]{1,0:T(2,128)S(1)}, f32[2,13312]{1,0:T(2,128)S(1)}, u32[]{:S(2)}, u32[]{:S(2)}) collective-permute-start(f32[2,13312]{1,0:T(2,128)S(1)} %get-tuple-element.220), channel_id=1, source_target_pairs={{0,16},{4,20},{8,24},{12,28},{16,0},{20,4},{24,8},{28,12},{1,17},{... | collective-permute-start | bytes 319496 | tf_op jit(solution)/shard_map/ppermute | solution.py:638
  43.4 11.7 %collective-permute-start.8 = (f32[2,13312]{1,0:T(2,128)S(1)}, f32[2,13312]{1,0:T(2,128)S(1)}, u32[]{:S(2)}, u32[]{:S(2)}) collective-permute-start(f32[2,13312]{1,0:T(2,128)S(1)} %get-tuple-element.219), channel_id=1, source_target_pairs={{0,8},{4,12},{8,16},{12,20},{16,24},{20,28},{24,0},{28,4},{1,9},{5... | collective-permute-start | bytes 319496 | tf_op jit(solution)/shard_map/ppermute | solution.py:638
  55.3 7.5 %collective-permute-start.9 = (f32[13312]{0:T(1024)S(1)}, f32[13312]{0:T(1024)S(1)}, u32[]{:S(2)}, u32[]{:S(2)}) collective-permute-start(f32[13312]{0:T(1024)S(1)} %bitcast.192), channel_id=1, source_target_pairs={{0,2},{1,3},{2,0},{3,1},{4,6},{5,7},{6,4},{7,5},{8,10},{9,11},{10,... | collective-permute-start | bytes 159752 | tf_op jit(solution)/shard_map/ppermute | solution.py:638
  62.8 4.1 collective-permute-start.10
  103.1 11.0 %collective-permute-start.13 = (bf16[512,1536]{1,0:T(8,128)(2,1)}, bf16[512,1536]{1,0:T(8,128)(2,1)S(1)}, u32[]{:S(2)}, u32[]{:S(2)}) collective-permute-start(bf16[512,1536]{1,0:T(8,128)(2,1)} %get-tuple-element.114.refs_2_.refs_7_), channel_id=1, source_target_pairs={{0,1},{1,0},{2,3},{3,2},{4,5},{5,4},{6,7},{7,6},{8,9},{9,8},{10,11... | collective-permute-start | bytes 4718600 | tf_op jit(solution)/shard_map/ppermute | solution.py:789
  103.4 10.7 %collective-permute-start.14 = (bf16[512,1536]{1,0:T(8,128)(2,1)}, bf16[512,1536]{1,0:T(8,128)(2,1)}, u32[]{:S(2)}, u32[]{:S(2)}) collective-permute-start(bf16[512,1536]{1,0:T(8,128)(2,1)} %get-tuple-element.115.refs_4_.refs_9_), channel_id=1, source_target_pairs={{0,1},{1,0},{2,3},{3,2},{4,5},{5,4},{6,7},{7,6},{8,9},{9,8},{10,11... | collective-permute-start | bytes 4718600 | tf_op jit(solution)/shard_map/ppermute | solution.py:789
  103.6 63.2 %collective-permute-start.11 = (bf16[512,1536]{1,0:T(8,128)(2,1)}, bf16[512,1536]{1,0:T(8,128)(2,1)}, u32[]{:S(2)}, u32[]{:S(2)}) collective-permute-start(bf16[512,1536]{1,0:T(8,128)(2,1)} %get-tuple-element.111.refs_2_.refs_7_), channel_id=1, source_target_pairs={{0,1},{1,0},{2,3},{3,2},{4,5},{5,4},{6,7},{7,6},{8,9},{9,8},{10,11... | collective-permute-start | bytes 4718600 | tf_op jit(solution)/shard_map/ppermute | solution.py:789
  103.9 114.4 %collective-permute-start.15 = (bf16[768,1024]{1,0:T(8,128)(2,1)}, bf16[768,1024]{1,0:T(8,128)(2,1)}, u32[]{:S(2)}, u32[]{:S(2)}) collective-permute-start(bf16[768,1024]{1,0:T(8,128)(2,1)} %get-tuple-element.119), channel_id=1, source_target_pairs={{0,2},{1,3},{2,0},{3,1},{4,6},{5,7},{6,4},{7,5},{8,10},{9,11},{10,... | collective-permute-start | bytes 4718600 | tf_op jit(solution)/shard_map/ppermute | solution.py:638
  105.3 61.5 %collective-permute-start.12 = (bf16[512,1536]{1,0:T(8,128)(2,1)}, bf16[512,1536]{1,0:T(8,128)(2,1)}, u32[]{:S(2)}, u32[]{:S(2)}) collective-permute-start(bf16[512,1536]{1,0:T(8,128)(2,1)} %get-tuple-element.112.refs_4_.refs_9_), channel_id=1, source_target_pairs={{0,1},{1,0},{2,3},{3,2},{4,5},{5,4},{6,7},{7,6},{8,9},{9,8},{10,11... | collective-permute-start | bytes 4718600 | tf_op jit(solution)/shard_map/ppermute | solution.py:789
  391.0 26.5 %collective-permute-start.16 = (bf16[512,1536]{1,0:T(8,128)(2,1)}, bf16[512,1536]{1,0:T(8,128)(2,1)S(1)}, u32[]{:S(2)}, u32[]{:S(2)}) collective-permute-start(bf16[512,1536]{1,0:T(8,128)(2,1)} %get-tuple-element.130), channel_id=1, source_target_pairs={{0,1},{1,0},{2,3},{3,2},{4,5},{5,4},{6,7},{7,6},{8,9},{9,8},{10,11... | collective-permute-start | bytes 4718600 | tf_op jit(solution)/shard_map/ppermute | solution.py:835
  391.6 26.0 %collective-permute-start.17 = (bf16[512,1536]{1,0:T(8,128)(2,1)}, bf16[512,1536]{1,0:T(8,128)(2,1)}, u32[]{:S(2)}, u32[]{:S(2)}) collective-permute-start(bf16[512,1536]{1,0:T(8,128)(2,1)} %get-tuple-element.132), channel_id=1, source_target_pairs={{0,1},{1,0},{2,3},{3,2},{4,5},{5,4},{6,7},{7,6},{8,9},{9,8},{10,11... | collective-permute-start | bytes 4718600 | tf_op jit(solution)/shard_map/ppermute | solution.py:836
  416.8 55.5 %collective-permute-start.18 = (bf16[768,1024]{1,0:T(8,128)(2,1)}, bf16[768,1024]{1,0:T(8,128)(2,1)}, u32[]{:S(2)}, u32[]{:S(2)}) collective-permute-start(bf16[768,1024]{1,0:T(8,128)(2,1)} %get-tuple-element.134), channel_id=1, source_target_pairs={{0,2},{1,3},{2,0},{3,1},{4,6},{5,7},{6,4},{7,5},{8,10},{9,11},{10,... | collective-permute-start | bytes 4718600 | tf_op jit(solution)/shard_map/ppermute | solution.py:638
  433.4 63.8 %collective-permute-start.19 = (bf16[8,2,32,1536]{3,2,0,1:T(8,128)(2,1)S(1)}, bf16[8,2,32,1536]{3,2,0,1:T(8,128)(2,1)}, u32[]{:S(2)}, u32[]{:S(2)}) collective-permute-start(bf16[8,2,32,1536]{3,2,0,1:T(8,128)(2,1)S(1)} %bitcast.169), channel_id=1, source_target_pairs={{0,1},{1,0},{2,3},{3,2},{4,5},{5,4},{6,7},{7,6},{8,9},{9,8},{10,11... | collective-permute-start | bytes 4718600 | tf_op jit(solution)/shard_map/ppermute | solution.py:709
  500.5 48.6 %collective-permute-start.24 = (bf16[8,32,1536]{2,1,0:T(8,128)(2,1)}, bf16[8,32,1536]{2,1,0:T(8,128)(2,1)}, u32[]{:S(2)}, u32[]{:S(2)}) collective-permute-start(bf16[8,32,1536]{2,1,0:T(8,128)(2,1)} %dynamic-slice_bitcast_fusion.6), channel_id=1, source_target_pairs={{0,2},{1,3},{2,0},{3,1},{4,6},{5,7},{6,4},{7,5},{8,10},{9,11},{10,... | collective-permute-start | bytes 2359304 | tf_op jit(solution)/shard_map/ppermute | solution.py:638
  500.5 50.0 %collective-permute-start.26 = (bf16[128,1536]{1,0:T(8,128)(2,1)}, bf16[128,1536]{1,0:T(8,128)(2,1)}, u32[]{:S(2)}, u32[]{:S(2)}) collective-permute-start(bf16[128,1536]{1,0:T(8,128)(2,1)} %get-tuple-element.159), channel_id=1, source_target_pairs={{0,1},{1,0},{2,3},{3,2},{4,5},{5,4},{6,7},{7,6},{8,9},{9,8},{10,11... | collective-permute-start | bytes 1179656 | tf_op jit(solution)/shard_map/ppermute | solution.py:835
  500.5 50.9 %collective-permute-start.27 = (bf16[128,1536]{1,0:T(8,128)(2,1)}, bf16[128,1536]{1,0:T(8,128)(2,1)}, u32[]{:S(2)}, u32[]{:S(2)}) collective-permute-start(bf16[128,1536]{1,0:T(8,128)(2,1)} %get-tuple-element.161), channel_id=1, source_target_pairs={{0,1},{1,0},{2,3},{3,2},{4,5},{5,4},{6,7},{7,6},{8,9},{9,8},{10,11... | collective-permute-start | bytes 1179656 | tf_op jit(solution)/shard_map/ppermute | solution.py:836
  501.0 60.6 %collective-permute-start.20 = (bf16[128,1536]{1,0:T(8,128)(2,1)}, bf16[128,1536]{1,0:T(8,128)(2,1)S(1)}, u32[]{:S(2)}, u32[]{:S(2)}) collective-permute-start(bf16[128,1536]{1,0:T(8,128)(2,1)} %get-tuple-element.143), channel_id=1, source_target_pairs={{0,1},{1,0},{2,3},{3,2},{4,5},{5,4},{6,7},{7,6},{8,9},{9,8},{10,11... | collective-permute-start | bytes 1179656 | tf_op jit(solution)/shard_map/ppermute | solution.py:835
  548.5 24.6 %collective-permute-start.22 = (bf16[256,1536]{1,0:T(8,128)(2,1)}, bf16[256,1536]{1,0:T(8,128)(2,1)}, u32[]{:S(2)}, u32[]{:S(2)}) collective-permute-start(bf16[256,1536]{1,0:T(8,128)(2,1)} %get-tuple-element.149), channel_id=1, source_target_pairs={{0,1},{1,0},{2,3},{3,2},{4,5},{5,4},{6,7},{7,6},{8,9},{9,8},{10,11... | collective-permute-start | bytes 2359304 | tf_op jit(solution)/shard_map/ppermute | solution.py:835
  549.0 24.0 %collective-permute-start.23 = (bf16[256,1536]{1,0:T(8,128)(2,1)}, bf16[256,1536]{1,0:T(8,128)(2,1)}, u32[]{:S(2)}, u32[]{:S(2)}) collective-permute-start(bf16[256,1536]{1,0:T(8,128)(2,1)} %get-tuple-element.151), channel_id=1, source_target_pairs={{0,1},{1,0},{2,3},{3,2},{4,5},{5,4},{6,7},{7,6},{8,9},{9,8},{10,11... | collective-permute-start | bytes 2359304 | tf_op jit(solution)/shard_map/ppermute | solution.py:836
  550.5 11.3 %collective-permute-start.21 = (bf16[128,1536]{1,0:T(8,128)(2,1)}, bf16[128,1536]{1,0:T(8,128)(2,1)S(1)}, u32[]{:S(2)}, u32[]{:S(2)}) collective-permute-start(bf16[128,1536]{1,0:T(8,128)(2,1)} %get-tuple-element.145), channel_id=1, source_target_pairs={{0,1},{1,0},{2,3},{3,2},{4,5},{5,4},{6,7},{7,6},{8,9},{9,8},{10,11... | collective-permute-start | bytes 1179656 | tf_op jit(solution)/shard_map/ppermute | solution.py:836
  551.4 28.9 %collective-permute-start.25 = (bf16[4,32,1536]{2,1,0:T(8,128)(2,1)S(1)}, bf16[4,32,1536]{2,1,0:T(8,128)(2,1)S(1)}, u32[]{:S(2)}, u32[]{:S(2)}) collective-permute-start(bf16[4,32,1536]{2,1,0:T(8,128)(2,1)S(1)} %dynamic-slice_bitcast_fusion.9), channel_id=1, source_target_pairs={{0,4},{4,0},{8,12},{12,8},{16,20},{20,16},{24,28},{28,24},{1,5},{5... | collective-permute-start | bytes 1179656 | tf_op jit(solution)/shard_map/ppermute | solution.py:709
  552.5 6.6 copy-start.17
  561.6 31.9 %collective-permute-start.28 = (bf16[8,2,32,384]{3,2,1,0:T(8,128)(2,1)}, bf16[8,2,32,384]{3,2,1,0:T(8,128)(2,1)}, u32[]{:S(2)}, u32[]{:S(2)}) collective-permute-start(bf16[8,2,32,384]{3,2,1,0:T(8,128)(2,1)} %dynamic-slice_bitcast_fusion.8), channel_id=1, source_target_pairs={{0,1},{1,0},{2,3},{3,2},{4,5},{5,4},{6,7},{7,6},{8,9},{9,8},{10,11... | collective-permute-start | bytes 1179656 | tf_op jit(solution)/shard_map/ppermute | solution.py:709
  569.3 24.1 %collective-permute-start.29 = (bf16[8,2,32,384]{3,2,1,0:T(8,128)(2,1)}, bf16[8,2,32,384]{3,2,1,0:T(8,128)(2,1)}, u32[]{:S(2)}, u32[]{:S(2)}) collective-permute-start(bf16[8,2,32,384]{3,2,1,0:T(8,128)(2,1)} %dynamic-slice_bitcast_fusion.7), channel_id=1, source_target_pairs={{0,1},{1,0},{2,3},{3,2},{4,5},{5,4},{6,7},{7,6},{8,9},{9,8},{10,11... | collective-permute-start | bytes 1179656 | tf_op jit(solution)/shard_map/ppermute | solution.py:709
  573.1 7.3 %copy-start.6 = (bf16[8,32,1536]{2,1,0:T(8,128)(2,1)S(1)}, bf16[8,32,1536]{2,1,0:T(8,128)(2,1)}, u32[]{:S(2)}) copy-start(bf16[8,32,1536]{2,1,0:T(8,128)(2,1)} %copy-done.5) | copy-start | bytes 2359300
  581.7 16.7 %collective-permute-start.30 = (bf16[8,2,32,768]{3,2,1,0:T(8,128)(2,1)S(1)}, bf16[8,2,32,768]{3,2,1,0:T(8,128)(2,1)S(1)}, u32[]{:S(2)}, u32[]{:S(2)}) collective-permute-start(bf16[8,2,32,768]{3,2,1,0:T(8,128)(2,1)S(1)} %dynamic-slice_bitcast_fusion.5), channel_id=1, source_target_pairs={{0,1},{1,0},{2,3},{3,2},{4,5},{5,4},{6,7},{7,6},{8,9},{9,8},{10,11... | collective-permute-start | bytes 2359304 | tf_op jit(solution)/shard_map/ppermute | solution.py:709
  593.5 4.9 copy-start.9
  599.7 41.1 %collective-permute-start.34 = (bf16[4,2,32,1536]{3,2,1,0:T(8,128)(2,1)}, bf16[4,2,32,1536]{3,2,1,0:T(8,128)(2,1)}, u32[]{:S(2)}, u32[]{:S(2)}) collective-permute-start(bf16[4,2,32,1536]{3,2,1,0:T(8,128)(2,1)} %dynamic-slice_bitcast_fusion.4), channel_id=1, source_target_pairs={{0,4},{4,0},{8,12},{12,8},{16,20},{20,16},{24,28},{28,24},{1,5},{5... | collective-permute-start | bytes 2359304 | tf_op jit(solution)/shard_map/ppermute | solution.py:709
  601.9 16.4 %collective-permute-start.31 = (bf16[256,1024]{1,0:T(8,128)(2,1)}, bf16[256,1024]{1,0:T(8,128)(2,1)}, u32[]{:S(2)}, u32[]{:S(2)}) collective-permute-start(bf16[256,1024]{1,0:T(8,128)(2,1)} %get-tuple-element.207), channel_id=1, source_target_pairs={{0,2},{1,3},{2,0},{3,1},{4,6},{5,7},{6,4},{7,5},{8,10},{9,11},{10,... | collective-permute-start | bytes 1572872 | tf_op jit(solution)/shard_map/ppermute | solution.py:638
  603.9 24.3 %collective-permute-start.32 = (bf16[256,1024]{1,0:T(8,128)(2,1)}, bf16[256,1024]{1,0:T(8,128)(2,1)}, u32[]{:S(2)}, u32[]{:S(2)}) collective-permute-start(bf16[256,1024]{1,0:T(8,128)(2,1)} %get-tuple-element.206), channel_id=1, source_target_pairs={{0,2},{1,3},{2,0},{3,1},{4,6},{5,7},{6,4},{7,5},{8,10},{9,11},{10,... | collective-permute-start | bytes 1572872 | tf_op jit(solution)/shard_map/ppermute | solution.py:638
  604.0 14.3 %copy-start.21 = (f32[8,1024]{1,0:T(8,128)S(1)}, f32[8,1024]{1,0:T(8,128)}, u32[]{:S(2)}) copy-start(f32[8,1024]{1,0:T(8,128)} %get-tuple-element.177) | copy-start | bytes 98308
  604.0 34.9 %collective-permute-start.39 = (bf16[256,1024]{1,0:T(8,128)(2,1)}, bf16[256,1024]{1,0:T(8,128)(2,1)}, u32[]{:S(2)}, u32[]{:S(2)}) collective-permute-start(bf16[256,1024]{1,0:T(8,128)(2,1)} %get-tuple-element.205), channel_id=1, source_target_pairs={{0,2},{1,3},{2,0},{3,1},{4,6},{5,7},{6,4},{7,5},{8,10},{9,11},{10,... | collective-permute-start | bytes 1572872 | tf_op jit(solution)/shard_map/ppermute | solution.py:638
  628.2 12.5 %collective-permute-start.33 = (f32[13,1024]{1,0:T(8,128)S(1)}, f32[13,1024]{1,0:T(8,128)S(1)}, u32[]{:S(2)}, u32[]{:S(2)}) collective-permute-start(f32[13,1024]{1,0:T(8,128)S(1)} %pad_maximum_fusion.8), channel_id=1, source_target_pairs={{0,1},{1,0},{2,3},{3,2},{4,5},{5,4},{6,7},{7,6},{8,9},{9,8},{10,11... | collective-permute-start | bytes 159752 | tf_op jit(solution)/shard_map/ppermute | solution.py:875
  632.0 14.5 %copy-start.7 = (f32[32,5120]{1,0:T(8,128)S(1)}, f32[32,5120]{1,0:T(8,128)}, u32[]{:S(2)}) copy-start(f32[32,5120]{1,0:T(8,128)} %convert_element_type.207) | copy-start | bytes 1966084
  642.1 12.1 %collective-permute-start.35 = (f32[13,1024]{1,0:T(8,128)S(1)}, f32[13,1024]{1,0:T(8,128)S(1)}, u32[]{:S(2)}, u32[]{:S(2)}) collective-permute-start(f32[13,1024]{1,0:T(8,128)S(1)} %add.370), channel_id=1, source_target_pairs={{0,8},{4,12},{8,16},{12,20},{16,24},{20,28},{24,0},{28,4},{1,9},{5... | collective-permute-start | bytes 159752 | tf_op jit(solution)/shard_map/ppermute | solution.py:638
  642.2 14.5 %collective-permute-start.36 = (f32[13,1024]{1,0:T(8,128)S(1)}, f32[13,1024]{1,0:T(8,128)S(1)}, u32[]{:S(2)}, u32[]{:S(2)}) collective-permute-start(f32[13,1024]{1,0:T(8,128)S(1)} %add.370), channel_id=1, source_target_pairs={{0,16},{4,20},{8,24},{12,28},{16,0},{20,4},{24,8},{28,12},{1,17},{... | collective-permute-start | bytes 159752 | tf_op jit(solution)/shard_map/ppermute | solution.py:638
  646.4 10.3 %collective-permute-start.37 = (f32[13,1024]{1,0:T(8,128)S(1)}, f32[13,1024]{1,0:T(8,128)S(1)}, u32[]{:S(2)}, u32[]{:S(2)}) collective-permute-start(f32[13,1024]{1,0:T(8,128)S(1)} %add.370), channel_id=1, source_target_pairs={{0,24},{4,28},{8,0},{12,4},{16,8},{20,12},{24,16},{28,20},{1,25},{... | collective-permute-start | bytes 159752 | tf_op jit(solution)/shard_map/ppermute | solution.py:638
  647.1 3.8 slice-start
  648.1 17.1 %collective-permute-start.41 = (bf16[3,32,1536]{2,1,0:T(8,128)(2,1)}, bf16[3,32,1536]{2,1,0:T(8,128)(2,1)}, u32[]{:S(2)}, u32[]{:S(2)}) collective-permute-start(bf16[3,32,1536]{2,1,0:T(8,128)(2,1)} %get-tuple-element.208), channel_id=1, source_target_pairs={{0,8},{4,12},{8,16},{12,20},{16,24},{20,28},{24,0},{28,4},{1,9},{5... | collective-permute-start | bytes 884744 | tf_op jit(solution)/shard_map/ppermute | solution.py:638
  650.2 20.6 %collective-permute-start.42 = (bf16[3,32,1536]{2,1,0:T(8,128)(2,1)}, bf16[3,32,1536]{2,1,0:T(8,128)(2,1)}, u32[]{:S(2)}, u32[]{:S(2)}) collective-permute-start(bf16[3,32,1536]{2,1,0:T(8,128)(2,1)} %get-tuple-element.209), channel_id=1, source_target_pairs={{0,16},{4,20},{8,24},{12,28},{16,0},{20,4},{24,8},{28,12},{1,17},{... | collective-permute-start | bytes 884744 | tf_op jit(solution)/shard_map/ppermute | solution.py:638
  654.2 16.7 %collective-permute-start.43 = (bf16[3,32,1536]{2,1,0:T(8,128)(2,1)}, bf16[3,32,1536]{2,1,0:T(8,128)(2,1)S(1)}, u32[]{:S(2)}, u32[]{:S(2)}) collective-permute-start(bf16[3,32,1536]{2,1,0:T(8,128)(2,1)} %get-tuple-element.210), channel_id=1, source_target_pairs={{0,24},{4,28},{8,0},{12,4},{16,8},{20,12},{24,16},{28,20},{1,25},{... | collective-permute-start | bytes 884744 | tf_op jit(solution)/shard_map/ppermute | solution.py:638
  656.8 6.4 collective-permute-start.38
  663.4 16.2 %collective-permute-start.40 = (f32[55,1024]{1,0:T(8,128)S(1)}, f32[55,1024]{1,0:T(8,128)S(1)}, u32[]{:S(2)}, u32[]{:S(2)}) collective-permute-start(f32[55,1024]{1,0:T(8,128)S(1)} %pad_maximum_fusion.6), channel_id=1, source_target_pairs={{0,2},{1,3},{2,0},{3,1},{4,6},{5,7},{6,4},{7,5},{8,10},{9,11},{10,... | collective-permute-start | bytes 675848 | tf_op jit(solution)/shard_map/ppermute | solution.py:638
  672.1 4.7 collective-permute-start.44
  680.7 4.9 copy-start.1
  (16 other events, 24.1 us)
Sparse Core Ops, SparseCore 0:
  11.5 77.9 all-gather.2
  92.3 94.8 all-gather.4
  300.5 157.3 reduce-scatter.1

commit v7 on v6

--- a/solution.py
+++ b/solution.py
@@ -508,9 +508,9 @@
     )(slot, *heads_out, *inputs, *cotangent, keep, packed, vectors)
 
 
-def weight_grads_kernel(parts, h_ref, dq_ref, *refs):
+def weight_grads_kernel(parts, shard, core_ref, h_ref, dq_ref, *refs):
     dk_refs, dv_refs = refs[:parts], refs[parts : 2 * parts]
-    dk_out, dv_out, weight_ref, bias_ref = refs[2 * parts :]
+    dk_out, dv_out, keep_ref, send_ref, bias_ref = refs[2 * parts :]
 
     def summed(pieces):
         total = pieces[0][...]
@@ -521,38 +521,68 @@
     grads = [dq_ref[...], summed(dk_refs), summed(dv_refs)]
     dk_out[...] = grads[1]
     dv_out[...] = grads[2]
-    weight_ref[...] = dot(jnp.concatenate(grads, axis=0), h_ref[...], 1, 0).T.astype(BF16)
+    weight_grad = dot(jnp.concatenate(grads, axis=0), h_ref[...], 1, 0).T.astype(BF16)
     for i, grad in enumerate(grads):
         bias_ref[:, i : i + 1] = jnp.sum(grad.astype(F32), axis=1, keepdims=True)
-
-
-def weight_grads(h_one, d_query, dk_parts, dv_parts):
+    if not shard:
+        keep_ref[...] = weight_grad
+        return
+
+    def store(even_ref, odd_ref):
+        for i in range(0, weight_grad.shape[0] // 2, shard):
+            even_ref[i : i + shard, :] = weight_grad[2 * i : 2 * i + shard]
+            odd_ref[i : i + shard, :] = weight_grad[2 * i + shard : 2 * (i + shard)]
+
+    @pl.when(core_ref[0] == 0)
+    def _():
+        store(keep_ref, send_ref)
+
+    @pl.when(core_ref[0] != 0)
+    def _():
+        store(send_ref, keep_ref)
+
+
+def weight_grads(core, shard, h_one, d_query, dk_parts, dv_parts):
     rows, width = h_one.shape
     tall = d_query.shape[0]
     block = pick_block(tall, 128)
-    spec = pl.BlockSpec((block, rows), lambda i: (i, 0))
+    spec = pl.BlockSpec((block, rows), lambda i, *_: (i, 0))
     kinds = jax.ShapeDtypeStruct
     parts = len(dk_parts)
-    return pl.pallas_call(
-        functools.partial(weight_grads_kernel, parts),
-        grid=(tall // block,),
-        in_specs=[whole_spec((rows, width))] + [spec] * (1 + 2 * parts),
-        out_specs=[
-            spec,
-            spec,
-            pl.BlockSpec((width, 3 * block), lambda i: (0, i)),
-            pl.BlockSpec((block, 128), lambda i: (i, 0)),
-        ],
+    in_kernel = shard % 16 == 0
+    height = width // 2 if in_kernel else width
+    columns = lambda height: pl.BlockSpec((height, 3 * block), lambda i, *_: (0, i))
+    dk, dv, keep, send, bias = pl.pallas_call(
+        functools.partial(weight_grads_kernel, parts, shard if in_kernel else 0),
+        grid_spec=pltpu.PrefetchScalarGridSpec(
+            num_scalar_prefetch=1,
+            grid=(tall // block,),
+            in_specs=[whole_spec((rows, width))] + [spec] * (1 + 2 * parts),
+            out_specs=[
+                spec,
+                spec,
+                columns(height),
+                columns(height if in_kernel else 16),
+                pl.BlockSpec((block, 128), lambda i, *_: (i, 0)),
+            ],
+        ),
         out_shape=[
             kinds((tall, rows), BF16),
             kinds((tall, rows), BF16),
-            kinds((width, 3 * tall), BF16),
+            kinds((height, 3 * tall), BF16),
+            kinds((height if in_kernel else 16, 3 * tall), BF16),
             kinds((tall, 128), F32),
         ],
         compiler_params=pltpu.CompilerParams(vmem_limit_bytes=VMEM_LIMIT),
         cost_estimate=pl.CostEstimate(flops=0, bytes_accessed=0, transcendentals=0),
         name="weight_grads",
-    )(h_one, d_query, *dk_parts, *dv_parts)
+    )(core, h_one, d_query, *dk_parts, *dv_parts)
+    if not in_kernel:
+        both = keep.reshape(-1, 2, shard, 3 * tall)
+        keep, send = [
+            lax.dynamic_index_in_dim(both, at, 1, keepdims=False).reshape(-1, 3 * tall) for at in (core[0], 1 - core[0])
+        ]
+    return dk, dv, keep, send, bias
 
 
 def input_grads_kernel(counts, slot_ref, x_ref, d_res_ref, vectors_ref, w_ref, *refs):
@@ -682,11 +712,8 @@
             parts = own, shift(away, "fsdp", n_fsdp, group)
             return parts if split else (jnp.concatenate(parts),) * 2
 
-        def swap_out(away, pieces=1):
-            arrived = []
-            for first in range(0, local, local // pieces):
-                arrived.append(shift(away[first : first + local // pieces], "fsdp", n_fsdp, group))
-            return arrived
+        def swap_out(*pieces):
+            return [shift(piece, "fsdp", n_fsdp, group) for piece in pieces]
 
         def placed_away(whole, arrived):
             first = 0
@@ -708,10 +735,10 @@
         def swap(values, axis, size):
             return lax.ppermute(values, axis, [(i, i ^ 1) for i in range(size)])
 
-        def sum_core(values, *others):
-            values = values.reshape(n_dp, n_pairs, 2, shard, values.shape[1])
-            arrived = after(swap(pick(values, 1 - core, 2), "fsdp", n_fsdp), *others)
-            return pick(values, core, 2).astype(F32) + arrived.astype(F32)
+        def sum_core(keep, send, *others):
+            arrived = after(swap(send, "fsdp", n_fsdp), *others)
+            total = keep.astype(F32) + arrived.astype(F32)
+            return total.astype(BF16).reshape(n_dp, n_pairs, shard, keep.shape[1])
 
         def sum_pairs(values, *others):
             axis = values.ndim - 3
@@ -801,20 +828,21 @@
             mixed, away_mixed = placed_own(mixed[:local]), mixed[local:]
         mixed_arrived = swap_out(away_mixed)
 
-        sum_rows = lax.psum_scatter(g_rows, AXES, scatter_dimension=0, tiled=True).astype(F32)
-
-        grads, d_biases, weight_sums = ([], [], []), [], []
-
-        def sum_parts(pieces):
-            sums = [weight_grads(h_one, *piece) for piece in pieces]
-            for piece, (dk, dv, _, bias_grad) in zip(pieces, sums):
-                for kind, grad in zip(grads, (piece[0], dk, dv)):
-                    kind.append(grad)
-                d_biases.append(bias_grad[:, :3])
-            return [values[2] for values in sums]
-
-        counts = (tall, tall // 4, tall // 4, tall // 2)
-        first, ready, arrived, moving = 0, d_heads, [], None
+        sum_rows = lax.psum_scatter(g_rows, AXES, scatter_dimension=0, tiled=True)
+
+        grads, d_biases = ([], [], []), []
+        at_core = core.reshape(1).astype(jnp.int32)
+
+        def sum_parts(dq, dk_parts, dv_parts, *others):
+            dk_parts = [after(dk_parts[0], *others)] + dk_parts[1:]
+            dk, dv, keep, send, bias_grad = weight_grads(at_core, shard, h_one, dq, dk_parts, dv_parts)
+            for kind, grad in zip(grads, (dq, dk, dv)):
+                kind.append(grad)
+            d_biases.append(bias_grad[:, :3])
+            return keep, send
+
+        counts = (tall, tall // 2, tall // 2)
+        first, ready, arrived = 0, d_heads, []
         for step, each in enumerate(counts):
             part, within = first // tall, first % tall
             dq, dk_parts, dv_parts = attend_back(
@@ -836,47 +864,40 @@
             dv_parts = [dv_parts[0]] + [lax.ppermute(dv_parts[by], "fsdp", ring(-by)) for by in range(1, group)]
             arrived.append((dq, dk_parts, dv_parts))
             if step == 1:
-                arrived[0][1][0] = after(arrived[0][1][0], dq)
-                weight_sums += sum_parts([arrived[0]])
-                moving = sum_core(weight_sums[0]).astype(BF16)
-                ready = after(d_heads, dq, weight_sums[0], *mixed_arrived)
-            if step == 2:
-                arrived[1][1][0] = after(arrived[1][1][0], dq)
-                moving = after(moving, dq)
-                ready = after(d_heads, dq, moving)
-        early_sum = sum_pairs(moving, dq).astype(BF16)
-        arrived[2][1][0] = after(arrived[2][1][0], dq)
-        weight_sums += sum_parts(arrived[1:3])
-        arrived[3][1][0] = after(arrived[3][1][0], weight_sums[2], sum_rows)
-        weight_sums += sum_parts(arrived[3:])
-        early_sum = sum_side(early_sum, weight_sums[3]).astype(BF16)
+                early = sum_parts(*arrived[0], dq)
+                ready = after(d_heads, dq, early[0])
+        early_sum = sum_core(*early, dq)
+        middle = sum_parts(*arrived[1], dq)
+        last = sum_parts(*arrived[2], middle[0], sum_rows, *mixed_arrived)
+        early_sum = sum_pairs(early_sum, last[0]).astype(BF16)
         if split:
-            rest = after(d_residual, weight_sums[3], early_sum)
+            rest = after(d_residual, last[0], early_sum)
             away_frames, sums_away = input_grads(at_slot, 0, inputs[1], 1, rest, vectors, packed, grads)
-            core_sums = [sum_core(values, away_frames) for values in weight_sums[1:]]
-            core_sums = jnp.concatenate(core_sums, axis=-1).astype(BF16)
-            rest, away_frames, core_sums = lax.optimization_barrier((d_residual, away_frames, core_sums))
+            core_sums = jnp.concatenate([sum_core(*sums, away_frames) for sums in (middle, last)], axis=-1)
+            rest, core_sums, _ = lax.optimization_barrier((d_residual, core_sums, away_frames))
             own_frames, sums_own = input_grads(at_slot, slots, inputs[0], 0, rest, vectors, packed, grads)
             sums_one = sums_own + sums_away
         else:
-            core_sums = jnp.concatenate([sum_core(values) for values in weight_sums[1:]], axis=-1).astype(BF16)
+            core_sums = jnp.concatenate([sum_core(*sums) for sums in (middle, last)], axis=-1)
             both, sums_one = input_grads(at_slot, 0, inputs[0], 0, d_residual, vectors, packed, grads)
             own_frames, away_frames = placed_own(both[:local]), both[local:]
-        frames_arrived = swap_out(away_frames, 3)
+        cut = local * 2 // 3 // 16 * 16
+        frames_arrived = swap_out(away_frames[:cut], after(away_frames[cut:], core_sums))
         side_sums = sum_side(core_sums).astype(BF16)
+        early_sum = sum_side(early_sum, side_sums).astype(BF16)
 
         vector = jnp.concatenate(
             [sums_one[:2], sums_two[: 6 + ups], jnp.concatenate(d_biases).T]
         )
         for_slot = 6
-        vector = after(vector, *frames_arrived[:2])
+        vector = after(vector, frames_arrived[0])
         total = vector
         for by in range(1, group):
             total = total + lax.ppermute(vector, "fsdp", ring(by))
         total, side_sums = lax.optimization_barrier((total, side_sums))
         all_sums = sum_far(jnp.concatenate([early_sum[:, None], side_sums], axis=1))
         sums = [all_sums[0], sum_pairs(all_sums[1:].astype(BF16))]
-        sum_rows, mixed = after(sum_rows, total), after(mixed, total)
+        sum_rows, mixed = after(sum_rows, total).astype(F32), after(mixed, total)
         g_out = sum_rows[:, :width]
         g_up = sum_rows[:, width : width + hidden_width].reshape(shard, ups, n_dp * n_fsdp, shard)
         g_up = g_up.swapaxes(1, 2).reshape(w_up.shape)
@@ -885,7 +906,7 @@
         packs = gather_dp(total).reshape(n_dp, -1, width)
         pack = jnp.concatenate([packs[:, :for_slot].reshape(-1, width), jnp.sum(packs[:, for_slot:], axis=0)])
         pack, g_out, g_up, g_down, mixed, _ = lax.optimization_barrier(
-            (pack, g_out, g_up, g_down, mixed, frames_arrived[2])
+            (pack, g_out, g_up, g_down, mixed, frames_arrived[1])
         )
         grad_frames = placed_away(own_frames, frames_arrived)
         across = shift(pack, "fsdp", n_fsdp, group)

time: 703 us -> 643 us (0.915)
  waiting for transfers between devices: 108 us -> 64.7 us
  local copies, waits for them, and re-layouts: 53.2 us -> 43.5 us
    ppermute x22 -> x21, waiting for transfers between devices: 77.3 us -> 38.2 us  [shift(): lax.ppermute(values, axis, [(i, (i + by) % size) for i in range(size)])]
    pallas_call x4 -> x3, Pallas kernels: 188 us -> 184 us  [attend_back(): pl.pallas_call(functools.partial(attend_back_kernel, parts, chunk), grid=...]
    ppermute x22 -> x21, starting transfers between devices: 30.7 us -> 27.4 us  [shift(): lax.ppermute(values, axis, [(i, (i + by) % size) for i in range(size)])]
    pallas_call x4 -> x3, Pallas kernels: 28.6 us -> 28.1 us  [weight_grads(): pl.pallas_call(functools.partial(weight_grads_kernel, parts, shard if in_...]
  transfers between devices with their start and end apart: 48 -> 44, of which waited for: 12 -> 14; matrix products, arithmetic and copies ran while one was open for 10% -> 10% of each run, Pallas kernels for 53% -> 57%
where the time goes in v7:
time: 643 us; the launch traced here: 634 us
  Pallas kernels  444 us (69%)
  waiting for transfers between devices  64.7 us (10%)
  local copies, waits for them, and re-layouts  43.5 us (7%)
  starting transfers between devices  37 us (6%)
  other arithmetic  28 us (4%)
  between operations  15 us (2%)
    pallas_call x3, Pallas kernels, attend_back(): pl.pallas_call(functools.partial(attend_back_kernel, parts, chunk), grid=...  184 us
    pallas_call x2, Pallas kernels, attend(): pl.pallas_call(functools.partial(attend_kernel, parts, chunk), grid=(head...  103 us
    pallas_call x1, Pallas kernels, feed_forward(): pl.pallas_call(functools.partial(feed_forward_kernel, len(heads_out), pie...  82.3 us
    ppermute x21, waiting for transfers between devices, shift(): lax.ppermute(values, axis, [(i, (i + by) % size) for i in range(size)])  38.2 us
    pallas_call x3, Pallas kernels, weight_grads(): pl.pallas_call(functools.partial(weight_grads_kernel, parts, shard if in_...  28.1 us
    ppermute x21, starting transfers between devices, shift(): lax.ppermute(values, axis, [(i, (i + by) % size) for i in range(size)])  27.4 us
    pallas_call x2, Pallas kernels, input_grads(): pl.pallas_call(functools.partial(input_grads_kernel, [len(kind) for kind...  24 us
    all_gather x1, waiting for transfers between devices, body(): lax.all_gather(jnp.concatenate([w_key, w_value, w_query], axis=1), AXES,...  19.1 us
  transfers between devices with their start and end apart: 44, of which 14 were waited for; matrix products, arithmetic and copies ran while one was open for 10% of the time, Pallas kernels for 57%

profile of v7, /device:TPU:0, one launch (start us, length us, event | category | flops | bytes accessed | tf_op | source)
XLA Modules:
  0.0 634.4 jit_solution(2352030752551309840)
XLA Ops:
  7.2 1.6 pad_maximum_fusion.7
  9.0 3.1 collective-permute-start.1
  12.0 2.1 collective-permute-start.3
  15.1 3.9 dynamic-slice_bitcast_fusion.2
  19.0 1.5 collective-permute-start
  23.8 1.5 collective-permute-start.4
  25.4 2.1 collective-permute-done.4
  30.4 1.5 collective-permute-start.5
  31.9 2.2 multiply_sine_fusion
  34.8 1.3 fusion.18
  36.0 2.2 squeeze.83
  38.2 2.2 collective-permute-done.5
  40.4 1.5 add.309
  41.9 1.2 collective-permute-start.6
  44.2 2.1 collective-permute-start.7
  46.3 1.9 add_compare_fusion
  48.9 4.4 collective-permute-done.8
  53.3 4.3 collective-permute-done.7
  58.4 2.0 dynamic-slice_bitcast_fusion
  60.4 2.3 collective-permute-done.9
  62.7 1.3 compare_select_fusion.1
  66.0 1.2 copy.92
  70.4 19.1 %all-gather.3.cloned.1.call-done.w_ref = bf16[1024,3072]{1,0:T(8,128)(2,1)} async-done(((bf16[32,3072]{1,0:T(8,128)(2,1)}), bf16[1024,3072]{1,0:T(8,128)(2,1)}) %all-gather.3.cloned.1.call-update) | async-done | bytes 6291472 | tf_op jit(solution)/shard_map/all_gather | solution.py:767
  89.5 13.7 %project_kv.1 = (bf16[1536,1024]{1,0:T(8,128)(2,1)}, bf16[512,1536]{1,0:T(8,128)(2,1)}, bf16[512,1536]{1,0:T(8,128)(2,1)}, bf16[512,1536]{1,0:T(8,128)(2,1)}, bf16[512,1536]{1,0:T(8,128)(2,1)}) custom-call(bf16[768,1024]{1,0:T(8,128)(2,1)} %get-tuple-element.184.x_ref.refs_2_, bf16[768,1024]{1,0:T(8,128)(2,1)} %collective-permute-done.y_ref.refs_3_.x_ref, ...), custom_call_target="tpu_custom_call" | custom-call | flops 12884901888 | bytes 16777216 | tf_op jit(solution)/shard_map/project_kv/pallas_call | solution.py:338
  104.0 1.4 collective-permute-start.15
  105.4 8.8 %project_q.1.refs_0_ = bf16[1024,1536]{1,0:T(8,128)(2,1)} custom-call(bf16[1536,1024]{1,0:T(8,128)(2,1)} %get-tuple-element.100.h_ref, f32[16,1024]{1,0:T(8,128)} %pad.8.vectors_ref.refs_8_, bf16[1024,3072]{1,0:T(8,128)(2,1)} %all-gather.3.cloned.1.call-done.w_ref, f32[32,1536]{1,0:T(8,128)} %slice.125.cos_ref, f32[32,1536]{1,0:T(8,128)} %slice.126.sin_ref), custom_call_target="tpu_custom_call" | custom-call | flops 6442450944 | bytes 8388608 | tf_op jit(solution)/shard_map/project_q/pallas_call | solution.py:352
  114.2 51.6 %attend.3 = (bf16[512,1536]{1,0:T(8,128)(2,1)}, f32[8,1,1536]{2,1,0:T(1,128)}) custom-call(bf16[1024,1536]{1,0:T(8,128)(2,1)} %project_q.1.refs_0_, bf16[3072,64]{1,0:T(8,128)(2,1)} %pad.9.refs_1_, bf16[512,1536]{1,0:T(8,128)(2,1)} %get-tuple-element.105.refs_2_.refs_7_, bf16[512,1536]{1,0:T(8,128)(2,1)} %collective-permute-done.13.refs_3_.refs_8_, ...), custom_call_target="tpu_custom_call" | custom-call | flops 38654705664 | bytes 9437184 | tf_op jit(solution)/shard_map/attend/pallas_call | solution.py:91
  165.8 51.5 %attend.2 = (bf16[512,1536]{1,0:T(8,128)(2,1)}, f32[8,1,1536]{2,1,0:T(1,128)}) custom-call(bf16[1024,1536]{1,0:T(8,128)(2,1)} %project_q.1.refs_0_, bf16[3072,64]{1,0:T(8,128)(2,1)} %pad.9.refs_1_, bf16[512,1536]{1,0:T(8,128)(2,1)} %get-tuple-element.102.refs_2_.refs_7_, bf16[512,1536]{1,0:T(8,128)(2,1)} %collective-permute-done.11.refs_3_.refs_8_, ...), custom_call_target="tpu_custom_call" | custom-call | flops 38654705664 | bytes 9437184 | tf_op jit(solution)/shard_map/attend/pallas_call | solution.py:91
  217.3 82.3 %feed_forward.1 = (bf16[2,768,1024]{2,1,0:T(8,128)(2,1)}, bf16[768,1024]{1,0:T(8,128)(2,1)}, f32[1536,1024]{1,0:T(8,128)}, bf16[1024,1536]{1,0:T(8,128)(2,1)}, b...) custom-call(s32[1]{0:T(128)} %bitcast.slot_ref, bf16[512,1536]{1,0:T(8,128)(2,1)} %get-tuple-element.104.refs_0_.refs_2_, ...), custom_call_target="tpu_custom_call" | custom-call | flops 48318382080 | bytes 33554432 | tf_op jit(solution)/shard_map/feed_forward/pallas_call | solution.py:466
  299.6 90.7 %attend_back.4 = (bf16[512,1536]{1,0:T(8,128)(2,1)}, f32[512,1536]{1,0:T(8,128)}, bf16[512,1536]{1,0:T(8,128)(2,1)}, f32[512,1536]{1,0:T(8,128)}, bf16[512,1536]{1,0:T(8,128)(2,1)}) custom-call(bf16[1024,1536]{1,0:T(8,128)(2,1)} %project_q.1.refs_0_, bf16[1024,1536]{1,0:T(8,128)(2,1)} %get-tuple-element.126.refs_1_, ...), custom_call_target="tpu_custom_call" | custom-call | flops 12079595520 | tf_op jit(solution)/shard_map/attend_back/pallas_call | solution.py:223
  391.0 46.9 %attend_back.3 = (bf16[256,1536]{1,0:T(8,128)(2,1)}, f32[256,1536]{1,0:T(8,128)}, bf16[256,1536]{1,0:T(8,128)(2,1)}, f32[256,1536]{1,0:T(8,128)}, bf16[256,1536]{1,0:T(8,128)(2,1)}) custom-call(bf16[1024,1536]{1,0:T(8,128)(2,1)} %project_q.1.refs_0_, bf16[1024,1536]{1,0:T(8,128)(2,1)} %get-tuple-element.126.refs_1_, ...), custom_call_target="tpu_custom_call" | custom-call | flops 6039797760 | tf_op jit(solution)/shard_map/attend_back/pallas_call | solution.py:223
  438.0 1.1 copy-done.7
  439.1 12.0 %weight_grads.3 = (bf16[512,1536]{1,0:T(8,128)(2,1)}, bf16[512,1536]{1,0:T(8,128)(2,1)}, bf16[512,1536]{1,0:T(8,128)(2,1)}, bf16[512,1536]{1,0:T(8,128)(2,1)}, f32[512,128]{1,0:T(8,128)}) custom-call(s32[1]{0:T(128)} %bitcast.19.core_ref, bf16[1536,1024]{1,0:T(8,128)(2,1)} %get-tuple-element.100.h_ref, bf16[512,1536]{1,0:T(8,128)(2,1)} %get-tuple-element.119.dq_ref.refs_0_, ...), custom_call_target="tpu_custom_call" | custom-call | tf_op jit(solution)/shard_map/weight_grads/pallas_call | solution.py:555
  452.8 46.8 %attend_back.5 = (bf16[256,1536]{1,0:T(8,128)(2,1)}, f32[256,1536]{1,0:T(8,128)}, bf16[256,1536]{1,0:T(8,128)(2,1)}, f32[256,1536]{1,0:T(8,128)}, bf16[256,1536]{1,0:T(8,128)(2,1)}) custom-call(bf16[1024,1536]{1,0:T(8,128)(2,1)} %project_q.1.refs_0_, bf16[1024,1536]{1,0:T(8,128)(2,1)} %get-tuple-element.126.refs_1_, ...), custom_call_target="tpu_custom_call" | custom-call | flops 6039797760 | tf_op jit(solution)/shard_map/attend_back/pallas_call | solution.py:223
  500.9 2.3 add_convert_fusion
  504.2 1.3 collective-permute-start.25
  505.6 8.2 %weight_grads.4 = (bf16[256,1536]{1,0:T(8,128)(2,1)}, bf16[256,1536]{1,0:T(8,128)(2,1)}, bf16[512,768]{1,0:T(8,128)(2,1)}, bf16[512,768]{1,0:T(8,128)(2,1)}, f32[256,128]{1,0:T(8,128)}) custom-call(s32[1]{0:T(128)} %bitcast.19.core_ref, bf16[1536,1024]{1,0:T(8,128)(2,1)} %get-tuple-element.100.h_ref, bf16[256,1536]{1,0:T(8,128)(2,1)} %get-tuple-element.116.dq_ref.refs_1_, ...), custom_call_target="tpu_custom_call" | custom-call | tf_op jit(solution)/shard_map/weight_grads/pallas_call | solution.py:555
  515.1 7.8 %weight_grads.5 = (bf16[256,1536]{1,0:T(8,128)(2,1)}, bf16[256,1536]{1,0:T(8,128)(2,1)}, bf16[512,768]{1,0:T(8,128)(2,1)}, bf16[512,768]{1,0:T(8,128)(2,1)}, f32[256,128]{1,0:T(8,128)}) custom-call(s32[1]{0:T(128)} %bitcast.19.core_ref, bf16[1536,1024]{1,0:T(8,128)(2,1)} %get-tuple-element.100.h_ref, bf16[256,1536]{1,0:T(8,128)(2,1)} %get-tuple-element.127.dq_ref.refs_2_, ...), custom_call_target="tpu_custom_call" | custom-call | tf_op jit(solution)/shard_map/weight_grads/pallas_call | solution.py:555
  523.3 1.1 collective-permute-done.25
  524.4 2.2 fusion.2
  526.6 12.0 %input_grads.2 = (bf16[768,1024]{1,0:T(8,128)(2,1)}, f32[8,1024]{1,0:T(8,128)}) custom-call(s32[1]{0:T(128)} %bitcast.slot_ref, bf16[768,1024]{1,0:T(8,128)(2,1)} %collective-permute-done.y_ref.refs_3_.x_ref, f32[1536,1024]{1,0:T(8,128)} %get-tuple-element.156.d_res_ref, f32[16,1024]{1,0:T(8,128)} %pad.8.vectors_ref.refs_8_, ...), custom_call_target="tpu_custom_call" | custom-call | flops 12884901888 | bytes 17301504 | tf_op jit(solution)/shard_map/input_grads/pallas_call | solution.py:622
  538.7 1.9 slice.140
  540.6 2.4 slice.133
  543.1 1.4 collective-permute-start.36
  545.2 1.3 add_convert_fusion.2
  546.5 1.3 add_convert_fusion.1
  547.9 1.5 collective-permute-start.34
  551.1 12.0 %input_grads.3 = (bf16[2,768,1024]{2,1,0:T(8,128)(2,1)}, f32[8,1024]{1,0:T(8,128)}) custom-call(s32[1]{0:T(128)} %bitcast.slot_ref, bf16[768,1024]{1,0:T(8,128)(2,1)} %get-tuple-element.184.x_ref.refs_2_, f32[1536,1024]{1,0:T(8,128)} %get-tuple-element.156.d_res_ref, f32[16,1024]{1,0:T(8,128)} %pad.8.vectors_ref.refs_8_, ...), custom_call_target="tpu_custom_call" | custom-call | flops 12884901888 | bytes 17301504 | tf_op jit(solution)/shard_map/input_grads/pallas_call | solution.py:622
  563.9 7.1 %collective-permute-done.27 = bf16[512,1024]{1,0:T(8,128)(2,1)} collective-permute-done((bf16[512,1024]{1,0:T(8,128)(2,1)}, bf16[512,1024]{1,0:T(8,128)(2,1)}, u32[]{:S(2)}, u32[]{:S(2)}) %collective-permute-start.27) | collective-permute-done | bytes 1048608 | tf_op jit(solution)/shard_map/ppermute | solution.py:668
  571.0 2.3 bitcast_dynamic-update-slice_fusion.1
  573.3 7.3 %collective-permute-done.34 = bf16[256,1024]{1,0:T(8,128)(2,1)} collective-permute-done((bf16[256,1024]{1,0:T(8,128)(2,1)}, bf16[256,1024]{1,0:T(8,128)(2,1)}, u32[]{:S(2)}, u32[]{:S(2)}) %collective-permute-start.34) | collective-permute-done | bytes 524320 | tf_op jit(solution)/shard_map/ppermute | solution.py:668
  580.6 1.9 bitcast_dynamic-update-slice_fusion.2
  582.5 1.4 fusion.1
  583.9 2.0 collective-permute-start.32
  587.8 1.1 fusion.6
  590.5 1.6 collective-permute-start.37
  592.1 1.9 collective-permute-start.38
  596.0 2.1 reshape.252
  599.4 2.7 bitcast_dynamic-update-slice_fusion
  602.1 3.0 collective-permute-done.33
  606.0 6.2 collective-permute-done.38
  612.9 1.2 fusion.5
  614.9 4.0 collective-permute-done.40
  623.7 1.5 fusion.28
  (245 shorter events, 41.9 us)
Async XLA Ops:
  7.2 20.8 %copy-start = (bf16[32,6144]{1,0:T(8,128)(2,1)S(1)}, bf16[32,6144]{1,0:T(8,128)(2,1)}, u32[]{:S(2)}) copy-start(bf16[32,6144]{1,0:T(8,128)(2,1)} %param.21) | copy-start | bytes 1179652
  7.2 82.3 %all-gather.3.cloned.1.call-start = ((), (), s32[]{:S(2)}) async-start(), calls=%async_computation.1 | async-start | bytes 6488064 | tf_op jit(solution)/shard_map/all_gather | solution.py:767
  8.9 208.4 %all-gather.5.cloned.1.call-start = ((), (), s32[]{:S(2)}) async-start(), calls=%async_computation.2 | async-start | bytes 10813440 | tf_op jit(solution)/shard_map/all_gather | solution.py:771
  9.0 14.7 %collective-permute-start.1 = (s32[2]{0:T(128)}, s32[2]{0:T(128)S(1)}, u32[]{:S(2)}, u32[]{:S(2)}) collective-permute-start(s32[2]{0:T(128)} %param.20), channel_id=1, source_target_pairs={{0,8},{4,12},{8,16},{12,20},{16,24},{20,28},{24,0},{28,4},{1,9},{5... | collective-permute-start | bytes 32 | tf_op jit(solution)/shard_map/ppermute | solution.py:668
  12.0 11.7 %collective-permute-start.3 = (s32[2]{0:T(128)}, s32[2]{0:T(128)S(1)}, u32[]{:S(2)}, u32[]{:S(2)}) collective-permute-start(s32[2]{0:T(128)} %param.20), channel_id=1, source_target_pairs={{0,24},{4,28},{8,0},{12,4},{16,8},{20,12},{24,16},{28,20},{1,25},{... | collective-permute-start | bytes 32 | tf_op jit(solution)/shard_map/ppermute | solution.py:668
  14.1 9.6 %collective-permute-start.2 = (s32[2]{0:T(128)}, s32[2]{0:T(128)S(1)}, u32[]{:S(2)}, u32[]{:S(2)}) collective-permute-start(s32[2]{0:T(128)} %param.20), channel_id=1, source_target_pairs={{0,16},{4,20},{8,24},{12,28},{16,0},{20,4},{24,8},{28,12},{1,17},{... | collective-permute-start | bytes 32 | tf_op jit(solution)/shard_map/ppermute | solution.py:668
  15.1 5.4 copy-start.18
  19.0 2.6 copy-start.19
  19.0 2.7 copy-start.21
  19.0 51.4 %collective-permute-start = (bf16[768,1024]{1,0:T(8,128)(2,1)}, bf16[768,1024]{1,0:T(8,128)(2,1)}, u32[]{:S(2)}, u32[]{:S(2)}) collective-permute-start(bf16[768,1024]{1,0:T(8,128)(2,1)} %get-tuple-element.183), channel_id=1, source_target_pairs={{0,2},{1,3},{2,0},{3,1},{4,6},{5,7},{6,4},{7,5},{8,10},{9,11},{10,... | collective-permute-start | bytes 4718600 | tf_op jit(solution)/shard_map/ppermute | solution.py:668
  20.9 2.5 copy-start.32
  20.9 2.6 copy-start.25
  20.9 2.8 copy-start.26
  22.4 492.6 %reduce-scatter.2.cloned.1.call-start = ((), (), s32[]{:S(2)}) async-start(), calls=%async_computation.3 | async-start | bytes 10813440 | tf_op jit(solution)/shard_map/reduce_scatter | solution.py:831
  23.8 3.6 collective-permute-start.4
  28.6 5.6 copy-start.33
  30.4 10.0 %collective-permute-start.5 = (f32[4,2,13312]{2,1,0:T(2,128)}, f32[4,2,13312]{2,1,0:T(2,128)}, u32[]{:S(2)}, u32[]{:S(2)}) collective-permute-start(f32[4,2,13312]{2,1,0:T(2,128)} %squeeze.84), channel_id=1, source_target_pairs={{0,4},{4,0},{8,12},{12,8},{16,20},{20,16},{24,28},{28,24},{1,5},{5... | collective-permute-start | bytes 1277960 | tf_op jit(solution)/shard_map/ppermute | solution.py:736
  34.1 35.5 %copy-start.9 = (f32[32,3072]{1,0:T(8,128)}, f32[32,3072]{1,0:T(8,128)S(1)}, u32[]{:S(2)}) copy-start(f32[32,3072]{1,0:T(8,128)S(1)} %get-tuple-element.99.refs_6_) | copy-start | bytes 1179652
  36.0 22.4 %copy-start.4 = (bf16[2,768,1024]{2,1,0:T(8,128)(2,1)S(1)}, bf16[2,768,1024]{2,1,0:T(8,128)(2,1)}, u32[]{:S(2)}) copy-start(bf16[2,768,1024]{2,1,0:T(8,128)(2,1)} %param.35) | copy-start | bytes 9437188
  41.9 7.0 %collective-permute-start.6 = (f32[2,13312]{1,0:T(2,128)S(1)}, f32[2,13312]{1,0:T(2,128)S(1)}, u32[]{:S(2)}, u32[]{:S(2)}) collective-permute-start(f32[2,13312]{1,0:T(2,128)S(1)} %get-tuple-element.192), channel_id=1, source_target_pairs={{0,24},{4,28},{8,0},{12,4},{16,8},{20,12},{24,16},{28,20},{1,25},{... | collective-permute-start | bytes 319496 | tf_op jit(solution)/shard_map/ppermute | solution.py:668
  43.2 10.1 %collective-permute-start.8 = (f32[2,13312]{1,0:T(2,128)S(1)}, f32[2,13312]{1,0:T(2,128)S(1)}, u32[]{:S(2)}, u32[]{:S(2)}) collective-permute-start(f32[2,13312]{1,0:T(2,128)S(1)} %get-tuple-element.193), channel_id=1, source_target_pairs={{0,8},{4,12},{8,16},{12,20},{16,24},{20,28},{24,0},{28,4},{1,9},{5... | collective-permute-start | bytes 319496 | tf_op jit(solution)/shard_map/ppermute | solution.py:668
  44.2 13.5 %collective-permute-start.7 = (f32[2,13312]{1,0:T(2,128)S(1)}, f32[2,13312]{1,0:T(2,128)S(1)}, u32[]{:S(2)}, u32[]{:S(2)}) collective-permute-start(f32[2,13312]{1,0:T(2,128)S(1)} %get-tuple-element.194), channel_id=1, source_target_pairs={{0,16},{4,20},{8,24},{12,28},{16,0},{20,4},{24,8},{28,12},{1,17},{... | collective-permute-start | bytes 319496 | tf_op jit(solution)/shard_map/ppermute | solution.py:668
  57.8 4.8 collective-permute-start.9
  62.7 5.6 collective-permute-start.10
  66.0 2.9 copy-start.10
  89.5 14.5 %copy-start.6 = (bf16[768,1024]{1,0:T(8,128)(2,1)S(1)}, bf16[768,1024]{1,0:T(8,128)(2,1)}, u32[]{:S(2)}) copy-start(bf16[768,1024]{1,0:T(8,128)(2,1)} %get-tuple-element.110) | copy-start | bytes 4718596
  103.1 11.1 %collective-permute-start.13 = (bf16[512,1536]{1,0:T(8,128)(2,1)}, bf16[512,1536]{1,0:T(8,128)(2,1)}, u32[]{:S(2)}, u32[]{:S(2)}) collective-permute-start(bf16[512,1536]{1,0:T(8,128)(2,1)} %get-tuple-element.105.refs_2_.refs_7_), channel_id=1, source_target_pairs={{0,1},{1,0},{2,3},{3,2},{4,5},{5,4},{6,7},{7,6},{8,9},{9,8},{10,11... | collective-permute-start | bytes 4718600 | tf_op jit(solution)/shard_map/ppermute | solution.py:816
  103.4 10.8 %collective-permute-start.14 = (bf16[512,1536]{1,0:T(8,128)(2,1)}, bf16[512,1536]{1,0:T(8,128)(2,1)}, u32[]{:S(2)}, u32[]{:S(2)}) collective-permute-start(bf16[512,1536]{1,0:T(8,128)(2,1)} %get-tuple-element.106.refs_4_.refs_9_), channel_id=1, source_target_pairs={{0,1},{1,0},{2,3},{3,2},{4,5},{5,4},{6,7},{7,6},{8,9},{9,8},{10,11... | collective-permute-start | bytes 4718600 | tf_op jit(solution)/shard_map/ppermute | solution.py:816
  103.7 62.2 %collective-permute-start.11 = (bf16[512,1536]{1,0:T(8,128)(2,1)}, bf16[512,1536]{1,0:T(8,128)(2,1)}, u32[]{:S(2)}, u32[]{:S(2)}) collective-permute-start(bf16[512,1536]{1,0:T(8,128)(2,1)} %get-tuple-element.102.refs_2_.refs_7_), channel_id=1, source_target_pairs={{0,1},{1,0},{2,3},{3,2},{4,5},{5,4},{6,7},{7,6},{8,9},{9,8},{10,11... | collective-permute-start | bytes 4718600 | tf_op jit(solution)/shard_map/ppermute | solution.py:816
  104.0 113.3 %collective-permute-start.15 = (bf16[768,1024]{1,0:T(8,128)(2,1)S(1)}, bf16[768,1024]{1,0:T(8,128)(2,1)}, u32[]{:S(2)}, u32[]{:S(2)}) collective-permute-start(bf16[768,1024]{1,0:T(8,128)(2,1)S(1)} %copy-done.6), channel_id=1, source_target_pairs={{0,2},{1,3},{2,0},{3,1},{4,6},{5,7},{6,4},{7,5},{8,10},{9,11},{10,... | collective-permute-start | bytes 4718600 | tf_op jit(solution)/shard_map/ppermute | solution.py:668
  105.4 60.5 %collective-permute-start.12 = (bf16[512,1536]{1,0:T(8,128)(2,1)}, bf16[512,1536]{1,0:T(8,128)(2,1)}, u32[]{:S(2)}, u32[]{:S(2)}) collective-permute-start(bf16[512,1536]{1,0:T(8,128)(2,1)} %get-tuple-element.103.refs_4_.refs_9_), channel_id=1, source_target_pairs={{0,1},{1,0},{2,3},{3,2},{4,5},{5,4},{6,7},{7,6},{8,9},{9,8},{10,11... | collective-permute-start | bytes 4718600 | tf_op jit(solution)/shard_map/ppermute | solution.py:816
  390.3 47.6 %collective-permute-start.16 = (bf16[512,1536]{1,0:T(8,128)(2,1)}, bf16[512,1536]{1,0:T(8,128)(2,1)S(1)}, u32[]{:S(2)}, u32[]{:S(2)}) collective-permute-start(bf16[512,1536]{1,0:T(8,128)(2,1)} %get-tuple-element.122), channel_id=1, source_target_pairs={{0,1},{1,0},{2,3},{3,2},{4,5},{5,4},{6,7},{7,6},{8,9},{9,8},{10,11... | collective-permute-start | bytes 4718600 | tf_op jit(solution)/shard_map/ppermute | solution.py:863
  390.9 47.0 %collective-permute-start.17 = (bf16[512,1536]{1,0:T(8,128)(2,1)}, bf16[512,1536]{1,0:T(8,128)(2,1)}, u32[]{:S(2)}, u32[]{:S(2)}) collective-permute-start(bf16[512,1536]{1,0:T(8,128)(2,1)} %get-tuple-element.124), channel_id=1, source_target_pairs={{0,1},{1,0},{2,3},{3,2},{4,5},{5,4},{6,7},{7,6},{8,9},{9,8},{10,11... | collective-permute-start | bytes 4718600 | tf_op jit(solution)/shard_map/ppermute | solution.py:864
  451.1 48.6 %collective-permute-start.24 = (bf16[512,1536]{1,0:T(8,128)(2,1)}, bf16[512,1536]{1,0:T(8,128)(2,1)S(1)}, u32[]{:S(2)}, u32[]{:S(2)}) collective-permute-start(bf16[512,1536]{1,0:T(8,128)(2,1)} %get-tuple-element.142), channel_id=1, source_target_pairs={{0,1},{1,0},{2,3},{3,2},{4,5},{5,4},{6,7},{7,6},{8,9},{9,8},{10,11... | collective-permute-start | bytes 4718600 | tf_op jit(solution)/shard_map/ppermute | solution.py:736
  451.6 63.5 %collective-permute-start.21 = (bf16[768,1024]{1,0:T(8,128)(2,1)}, bf16[768,1024]{1,0:T(8,128)(2,1)}, u32[]{:S(2)}, u32[]{:S(2)}) collective-permute-start(bf16[768,1024]{1,0:T(8,128)(2,1)} %get-tuple-element.136), channel_id=1, source_target_pairs={{0,2},{1,3},{2,0},{3,1},{4,6},{5,7},{6,4},{7,5},{8,10},{9,11},{10,... | collective-permute-start | bytes 4718600 | tf_op jit(solution)/shard_map/ppermute | solution.py:668
  452.3 51.9 %collective-permute-start.18 = (bf16[256,1536]{1,0:T(8,128)(2,1)}, bf16[256,1536]{1,0:T(8,128)(2,1)}, u32[]{:S(2)}, u32[]{:S(2)}) collective-permute-start(bf16[256,1536]{1,0:T(8,128)(2,1)} %get-tuple-element.129), channel_id=1, source_target_pairs={{0,1},{1,0},{2,3},{3,2},{4,5},{5,4},{6,7},{7,6},{8,9},{9,8},{10,11... | collective-permute-start | bytes 2359304 | tf_op jit(solution)/shard_map/ppermute | solution.py:863
  452.3 53.3 %collective-permute-start.19 = (bf16[256,1536]{1,0:T(8,128)(2,1)}, bf16[256,1536]{1,0:T(8,128)(2,1)}, u32[]{:S(2)}, u32[]{:S(2)}) collective-permute-start(bf16[256,1536]{1,0:T(8,128)(2,1)} %get-tuple-element.131), channel_id=1, source_target_pairs={{0,1},{1,0},{2,3},{3,2},{4,5},{5,4},{6,7},{7,6},{8,9},{9,8},{10,11... | collective-permute-start | bytes 2359304 | tf_op jit(solution)/shard_map/ppermute | solution.py:864
  499.6 15.4 %collective-permute-start.22 = (bf16[256,1536]{1,0:T(8,128)(2,1)}, bf16[256,1536]{1,0:T(8,128)(2,1)}, u32[]{:S(2)}, u32[]{:S(2)}) collective-permute-start(bf16[256,1536]{1,0:T(8,128)(2,1)} %get-tuple-element.138), channel_id=1, source_target_pairs={{0,1},{1,0},{2,3},{3,2},{4,5},{5,4},{6,7},{7,6},{8,9},{9,8},{10,11... | collective-permute-start | bytes 2359304 | tf_op jit(solution)/shard_map/ppermute | solution.py:863
  499.7 15.3 %collective-permute-start.23 = (bf16[256,1536]{1,0:T(8,128)(2,1)}, bf16[256,1536]{1,0:T(8,128)(2,1)}, u32[]{:S(2)}, u32[]{:S(2)}) collective-permute-start(bf16[256,1536]{1,0:T(8,128)(2,1)} %get-tuple-element.140), channel_id=1, source_target_pairs={{0,1},{1,0},{2,3},{3,2},{4,5},{5,4},{6,7},{7,6},{8,9},{9,8},{10,11... | collective-permute-start | bytes 2359304 | tf_op jit(solution)/shard_map/ppermute | solution.py:864
  504.2 20.3 %collective-permute-start.25 = (bf16[8,32,1536]{2,1,0:T(8,128)(2,1)}, bf16[8,32,1536]{2,1,0:T(8,128)(2,1)}, u32[]{:S(2)}, u32[]{:S(2)}) collective-permute-start(bf16[8,32,1536]{2,1,0:T(8,128)(2,1)} %dynamic-slice_bitcast_fusion.5), channel_id=1, source_target_pairs={{0,2},{1,3},{2,0},{3,1},{4,6},{5,7},{6,4},{7,5},{8,10},{9,11},{10,... | collective-permute-start | bytes 2359304 | tf_op jit(solution)/shard_map/ppermute | solution.py:668
  514.8 28.3 %collective-permute-start.20 = (bf16[512,768]{1,0:T(8,128)(2,1)}, bf16[512,768]{1,0:T(8,128)(2,1)}, u32[]{:S(2)}, u32[]{:S(2)}) collective-permute-start(bf16[512,768]{1,0:T(8,128)(2,1)} %get-tuple-element.133), channel_id=1, source_target_pairs={{0,1},{1,0},{2,3},{3,2},{4,5},{5,4},{6,7},{7,6},{8,9},{9,8},{10,11... | collective-permute-start | bytes 2359304 | tf_op jit(solution)/shard_map/ppermute | solution.py:736
  522.9 23.6 %collective-permute-start.26 = (bf16[512,768]{1,0:T(8,128)(2,1)}, bf16[512,768]{1,0:T(8,128)(2,1)}, u32[]{:S(2)}, u32[]{:S(2)}) collective-permute-start(bf16[512,768]{1,0:T(8,128)(2,1)} %get-tuple-element.154), channel_id=1, source_target_pairs={{0,1},{1,0},{2,3},{3,2},{4,5},{5,4},{6,7},{7,6},{8,9},{9,8},{10,11... | collective-permute-start | bytes 2359304 | tf_op jit(solution)/shard_map/ppermute | solution.py:736
  538.6 4.4 copy-start.20
  538.7 4.4 copy-start.2
  540.6 4.5 copy-start.11
  543.1 3.4 copy-start.12
  543.1 44.6 %collective-permute-start.36 = (bf16[4,32,1536]{2,1,0:T(8,128)(2,1)S(1)}, bf16[4,32,1536]{2,1,0:T(8,128)(2,1)}, u32[]{:S(2)}, u32[]{:S(2)}) collective-permute-start(bf16[4,32,1536]{2,1,0:T(8,128)(2,1)S(1)} %dynamic-slice_bitcast_fusion.6), channel_id=1, source_target_pairs={{0,4},{4,0},{8,12},{12,8},{16,20},{20,16},{24,28},{28,24},{1,5},{5... | collective-permute-start | bytes 1179656 | tf_op jit(solution)/shard_map/ppermute | solution.py:736
  544.6 26.4 %collective-permute-start.27 = (bf16[512,1024]{1,0:T(8,128)(2,1)}, bf16[512,1024]{1,0:T(8,128)(2,1)}, u32[]{:S(2)}, u32[]{:S(2)}) collective-permute-start(bf16[512,1024]{1,0:T(8,128)(2,1)} %slice.133), channel_id=1, source_target_pairs={{0,2},{1,3},{2,0},{3,1},{4,6},{5,7},{6,4},{7,5},{8,10},{9,11},{10,... | collective-permute-start | bytes 3145736 | tf_op jit(solution)/shard_map/ppermute | solution.py:668
  547.9 32.7 %collective-permute-start.34 = (bf16[256,1024]{1,0:T(8,128)(2,1)}, bf16[256,1024]{1,0:T(8,128)(2,1)}, u32[]{:S(2)}, u32[]{:S(2)}) collective-permute-start(bf16[256,1024]{1,0:T(8,128)(2,1)} %slice.140), channel_id=1, source_target_pairs={{0,2},{1,3},{2,0},{3,1},{4,6},{5,7},{6,4},{7,5},{8,10},{9,11},{10,... | collective-permute-start | bytes 1572872 | tf_op jit(solution)/shard_map/ppermute | solution.py:668
  550.4 13.5 %copy-start.22 = (f32[8,1024]{1,0:T(8,128)S(1)}, f32[8,1024]{1,0:T(8,128)}, u32[]{:S(2)}) copy-start(f32[8,1024]{1,0:T(8,128)} %get-tuple-element.159) | copy-start | bytes 98308
  550.4 32.1 %collective-permute-start.29 = (bf16[4,2,32,1536]{3,2,1,0:T(8,128)(2,1)}, bf16[4,2,32,1536]{3,2,1,0:T(8,128)(2,1)}, u32[]{:S(2)}, u32[]{:S(2)}) collective-permute-start(bf16[4,2,32,1536]{3,2,1,0:T(8,128)(2,1)} %dynamic-slice_bitcast_fusion.4), channel_id=1, source_target_pairs={{0,4},{4,0},{8,12},{12,8},{16,20},{20,16},{24,28},{28,24},{1,5},{5... | collective-permute-start | bytes 2359304 | tf_op jit(solution)/shard_map/ppermute | solution.py:736
  571.0 2.3 collective-permute-start.28
  573.3 14.5 %copy-start.3 = (bf16[8,32,1536]{2,1,0:T(8,128)(2,1)S(1)}, bf16[8,32,1536]{2,1,0:T(8,128)(2,1)}, u32[]{:S(2)}) copy-start(bf16[8,32,1536]{2,1,0:T(8,128)(2,1)} %fusion.2) | copy-start | bytes 2359300
  582.5 6.4 %copy-start.8 = (bf16[32,5120]{1,0:T(8,128)(2,1)S(1)}, bf16[32,5120]{1,0:T(8,128)(2,1)}, u32[]{:S(2)}) copy-start(bf16[32,5120]{1,0:T(8,128)(2,1)} %reduce-scatter.2.cloned.1.call-done) | copy-start | bytes 983044
  583.9 14.2 %collective-permute-start.32 = (f32[13,1024]{1,0:T(8,128)S(1)}, f32[13,1024]{1,0:T(8,128)S(1)}, u32[]{:S(2)}, u32[]{:S(2)}) collective-permute-start(f32[13,1024]{1,0:T(8,128)S(1)} %add.346), channel_id=1, source_target_pairs={{0,24},{4,28},{8,0},{12,4},{16,8},{20,12},{24,16},{28,20},{1,25},{... | collective-permute-start | bytes 159752 | tf_op jit(solution)/shard_map/ppermute | solution.py:668
  585.9 12.8 %collective-permute-start.31 = (f32[13,1024]{1,0:T(8,128)S(1)}, f32[13,1024]{1,0:T(8,128)S(1)}, u32[]{:S(2)}, u32[]{:S(2)}) collective-permute-start(f32[13,1024]{1,0:T(8,128)S(1)} %add.346), channel_id=1, source_target_pairs={{0,16},{4,20},{8,24},{12,28},{16,0},{20,4},{24,8},{28,12},{1,17},{... | collective-permute-start | bytes 159752 | tf_op jit(solution)/shard_map/ppermute | solution.py:668
  586.9 11.8 %collective-permute-start.30 = (f32[13,1024]{1,0:T(8,128)S(1)}, f32[13,1024]{1,0:T(8,128)S(1)}, u32[]{:S(2)}, u32[]{:S(2)}) collective-permute-start(f32[13,1024]{1,0:T(8,128)S(1)} %add.346), channel_id=1, source_target_pairs={{0,8},{4,12},{8,16},{12,20},{16,24},{20,28},{24,0},{28,4},{1,9},{5... | collective-permute-start | bytes 159752 | tf_op jit(solution)/shard_map/ppermute | solution.py:668
  590.5 15.5 %collective-permute-start.37 = (bf16[3,32,1536]{2,1,0:T(8,128)(2,1)}, bf16[3,32,1536]{2,1,0:T(8,128)(2,1)}, u32[]{:S(2)}, u32[]{:S(2)}) collective-permute-start(bf16[3,32,1536]{2,1,0:T(8,128)(2,1)} %get-tuple-element.185), channel_id=1, source_target_pairs={{0,8},{4,12},{8,16},{12,20},{16,24},{20,28},{24,0},{28,4},{1,9},{5... | collective-permute-start | bytes 884744 | tf_op jit(solution)/shard_map/ppermute | solution.py:668
  592.1 20.1 %collective-permute-start.38 = (bf16[3,32,1536]{2,1,0:T(8,128)(2,1)}, bf16[3,32,1536]{2,1,0:T(8,128)(2,1)}, u32[]{:S(2)}, u32[]{:S(2)}) collective-permute-start(bf16[3,32,1536]{2,1,0:T(8,128)(2,1)} %get-tuple-element.186), channel_id=1, source_target_pairs={{0,16},{4,20},{8,24},{12,28},{16,0},{20,4},{24,8},{28,12},{1,17},{... | collective-permute-start | bytes 884744 | tf_op jit(solution)/shard_map/ppermute | solution.py:668
  598.0 14.8 %collective-permute-start.39 = (bf16[3,32,1536]{2,1,0:T(8,128)(2,1)}, bf16[3,32,1536]{2,1,0:T(8,128)(2,1)S(1)}, u32[]{:S(2)}, u32[]{:S(2)}) collective-permute-start(bf16[3,32,1536]{2,1,0:T(8,128)(2,1)} %get-tuple-element.187), channel_id=1, source_target_pairs={{0,24},{4,28},{8,0},{12,4},{16,8},{20,12},{24,16},{28,20},{1,25},{... | collective-permute-start | bytes 884744 | tf_op jit(solution)/shard_map/ppermute | solution.py:668
  598.7 6.4 %collective-permute-start.33 = (f32[4,13,1024]{2,1,0:T(8,128)S(1)}, f32[4,13,1024]{2,1,0:T(8,128)S(1)}, u32[]{:S(2)}, u32[]{:S(2)}) collective-permute-start(f32[4,13,1024]{2,1,0:T(8,128)S(1)} %get-tuple-element.199), channel_id=1, source_target_pairs={{0,4},{4,0},{8,12},{12,8},{16,20},{20,16},{24,28},{28,24},{1,5},{5... | collective-permute-start | bytes 638984 | tf_op jit(solution)/shard_map/ppermute | solution.py:736
  605.3 16.3 %collective-permute-start.35 = (f32[55,1024]{1,0:T(8,128)S(1)}, f32[55,1024]{1,0:T(8,128)S(1)}, u32[]{:S(2)}, u32[]{:S(2)}) collective-permute-start(f32[55,1024]{1,0:T(8,128)S(1)} %pad_maximum_fusion.6), channel_id=1, source_target_pairs={{0,2},{1,3},{2,0},{3,1},{4,6},{5,7},{6,4},{7,5},{8,10},{9,11},{10,... | collective-permute-start | bytes 675848 | tf_op jit(solution)/shard_map/ppermute | solution.py:668
  614.3 4.7 collective-permute-start.40
  622.8 4.9 copy-start.1
  (14 other events, 23.3 us)
Sparse Core Ops, SparseCore 0:
  11.5 77.9 all-gather.2
  92.3 94.9 all-gather.4
  299.8 151.5 reduce-scatter.1

commit v8 on v7

--- a/solution.py
+++ b/solution.py
@@ -585,8 +585,9 @@
     return dk, dv, keep, send, bias
 
 
-def input_grads_kernel(counts, slot_ref, x_ref, d_res_ref, vectors_ref, w_ref, *refs):
-    grad_refs, (out_ref, sums_ref) = refs[:-2], refs[-2:]
+def input_grads_kernel(counts, cut, slot_ref, x_ref, d_res_ref, vectors_ref, w_ref, *refs):
+    outs = 2 if cut else 1
+    grad_refs, out_refs, sums_ref = refs[: -outs - 1], refs[-outs - 1 : -1], refs[-1]
     width = x_ref.shape[1]
 
     @pl.when(pl.program_id(0) == 0)
@@ -597,8 +598,14 @@
     used = 0
     for kind in range(3):
         first = (2, 0, 1)[kind] * width
-        grad = jnp.concatenate([ref[...] for ref in grad_refs[used : used + counts[kind]]], axis=0)
-        used += counts[kind]
+        groups = []
+        for parts in counts[kind]:
+            total = grad_refs[used][...]
+            for ref in grad_refs[used + 1 : used + parts]:
+                total = total + ref[...].astype(F32)
+            groups.append(total.astype(BF16))
+            used += parts
+        grad = jnp.concatenate(groups, axis=0)
         update = dot(w_ref[:, first : first + width], grad, 1, 0)
         turned = update if turned is None else turned + update
     d_h_one = turned.T
@@ -606,21 +613,39 @@
     sums_ref[0:1, :] += add_rows(d_h_one)
     sums_ref[1:2, :] += add_rows(d_h_one * normed)
     grad = (d_res_ref[...] + norm_back(normed, inverse, d_h_one * (1.0 + vectors_ref[1:2, :]))).astype(BF16)
-    out_ref[...] = grad.reshape(out_ref.shape)
-
-
-def input_grads(slot, slots, inputs, half, d_residual, vectors, packed, grads):
+    if not cut:
+        out_refs[0][...] = grad.reshape(out_refs[0].shape)
+        return
+
+    @pl.when(pl.program_id(0) < cut)
+    def _():
+        out_refs[0][...] = grad
+
+    @pl.when(pl.program_id(0) >= cut)
+    def _():
+        out_refs[1][...] = grad
+
+
+def input_grads(slot, slots, inputs, half, d_residual, vectors, packed, grads, in_two=False):
     rows, width = inputs.shape
     block = pick_block(rows, 256)
     first = half * (rows // block)
     row_spec = pl.BlockSpec((block, width), lambda i, *_: (i, 0))
-    flat = [grad for kind in grads for grad in kind]
+    flat = [part for kind in grads for group in kind for part in group]
     out_spec, out_shape = row_spec, (rows, width)
     if slots:
         out_spec = pl.BlockSpec((1, block, width), lambda i, at: (at[0], i, 0))
         out_shape = (slots, rows, width)
+    out_specs, out_shapes = [out_spec], [out_shape]
+    cut = rows // block // 3 if in_two else 0
+    if cut:
+        out_specs = [
+            pl.BlockSpec((block, width), lambda i, *_: (jnp.minimum(i, cut - 1), 0)),
+            pl.BlockSpec((block, width), lambda i, *_: (jnp.maximum(i - cut, 0), 0)),
+        ]
+        out_shapes = [(cut * block, width), (rows - cut * block, width)]
     return pl.pallas_call(
-        functools.partial(input_grads_kernel, [len(kind) for kind in grads]),
+        functools.partial(input_grads_kernel, [[len(group) for group in kind] for kind in grads], cut),
         grid_spec=pltpu.PrefetchScalarGridSpec(
             num_scalar_prefetch=1,
             grid=(rows // block,),
@@ -631,9 +656,9 @@
                 whole_spec((width, 3 * width)),
             ]
             + [pl.BlockSpec((grad.shape[0], block), lambda i, *_: (0, i + first)) for grad in flat],
-            out_specs=[out_spec, whole_spec((8, width))],
+            out_specs=out_specs + [whole_spec((8, width))],
         ),
-        out_shape=[jax.ShapeDtypeStruct(out_shape, BF16), jax.ShapeDtypeStruct((8, width), F32)],
+        out_shape=[jax.ShapeDtypeStruct(shape, BF16) for shape in out_shapes] + [jax.ShapeDtypeStruct((8, width), F32)],
         compiler_params=pltpu.CompilerParams(vmem_limit_bytes=VMEM_LIMIT),
         cost_estimate=pl.CostEstimate(
             flops=16 * rows * width * width, bytes_accessed=14 * rows * width + 6 * width * width, transcendentals=0
@@ -837,7 +862,7 @@
             dk_parts = [after(dk_parts[0], *others)] + dk_parts[1:]
             dk, dv, keep, send, bias_grad = weight_grads(at_core, shard, h_one, dq, dk_parts, dv_parts)
             for kind, grad in zip(grads, (dq, dk, dv)):
-                kind.append(grad)
+                kind.append([grad])
             d_biases.append(bias_grad[:, :3])
             return keep, send
 
@@ -867,22 +892,28 @@
                 early = sum_parts(*arrived[0], dq)
                 ready = after(d_heads, dq, early[0])
         early_sum = sum_core(*early, dq)
-        middle = sum_parts(*arrived[1], dq)
-        last = sum_parts(*arrived[2], middle[0], sum_rows, *mixed_arrived)
-        early_sum = sum_pairs(early_sum, last[0]).astype(BF16)
         if split:
-            rest = after(d_residual, last[0], early_sum)
-            away_frames, sums_away = input_grads(at_slot, 0, inputs[1], 1, rest, vectors, packed, grads)
-            core_sums = jnp.concatenate([sum_core(*sums, away_frames) for sums in (middle, last)], axis=-1)
-            rest, core_sums, _ = lax.optimization_barrier((d_residual, core_sums, away_frames))
+            in_parts = [
+                grads[0] + [[piece[0]] for piece in arrived[1:]],
+                grads[1] + [piece[1] for piece in arrived[1:]],
+                grads[2] + [piece[2] for piece in arrived[1:]],
+            ]
+            rest = after(d_residual, early_sum)
+            *away_frames, sums_away = input_grads(at_slot, 0, inputs[1], 1, rest, vectors, packed, in_parts, True)
+            frames_arrived = swap_out(*away_frames)
+            early_sum = sum_pairs(early_sum, sums_away).astype(BF16)
+            middle = sum_parts(*arrived[1], sums_away)
+            last = sum_parts(*arrived[2], middle[0], sum_rows, *mixed_arrived, frames_arrived[0])
+            core_sums = jnp.concatenate([sum_core(*sums, last[0]) for sums in (middle, last)], axis=-1)
+            rest, core_sums = lax.optimization_barrier((d_residual, core_sums))
             own_frames, sums_own = input_grads(at_slot, slots, inputs[0], 0, rest, vectors, packed, grads)
             sums_one = sums_own + sums_away
         else:
+            early_sum = sum_pairs(early_sum).astype(BF16)
+            middle, last = sum_parts(*arrived[1]), sum_parts(*arrived[2])
             core_sums = jnp.concatenate([sum_core(*sums) for sums in (middle, last)], axis=-1)
             both, sums_one = input_grads(at_slot, 0, inputs[0], 0, d_residual, vectors, packed, grads)
-            own_frames, away_frames = placed_own(both[:local]), both[local:]
-        cut = local * 2 // 3 // 16 * 16
-        frames_arrived = swap_out(away_frames[:cut], after(away_frames[cut:], core_sums))
+            own_frames, frames_arrived = placed_own(both[:local]), swap_out(both[local:])
         side_sums = sum_side(core_sums).astype(BF16)
         early_sum = sum_side(early_sum, side_sums).astype(BF16)
 
@@ -890,7 +921,7 @@
             [sums_one[:2], sums_two[: 6 + ups], jnp.concatenate(d_biases).T]
         )
         for_slot = 6
-        vector = after(vector, frames_arrived[0])
+        vector = after(vector, *frames_arrived)
         total = vector
         for by in range(1, group):
             total = total + lax.ppermute(vector, "fsdp", ring(by))
@@ -905,9 +936,7 @@
         mixed = placed_away(mixed, mixed_arrived)
         packs = gather_dp(total).reshape(n_dp, -1, width)
         pack = jnp.concatenate([packs[:, :for_slot].reshape(-1, width), jnp.sum(packs[:, for_slot:], axis=0)])
-        pack, g_out, g_up, g_down, mixed, _ = lax.optimization_barrier(
-            (pack, g_out, g_up, g_down, mixed, frames_arrived[1])
-        )
+        pack, g_out, g_up, g_down, mixed = lax.optimization_barrier((pack, g_out, g_up, g_down, mixed))
         grad_frames = placed_away(own_frames, frames_arrived)
         across = shift(pack, "fsdp", n_fsdp, group)
         count = n_dp * for_slot

time: 643 us -> 636 us (0.989)
  waiting for transfers between devices: 64.7 us -> 58.2 us
    ppermute x21, waiting for transfers between devices: 38.2 us -> 27.9 us  [shift(): lax.ppermute(values, axis, [(i, (i + by) % size) for i in range(size)])]
  transfers between devices with their start and end apart: 44 -> 44, of which waited for: 14 -> 13; matrix products, arithmetic and copies ran while one was open for 10% -> 9% of each run, Pallas kernels for 57% -> 58%
where the time goes in v8:
time: 636 us; the launch traced here: 627 us
  Pallas kernels  445 us (70%)
  waiting for transfers between devices  58.2 us (9%)
  local copies, waits for them, and re-layouts  40.9 us (6%)
  starting transfers between devices  39 us (6%)
  other arithmetic  27.2 us (4%)
  between operations  15.2 us (2%)
    pallas_call x3, Pallas kernels, attend_back(): pl.pallas_call(functools.partial(attend_back_kernel, parts, chunk), grid=...  184 us
    pallas_call x2, Pallas kernels, attend(): pl.pallas_call(functools.partial(attend_kernel, parts, chunk), grid=(head...  103 us
    pallas_call x1, Pallas kernels, feed_forward(): pl.pallas_call(functools.partial(feed_forward_kernel, len(heads_out), pie...  82.3 us
    ppermute x21, starting transfers between devices, shift(): lax.ppermute(values, axis, [(i, (i + by) % size) for i in range(size)])  29 us
    ppermute x21, waiting for transfers between devices, shift(): lax.ppermute(values, axis, [(i, (i + by) % size) for i in range(size)])  27.9 us
    pallas_call x3, Pallas kernels, weight_grads(): pl.pallas_call(functools.partial(weight_grads_kernel, parts, shard if in_...  27.7 us
    pallas_call x2, Pallas kernels, input_grads(): pl.pallas_call(functools.partial(input_grads_kernel, [[len(group) for gro...  24.8 us
    all_gather x1, waiting for transfers between devices, body(): lax.all_gather(jnp.concatenate([w_key, w_value, w_query], axis=1), AXES,...  19.1 us
  transfers between devices with their start and end apart: 44, of which 13 were waited for; matrix products, arithmetic and copies ran while one was open for 9% of the time, Pallas kernels for 58%

profile of v8, /device:TPU:0, one launch (start us, length us, event | category | flops | bytes accessed | tf_op | source)
XLA Modules:
  0.0 626.9 jit_solution(8348472868931316963)
XLA Ops:
  7.2 1.6 pad_maximum_fusion.7
  9.0 3.1 collective-permute-start.1
  12.0 2.1 collective-permute-start.3
  15.1 3.9 dynamic-slice_bitcast_fusion.2
  19.0 1.5 collective-permute-start
  23.8 1.5 collective-permute-start.4
  25.4 2.1 collective-permute-done.4
  30.4 1.5 collective-permute-start.5
  31.9 2.2 multiply_sine_fusion
  34.8 1.3 fusion.18
  36.1 2.2 squeeze.83
  38.2 2.2 collective-permute-done.5
  40.4 1.5 add.309
  41.9 1.2 collective-permute-start.6
  44.2 2.1 collective-permute-start.7
  46.3 1.9 add_compare_fusion
  48.9 4.4 collective-permute-done.8
  53.3 4.3 collective-permute-done.7
  58.4 2.0 dynamic-slice_bitcast_fusion
  60.4 2.3 collective-permute-done.9
  62.8 1.3 compare_select_fusion.1
  66.0 1.2 copy.92
  70.4 19.1 %all-gather.3.cloned.1.call-done.w_ref = bf16[1024,3072]{1,0:T(8,128)(2,1)} async-done(((bf16[32,3072]{1,0:T(8,128)(2,1)}), bf16[1024,3072]{1,0:T(8,128)(2,1)}) %all-gather.3.cloned.1.call-update) | async-done | bytes 6291472 | tf_op jit(solution)/shard_map/all_gather | solution.py:792
  89.5 13.7 %project_kv.1 = (bf16[1536,1024]{1,0:T(8,128)(2,1)}, bf16[512,1536]{1,0:T(8,128)(2,1)}, bf16[512,1536]{1,0:T(8,128)(2,1)}, bf16[512,1536]{1,0:T(8,128)(2,1)}, bf16[512,1536]{1,0:T(8,128)(2,1)}) custom-call(bf16[768,1024]{1,0:T(8,128)(2,1)} %get-tuple-element.184.x_ref.refs_2_, bf16[768,1024]{1,0:T(8,128)(2,1)} %collective-permute-done.y_ref.refs_3_.x_ref, ...), custom_call_target="tpu_custom_call" | custom-call | flops 12884901888 | bytes 16777216 | tf_op jit(solution)/shard_map/project_kv/pallas_call | solution.py:338
  103.9 1.4 collective-permute-start.15
  105.4 8.8 %project_q.1.refs_0_ = bf16[1024,1536]{1,0:T(8,128)(2,1)} custom-call(bf16[1536,1024]{1,0:T(8,128)(2,1)} %get-tuple-element.100.h_ref, f32[16,1024]{1,0:T(8,128)} %pad.8.vectors_ref.refs_8_, bf16[1024,3072]{1,0:T(8,128)(2,1)} %all-gather.3.cloned.1.call-done.w_ref, f32[32,1536]{1,0:T(8,128)} %slice.119.cos_ref, f32[32,1536]{1,0:T(8,128)} %slice.120.sin_ref), custom_call_target="tpu_custom_call" | custom-call | flops 6442450944 | bytes 8388608 | tf_op jit(solution)/shard_map/project_q/pallas_call | solution.py:352
  114.1 51.6 %attend.3 = (bf16[512,1536]{1,0:T(8,128)(2,1)}, f32[8,1,1536]{2,1,0:T(1,128)}) custom-call(bf16[1024,1536]{1,0:T(8,128)(2,1)} %project_q.1.refs_0_, bf16[3072,64]{1,0:T(8,128)(2,1)} %pad.9.refs_1_, bf16[512,1536]{1,0:T(8,128)(2,1)} %get-tuple-element.105.refs_2_.refs_7_, bf16[512,1536]{1,0:T(8,128)(2,1)} %collective-permute-done.13.refs_3_.refs_8_, ...), custom_call_target="tpu_custom_call" | custom-call | flops 38654705664 | bytes 9437184 | tf_op jit(solution)/shard_map/attend/pallas_call | solution.py:91
  165.8 51.5 %attend.2 = (bf16[512,1536]{1,0:T(8,128)(2,1)}, f32[8,1,1536]{2,1,0:T(1,128)}) custom-call(bf16[1024,1536]{1,0:T(8,128)(2,1)} %project_q.1.refs_0_, bf16[3072,64]{1,0:T(8,128)(2,1)} %pad.9.refs_1_, bf16[512,1536]{1,0:T(8,128)(2,1)} %get-tuple-element.102.refs_2_.refs_7_, bf16[512,1536]{1,0:T(8,128)(2,1)} %collective-permute-done.11.refs_3_.refs_8_, ...), custom_call_target="tpu_custom_call" | custom-call | flops 38654705664 | bytes 9437184 | tf_op jit(solution)/shard_map/attend/pallas_call | solution.py:91
  217.3 82.3 %feed_forward.1 = (bf16[2,768,1024]{2,1,0:T(8,128)(2,1)}, bf16[768,1024]{1,0:T(8,128)(2,1)}, f32[1536,1024]{1,0:T(8,128)}, bf16[1024,1536]{1,0:T(8,128)(2,1)}, b...) custom-call(s32[1]{0:T(128)} %bitcast.slot_ref, bf16[512,1536]{1,0:T(8,128)(2,1)} %get-tuple-element.104.refs_0_.refs_2_, ...), custom_call_target="tpu_custom_call" | custom-call | flops 48318382080 | bytes 33554432 | tf_op jit(solution)/shard_map/feed_forward/pallas_call | solution.py:466
  299.6 90.6 %attend_back.4 = (bf16[512,1536]{1,0:T(8,128)(2,1)}, f32[512,1536]{1,0:T(8,128)}, bf16[512,1536]{1,0:T(8,128)(2,1)}, f32[512,1536]{1,0:T(8,128)}, bf16[512,1536]{1,0:T(8,128)(2,1)}) custom-call(bf16[1024,1536]{1,0:T(8,128)(2,1)} %project_q.1.refs_0_, bf16[1024,1536]{1,0:T(8,128)(2,1)} %get-tuple-element.127.refs_1_, ...), custom_call_target="tpu_custom_call" | custom-call | flops 12079595520 | tf_op jit(solution)/shard_map/attend_back/pallas_call | solution.py:223
  390.8 46.9 %attend_back.3 = (bf16[256,1536]{1,0:T(8,128)(2,1)}, f32[256,1536]{1,0:T(8,128)}, bf16[256,1536]{1,0:T(8,128)(2,1)}, f32[256,1536]{1,0:T(8,128)}, bf16[256,1536]{1,0:T(8,128)(2,1)}) custom-call(bf16[1024,1536]{1,0:T(8,128)(2,1)} %project_q.1.refs_0_, bf16[1024,1536]{1,0:T(8,128)(2,1)} %get-tuple-element.127.refs_1_, ...), custom_call_target="tpu_custom_call" | custom-call | flops 6039797760 | tf_op jit(solution)/shard_map/attend_back/pallas_call | solution.py:223
  437.8 1.1 copy-done.7
  438.9 12.0 %weight_grads.3 = (bf16[512,1536]{1,0:T(8,128)(2,1)}, bf16[512,1536]{1,0:T(8,128)(2,1)}, bf16[512,1536]{1,0:T(8,128)(2,1)}, bf16[512,1536]{1,0:T(8,128)(2,1)}, f32[512,128]{1,0:T(8,128)}) custom-call(s32[1]{0:T(128)} %bitcast.19.core_ref, bf16[1536,1024]{1,0:T(8,128)(2,1)} %get-tuple-element.100.h_ref, bf16[512,1536]{1,0:T(8,128)(2,1)} %get-tuple-element.119.dq_ref.refs_0_, ...), custom_call_target="tpu_custom_call" | custom-call | tf_op jit(solution)/shard_map/weight_grads/pallas_call | solution.py:555
  452.6 46.8 %attend_back.5 = (bf16[256,1536]{1,0:T(8,128)(2,1)}, f32[256,1536]{1,0:T(8,128)}, bf16[256,1536]{1,0:T(8,128)(2,1)}, f32[256,1536]{1,0:T(8,128)}, bf16[256,1536]{1,0:T(8,128)(2,1)}) custom-call(bf16[1024,1536]{1,0:T(8,128)(2,1)} %project_q.1.refs_0_, bf16[1024,1536]{1,0:T(8,128)(2,1)} %get-tuple-element.127.refs_1_, ...), custom_call_target="tpu_custom_call" | custom-call | flops 6039797760 | tf_op jit(solution)/shard_map/attend_back/pallas_call | solution.py:223
  500.8 2.3 add_convert_fusion
  504.0 1.3 collective-permute-start.35
  505.3 12.8 %input_grads.2 = (bf16[256,1024]{1,0:T(8,128)(2,1)}, bf16[512,1024]{1,0:T(8,128)(2,1)}, f32[8,1024]{1,0:T(8,128)}) custom-call(s32[1]{0:T(128)} %bitcast.slot_ref, bf16[768,1024]{1,0:T(8,128)(2,1)} %collective-permute-done.y_ref.refs_3_.x_ref, f32[1536,1024]{1,0:T(8,128)} %get-tuple-element.152.d_res_ref, f32[16,1024]{1,0:T(8,128)} %pad.8.vectors_ref.refs_8_, ...), custom_call_target="tpu_custom_call" | custom-call | flops 12884901888 | bytes 17301504 | tf_op jit(solution)/shard_map/input_grads/pallas_call | solution.py:647
  518.9 7.9 %weight_grads.4 = (bf16[256,1536]{1,0:T(8,128)(2,1)}, bf16[256,1536]{1,0:T(8,128)(2,1)}, bf16[512,768]{1,0:T(8,128)(2,1)}, bf16[512,768]{1,0:T(8,128)(2,1)}, f32[256,128]{1,0:T(8,128)}) custom-call(s32[1]{0:T(128)} %bitcast.19.core_ref, bf16[1536,1024]{1,0:T(8,128)(2,1)} %get-tuple-element.100.h_ref, bf16[256,1536]{1,0:T(8,128)(2,1)} %get-tuple-element.116.refs_1_.dq_ref, ...), custom_call_target="tpu_custom_call" | custom-call | tf_op jit(solution)/shard_map/weight_grads/pallas_call | solution.py:555
  528.1 1.4 collective-permute-start.27
  529.4 6.4 %collective-permute-done.25 = bf16[256,1024]{1,0:T(8,128)(2,1)} collective-permute-done((bf16[256,1024]{1,0:T(8,128)(2,1)}, bf16[256,1024]{1,0:T(8,128)(2,1)}, u32[]{:S(2)}, u32[]{:S(2)}) %collective-permute-start.25) | collective-permute-done | bytes 524320 | tf_op jit(solution)/shard_map/ppermute | solution.py:693
  535.9 7.8 %weight_grads.5 = (bf16[256,1536]{1,0:T(8,128)(2,1)}, bf16[256,1536]{1,0:T(8,128)(2,1)}, bf16[512,768]{1,0:T(8,128)(2,1)}, bf16[512,768]{1,0:T(8,128)(2,1)}, f32[256,128]{1,0:T(8,128)}) custom-call(s32[1]{0:T(128)} %bitcast.19.core_ref, bf16[1536,1024]{1,0:T(8,128)(2,1)} %get-tuple-element.100.h_ref, bf16[256,1536]{1,0:T(8,128)(2,1)} %get-tuple-element.128.refs_2_.dq_ref, ...), custom_call_target="tpu_custom_call" | custom-call | tf_op jit(solution)/shard_map/weight_grads/pallas_call | solution.py:555
  543.8 1.4 fusion.1
  546.1 1.4 collective-permute-start.36
  548.5 1.3 add_convert_fusion.2
  549.8 1.3 add_convert_fusion.1
  552.9 12.0 %input_grads.3 = (bf16[2,768,1024]{2,1,0:T(8,128)(2,1)}, f32[8,1024]{1,0:T(8,128)}) custom-call(s32[1]{0:T(128)} %bitcast.slot_ref, bf16[768,1024]{1,0:T(8,128)(2,1)} %get-tuple-element.184.x_ref.refs_2_, f32[1536,1024]{1,0:T(8,128)} %get-tuple-element.152.d_res_ref, f32[16,1024]{1,0:T(8,128)} %pad.8.vectors_ref.refs_8_, ...), custom_call_target="tpu_custom_call" | custom-call | flops 12884901888 | bytes 17301504 | tf_op jit(solution)/shard_map/input_grads/pallas_call | solution.py:647
  565.8 1.9 bitcast_dynamic-update-slice_fusion.2
  567.7 2.3 bitcast_dynamic-update-slice_fusion.1
  570.0 4.6 collective-permute-done.29
  574.6 1.3 fusion.2
  575.9 1.9 collective-permute-start.32
  579.7 1.1 fusion.6
  582.4 1.7 collective-permute-start.37
  584.1 1.9 collective-permute-start.38
  587.9 2.1 reshape.252
  590.7 1.4 collective-permute-start.33
  592.2 2.7 bitcast_dynamic-update-slice_fusion
  594.8 2.3 collective-permute-done.33
  597.4 1.4 collective-permute-start.34
  598.8 6.3 collective-permute-done.38
  605.3 1.2 fusion.5
  606.7 1.5 collective-permute-start.40
  608.3 3.1 collective-permute-done.40
  616.2 1.5 fusion.28
  (241 shorter events, 41.2 us)
Async XLA Ops:
  7.2 20.8 %copy-start = (bf16[32,6144]{1,0:T(8,128)(2,1)S(1)}, bf16[32,6144]{1,0:T(8,128)(2,1)}, u32[]{:S(2)}) copy-start(bf16[32,6144]{1,0:T(8,128)(2,1)} %param.21) | copy-start | bytes 1179652
  7.2 82.3 %all-gather.3.cloned.1.call-start = ((), (), s32[]{:S(2)}) async-start(), calls=%async_computation.1 | async-start | bytes 6488064 | tf_op jit(solution)/shard_map/all_gather | solution.py:792
  8.9 208.3 %all-gather.5.cloned.1.call-start = ((), (), s32[]{:S(2)}) async-start(), calls=%async_computation.2 | async-start | bytes 10813440 | tf_op jit(solution)/shard_map/all_gather | solution.py:796
  9.0 14.7 %collective-permute-start.1 = (s32[2]{0:T(128)}, s32[2]{0:T(128)S(1)}, u32[]{:S(2)}, u32[]{:S(2)}) collective-permute-start(s32[2]{0:T(128)} %param.20), channel_id=1, source_target_pairs={{0,8},{4,12},{8,16},{12,20},{16,24},{20,28},{24,0},{28,4},{1,9},{5... | collective-permute-start | bytes 32 | tf_op jit(solution)/shard_map/ppermute | solution.py:693
  12.0 11.7 %collective-permute-start.3 = (s32[2]{0:T(128)}, s32[2]{0:T(128)S(1)}, u32[]{:S(2)}, u32[]{:S(2)}) collective-permute-start(s32[2]{0:T(128)} %param.20), channel_id=1, source_target_pairs={{0,24},{4,28},{8,0},{12,4},{16,8},{20,12},{24,16},{28,20},{1,25},{... | collective-permute-start | bytes 32 | tf_op jit(solution)/shard_map/ppermute | solution.py:693
  14.1 9.6 %collective-permute-start.2 = (s32[2]{0:T(128)}, s32[2]{0:T(128)S(1)}, u32[]{:S(2)}, u32[]{:S(2)}) collective-permute-start(s32[2]{0:T(128)} %param.20), channel_id=1, source_target_pairs={{0,16},{4,20},{8,24},{12,28},{16,0},{20,4},{24,8},{28,12},{1,17},{... | collective-permute-start | bytes 32 | tf_op jit(solution)/shard_map/ppermute | solution.py:693
  15.1 5.4 copy-start.18
  19.0 2.6 copy-start.19
  19.0 2.7 copy-start.20
  19.0 51.4 %collective-permute-start = (bf16[768,1024]{1,0:T(8,128)(2,1)}, bf16[768,1024]{1,0:T(8,128)(2,1)}, u32[]{:S(2)}, u32[]{:S(2)}) collective-permute-start(bf16[768,1024]{1,0:T(8,128)(2,1)} %get-tuple-element.183), channel_id=1, source_target_pairs={{0,2},{1,3},{2,0},{3,1},{4,6},{5,7},{6,4},{7,5},{8,10},{9,11},{10,... | collective-permute-start | bytes 4718600 | tf_op jit(solution)/shard_map/ppermute | solution.py:693
  20.9 2.4 copy-start.30
  20.9 2.5 copy-start.31
  20.9 2.6 copy-start.24
  20.9 2.8 copy-start.25
  22.4 513.4 %reduce-scatter.2.cloned.1.call-start = ((), (), s32[]{:S(2)}) async-start(), calls=%async_computation.3 | async-start | bytes 10813440 | tf_op jit(solution)/shard_map/reduce_scatter | solution.py:856
  23.8 3.6 collective-permute-start.4
  28.6 5.6 copy-start.32
  30.4 10.0 %collective-permute-start.5 = (f32[4,2,13312]{2,1,0:T(2,128)}, f32[4,2,13312]{2,1,0:T(2,128)}, u32[]{:S(2)}, u32[]{:S(2)}) collective-permute-start(f32[4,2,13312]{2,1,0:T(2,128)} %squeeze.84), channel_id=1, source_target_pairs={{0,4},{4,0},{8,12},{12,8},{16,20},{20,16},{24,28},{28,24},{1,5},{5... | collective-permute-start | bytes 1277960 | tf_op jit(solution)/shard_map/ppermute | solution.py:761
  34.1 35.5 %copy-start.9 = (f32[32,3072]{1,0:T(8,128)}, f32[32,3072]{1,0:T(8,128)S(1)}, u32[]{:S(2)}) copy-start(f32[32,3072]{1,0:T(8,128)S(1)} %get-tuple-element.99.refs_6_) | copy-start | bytes 1179652
  36.1 22.4 %copy-start.4 = (bf16[2,768,1024]{2,1,0:T(8,128)(2,1)S(1)}, bf16[2,768,1024]{2,1,0:T(8,128)(2,1)}, u32[]{:S(2)}) copy-start(bf16[2,768,1024]{2,1,0:T(8,128)(2,1)} %param.35) | copy-start | bytes 9437188
  41.9 7.0 %collective-permute-start.6 = (f32[2,13312]{1,0:T(2,128)S(1)}, f32[2,13312]{1,0:T(2,128)S(1)}, u32[]{:S(2)}, u32[]{:S(2)}) collective-permute-start(f32[2,13312]{1,0:T(2,128)S(1)} %get-tuple-element.192), channel_id=1, source_target_pairs={{0,24},{4,28},{8,0},{12,4},{16,8},{20,12},{24,16},{28,20},{1,25},{... | collective-permute-start | bytes 319496 | tf_op jit(solution)/shard_map/ppermute | solution.py:693
  43.2 10.1 %collective-permute-start.8 = (f32[2,13312]{1,0:T(2,128)S(1)}, f32[2,13312]{1,0:T(2,128)S(1)}, u32[]{:S(2)}, u32[]{:S(2)}) collective-permute-start(f32[2,13312]{1,0:T(2,128)S(1)} %get-tuple-element.193), channel_id=1, source_target_pairs={{0,8},{4,12},{8,16},{12,20},{16,24},{20,28},{24,0},{28,4},{1,9},{5... | collective-permute-start | bytes 319496 | tf_op jit(solution)/shard_map/ppermute | solution.py:693
  44.2 13.5 %collective-permute-start.7 = (f32[2,13312]{1,0:T(2,128)S(1)}, f32[2,13312]{1,0:T(2,128)S(1)}, u32[]{:S(2)}, u32[]{:S(2)}) collective-permute-start(f32[2,13312]{1,0:T(2,128)S(1)} %get-tuple-element.194), channel_id=1, source_target_pairs={{0,16},{4,20},{8,24},{12,28},{16,0},{20,4},{24,8},{28,12},{1,17},{... | collective-permute-start | bytes 319496 | tf_op jit(solution)/shard_map/ppermute | solution.py:693
  57.9 4.8 collective-permute-start.9
  62.7 5.6 collective-permute-start.10
  66.0 2.9 copy-start.10
  89.5 14.5 %copy-start.6 = (bf16[768,1024]{1,0:T(8,128)(2,1)S(1)}, bf16[768,1024]{1,0:T(8,128)(2,1)}, u32[]{:S(2)}) copy-start(bf16[768,1024]{1,0:T(8,128)(2,1)} %get-tuple-element.110) | copy-start | bytes 4718596
  103.1 11.0 %collective-permute-start.13 = (bf16[512,1536]{1,0:T(8,128)(2,1)}, bf16[512,1536]{1,0:T(8,128)(2,1)}, u32[]{:S(2)}, u32[]{:S(2)}) collective-permute-start(bf16[512,1536]{1,0:T(8,128)(2,1)} %get-tuple-element.105.refs_2_.refs_7_), channel_id=1, source_target_pairs={{0,1},{1,0},{2,3},{3,2},{4,5},{5,4},{6,7},{7,6},{8,9},{9,8},{10,11... | collective-permute-start | bytes 4718600 | tf_op jit(solution)/shard_map/ppermute | solution.py:841
  103.4 10.7 %collective-permute-start.14 = (bf16[512,1536]{1,0:T(8,128)(2,1)}, bf16[512,1536]{1,0:T(8,128)(2,1)}, u32[]{:S(2)}, u32[]{:S(2)}) collective-permute-start(bf16[512,1536]{1,0:T(8,128)(2,1)} %get-tuple-element.106.refs_4_.refs_9_), channel_id=1, source_target_pairs={{0,1},{1,0},{2,3},{3,2},{4,5},{5,4},{6,7},{7,6},{8,9},{9,8},{10,11... | collective-permute-start | bytes 4718600 | tf_op jit(solution)/shard_map/ppermute | solution.py:841
  103.7 62.1 %collective-permute-start.11 = (bf16[512,1536]{1,0:T(8,128)(2,1)}, bf16[512,1536]{1,0:T(8,128)(2,1)}, u32[]{:S(2)}, u32[]{:S(2)}) collective-permute-start(bf16[512,1536]{1,0:T(8,128)(2,1)} %get-tuple-element.102.refs_2_.refs_7_), channel_id=1, source_target_pairs={{0,1},{1,0},{2,3},{3,2},{4,5},{5,4},{6,7},{7,6},{8,9},{9,8},{10,11... | collective-permute-start | bytes 4718600 | tf_op jit(solution)/shard_map/ppermute | solution.py:841
  103.9 113.3 %collective-permute-start.15 = (bf16[768,1024]{1,0:T(8,128)(2,1)S(1)}, bf16[768,1024]{1,0:T(8,128)(2,1)}, u32[]{:S(2)}, u32[]{:S(2)}) collective-permute-start(bf16[768,1024]{1,0:T(8,128)(2,1)S(1)} %copy-done.6), channel_id=1, source_target_pairs={{0,2},{1,3},{2,0},{3,1},{4,6},{5,7},{6,4},{7,5},{8,10},{9,11},{10,... | collective-permute-start | bytes 4718600 | tf_op jit(solution)/shard_map/ppermute | solution.py:693
  105.3 60.4 %collective-permute-start.12 = (bf16[512,1536]{1,0:T(8,128)(2,1)}, bf16[512,1536]{1,0:T(8,128)(2,1)}, u32[]{:S(2)}, u32[]{:S(2)}) collective-permute-start(bf16[512,1536]{1,0:T(8,128)(2,1)} %get-tuple-element.103.refs_4_.refs_9_), channel_id=1, source_target_pairs={{0,1},{1,0},{2,3},{3,2},{4,5},{5,4},{6,7},{7,6},{8,9},{9,8},{10,11... | collective-permute-start | bytes 4718600 | tf_op jit(solution)/shard_map/ppermute | solution.py:841
  390.2 47.6 %collective-permute-start.16 = (bf16[512,1536]{1,0:T(8,128)(2,1)}, bf16[512,1536]{1,0:T(8,128)(2,1)S(1)}, u32[]{:S(2)}, u32[]{:S(2)}) collective-permute-start(bf16[512,1536]{1,0:T(8,128)(2,1)} %get-tuple-element.122), channel_id=1, source_target_pairs={{0,1},{1,0},{2,3},{3,2},{4,5},{5,4},{6,7},{7,6},{8,9},{9,8},{10,11... | collective-permute-start | bytes 4718600 | tf_op jit(solution)/shard_map/ppermute | solution.py:888
  390.7 47.0 %collective-permute-start.17 = (bf16[512,1536]{1,0:T(8,128)(2,1)}, bf16[512,1536]{1,0:T(8,128)(2,1)}, u32[]{:S(2)}, u32[]{:S(2)}) collective-permute-start(bf16[512,1536]{1,0:T(8,128)(2,1)} %get-tuple-element.124), channel_id=1, source_target_pairs={{0,1},{1,0},{2,3},{3,2},{4,5},{5,4},{6,7},{7,6},{8,9},{9,8},{10,11... | collective-permute-start | bytes 4718600 | tf_op jit(solution)/shard_map/ppermute | solution.py:889
  451.0 48.6 %collective-permute-start.18 = (bf16[512,1536]{1,0:T(8,128)(2,1)}, bf16[512,1536]{1,0:T(8,128)(2,1)S(1)}, u32[]{:S(2)}, u32[]{:S(2)}) collective-permute-start(bf16[512,1536]{1,0:T(8,128)(2,1)} %get-tuple-element.126), channel_id=1, source_target_pairs={{0,1},{1,0},{2,3},{3,2},{4,5},{5,4},{6,7},{7,6},{8,9},{9,8},{10,11... | collective-permute-start | bytes 4718600 | tf_op jit(solution)/shard_map/ppermute | solution.py:761
  451.4 78.0 %collective-permute-start.24 = (bf16[768,1024]{1,0:T(8,128)(2,1)}, bf16[768,1024]{1,0:T(8,128)(2,1)}, u32[]{:S(2)}, u32[]{:S(2)}) collective-permute-start(bf16[768,1024]{1,0:T(8,128)(2,1)} %get-tuple-element.145), channel_id=1, source_target_pairs={{0,2},{1,3},{2,0},{3,1},{4,6},{5,7},{6,4},{7,5},{8,10},{9,11},{10,... | collective-permute-start | bytes 4718600 | tf_op jit(solution)/shard_map/ppermute | solution.py:693
  452.1 51.8 %collective-permute-start.19 = (bf16[256,1536]{1,0:T(8,128)(2,1)}, bf16[256,1536]{1,0:T(8,128)(2,1)}, u32[]{:S(2)}, u32[]{:S(2)}) collective-permute-start(bf16[256,1536]{1,0:T(8,128)(2,1)} %get-tuple-element.132), channel_id=1, source_target_pairs={{0,1},{1,0},{2,3},{3,2},{4,5},{5,4},{6,7},{7,6},{8,9},{9,8},{10,11... | collective-permute-start | bytes 2359304 | tf_op jit(solution)/shard_map/ppermute | solution.py:888
  452.1 53.2 %collective-permute-start.21 = (bf16[256,1536]{1,0:T(8,128)(2,1)}, bf16[256,1536]{1,0:T(8,128)(2,1)}, u32[]{:S(2)}, u32[]{:S(2)}) collective-permute-start(bf16[256,1536]{1,0:T(8,128)(2,1)} %get-tuple-element.137), channel_id=1, source_target_pairs={{0,1},{1,0},{2,3},{3,2},{4,5},{5,4},{6,7},{7,6},{8,9},{9,8},{10,11... | collective-permute-start | bytes 2359304 | tf_op jit(solution)/shard_map/ppermute | solution.py:889
  499.5 5.8 collective-permute-start.20
  499.6 5.7 collective-permute-start.22
  504.0 25.5 %collective-permute-start.35 = (bf16[8,32,1536]{2,1,0:T(8,128)(2,1)}, bf16[8,32,1536]{2,1,0:T(8,128)(2,1)}, u32[]{:S(2)}, u32[]{:S(2)}) collective-permute-start(bf16[8,32,1536]{2,1,0:T(8,128)(2,1)} %dynamic-slice_bitcast_fusion.4), channel_id=1, source_target_pairs={{0,2},{1,3},{2,0},{3,1},{4,6},{5,7},{6,4},{7,5},{8,10},{9,11},{10,... | collective-permute-start | bytes 2359304 | tf_op jit(solution)/shard_map/ppermute | solution.py:693
  518.1 17.7 %collective-permute-start.25 = (bf16[256,1024]{1,0:T(8,128)(2,1)}, bf16[256,1024]{1,0:T(8,128)(2,1)}, u32[]{:S(2)}, u32[]{:S(2)}) collective-permute-start(bf16[256,1024]{1,0:T(8,128)(2,1)} %get-tuple-element.146), channel_id=1, source_target_pairs={{0,2},{1,3},{2,0},{3,1},{4,6},{5,7},{6,4},{7,5},{8,10},{9,11},{10,... | collective-permute-start | bytes 1572872 | tf_op jit(solution)/shard_map/ppermute | solution.py:693
  518.9 8.1 %copy-start.17 = (f32[512,128]{1,0:T(8,128)S(1)}, f32[512,128]{1,0:T(8,128)}, u32[]{:S(2)}) copy-start(f32[512,128]{1,0:T(8,128)} %get-tuple-element.159) | copy-start | bytes 786436
  526.8 21.7 %collective-permute-start.23 = (bf16[512,768]{1,0:T(8,128)(2,1)}, bf16[512,768]{1,0:T(8,128)(2,1)}, u32[]{:S(2)}, u32[]{:S(2)}) collective-permute-start(bf16[512,768]{1,0:T(8,128)(2,1)} %get-tuple-element.143), channel_id=1, source_target_pairs={{0,1},{1,0},{2,3},{3,2},{4,5},{5,4},{6,7},{7,6},{8,9},{9,8},{10,11... | collective-permute-start | bytes 2359304 | tf_op jit(solution)/shard_map/ppermute | solution.py:761
  528.1 37.6 %collective-permute-start.27 = (bf16[512,1024]{1,0:T(8,128)(2,1)}, bf16[512,1024]{1,0:T(8,128)(2,1)}, u32[]{:S(2)}, u32[]{:S(2)}) collective-permute-start(bf16[512,1024]{1,0:T(8,128)(2,1)} %get-tuple-element.162), channel_id=1, source_target_pairs={{0,2},{1,3},{2,0},{3,1},{4,6},{5,7},{6,4},{7,5},{8,10},{9,11},{10,... | collective-permute-start | bytes 3145736 | tf_op jit(solution)/shard_map/ppermute | solution.py:693
  543.7 4.8 copy-start.11
  543.7 6.2 collective-permute-start.26
  546.0 3.8 copy-start.12
  546.1 33.6 %collective-permute-start.36 = (bf16[4,32,1536]{2,1,0:T(8,128)(2,1)S(1)}, bf16[4,32,1536]{2,1,0:T(8,128)(2,1)}, u32[]{:S(2)}, u32[]{:S(2)}) collective-permute-start(bf16[4,32,1536]{2,1,0:T(8,128)(2,1)S(1)} %dynamic-slice_bitcast_fusion.6), channel_id=1, source_target_pairs={{0,4},{4,0},{8,12},{12,8},{16,20},{20,16},{24,28},{28,24},{1,5},{5... | collective-permute-start | bytes 1179656 | tf_op jit(solution)/shard_map/ppermute | solution.py:761
  552.2 22.3 %collective-permute-start.29 = (bf16[4,2,32,1536]{3,2,1,0:T(8,128)(2,1)}, bf16[4,2,32,1536]{3,2,1,0:T(8,128)(2,1)}, u32[]{:S(2)}, u32[]{:S(2)}) collective-permute-start(bf16[4,2,32,1536]{3,2,1,0:T(8,128)(2,1)} %dynamic-slice_bitcast_fusion.5), channel_id=1, source_target_pairs={{0,4},{4,0},{8,12},{12,8},{16,20},{20,16},{24,28},{28,24},{1,5},{5... | collective-permute-start | bytes 2359304 | tf_op jit(solution)/shard_map/ppermute | solution.py:761
  552.9 12.8 %copy-start.21 = (f32[8,1024]{1,0:T(8,128)S(1)}, f32[8,1024]{1,0:T(8,128)}, u32[]{:S(2)}) copy-start(f32[8,1024]{1,0:T(8,128)} %get-tuple-element.158) | copy-start | bytes 98308
  565.7 4.2 collective-permute-start.28
  569.9 9.7 %copy-start.3 = (bf16[8,32,1536]{2,1,0:T(8,128)(2,1)S(1)}, bf16[8,32,1536]{2,1,0:T(8,128)(2,1)}, u32[]{:S(2)}) copy-start(bf16[8,32,1536]{2,1,0:T(8,128)(2,1)} %copy-done.2) | copy-start | bytes 2359300
  570.0 10.8 %copy-start.8 = (bf16[32,5120]{1,0:T(8,128)(2,1)S(1)}, bf16[32,5120]{1,0:T(8,128)(2,1)}, u32[]{:S(2)}) copy-start(bf16[32,5120]{1,0:T(8,128)(2,1)} %reduce-scatter.2.cloned.1.call-done) | copy-start | bytes 983044
  575.9 14.0 %collective-permute-start.32 = (f32[13,1024]{1,0:T(8,128)S(1)}, f32[13,1024]{1,0:T(8,128)S(1)}, u32[]{:S(2)}, u32[]{:S(2)}) collective-permute-start(f32[13,1024]{1,0:T(8,128)S(1)} %add.342), channel_id=1, source_target_pairs={{0,24},{4,28},{8,0},{12,4},{16,8},{20,12},{24,16},{28,20},{1,25},{... | collective-permute-start | bytes 159752 | tf_op jit(solution)/shard_map/ppermute | solution.py:693
  577.8 12.9 %collective-permute-start.31 = (f32[13,1024]{1,0:T(8,128)S(1)}, f32[13,1024]{1,0:T(8,128)S(1)}, u32[]{:S(2)}, u32[]{:S(2)}) collective-permute-start(f32[13,1024]{1,0:T(8,128)S(1)} %add.342), channel_id=1, source_target_pairs={{0,16},{4,20},{8,24},{12,28},{16,0},{20,4},{24,8},{28,12},{1,17},{... | collective-permute-start | bytes 159752 | tf_op jit(solution)/shard_map/ppermute | solution.py:693
  578.8 11.9 %collective-permute-start.30 = (f32[13,1024]{1,0:T(8,128)S(1)}, f32[13,1024]{1,0:T(8,128)S(1)}, u32[]{:S(2)}, u32[]{:S(2)}) collective-permute-start(f32[13,1024]{1,0:T(8,128)S(1)} %add.342), channel_id=1, source_target_pairs={{0,8},{4,12},{8,16},{12,20},{16,24},{20,28},{24,0},{28,4},{1,9},{5... | collective-permute-start | bytes 159752 | tf_op jit(solution)/shard_map/ppermute | solution.py:693
  582.4 16.4 %collective-permute-start.37 = (bf16[3,32,1536]{2,1,0:T(8,128)(2,1)}, bf16[3,32,1536]{2,1,0:T(8,128)(2,1)}, u32[]{:S(2)}, u32[]{:S(2)}) collective-permute-start(bf16[3,32,1536]{2,1,0:T(8,128)(2,1)} %get-tuple-element.185), channel_id=1, source_target_pairs={{0,8},{4,12},{8,16},{12,20},{16,24},{20,28},{24,0},{28,4},{1,9},{5... | collective-permute-start | bytes 884744 | tf_op jit(solution)/shard_map/ppermute | solution.py:693
  584.1 21.0 %collective-permute-start.38 = (bf16[3,32,1536]{2,1,0:T(8,128)(2,1)}, bf16[3,32,1536]{2,1,0:T(8,128)(2,1)}, u32[]{:S(2)}, u32[]{:S(2)}) collective-permute-start(bf16[3,32,1536]{2,1,0:T(8,128)(2,1)} %get-tuple-element.186), channel_id=1, source_target_pairs={{0,16},{4,20},{8,24},{12,28},{16,0},{20,4},{24,8},{28,12},{1,17},{... | collective-permute-start | bytes 884744 | tf_op jit(solution)/shard_map/ppermute | solution.py:693
  589.9 15.4 %collective-permute-start.39 = (bf16[3,32,1536]{2,1,0:T(8,128)(2,1)}, bf16[3,32,1536]{2,1,0:T(8,128)(2,1)S(1)}, u32[]{:S(2)}, u32[]{:S(2)}) collective-permute-start(bf16[3,32,1536]{2,1,0:T(8,128)(2,1)} %get-tuple-element.187), channel_id=1, source_target_pairs={{0,24},{4,28},{8,0},{12,4},{16,8},{20,12},{24,16},{28,20},{1,25},{... | collective-permute-start | bytes 884744 | tf_op jit(solution)/shard_map/ppermute | solution.py:693
  590.7 6.4 %collective-permute-start.33 = (f32[4,13,1024]{2,1,0:T(8,128)S(1)}, f32[4,13,1024]{2,1,0:T(8,128)S(1)}, u32[]{:S(2)}, u32[]{:S(2)}) collective-permute-start(f32[4,13,1024]{2,1,0:T(8,128)S(1)} %get-tuple-element.199), channel_id=1, source_target_pairs={{0,4},{4,0},{8,12},{12,8},{16,20},{20,16},{24,28},{28,24},{1,5},{5... | collective-permute-start | bytes 638984 | tf_op jit(solution)/shard_map/ppermute | solution.py:761
  597.4 16.8 %collective-permute-start.34 = (f32[55,1024]{1,0:T(8,128)S(1)}, f32[55,1024]{1,0:T(8,128)S(1)}, u32[]{:S(2)}, u32[]{:S(2)}) collective-permute-start(f32[55,1024]{1,0:T(8,128)S(1)} %pad_maximum_fusion.6), channel_id=1, source_target_pairs={{0,2},{1,3},{2,0},{3,1},{4,6},{5,7},{6,4},{7,5},{8,10},{9,11},{10,... | collective-permute-start | bytes 675848 | tf_op jit(solution)/shard_map/ppermute | solution.py:693
  606.7 4.7 collective-permute-start.40
  615.3 4.9 copy-start.1
  (13 other events, 19.4 us)
Sparse Core Ops, SparseCore 0:
  11.5 77.9 all-gather.2
  92.3 94.9 all-gather.4
  299.7 151.4 reduce-scatter.1

commit v9 on v8

--- a/solution.py
+++ b/solution.py
@@ -85,7 +85,7 @@
     span = parts * rows
     heads = width // HDIM
     q_rows = pick_block(rows, 768)
-    chunk = pick_block(span, 512)
+    chunk = pick_block(span, 256)
     q_spec = pl.BlockSpec((HDIM, q_rows), lambda h, j: (h + first, j))
     k_spec = pl.BlockSpec((HDIM, rows), lambda h, j: (h, 0))
     return pl.pallas_call(
@@ -213,7 +213,7 @@
     parts = len(k_parts)
     span = parts * rows
     q_rows = pick_block(rows, 1536)
-    chunk = pick_block(span, 256)
+    chunk = pick_block(span, 128)
     q_spec = pl.BlockSpec((HDIM, q_rows), lambda h, j: (h + first, j))
     k_spec = pl.BlockSpec((HDIM, rows), lambda h, j: (h + within, 0))
     whole = lambda array: pl.BlockSpec(array.shape, lambda h, j: (0, 0))
@@ -903,9 +903,9 @@
             frames_arrived = swap_out(*away_frames)
             early_sum = sum_pairs(early_sum, sums_away).astype(BF16)
             middle = sum_parts(*arrived[1], sums_away)
-            last = sum_parts(*arrived[2], middle[0], sum_rows, *mixed_arrived, frames_arrived[0])
+            last = sum_parts(*arrived[2], middle[0], sum_rows, *mixed_arrived)
             core_sums = jnp.concatenate([sum_core(*sums, last[0]) for sums in (middle, last)], axis=-1)
-            rest, core_sums = lax.optimization_barrier((d_residual, core_sums))
+            rest, core_sums, _ = lax.optimization_barrier((d_residual, core_sums, frames_arrived[0]))
             own_frames, sums_own = input_grads(at_slot, slots, inputs[0], 0, rest, vectors, packed, grads)
             sums_one = sums_own + sums_away
         else:

time: 636 us -> 616 us (0.969)
  Pallas kernels: 445 us -> 430 us
    pallas_call x3, Pallas kernels: 184 us -> 175 us  [attend_back(): pl.pallas_call(functools.partial(attend_back_kernel, parts, chunk), grid=...]
  transfers between devices with their start and end apart: 44 -> 44, of which waited for: 13 -> 11; matrix products, arithmetic and copies ran while one was open for 9% -> 10% of each run, Pallas kernels for 58% -> 57%
where the time goes in v9:
time: 616 us; the launch traced here: 607 us
  Pallas kernels  430 us (70%)
  waiting for transfers between devices  55.2 us (9%)
  local copies, waits for them, and re-layouts  41 us (7%)
  starting transfers between devices  36.6 us (6%)
  other arithmetic  27.3 us (4%)
  between operations  15.1 us (2%)
    pallas_call x3, Pallas kernels, attend_back(): pl.pallas_call(functools.partial(attend_back_kernel, parts, chunk), grid=...  175 us
    pallas_call x2, Pallas kernels, attend(): pl.pallas_call(functools.partial(attend_kernel, parts, chunk), grid=(head...  97.1 us
    pallas_call x1, Pallas kernels, feed_forward(): pl.pallas_call(functools.partial(feed_forward_kernel, len(heads_out), pie...  82.3 us
    pallas_call x3, Pallas kernels, weight_grads(): pl.pallas_call(functools.partial(weight_grads_kernel, parts, shard if in_...  27.8 us
    ppermute x21, waiting for transfers between devices, shift(): lax.ppermute(values, axis, [(i, (i + by) % size) for i in range(size)])  27.7 us
    ppermute x21, starting transfers between devices, shift(): lax.ppermute(values, axis, [(i, (i + by) % size) for i in range(size)])  27.4 us
    pallas_call x2, Pallas kernels, input_grads(): pl.pallas_call(functools.partial(input_grads_kernel, [[len(group) for gro...  24.8 us
    all_gather x1, waiting for transfers between devices, body(): lax.all_gather(jnp.concatenate([w_key, w_value, w_query], axis=1), AXES,...  19.1 us
  transfers between devices with their start and end apart: 44, of which 11 were waited for; matrix products, arithmetic and copies ran while one was open for 10% of the time, Pallas kernels for 57%

profile of v9, /device:TPU:0, one launch (start us, length us, event | category | flops | bytes accessed | tf_op | source)
XLA Modules:
  0.0 606.6 jit_solution(11860657281504007040)
XLA Ops:
  7.2 1.6 pad_maximum_fusion.7
  9.0 3.1 collective-permute-start.1
  12.0 2.1 collective-permute-start.3
  15.1 3.9 dynamic-slice_bitcast_fusion.2
  19.0 1.5 collective-permute-start
  23.8 1.5 collective-permute-start.4
  25.4 2.1 collective-permute-done.4
  30.4 1.5 collective-permute-start.5
  31.9 2.2 multiply_sine_fusion
  34.8 1.3 fusion.18
  36.0 2.2 squeeze.83
  38.2 2.2 collective-permute-done.5
  40.4 1.5 add.309
  41.9 1.2 collective-permute-start.6
  44.2 2.1 collective-permute-start.7
  46.3 1.9 add_compare_fusion
  48.9 4.4 collective-permute-done.8
  53.3 4.3 collective-permute-done.7
  58.4 2.0 dynamic-slice_bitcast_fusion
  60.4 2.3 collective-permute-done.9
  62.8 1.3 compare_select_fusion.1
  64.0 1.1 copy.93
  66.0 1.2 copy.92
  67.3 1.0 pad.9.refs_1_
  70.4 19.1 %all-gather.3.cloned.1.call-done.w_ref = bf16[1024,3072]{1,0:T(8,128)(2,1)} async-done(((bf16[32,3072]{1,0:T(8,128)(2,1)}), bf16[1024,3072]{1,0:T(8,128)(2,1)}) %all-gather.3.cloned.1.call-update) | async-done | bytes 6291472 | tf_op jit(solution)/shard_map/all_gather | solution.py:792
  89.5 13.7 %project_kv.1 = (bf16[1536,1024]{1,0:T(8,128)(2,1)}, bf16[512,1536]{1,0:T(8,128)(2,1)}, bf16[512,1536]{1,0:T(8,128)(2,1)}, bf16[512,1536]{1,0:T(8,128)(2,1)}, bf16[512,1536]{1,0:T(8,128)(2,1)}) custom-call(bf16[768,1024]{1,0:T(8,128)(2,1)} %get-tuple-element.184.x_ref.refs_2_, bf16[768,1024]{1,0:T(8,128)(2,1)} %collective-permute-done.y_ref.refs_3_.x_ref, ...), custom_call_target="tpu_custom_call" | custom-call | flops 12884901888 | bytes 16777216 | tf_op jit(solution)/shard_map/project_kv/pallas_call | solution.py:338
  103.9 1.4 collective-permute-start.15
  105.4 8.8 %project_q.1.refs_0_ = bf16[1024,1536]{1,0:T(8,128)(2,1)} custom-call(bf16[1536,1024]{1,0:T(8,128)(2,1)} %get-tuple-element.100.h_ref, f32[16,1024]{1,0:T(8,128)} %pad.8.vectors_ref.refs_8_, bf16[1024,3072]{1,0:T(8,128)(2,1)} %all-gather.3.cloned.1.call-done.w_ref, f32[32,1536]{1,0:T(8,128)} %slice.119.cos_ref, f32[32,1536]{1,0:T(8,128)} %slice.120.sin_ref), custom_call_target="tpu_custom_call" | custom-call | flops 6442450944 | bytes 8388608 | tf_op jit(solution)/shard_map/project_q/pallas_call | solution.py:352
  114.1 48.6 %attend.3 = (bf16[512,1536]{1,0:T(8,128)(2,1)}, f32[8,1,1536]{2,1,0:T(1,128)}) custom-call(bf16[1024,1536]{1,0:T(8,128)(2,1)} %project_q.1.refs_0_, bf16[3072,64]{1,0:T(8,128)(2,1)} %pad.9.refs_1_, bf16[512,1536]{1,0:T(8,128)(2,1)} %get-tuple-element.105.refs_2_.refs_7_, bf16[512,1536]{1,0:T(8,128)(2,1)} %collective-permute-done.13.refs_3_.refs_8_, ...), custom_call_target="tpu_custom_call" | custom-call | flops 38654705664 | bytes 9437184 | tf_op jit(solution)/shard_map/attend/pallas_call | solution.py:91
  162.7 48.5 %attend.2 = (bf16[512,1536]{1,0:T(8,128)(2,1)}, f32[8,1,1536]{2,1,0:T(1,128)}) custom-call(bf16[1024,1536]{1,0:T(8,128)(2,1)} %project_q.1.refs_0_, bf16[3072,64]{1,0:T(8,128)(2,1)} %pad.9.refs_1_, bf16[512,1536]{1,0:T(8,128)(2,1)} %get-tuple-element.102.refs_2_.refs_7_, bf16[512,1536]{1,0:T(8,128)(2,1)} %collective-permute-done.11.refs_3_.refs_8_, ...), custom_call_target="tpu_custom_call" | custom-call | flops 38654705664 | bytes 9437184 | tf_op jit(solution)/shard_map/attend/pallas_call | solution.py:91
  211.2 82.3 %feed_forward.1 = (bf16[2,768,1024]{2,1,0:T(8,128)(2,1)}, bf16[768,1024]{1,0:T(8,128)(2,1)}, f32[1536,1024]{1,0:T(8,128)}, bf16[1024,1536]{1,0:T(8,128)(2,1)}, b...) custom-call(s32[1]{0:T(128)} %bitcast.slot_ref, bf16[512,1536]{1,0:T(8,128)(2,1)} %get-tuple-element.104.refs_0_.refs_2_, ...), custom_call_target="tpu_custom_call" | custom-call | flops 48318382080 | bytes 33554432 | tf_op jit(solution)/shard_map/feed_forward/pallas_call | solution.py:466
  293.5 86.2 %attend_back.4 = (bf16[512,1536]{1,0:T(8,128)(2,1)}, f32[512,1536]{1,0:T(8,128)}, bf16[512,1536]{1,0:T(8,128)(2,1)}, f32[512,1536]{1,0:T(8,128)}, bf16[512,1536]{1,0:T(8,128)(2,1)}) custom-call(bf16[1024,1536]{1,0:T(8,128)(2,1)} %project_q.1.refs_0_, bf16[1024,1536]{1,0:T(8,128)(2,1)} %get-tuple-element.127.refs_1_, ...), custom_call_target="tpu_custom_call" | custom-call | flops 12079595520 | tf_op jit(solution)/shard_map/attend_back/pallas_call | solution.py:223
  380.4 44.7 %attend_back.3 = (bf16[256,1536]{1,0:T(8,128)(2,1)}, f32[256,1536]{1,0:T(8,128)}, bf16[256,1536]{1,0:T(8,128)(2,1)}, f32[256,1536]{1,0:T(8,128)}, bf16[256,1536]{1,0:T(8,128)(2,1)}) custom-call(bf16[1024,1536]{1,0:T(8,128)(2,1)} %project_q.1.refs_0_, bf16[1024,1536]{1,0:T(8,128)(2,1)} %get-tuple-element.127.refs_1_, ...), custom_call_target="tpu_custom_call" | custom-call | flops 6039797760 | tf_op jit(solution)/shard_map/attend_back/pallas_call | solution.py:223
  425.2 1.1 copy-done.7
  426.3 12.1 %weight_grads.3 = (bf16[512,1536]{1,0:T(8,128)(2,1)}, bf16[512,1536]{1,0:T(8,128)(2,1)}, bf16[512,1536]{1,0:T(8,128)(2,1)}, bf16[512,1536]{1,0:T(8,128)(2,1)}, f32[512,128]{1,0:T(8,128)}) custom-call(s32[1]{0:T(128)} %bitcast.19.core_ref, bf16[1536,1024]{1,0:T(8,128)(2,1)} %get-tuple-element.100.h_ref, bf16[512,1536]{1,0:T(8,128)(2,1)} %get-tuple-element.119.dq_ref.refs_0_, ...), custom_call_target="tpu_custom_call" | custom-call | tf_op jit(solution)/shard_map/weight_grads/pallas_call | solution.py:555
  439.8 44.6 %attend_back.5 = (bf16[256,1536]{1,0:T(8,128)(2,1)}, f32[256,1536]{1,0:T(8,128)}, bf16[256,1536]{1,0:T(8,128)(2,1)}, f32[256,1536]{1,0:T(8,128)}, bf16[256,1536]{1,0:T(8,128)(2,1)}) custom-call(bf16[1024,1536]{1,0:T(8,128)(2,1)} %project_q.1.refs_0_, bf16[1024,1536]{1,0:T(8,128)(2,1)} %get-tuple-element.127.refs_1_, ...), custom_call_target="tpu_custom_call" | custom-call | flops 6039797760 | tf_op jit(solution)/shard_map/attend_back/pallas_call | solution.py:223
  485.7 2.3 add_convert_fusion
  488.9 1.6 collective-permute-start.35
  490.5 12.8 %input_grads.2 = (bf16[256,1024]{1,0:T(8,128)(2,1)}, bf16[512,1024]{1,0:T(8,128)(2,1)}, f32[8,1024]{1,0:T(8,128)}) custom-call(s32[1]{0:T(128)} %bitcast.slot_ref, bf16[768,1024]{1,0:T(8,128)(2,1)} %collective-permute-done.y_ref.refs_3_.x_ref, f32[1536,1024]{1,0:T(8,128)} %get-tuple-element.152.d_res_ref, f32[16,1024]{1,0:T(8,128)} %pad.8.vectors_ref.refs_8_, ...), custom_call_target="tpu_custom_call" | custom-call | flops 12884901888 | bytes 17301504 | tf_op jit(solution)/shard_map/input_grads/pallas_call | solution.py:647
  503.3 7.9 %weight_grads.4 = (bf16[256,1536]{1,0:T(8,128)(2,1)}, bf16[256,1536]{1,0:T(8,128)(2,1)}, bf16[512,768]{1,0:T(8,128)(2,1)}, bf16[512,768]{1,0:T(8,128)(2,1)}, f32[256,128]{1,0:T(8,128)}) custom-call(s32[1]{0:T(128)} %bitcast.19.core_ref, bf16[1536,1024]{1,0:T(8,128)(2,1)} %get-tuple-element.100.h_ref, bf16[256,1536]{1,0:T(8,128)(2,1)} %get-tuple-element.116.refs_1_.dq_ref, ...), custom_call_target="tpu_custom_call" | custom-call | tf_op jit(solution)/shard_map/weight_grads/pallas_call | solution.py:555
  513.0 1.6 collective-permute-start.27
  514.6 7.8 %weight_grads.5 = (bf16[256,1536]{1,0:T(8,128)(2,1)}, bf16[256,1536]{1,0:T(8,128)(2,1)}, bf16[512,768]{1,0:T(8,128)(2,1)}, bf16[512,768]{1,0:T(8,128)(2,1)}, f32[256,128]{1,0:T(8,128)}) custom-call(s32[1]{0:T(128)} %bitcast.19.core_ref, bf16[1536,1024]{1,0:T(8,128)(2,1)} %get-tuple-element.100.h_ref, bf16[256,1536]{1,0:T(8,128)(2,1)} %get-tuple-element.128.refs_2_.dq_ref, ...), custom_call_target="tpu_custom_call" | custom-call | tf_op jit(solution)/shard_map/weight_grads/pallas_call | solution.py:555
  522.6 1.4 fusion.1
  526.4 1.3 add_convert_fusion.2
  527.7 1.3 add_convert_fusion.1
  530.2 1.6 collective-permute-start.29
  531.8 12.0 %input_grads.3 = (bf16[2,768,1024]{2,1,0:T(8,128)(2,1)}, f32[8,1024]{1,0:T(8,128)}) custom-call(s32[1]{0:T(128)} %bitcast.slot_ref, bf16[768,1024]{1,0:T(8,128)(2,1)} %get-tuple-element.184.x_ref.refs_2_, f32[1536,1024]{1,0:T(8,128)} %get-tuple-element.152.d_res_ref, f32[16,1024]{1,0:T(8,128)} %pad.8.vectors_ref.refs_8_, ...), custom_call_target="tpu_custom_call" | custom-call | flops 12884901888 | bytes 17301504 | tf_op jit(solution)/shard_map/input_grads/pallas_call | solution.py:647
  544.6 4.9 collective-permute-done.27
  549.5 1.9 bitcast_dynamic-update-slice_fusion.2
  551.4 2.3 bitcast_dynamic-update-slice_fusion.1
  553.7 1.4 fusion.2
  555.1 1.7 collective-permute-start.32
  556.8 1.2 collective-permute-start.31
  558.8 1.1 fusion.6
  561.6 1.5 collective-permute-start.37
  563.1 2.1 collective-permute-start.38
  567.1 2.1 reshape.252
  570.4 2.7 bitcast_dynamic-update-slice_fusion
  573.1 4.0 collective-permute-done.33
  577.9 7.1 %collective-permute-done.38 = bf16[3,32,1536]{2,1,0:T(8,128)(2,1)} collective-permute-done((bf16[3,32,1536]{2,1,0:T(8,128)(2,1)}, bf16[3,32,1536]{2,1,0:T(8,128)(2,1)}, u32[]{:S(2)}, u32[]{:S(2)}) %collective-permute-start.38) | collective-permute-done | bytes 294944 | tf_op jit(solution)/shard_map/ppermute | solution.py:693
  585.0 1.2 fusion.5
  587.2 3.9 collective-permute-done.40
  591.4 1.0 slice_reduce_fusion.1
  595.9 1.5 fusion.28
  (241 shorter events, 38.0 us)
Async XLA Ops:
  7.2 20.8 %copy-start = (bf16[32,6144]{1,0:T(8,128)(2,1)S(1)}, bf16[32,6144]{1,0:T(8,128)(2,1)}, u32[]{:S(2)}) copy-start(bf16[32,6144]{1,0:T(8,128)(2,1)} %param.21) | copy-start | bytes 1179652
  7.2 82.3 %all-gather.3.cloned.1.call-start = ((), (), s32[]{:S(2)}) async-start(), calls=%async_computation.1 | async-start | bytes 6488064 | tf_op jit(solution)/shard_map/all_gather | solution.py:792
  8.9 202.3 %all-gather.5.cloned.1.call-start = ((), (), s32[]{:S(2)}) async-start(), calls=%async_computation.2 | async-start | bytes 10813440 | tf_op jit(solution)/shard_map/all_gather | solution.py:796
  9.0 14.7 %collective-permute-start.1 = (s32[2]{0:T(128)}, s32[2]{0:T(128)S(1)}, u32[]{:S(2)}, u32[]{:S(2)}) collective-permute-start(s32[2]{0:T(128)} %param.20), channel_id=1, source_target_pairs={{0,8},{4,12},{8,16},{12,20},{16,24},{20,28},{24,0},{28,4},{1,9},{5... | collective-permute-start | bytes 32 | tf_op jit(solution)/shard_map/ppermute | solution.py:693
  12.0 11.7 %collective-permute-start.3 = (s32[2]{0:T(128)}, s32[2]{0:T(128)S(1)}, u32[]{:S(2)}, u32[]{:S(2)}) collective-permute-start(s32[2]{0:T(128)} %param.20), channel_id=1, source_target_pairs={{0,24},{4,28},{8,0},{12,4},{16,8},{20,12},{24,16},{28,20},{1,25},{... | collective-permute-start | bytes 32 | tf_op jit(solution)/shard_map/ppermute | solution.py:693
  14.1 9.6 %collective-permute-start.2 = (s32[2]{0:T(128)}, s32[2]{0:T(128)S(1)}, u32[]{:S(2)}, u32[]{:S(2)}) collective-permute-start(s32[2]{0:T(128)} %param.20), channel_id=1, source_target_pairs={{0,16},{4,20},{8,24},{12,28},{16,0},{20,4},{24,8},{28,12},{1,17},{... | collective-permute-start | bytes 32 | tf_op jit(solution)/shard_map/ppermute | solution.py:693
  15.1 5.4 copy-start.18
  19.0 2.6 copy-start.19
  19.0 2.7 copy-start.20
  19.0 51.4 %collective-permute-start = (bf16[768,1024]{1,0:T(8,128)(2,1)}, bf16[768,1024]{1,0:T(8,128)(2,1)}, u32[]{:S(2)}, u32[]{:S(2)}) collective-permute-start(bf16[768,1024]{1,0:T(8,128)(2,1)} %get-tuple-element.183), channel_id=1, source_target_pairs={{0,2},{1,3},{2,0},{3,1},{4,6},{5,7},{6,4},{7,5},{8,10},{9,11},{10,... | collective-permute-start | bytes 4718600 | tf_op jit(solution)/shard_map/ppermute | solution.py:693
  20.9 2.4 copy-start.30
  20.9 2.5 copy-start.31
  20.9 2.6 copy-start.24
  20.9 2.8 copy-start.25
  22.4 492.2 %reduce-scatter.2.cloned.1.call-start = ((), (), s32[]{:S(2)}) async-start(), calls=%async_computation.3 | async-start | bytes 10813440 | tf_op jit(solution)/shard_map/reduce_scatter | solution.py:856
  23.8 3.6 collective-permute-start.4
  28.6 5.6 copy-start.32
  30.4 10.0 %collective-permute-start.5 = (f32[4,2,13312]{2,1,0:T(2,128)}, f32[4,2,13312]{2,1,0:T(2,128)}, u32[]{:S(2)}, u32[]{:S(2)}) collective-permute-start(f32[4,2,13312]{2,1,0:T(2,128)} %squeeze.84), channel_id=1, source_target_pairs={{0,4},{4,0},{8,12},{12,8},{16,20},{20,16},{24,28},{28,24},{1,5},{5... | collective-permute-start | bytes 1277960 | tf_op jit(solution)/shard_map/ppermute | solution.py:761
  34.1 35.6 %copy-start.9 = (f32[32,3072]{1,0:T(8,128)}, f32[32,3072]{1,0:T(8,128)S(1)}, u32[]{:S(2)}) copy-start(f32[32,3072]{1,0:T(8,128)S(1)} %get-tuple-element.99.refs_6_) | copy-start | bytes 1179652
  36.0 22.4 %copy-start.4 = (bf16[2,768,1024]{2,1,0:T(8,128)(2,1)S(1)}, bf16[2,768,1024]{2,1,0:T(8,128)(2,1)}, u32[]{:S(2)}) copy-start(bf16[2,768,1024]{2,1,0:T(8,128)(2,1)} %param.35) | copy-start | bytes 9437188
  41.9 7.0 %collective-permute-start.6 = (f32[2,13312]{1,0:T(2,128)S(1)}, f32[2,13312]{1,0:T(2,128)S(1)}, u32[]{:S(2)}, u32[]{:S(2)}) collective-permute-start(f32[2,13312]{1,0:T(2,128)S(1)} %get-tuple-element.192), channel_id=1, source_target_pairs={{0,24},{4,28},{8,0},{12,4},{16,8},{20,12},{24,16},{28,20},{1,25},{... | collective-permute-start | bytes 319496 | tf_op jit(solution)/shard_map/ppermute | solution.py:693
  43.2 10.1 %collective-permute-start.8 = (f32[2,13312]{1,0:T(2,128)S(1)}, f32[2,13312]{1,0:T(2,128)S(1)}, u32[]{:S(2)}, u32[]{:S(2)}) collective-permute-start(f32[2,13312]{1,0:T(2,128)S(1)} %get-tuple-element.193), channel_id=1, source_target_pairs={{0,8},{4,12},{8,16},{12,20},{16,24},{20,28},{24,0},{28,4},{1,9},{5... | collective-permute-start | bytes 319496 | tf_op jit(solution)/shard_map/ppermute | solution.py:693
  44.2 13.5 %collective-permute-start.7 = (f32[2,13312]{1,0:T(2,128)S(1)}, f32[2,13312]{1,0:T(2,128)S(1)}, u32[]{:S(2)}, u32[]{:S(2)}) collective-permute-start(f32[2,13312]{1,0:T(2,128)S(1)} %get-tuple-element.194), channel_id=1, source_target_pairs={{0,16},{4,20},{8,24},{12,28},{16,0},{20,4},{24,8},{28,12},{1,17},{... | collective-permute-start | bytes 319496 | tf_op jit(solution)/shard_map/ppermute | solution.py:693
  57.8 4.8 collective-permute-start.9
  62.7 5.6 collective-permute-start.10
  66.0 2.9 copy-start.10
  89.5 14.5 %copy-start.6 = (bf16[768,1024]{1,0:T(8,128)(2,1)S(1)}, bf16[768,1024]{1,0:T(8,128)(2,1)}, u32[]{:S(2)}) copy-start(bf16[768,1024]{1,0:T(8,128)(2,1)} %get-tuple-element.110) | copy-start | bytes 4718596
  103.1 11.0 %collective-permute-start.13 = (bf16[512,1536]{1,0:T(8,128)(2,1)}, bf16[512,1536]{1,0:T(8,128)(2,1)}, u32[]{:S(2)}, u32[]{:S(2)}) collective-permute-start(bf16[512,1536]{1,0:T(8,128)(2,1)} %get-tuple-element.105.refs_2_.refs_7_), channel_id=1, source_target_pairs={{0,1},{1,0},{2,3},{3,2},{4,5},{5,4},{6,7},{7,6},{8,9},{9,8},{10,11... | collective-permute-start | bytes 4718600 | tf_op jit(solution)/shard_map/ppermute | solution.py:841
  103.4 10.7 %collective-permute-start.14 = (bf16[512,1536]{1,0:T(8,128)(2,1)}, bf16[512,1536]{1,0:T(8,128)(2,1)}, u32[]{:S(2)}, u32[]{:S(2)}) collective-permute-start(bf16[512,1536]{1,0:T(8,128)(2,1)} %get-tuple-element.106.refs_4_.refs_9_), channel_id=1, source_target_pairs={{0,1},{1,0},{2,3},{3,2},{4,5},{5,4},{6,7},{7,6},{8,9},{9,8},{10,11... | collective-permute-start | bytes 4718600 | tf_op jit(solution)/shard_map/ppermute | solution.py:841
  103.7 59.1 %collective-permute-start.11 = (bf16[512,1536]{1,0:T(8,128)(2,1)}, bf16[512,1536]{1,0:T(8,128)(2,1)}, u32[]{:S(2)}, u32[]{:S(2)}) collective-permute-start(bf16[512,1536]{1,0:T(8,128)(2,1)} %get-tuple-element.102.refs_2_.refs_7_), channel_id=1, source_target_pairs={{0,1},{1,0},{2,3},{3,2},{4,5},{5,4},{6,7},{7,6},{8,9},{9,8},{10,11... | collective-permute-start | bytes 4718600 | tf_op jit(solution)/shard_map/ppermute | solution.py:841
  103.9 107.3 %collective-permute-start.15 = (bf16[768,1024]{1,0:T(8,128)(2,1)S(1)}, bf16[768,1024]{1,0:T(8,128)(2,1)}, u32[]{:S(2)}, u32[]{:S(2)}) collective-permute-start(bf16[768,1024]{1,0:T(8,128)(2,1)S(1)} %copy-done.6), channel_id=1, source_target_pairs={{0,2},{1,3},{2,0},{3,1},{4,6},{5,7},{6,4},{7,5},{8,10},{9,11},{10,... | collective-permute-start | bytes 4718600 | tf_op jit(solution)/shard_map/ppermute | solution.py:693
  105.3 57.4 %collective-permute-start.12 = (bf16[512,1536]{1,0:T(8,128)(2,1)}, bf16[512,1536]{1,0:T(8,128)(2,1)}, u32[]{:S(2)}, u32[]{:S(2)}) collective-permute-start(bf16[512,1536]{1,0:T(8,128)(2,1)} %get-tuple-element.103.refs_4_.refs_9_), channel_id=1, source_target_pairs={{0,1},{1,0},{2,3},{3,2},{4,5},{5,4},{6,7},{7,6},{8,9},{9,8},{10,11... | collective-permute-start | bytes 4718600 | tf_op jit(solution)/shard_map/ppermute | solution.py:841
  379.7 45.4 %collective-permute-start.16 = (bf16[512,1536]{1,0:T(8,128)(2,1)}, bf16[512,1536]{1,0:T(8,128)(2,1)S(1)}, u32[]{:S(2)}, u32[]{:S(2)}) collective-permute-start(bf16[512,1536]{1,0:T(8,128)(2,1)} %get-tuple-element.122), channel_id=1, source_target_pairs={{0,1},{1,0},{2,3},{3,2},{4,5},{5,4},{6,7},{7,6},{8,9},{9,8},{10,11... | collective-permute-start | bytes 4718600 | tf_op jit(solution)/shard_map/ppermute | solution.py:888
  380.4 44.8 %collective-permute-start.17 = (bf16[512,1536]{1,0:T(8,128)(2,1)}, bf16[512,1536]{1,0:T(8,128)(2,1)}, u32[]{:S(2)}, u32[]{:S(2)}) collective-permute-start(bf16[512,1536]{1,0:T(8,128)(2,1)} %get-tuple-element.124), channel_id=1, source_target_pairs={{0,1},{1,0},{2,3},{3,2},{4,5},{5,4},{6,7},{7,6},{8,9},{9,8},{10,11... | collective-permute-start | bytes 4718600 | tf_op jit(solution)/shard_map/ppermute | solution.py:889
  438.4 46.1 %collective-permute-start.18 = (bf16[512,1536]{1,0:T(8,128)(2,1)}, bf16[512,1536]{1,0:T(8,128)(2,1)S(1)}, u32[]{:S(2)}, u32[]{:S(2)}) collective-permute-start(bf16[512,1536]{1,0:T(8,128)(2,1)} %get-tuple-element.126), channel_id=1, source_target_pairs={{0,1},{1,0},{2,3},{3,2},{4,5},{5,4},{6,7},{7,6},{8,9},{9,8},{10,11... | collective-permute-start | bytes 4718600 | tf_op jit(solution)/shard_map/ppermute | solution.py:761
  438.9 75.7 %collective-permute-start.24 = (bf16[768,1024]{1,0:T(8,128)(2,1)}, bf16[768,1024]{1,0:T(8,128)(2,1)}, u32[]{:S(2)}, u32[]{:S(2)}) collective-permute-start(bf16[768,1024]{1,0:T(8,128)(2,1)} %get-tuple-element.145), channel_id=1, source_target_pairs={{0,2},{1,3},{2,0},{3,1},{4,6},{5,7},{6,4},{7,5},{8,10},{9,11},{10,... | collective-permute-start | bytes 4718600 | tf_op jit(solution)/shard_map/ppermute | solution.py:693
  439.3 49.6 %collective-permute-start.19 = (bf16[256,1536]{1,0:T(8,128)(2,1)}, bf16[256,1536]{1,0:T(8,128)(2,1)}, u32[]{:S(2)}, u32[]{:S(2)}) collective-permute-start(bf16[256,1536]{1,0:T(8,128)(2,1)} %get-tuple-element.132), channel_id=1, source_target_pairs={{0,1},{1,0},{2,3},{3,2},{4,5},{5,4},{6,7},{7,6},{8,9},{9,8},{10,11... | collective-permute-start | bytes 2359304 | tf_op jit(solution)/shard_map/ppermute | solution.py:888
  439.3 51.2 %collective-permute-start.21 = (bf16[256,1536]{1,0:T(8,128)(2,1)}, bf16[256,1536]{1,0:T(8,128)(2,1)}, u32[]{:S(2)}, u32[]{:S(2)}) collective-permute-start(bf16[256,1536]{1,0:T(8,128)(2,1)} %get-tuple-element.137), channel_id=1, source_target_pairs={{0,1},{1,0},{2,3},{3,2},{4,5},{5,4},{6,7},{7,6},{8,9},{9,8},{10,11... | collective-permute-start | bytes 2359304 | tf_op jit(solution)/shard_map/ppermute | solution.py:889
  484.4 6.1 %collective-permute-start.20 = (bf16[256,1536]{1,0:T(8,128)(2,1)}, bf16[256,1536]{1,0:T(8,128)(2,1)}, u32[]{:S(2)}, u32[]{:S(2)}) collective-permute-start(bf16[256,1536]{1,0:T(8,128)(2,1)} %get-tuple-element.134), channel_id=1, source_target_pairs={{0,1},{1,0},{2,3},{3,2},{4,5},{5,4},{6,7},{7,6},{8,9},{9,8},{10,11... | collective-permute-start | bytes 2359304 | tf_op jit(solution)/shard_map/ppermute | solution.py:888
  484.5 6.0 collective-permute-start.22
  488.9 25.7 %collective-permute-start.35 = (bf16[8,32,1536]{2,1,0:T(8,128)(2,1)}, bf16[8,32,1536]{2,1,0:T(8,128)(2,1)}, u32[]{:S(2)}, u32[]{:S(2)}) collective-permute-start(bf16[8,32,1536]{2,1,0:T(8,128)(2,1)} %dynamic-slice_bitcast_fusion.4), channel_id=1, source_target_pairs={{0,2},{1,3},{2,0},{3,1},{4,6},{5,7},{6,4},{7,5},{8,10},{9,11},{10,... | collective-permute-start | bytes 2359304 | tf_op jit(solution)/shard_map/ppermute | solution.py:693
  503.3 8.1 %copy-start.17 = (f32[512,128]{1,0:T(8,128)S(1)}, f32[512,128]{1,0:T(8,128)}, u32[]{:S(2)}) copy-start(f32[512,128]{1,0:T(8,128)} %get-tuple-element.159) | copy-start | bytes 786436
  511.2 15.2 %collective-permute-start.23 = (bf16[512,768]{1,0:T(8,128)(2,1)}, bf16[512,768]{1,0:T(8,128)(2,1)}, u32[]{:S(2)}, u32[]{:S(2)}) collective-permute-start(bf16[512,768]{1,0:T(8,128)(2,1)} %get-tuple-element.143), channel_id=1, source_target_pairs={{0,1},{1,0},{2,3},{3,2},{4,5},{5,4},{6,7},{7,6},{8,9},{9,8},{10,11... | collective-permute-start | bytes 2359304 | tf_op jit(solution)/shard_map/ppermute | solution.py:761
  512.6 16.6 %collective-permute-start.26 = (bf16[256,1024]{1,0:T(8,128)(2,1)}, bf16[256,1024]{1,0:T(8,128)(2,1)}, u32[]{:S(2)}, u32[]{:S(2)}) collective-permute-start(bf16[256,1024]{1,0:T(8,128)(2,1)} %get-tuple-element.151), channel_id=1, source_target_pairs={{0,2},{1,3},{2,0},{3,1},{4,6},{5,7},{6,4},{7,5},{8,10},{9,11},{10,... | collective-permute-start | bytes 1572872 | tf_op jit(solution)/shard_map/ppermute | solution.py:693
  513.0 36.5 %collective-permute-start.27 = (bf16[512,1024]{1,0:T(8,128)(2,1)}, bf16[512,1024]{1,0:T(8,128)(2,1)}, u32[]{:S(2)}, u32[]{:S(2)}) collective-permute-start(bf16[512,1024]{1,0:T(8,128)(2,1)} %get-tuple-element.162), channel_id=1, source_target_pairs={{0,2},{1,3},{2,0},{3,1},{4,6},{5,7},{6,4},{7,5},{8,10},{9,11},{10,... | collective-permute-start | bytes 3145736 | tf_op jit(solution)/shard_map/ppermute | solution.py:693
  522.5 3.9 copy-start.11
  522.5 5.2 collective-permute-start.25
  524.9 2.8 copy-start.12
  524.9 33.9 %collective-permute-start.36 = (bf16[4,32,1536]{2,1,0:T(8,128)(2,1)S(1)}, bf16[4,32,1536]{2,1,0:T(8,128)(2,1)}, u32[]{:S(2)}, u32[]{:S(2)}) collective-permute-start(bf16[4,32,1536]{2,1,0:T(8,128)(2,1)S(1)} %dynamic-slice_bitcast_fusion.6), channel_id=1, source_target_pairs={{0,4},{4,0},{8,12},{12,8},{16,20},{20,16},{24,28},{28,24},{1,5},{5... | collective-permute-start | bytes 1179656 | tf_op jit(solution)/shard_map/ppermute | solution.py:761
  530.2 23.5 %collective-permute-start.29 = (bf16[4,2,32,1536]{3,2,1,0:T(8,128)(2,1)}, bf16[4,2,32,1536]{3,2,1,0:T(8,128)(2,1)}, u32[]{:S(2)}, u32[]{:S(2)}) collective-permute-start(bf16[4,2,32,1536]{3,2,1,0:T(8,128)(2,1)} %dynamic-slice_bitcast_fusion.5), channel_id=1, source_target_pairs={{0,4},{4,0},{8,12},{12,8},{16,20},{20,16},{24,28},{28,24},{1,5},{5... | collective-permute-start | bytes 2359304 | tf_op jit(solution)/shard_map/ppermute | solution.py:761
  531.8 12.8 %copy-start.21 = (f32[8,1024]{1,0:T(8,128)S(1)}, f32[8,1024]{1,0:T(8,128)}, u32[]{:S(2)}) copy-start(f32[8,1024]{1,0:T(8,128)} %get-tuple-element.158) | copy-start | bytes 98308
  549.5 4.1 collective-permute-start.28
  553.7 5.1 copy-start.3
  553.7 6.2 %copy-start.8 = (bf16[32,5120]{1,0:T(8,128)(2,1)S(1)}, bf16[32,5120]{1,0:T(8,128)(2,1)}, u32[]{:S(2)}) copy-start(bf16[32,5120]{1,0:T(8,128)(2,1)} %reduce-scatter.2.cloned.1.call-done) | copy-start | bytes 983044
  555.1 14.0 %collective-permute-start.32 = (f32[13,1024]{1,0:T(8,128)S(1)}, f32[13,1024]{1,0:T(8,128)S(1)}, u32[]{:S(2)}, u32[]{:S(2)}) collective-permute-start(f32[13,1024]{1,0:T(8,128)S(1)} %add.342), channel_id=1, source_target_pairs={{0,24},{4,28},{8,0},{12,4},{16,8},{20,12},{24,16},{28,20},{1,25},{... | collective-permute-start | bytes 159752 | tf_op jit(solution)/shard_map/ppermute | solution.py:693
  556.8 13.1 %collective-permute-start.31 = (f32[13,1024]{1,0:T(8,128)S(1)}, f32[13,1024]{1,0:T(8,128)S(1)}, u32[]{:S(2)}, u32[]{:S(2)}) collective-permute-start(f32[13,1024]{1,0:T(8,128)S(1)} %add.342), channel_id=1, source_target_pairs={{0,16},{4,20},{8,24},{12,28},{16,0},{20,4},{24,8},{28,12},{1,17},{... | collective-permute-start | bytes 159752 | tf_op jit(solution)/shard_map/ppermute | solution.py:693
  558.0 11.9 %collective-permute-start.30 = (f32[13,1024]{1,0:T(8,128)S(1)}, f32[13,1024]{1,0:T(8,128)S(1)}, u32[]{:S(2)}, u32[]{:S(2)}) collective-permute-start(f32[13,1024]{1,0:T(8,128)S(1)} %add.342), channel_id=1, source_target_pairs={{0,8},{4,12},{8,16},{12,20},{16,24},{20,28},{24,0},{28,4},{1,9},{5... | collective-permute-start | bytes 159752 | tf_op jit(solution)/shard_map/ppermute | solution.py:693
  561.6 16.4 %collective-permute-start.37 = (bf16[3,32,1536]{2,1,0:T(8,128)(2,1)}, bf16[3,32,1536]{2,1,0:T(8,128)(2,1)}, u32[]{:S(2)}, u32[]{:S(2)}) collective-permute-start(bf16[3,32,1536]{2,1,0:T(8,128)(2,1)} %get-tuple-element.185), channel_id=1, source_target_pairs={{0,8},{4,12},{8,16},{12,20},{16,24},{20,28},{24,0},{28,4},{1,9},{5... | collective-permute-start | bytes 884744 | tf_op jit(solution)/shard_map/ppermute | solution.py:693
  563.1 21.9 %collective-permute-start.38 = (bf16[3,32,1536]{2,1,0:T(8,128)(2,1)}, bf16[3,32,1536]{2,1,0:T(8,128)(2,1)}, u32[]{:S(2)}, u32[]{:S(2)}) collective-permute-start(bf16[3,32,1536]{2,1,0:T(8,128)(2,1)} %get-tuple-element.186), channel_id=1, source_target_pairs={{0,16},{4,20},{8,24},{12,28},{16,0},{20,4},{24,8},{28,12},{1,17},{... | collective-permute-start | bytes 884744 | tf_op jit(solution)/shard_map/ppermute | solution.py:693
  569.1 15.9 %collective-permute-start.39 = (bf16[3,32,1536]{2,1,0:T(8,128)(2,1)}, bf16[3,32,1536]{2,1,0:T(8,128)(2,1)S(1)}, u32[]{:S(2)}, u32[]{:S(2)}) collective-permute-start(bf16[3,32,1536]{2,1,0:T(8,128)(2,1)} %get-tuple-element.187), channel_id=1, source_target_pairs={{0,24},{4,28},{8,0},{12,4},{16,8},{20,12},{24,16},{28,20},{1,25},{... | collective-permute-start | bytes 884744 | tf_op jit(solution)/shard_map/ppermute | solution.py:693
  570.0 7.1 %collective-permute-start.33 = (f32[4,13,1024]{2,1,0:T(8,128)S(1)}, f32[4,13,1024]{2,1,0:T(8,128)S(1)}, u32[]{:S(2)}, u32[]{:S(2)}) collective-permute-start(f32[4,13,1024]{2,1,0:T(8,128)S(1)} %get-tuple-element.199), channel_id=1, source_target_pairs={{0,4},{4,0},{8,12},{12,8},{16,20},{20,16},{24,28},{28,24},{1,5},{5... | collective-permute-start | bytes 638984 | tf_op jit(solution)/shard_map/ppermute | solution.py:761
  577.3 16.5 %collective-permute-start.34 = (f32[55,1024]{1,0:T(8,128)S(1)}, f32[55,1024]{1,0:T(8,128)S(1)}, u32[]{:S(2)}, u32[]{:S(2)}) collective-permute-start(f32[55,1024]{1,0:T(8,128)S(1)} %pad_maximum_fusion.6), channel_id=1, source_target_pairs={{0,2},{1,3},{2,0},{3,1},{4,6},{5,7},{6,4},{7,5},{8,10},{9,11},{10,... | collective-permute-start | bytes 675848 | tf_op jit(solution)/shard_map/ppermute | solution.py:693
  586.4 4.7 collective-permute-start.40
  595.0 4.9 copy-start.1
  (13 other events, 19.5 us)
Sparse Core Ops, SparseCore 0:
  11.5 77.9 all-gather.2
  92.3 94.9 all-gather.4
  293.7 151.6 reduce-scatter.1
